TPU v7x, 32 devices: a whole 2x2x4 slice. The times are simulated.
32 devices in a mesh: parts: 2 (over x), seg: 2 (over core), sec: 8 (over z, y).
Axes of the slice: x: 2, y: 2, z: 4, core: 2. Of those that a mesh axis runs over, the one named last changes fastest.
Arguments:
- initial_state: bfloat16 [4, 16, 128, 128], P(('parts', 'seg'), 'sec'), parts along dimension 0, may hold values from -6 to 6
- left_blocks: bfloat16 [4, 16, 24, 128, 128], P(('parts', 'seg'), 'sec'), parts along dimension 0, may hold values from -2 to 3
- right_blocks: bfloat16 [4, 16, 24, 128, 128], P(('parts', 'seg'), 'sec'), parts along dimension 0, may hold values from -2 to 3
- sources: int32 [4, 16, 32], P(('parts', 'seg'), 'sec'), parts along dimension 0, may hold values from 0 to 15, as said below
- channels: int32 [4, 16, 32], P(('parts', 'seg'), 'sec'), parts along dimension 0, may hold values from 0 to 23
- couplings: float32 [4, 16, 32], P(('parts', 'seg'), 'sec'), parts along dimension 0, may hold values from -1 to 6
- kept_rank: int32 [4, 16], P(('parts', 'seg'), 'sec'), parts along dimension 0, may hold values from 32 to 128
Outputs:
- kept_state: bfloat16 [4, 16, 128, 128], P(('parts', 'seg'), 'sec'), parts along dimension 0
- energies: float32 [4, 3], P(('parts', 'seg')), parts along dimension 0
There are 2 independent parts, one for each index of `parts`. A program takes and returns all parts, laid end to end along the dimension named above; each array names one. Nothing has to cross between parts.
Inputs may be any that keep to these rules, and one draw needn't show every extreme that they name: `sources`: pair 0 of block t has source t. Block t keeps its first kept_rank columns.
All inputs are finite; a program needn't handle non-finite values.
Results may differ from a plain program's by a relative error of at most 0.017.
Values may be sent and summed in bfloat16 or wider, within the bound.
No kernel may reach another device: no remote copies, remote signals or barrier semaphores. Data moves between devices by JAX's collectives and lax.ppermute only.
A program may use at most 64 MiB of HBM per device.

v0:
```python
import jax
import jax.numpy as jnp
from jax import lax
from jax.sharding import PartitionSpec as P

ITERS = 3


step_length = 0.5
epsilon = 1e-06


def partner(block, axis, apart):
    count = lax.axis_size(axis)
    route = []
    for low in range(count):
        high = low | 1 << apart
        if high != low and high < count:
            route += [(low, high), (high, low)]
    return lax.ppermute(block, axis, route)


def local(initial_state, left_blocks, right_blocks, sources, channels, couplings, kept_rank):
    start_state = initial_state[0]
    left_env = left_blocks[0]
    right_env = partner(right_blocks[0], "seg", 0)
    local_count = start_state.shape[0]
    block_size = start_state.shape[1]
    mpo_width = left_env.shape[1]
    sectors = local_count * lax.axis_size("sec")
    entries = float(sectors * block_size * block_size)
    channel_ids = jnp.arange(mpo_width, dtype=jnp.int32)
    source_here = sources[0]
    coupling_here = couplings[0]
    channel_table = (channels[0][..., None] == channel_ids).astype(jnp.float32)

    def add_piece(shards):
        rows_here = shards.shape[0]
        flattened = shards.reshape(rows_here, block_size * block_size).astype(jnp.float32)
        inside = (source_here >= 0) & (source_here < rows_here)
        picked = jnp.take(flattened, jnp.clip(source_here, 0, rows_here - 1), axis=0)
        scaled = picked * jnp.where(inside, coupling_here, jnp.float32(0.0))[..., None]
        return jnp.einsum("tkw,tkx->twx", channel_table, scaled, precision=lax.Precision.HIGHEST)

    mixture = add_piece(lax.all_gather(start_state, "sec", axis=0, tiled=True))
    current = start_state.astype(jnp.float32)
    energy_list = []
    for iteration in range(ITERS):
        mixed_half = mixture.reshape(local_count, mpo_width, block_size, block_size).astype(
            jnp.bfloat16
        )
        partial_value = jnp.einsum(
            "twij,twjk->twik", left_env, mixed_half, preferred_element_type=jnp.float32
        ).astype(jnp.bfloat16)
        image_half = jnp.einsum(
            "twik,twlk->til", partial_value, right_env, preferred_element_type=jnp.float32
        ).astype(jnp.bfloat16)
        image = image_half.astype(jnp.float32)
        intersection, squares = lax.psum(
            (jnp.sum(current * image), jnp.sum(current * current)), "sec"
        )
        energy = intersection / squares
        growth = 1.0 + step_length * energy
        following = growth * current - step_length * image
        if iteration + 1 < ITERS:
            mixture = add_piece(
                lax.all_gather(following.astype(jnp.bfloat16), "sec", axis=0, tiled=True).astype(
                    jnp.float32
                )
            )
        current = following
        energy_list.append(energy)
    column_ids = jnp.arange(block_size, dtype=jnp.int32)
    keep_mask = column_ids[None, None, :] < kept_rank[0][:, None, None]
    truncated = jnp.where(keep_mask, current, jnp.float32(0.0))
    kept_sq = lax.psum(jnp.sum(truncated * truncated), "sec")
    kept_state = (truncated / jnp.sqrt(kept_sq / entries + epsilon)).astype(jnp.bfloat16)
    return (kept_state[None], jnp.stack(energy_list)[None, :])


def solution(mesh):
    return jax.shard_map(
        local,
        mesh=mesh,
        in_specs=(
            P(("parts", "seg"), "sec", None, None),
            P(("parts", "seg"), "sec", None, None, None),
            P(("parts", "seg"), "sec", None, None, None),
            P(("parts", "seg"), "sec", None),
            P(("parts", "seg"), "sec", None),
            P(("parts", "seg"), "sec", None),
            P(("parts", "seg"), "sec"),
        ),
        out_specs=(P(("parts", "seg"), "sec", None, None), P(("parts", "seg"), None)),
        check_vma=False,
    )
```

profile of v0, /device:TPU:0, one launch (start us, length us, event | category | flops | bytes accessed | tf_op | source)
XLA Modules:
  0.0 219.7 jit_solution(3080306980475488546)
XLA Ops:
  0.6 0.0 copy-start
  0.6 0.5 collective-permute-start
  1.2 0.7 compare_select_fusion
  1.8 0.1 reshape.123
  1.9 33.2 %all-gather = bf16[1,16,128,128]{3,2,0,1:T(8,128)(2,1)S(1)} all-gather(bf16[1,2,128,128]{3,2,0,1:T(8,128)(2,1)} %bitcast.229), channel_id=2, replica_groups=mesh['parts'=2,'seg'=2,'sec'=8] {'sec'}, dimensions={1}, use_global_device_ids=true | all-gather | bytes 589824 | tf_op jit(solution)/shard_map/all_gather | solution.py:45
  35.2 0.3 copy.24
  35.5 0.0 copy-start.3
  35.5 0.0 copy-start.4
  35.5 0.0 copy-start.2
  35.5 3.6 %gather_fusion = f32[64,16384]{1,0:T(8,128)} fusion(f32[16,16384]{1,0:T(8,128)S(1)} %bitcast.214, s32[1024]{0:T(1024)S(1)} %pad_clamp_fusion), kind=kCustom, calls=%fused_computation.clone | custom fusion | bytes 8388864 | tf_op jit(solution)/shard_map/jit(_take)/gather | solution.py:41
  39.1 0.0 copy-done.3
  39.2 0.0 copy-done.4
  39.2 0.0 copy-done.2
  39.2 4.5 %convolution_convert_fusion.2 = bf16[2,24,16384]{2,1,0:T(8,128)(2,1)S(1)} fusion(f32[2,32,16384]{2,1,0:T(8,128)} %bitcast.218, f32[2,32]{1,0:T(2,128)S(1)} %fusion.115, pred[2,32]{1,0:T(4,128)(4,1)S(1)} %compare_and_fusion, s32[2,32]{1,0:T(2,128)S(1)} %bitcast.230), kind=kOutput, calls=%fused_computation.5 | convolution fusion | flops 304875008 | bytes 5767744 | tf_op jit(solution)/shard_map/tkw,tkx->twx/dot_general | solution.py:43
  43.7 0.0 copy-start.5
  43.7 0.0 copy-start.1
  43.7 0.4 copy.14
  44.1 0.2 copy-done.5
  44.3 0.1 iota_compare_fusion.4
  44.4 0.0 collective-permute-done
  44.4 0.0 copy-done
  44.4 0.1 copy-done.1
  44.5 3.2 %fusion.109 = (f32[]{:T(128)}, f32[]{:T(128)}, f32[2,128,128]{2,1,0:T(8,128)S(1)}) fusion(bf16[1,2,128,128]{3,2,1,0:T(8,128)(2,1)S(1)} %copy-done.1, bf16[2,24,128,128]{3,2,1,0:T(8,128)(2,1)} %collective-permute-done, bf16[1,2,24,128,128]{4,3,2,1,0:T(8,128)(2,1)S(1)} %copy-done, bf16[2,24,128,128]{3,2,1,0:T(8,128)(2,1)S(1)} %bitcast.220), kind=kOutput, calls=%fused_computation.49 | convolution fusion | flops 403668992 | bytes 4915208 | tf_op jit(solution)/shard_map/twik,twlk->til/dot_general | solution.py:55
  47.7 21.8 %all-reduce.2 = (f32[]{:T(128)}, f32[]{:T(128)}) all-reduce(f32[]{:T(128)} %get-tuple-element.8, f32[]{:T(128)} %get-tuple-element.7), channel_id=1, replica_groups=mesh['parts'=2,'seg'=2,'sec'=8] {'sec'}, use_global_device_ids=true, to_apply=%region_1.3 | all-reduce | flops 2 | bytes 16 | tf_op jit(solution)/shard_map/psum | solution.py:59
  70.8 31.2 %all_gather.10 = bf16[16,128,128]{2,1,0:T(8,128)(2,1)S(1)} all-gather(bf16[2,128,128]{2,1,0:T(8,128)(2,1)S(1)} %fusion.119), channel_id=1, replica_groups=mesh['parts'=2,'seg'=2,'sec'=8] {'sec'}, dimensions={0}, use_global_device_ids=true | all-gather | bytes 589824 | tf_op jit(solution)/shard_map/all_gather | solution.py:67
  102.0 0.3 copy.23
  102.3 3.6 %gather_fusion.1 = f32[64,16384]{1,0:T(8,128)} fusion(f32[16,16384]{1,0:T(8,128)S(1)} %bitcast.216, s32[1024]{0:T(1024)S(1)} %pad_clamp_fusion), kind=kCustom, calls=%fused_computation.1.clone | custom fusion | bytes 8388864 | tf_op jit(solution)/shard_map/jit(_take)/gather | solution.py:41
  106.0 4.5 %convolution_convert_fusion.1 = bf16[2,24,16384]{2,1,0:T(8,128)(2,1)S(1)} fusion(f32[2,32,16384]{2,1,0:T(8,128)} %bitcast.219, f32[2,32]{1,0:T(2,128)S(1)} %fusion.115, pred[2,32]{1,0:T(4,128)(4,1)S(1)} %compare_and_fusion, s32[2,32]{1,0:T(2,128)S(1)} %bitcast.231), kind=kOutput, calls=%fused_computation.4 | convolution fusion | flops 304875008 | bytes 5767744 | tf_op jit(solution)/shard_map/tkw,tkx->twx/dot_general | solution.py:43
  110.4 0.4 copy.16
  110.8 3.8 %multiply_reduce_fusion.3 = (f32[]{:T(128)}, f32[]{:T(128)}, f32[2,128,128]{2,1,0:T(8,128)}) fusion(f32[2,128,128]{2,1,0:T(8,128)S(1)} %get-tuple-element.17, bf16[1,2,128,128]{3,2,1,0:T(8,128)(2,1)S(1)} %copy-done.1, f32[]{:T(128)S(6)} %add.32, bf16[2,24,128,128]{3,2,1,0:T(8,128)(2,1)} %collective-permute-done, ...), kind=kOutput, calls=%fused_computation.57 | convolution fusion | flops 403767296 | bytes 5046284 | tf_op jit(solution)/shard_map/twik,twlk->til/dot_general | solution.py:55
  114.6 18.0 %all-reduce.1 = (f32[]{:T(128)}, f32[]{:T(128)}) all-reduce(f32[]{:T(128)} %get-tuple-element.4, f32[]{:T(128)} %get-tuple-element.3), channel_id=1, replica_groups=mesh['parts'=2,'seg'=2,'sec'=8] {'sec'}, use_global_device_ids=true, to_apply=%region_5.7 | all-reduce | flops 2 | bytes 16 | tf_op jit(solution)/shard_map/psum | solution.py:59
  134.0 0.9 fusion.120
  134.9 31.4 %all_gather.11 = bf16[16,128,128]{2,1,0:T(8,128)(2,1)S(1)} all-gather(bf16[2,128,128]{2,1,0:T(8,128)(2,1)S(1)} %get-tuple-element.15), channel_id=1, replica_groups=mesh['parts'=2,'seg'=2,'sec'=8] {'sec'}, dimensions={0}, use_global_device_ids=true | all-gather | bytes 589824 | tf_op jit(solution)/shard_map/all_gather | solution.py:67
  166.3 0.3 copy.22
  166.6 3.6 %gather_fusion.2 = f32[64,16384]{1,0:T(8,128)} fusion(f32[16,16384]{1,0:T(8,128)S(1)} %bitcast.215, s32[1024]{0:T(1024)S(1)} %pad_clamp_fusion), kind=kCustom, calls=%fused_computation.2.clone | custom fusion | bytes 8388864 | tf_op jit(solution)/shard_map/jit(_take)/gather | solution.py:41
  170.2 4.5 %convolution_convert_fusion = bf16[2,24,16384]{2,1,0:T(8,128)(2,1)S(1)} fusion(f32[2,32,16384]{2,1,0:T(8,128)} %bitcast.217, f32[2,32]{1,0:T(2,128)S(1)} %fusion.115, pred[2,32]{1,0:T(4,128)(4,1)S(1)} %compare_and_fusion, s32[2,32]{1,0:T(2,128)S(1)} %bitcast.232), kind=kOutput, calls=%fused_computation.3 | convolution fusion | flops 304875008 | bytes 5767744 | tf_op jit(solution)/shard_map/tkw,tkx->twx/dot_general | solution.py:43
  174.7 0.4 copy.18
  175.1 3.2 %multiply_reduce_fusion.1 = (f32[]{:T(128)}, f32[]{:T(128)}, f32[2,128,128]{2,1,0:T(8,128)S(1)}) fusion(f32[2,128,128]{2,1,0:T(8,128)S(1)} %get-tuple-element.16, bf16[2,24,128,128]{3,2,1,0:T(8,128)(2,1)} %collective-permute-done, bf16[1,2,24,128,128]{4,3,2,1,0:T(8,128)(2,1)S(1)} %copy-done, bf16[2,24,128,128]{3,2,1,0:T(8,128)(2,1)S(1)} %bitcast.221), kind=kOutput, calls=%fused_computation.54 | convolution fusion | flops 403636224 | bytes 4980744 | tf_op jit(solution)/shard_map/twik,twlk->til/dot_general | solution.py:55
  178.3 19.5 %all-reduce = (f32[]{:T(128)}, f32[]{:T(128)}) all-reduce(f32[]{:T(128)} %get-tuple-element.6, f32[]{:T(128)} %get-tuple-element.5), channel_id=1, replica_groups=mesh['parts'=2,'seg'=2,'sec'=8] {'sec'}, use_global_device_ids=true, to_apply=%region_9.11 | all-reduce | flops 2 | bytes 16 | tf_op jit(solution)/shard_map/psum | solution.py:59
  199.1 0.6 multiply_reduce_fusion
  199.8 18.0 %psum.55 = f32[]{:T(128)} all-reduce(f32[]{:T(128)} %multiply_reduce_fusion), channel_id=1, replica_groups=mesh['parts'=2,'seg'=2,'sec'=8] {'sec'}, use_global_device_ids=true, to_apply=%region_13.15 | all-reduce | flops 1 | bytes 8 | tf_op jit(solution)/shard_map/psum | solution.py:76
  218.4 0.7 fusion.111
  219.1 0.6 maximum_bitcast_fusion
  (4 shorter events, 0.0 us)
Async XLA Ops:
  0.6 43.8 %copy-start = (bf16[1,2,24,128,128]{4,3,2,1,0:T(8,128)(2,1)S(1)}, bf16[1,2,24,128,128]{4,3,2,1,0:T(8,128)(2,1)}, u32[]{:S(2)}) copy-start(bf16[1,2,24,128,128]{4,3,2,1,0:T(8,128)(2,1)} %param.10) | copy-start | bytes 4718596
  0.6 43.7 %collective-permute-start = (bf16[2,24,128,128]{3,2,1,0:T(8,128)(2,1)}, bf16[2,24,128,128]{3,2,1,0:T(8,128)(2,1)}, u32[]{:S(2)}, u32[]{:S(2)}) collective-permute-start(bf16[2,24,128,128]{3,2,1,0:T(8,128)(2,1)} %bitcast.233), channel_id=1, source_target_pairs={{0,8},{8,0},{1,9},{9,1},{2,10},{10,2},{3,11},{11,3},{4,12},{12,4},... | collective-permute-start | bytes 4718600 | tf_op jit(solution)/shard_map/ppermute | solution.py:20
  35.5 3.7 %copy-start.3 = (s32[1,2,32]{2,1,0:T(2,128)S(1)}, s32[1,2,32]{2,1,0:T(2,128)}, u32[]{:S(2)}) copy-start(s32[1,2,32]{2,1,0:T(2,128)} %param.12) | copy-start | bytes 772
  35.5 3.7 %copy-start.4 = (f32[1,2,32]{2,1,0:T(2,128)S(1)}, f32[1,2,32]{2,1,0:T(2,128)}, u32[]{:S(2)}) copy-start(f32[1,2,32]{2,1,0:T(2,128)} %param.14) | copy-start | bytes 772
  35.5 3.7 %copy-start.2 = (s32[1,2,32]{2,1,0:T(2,128)S(1)}, s32[1,2,32]{2,1,0:T(2,128)}, u32[]{:S(2)}) copy-start(s32[1,2,32]{2,1,0:T(2,128)} %param.13) | copy-start | bytes 772
  43.7 0.7 copy-start.5
  43.7 0.8 copy-start.1
where the time goes:
time: 220 us
  blocking collectives  173 us (79%)
  matrix products  23.5 us (11%)
  local copies, waits for them, and re-layouts  13.4 us (6%)
  between operations  5.5 us (2%)
  other arithmetic  3.63 us (2%)
    all_gather x2, blocking collectives, local(): lax.all_gather(following.astype(jnp.bfloat16), 'sec', axis=0, tiled=True)  62.6 us
    psum x3, blocking collectives, local(): lax.psum((jnp.sum(current * image), jnp.sum(current * current)), 'sec')  59.3 us
    all_gather x1, blocking collectives, local(): mixture = add_piece(lax.all_gather(start_state, 'sec', axis=0, tiled=True))  33.2 us
    psum x1, blocking collectives, local(): kept_sq = lax.psum(jnp.sum(truncated * truncated), 'sec')  18 us
    dot_general x3, matrix products, add_piece(): jnp.einsum('tkw,tkx->twx', channel_table, scaled, precision=lax.Precision...  13.4 us
    gather x3, local copies, waits for them, and re-layouts, add_piece(): jnp.take(flattened, jnp.clip(source_here, 0, rows_here - 1), axis=0)  10.9 us
    dot_general x3, matrix products, local(): jnp.einsum('twik,twlk->til', partial_value, right_env, preferred_element_...  10.1 us
  transfers between devices with their start and end apart: 1, of which 0 were waited for; matrix products, arithmetic and copies ran while one was open for 4% of the time, Pallas kernels for 0%

commit v1 on v0

v1 whole, which is shorter than its diff:
```python
import functools

import jax
import jax.numpy as jnp
from jax import lax
from jax.experimental import pallas as pl
from jax.experimental.pallas import tpu as pltpu
from jax.sharding import PartitionSpec as P

ITERS = 3
STEP = 0.5
EPSILON = 1e-06
SMEM = pl.BlockSpec(memory_space=pltpu.SMEM)
VMEM = pl.BlockSpec(memory_space=pltpu.VMEM)
NEAR = (0, 1, 2, 4, 6, 3, 5, 7)


def hop(block, distance):
    count = lax.axis_size("sec")
    return lax.ppermute(block, "sec", [(a, a ^ distance) for a in range(count)])


def gather(block):
    if lax.axis_size("sec") != len(NEAR):
        return [lax.all_gather(block, "sec", axis=0, tiled=True)]
    return [block] + [hop(block, distance) for distance in NEAR[1:]]


def slots(sector, local_count):
    if lax.axis_size("sec") != len(NEAR):
        return sector
    place = sorted(range(len(NEAR)), key=lambda position: NEAR[position])
    apart = (sector // local_count) ^ lax.axis_index("sec")
    found = sum(jnp.where(apart == d, place[d], 0) for d in range(len(NEAR)))
    return found * local_count + sector % local_count


def pair_table(sources, channels, couplings, local_count):
    k = jnp.arange(sources.shape[1], dtype=jnp.int32)
    before = (channels[:, None, :] < channels[:, :, None]) | (
        (channels[:, None, :] == channels[:, :, None]) & (k[None, None, :] < k[None, :, None])
    )
    rank = jnp.sum(before.astype(jnp.int32), axis=2)
    chosen = rank[:, None, :] == k[None, :, None]

    def ordered(values):
        return jnp.sum(jnp.where(chosen, values[:, None, :], jnp.zeros((), values.dtype)), axis=2)

    channel = ordered(channels)
    same = jnp.concatenate(
        [jnp.zeros_like(channel[:, :1]), (channel[:, 1:] == channel[:, :-1]).astype(jnp.int32)], axis=1
    )
    ints = jnp.stack([ordered(slots(sources, local_count)), channel, same], axis=1)
    return ints, ordered(couplings)


def apply_operator(ints, floats, state, left, right, mixed, image):
    blocks, width = left.shape[0], left.shape[1]
    pairs = floats.shape[1]
    mixed[...] = jnp.zeros_like(mixed)
    for t in range(blocks):
        total = jnp.zeros(state.shape[1:], jnp.float32)
        for k in range(pairs):
            term = floats[t, k] * state[ints[t, 0, k]]
            total = term + jnp.where(ints[t, 2, k] == 1, total, 0.0)
            mixed[t, ints[t, 1, k]] = total.astype(jnp.bfloat16)
    for t in range(blocks):
        result = jnp.zeros(image.shape[1:], jnp.float32)
        for w in range(0, width, 2):
            halves = [
                jnp.dot(left[t, v], mixed[t, v], preferred_element_type=jnp.float32).astype(jnp.bfloat16)
                for v in (w, w + 1)
            ]
            result += lax.dot_general(
                jnp.concatenate(halves, axis=1),
                jnp.concatenate([right[t, w], right[t, w + 1]], axis=1),
                (((1,), (1,)), ((), ())),
                preferred_element_type=jnp.float32,
            )
        image[t] = result.astype(jnp.bfloat16)


def spread(pieces, target):
    at = 0
    for piece in pieces:
        size = piece.shape[0]
        target[at : at + size] = piece[...].astype(jnp.float32)
        at += size


def first_kernel(count, ints, floats, left, right, *refs):
    pieces, (image, state, mixed) = refs[:count], refs[count:]
    spread(pieces, state)
    apply_operator(ints, floats, state, left, right, mixed, image)


def rayleigh_update(before, images, after):
    shape = before[0].shape[1:]
    intersection = jnp.zeros(shape, jnp.float32)
    squares = jnp.zeros(shape, jnp.float32)
    at = 0
    flat = []
    for piece in before:
        flat += [(piece, s) for s in range(piece.shape[0])]
    pictures = []
    for piece in images:
        pictures += [(piece, s) for s in range(piece.shape[0])]
    for (piece, s), (picture, p) in zip(flat, pictures):
        value = piece[s].astype(jnp.float32)
        intersection += value * picture[p].astype(jnp.float32)
        squares += value * value
    energy = jnp.sum(intersection) / jnp.sum(squares)
    growth = 1.0 + STEP * energy
    for (piece, s), (picture, p) in zip(flat, pictures):
        after[at] = growth * piece[s].astype(jnp.float32) - STEP * picture[p].astype(jnp.float32)
        at += 1
    return energy


def middle_kernel(states, count, ints, floats, left, right, *refs):
    before, images = refs[:states], refs[states : states + count]
    energy, state, image, mixed = refs[states + count :]
    energy[0, 0] = rayleigh_update(before, images, state)
    apply_operator(ints, floats, state, left, right, mixed, image)


def last_kernel(states, count, ints, floats, ranks, left, right, *refs):
    before, images = refs[:states], refs[states : states + count]
    energy, own, image, sums, state, mixed = refs[states + count :]
    energy[0, 0] = rayleigh_update(before, images, state)
    apply_operator(ints, floats, state, left, right, mixed, image)
    blocks, size = image.shape[0], image.shape[1]
    own[...] = state[:blocks]
    intersection = jnp.zeros((size, size), jnp.float32)
    squares = jnp.zeros((size, size), jnp.float32)
    for t in range(blocks):
        value = own[t]
        intersection += value * image[t].astype(jnp.float32)
        squares += value * value
    intersection, squares = jnp.sum(intersection), jnp.sum(squares)
    here = jnp.where(squares > 1e-30, intersection / jnp.maximum(squares, 1e-30), 0.0)
    growth = 1.0 + STEP * here
    column = lax.broadcasted_iota(jnp.int32, (size, size), 1)
    dd = jnp.zeros((size, size), jnp.float32)
    dc = jnp.zeros((size, size), jnp.float32)
    cc = jnp.zeros((size, size), jnp.float32)
    for t in range(blocks):
        keep = column < ranks[t]
        value = jnp.where(keep, own[t], 0.0)
        moved = growth * value - STEP * jnp.where(keep, image[t].astype(jnp.float32), 0.0)
        dd += moved * moved
        dc += moved * value
        cc += value * value
    row = lax.broadcasted_iota(jnp.int32, sums.shape, 1)
    result = jnp.zeros(sums.shape, jnp.float32)
    for at, number in enumerate([intersection, squares, here, jnp.sum(dd), jnp.sum(dc), jnp.sum(cc)]):
        result = jnp.where(row == at, number, result)
    sums[...] = result


def finish_kernel(count, entries, ranks, own, image, *refs):
    gathered, (energy, kept) = refs[:count], refs[count:]
    rows = []
    for piece in gathered:
        rows += [piece[s] for s in range(piece.shape[0])]
    intersection = sum(row[0:1, :] for row in rows)
    squares = sum(row[1:2, :] for row in rows)
    total = intersection / squares
    kept_sq = jnp.zeros_like(total)
    for row in rows:
        shift = STEP * (total - row[2:3, :])
        kept_sq += row[3:4, :] + 2.0 * shift * row[4:5, :] + shift * shift * row[5:6, :]
    energy[...] = jnp.broadcast_to(total, energy.shape)
    growth = 1.0 + STEP * total
    scale = 1.0 / jnp.sqrt(jnp.maximum(kept_sq, 0.0) / entries + EPSILON)
    size = image.shape[1]
    column = lax.broadcasted_iota(jnp.int32, (size, size), 1)
    for t in range(image.shape[0]):
        value = growth * own[t] - STEP * image[t].astype(jnp.float32)
        kept[t] = (jnp.where(column < ranks[t], value, 0.0) * scale).astype(jnp.bfloat16)


def local(initial_state, left_blocks, right_blocks, sources, channels, couplings, kept_rank):
    start = initial_state[0]
    left = left_blocks[0]
    right = lax.ppermute(right_blocks[0], "seg", [(0, 1), (1, 0)])
    blocks, size = start.shape[0], start.shape[1]
    width = left.shape[1]
    sectors = blocks * lax.axis_size("sec")
    entries = float(sectors * size * size)
    ranks = kept_rank[0]
    ints, floats = pair_table(sources[0], channels[0], couplings[0], blocks)

    own_type = jax.ShapeDtypeStruct((blocks, size, size), jnp.bfloat16)
    number = jax.ShapeDtypeStruct((1, 1), jnp.float32)
    whole = (sectors, size, size)
    mixed = pltpu.VMEM((blocks, width, size, size), jnp.bfloat16)
    params = pltpu.CompilerParams(vmem_limit_bytes=24 * 2**20)

    states = gather(start)
    image = pl.pallas_call(
        functools.partial(first_kernel, len(states)),
        out_shape=own_type,
        in_specs=[SMEM, SMEM] + [VMEM] * (2 + len(states)),
        out_specs=VMEM,
        scratch_shapes=[pltpu.VMEM(whole, jnp.float32), mixed],
        compiler_params=params,
        name="first_image",
    )(ints, floats, left, right, *states)
    energies = []
    for iteration in range(1, ITERS - 1):
        images = gather(image)
        energy, state, image = pl.pallas_call(
            functools.partial(middle_kernel, len(states), len(images)),
            out_shape=(number, jax.ShapeDtypeStruct(whole, jnp.float32), own_type),
            in_specs=[SMEM, SMEM] + [VMEM] * (2 + len(states) + len(images)),
            out_specs=(SMEM, VMEM, VMEM),
            scratch_shapes=[mixed],
            compiler_params=params,
            name="middle_image",
        )(ints, floats, left, right, *states, *images)
        states = [state]
        energies.append(energy)
    images = gather(image)
    energy, own, image, sums = pl.pallas_call(
        functools.partial(last_kernel, len(states), len(images)),
        out_shape=(
            number,
            jax.ShapeDtypeStruct((blocks, size, size), jnp.float32),
            own_type,
            jax.ShapeDtypeStruct((1, 8, 128), jnp.float32),
        ),
        in_specs=[SMEM, SMEM, SMEM] + [VMEM] * (2 + len(states) + len(images)),
        out_specs=(SMEM, VMEM, VMEM, VMEM),
        scratch_shapes=[pltpu.VMEM(whole, jnp.float32), mixed],
        compiler_params=params,
        name="last_image",
    )(ints, floats, ranks, left, right, *states, *images)
    energies.append(energy)
    gathered = gather(sums)
    energy, kept = pl.pallas_call(
        functools.partial(finish_kernel, len(gathered), entries),
        out_shape=(jax.ShapeDtypeStruct((1, 128), jnp.float32), own_type),
        in_specs=[SMEM] + [VMEM] * (2 + len(gathered)),
        out_specs=(VMEM, VMEM),
        compiler_params=params,
        name="finish",
    )(ranks, own, image, *gathered)
    energies.append(energy[:, :1])
    return kept[None], jnp.concatenate(energies, axis=1)


def solution(mesh):
    return jax.shard_map(
        local,
        mesh=mesh,
        in_specs=(
            P(("parts", "seg"), "sec", None, None),
            P(("parts", "seg"), "sec", None, None, None),
            P(("parts", "seg"), "sec", None, None, None),
            P(("parts", "seg"), "sec", None),
            P(("parts", "seg"), "sec", None),
            P(("parts", "seg"), "sec", None),
            P(("parts", "seg"), "sec"),
        ),
        out_specs=(P(("parts", "seg"), "sec", None, None), P(("parts", "seg"), None)),
        check_vma=False,
    )
```

time: 220 us -> 80.2 us (0.36)
  blocking collectives: 173 us -> 0 us
  starting transfers between devices: 0.52 us -> 45.8 us
  matrix products: 23.5 us -> 0 us
  waiting for transfers between devices: 0.01 us -> 15.2 us
  local copies, waits for them, and re-layouts: 13.4 us -> 2.26 us
  Pallas kernels: 0 us -> 10.6 us
  between operations: 5.5 us -> 0.73 us
    all_gather x3 -> x0, blocking collectives: 95.8 us -> none  [the longest x2 62.6 us: local(): lax.all_gather(following.astype(jnp.bfloat16), 'sec', axis=0, tiled=True)]
    psum x4 -> x0, blocking collectives: 77.3 us -> none  [the longest x3 59.3 us: local(): lax.psum((jnp.sum(current * image), jnp.sum(current * current)), 'sec')]
    ppermute x1 -> x29, starting transfers between devices: 0.52 us -> 45.8 us  [the longest x28 45.3 us: hop(): return lax.ppermute(block, 'sec', [(a, a ^ distance) for a in range(count)])]
    dot_general x6 -> x0, matrix products: 23.5 us -> none  [the longest x3 13.4 us: add_piece(): jnp.einsum('tkw,tkx->twx', channel_table, scaled, precision=lax.Precision...]
    ppermute x1 -> x29, waiting for transfers between devices: 0.01 us -> 15.2 us  [the longest x28 15.2 us: hop(): return lax.ppermute(block, 'sec', [(a, a ^ distance) for a in range(count)])]
    gather x3 -> x0, local copies, waits for them, and re-layouts: 10.9 us -> none  [add_piece(): jnp.take(flattened, jnp.clip(source_here, 0, rows_here - 1), axis=0)]
    pallas_call x0 -> x4, Pallas kernels: none -> 10.6 us  [the longest x1 3.37 us: local(): pl.pallas_call(functools.partial(middle_kernel, len(states), len(images))...]
  transfers between devices with their start and end apart: 1 -> 29, of which waited for: 0 -> 10; matrix products, arithmetic and copies ran while one was open for 4% -> 4% of each run, Pallas kernels for 0% -> 0%
where the time goes in v1:
time: 80.2 us; the launch traced here: 79.9 us
  starting transfers between devices  45.8 us (57%)
  waiting for transfers between devices  15.2 us (19%)
  Pallas kernels  10.6 us (13%)
  other arithmetic  5.28 us (7%)
  local copies, waits for them, and re-layouts  2.26 us (3%)
    ppermute x28, starting transfers between devices, hop(): return lax.ppermute(block, 'sec', [(a, a ^ distance) for a in range(count)])  45.3 us
    ppermute x28, waiting for transfers between devices, hop(): return lax.ppermute(block, 'sec', [(a, a ^ distance) for a in range(count)])  15.2 us
    pallas_call x1, Pallas kernels, local(): pl.pallas_call(functools.partial(middle_kernel, len(states), len(images))...  3.37 us
    pallas_call x1, Pallas kernels, local(): pl.pallas_call(functools.partial(last_kernel, len(states), len(images)),...  3.37 us
    pallas_call x1, Pallas kernels, local(): pl.pallas_call(functools.partial(first_kernel, len(states)), out_shape=ow...  2.61 us
    unnamed x8, local copies, waits for them, and re-layouts  2.26 us
    concatenate x1, other arithmetic, local(): return (kept[None], jnp.concatenate(energies, axis=1))  1.88 us
  transfers between devices with their start and end apart: 29, of which 10 were waited for; matrix products, arithmetic and copies ran while one was open for 4% of the time, Pallas kernels for 0%

profile of v1, /device:TPU:0, one launch (start us, length us, event | category | flops | bytes accessed | tf_op | source)
XLA Modules:
  0.0 79.9 jit_solution(13627317007719363180)
XLA Ops:
  0.6 0.5 collective-permute-start
  1.1 5.6 %collective-permute-start.7 = (bf16[2,128,128]{2,1,0:T(8,128)(2,1)}, bf16[2,128,128]{2,1,0:T(8,128)(2,1)S(1)}, u32[]{:S(2)}, u32[]{:S(2)}) collective-permute-start(bf16[2,128,128]{2,1,0:T(8,128)(2,1)} %bitcast.34), channel_id=1, source_target_pairs={{0,7},{1,6},{2,5},{3,4},{4,3},{5,2},{6,1},{7,0},{8,15},{9,14},{10,... | collective-permute-start | bytes 196616 | tf_op jit(solution)/shard_map/ppermute | solution.py:20
  6.8 0.0 collective-permute-start.6
  6.8 1.7 %collective-permute-start.5 = (bf16[2,128,128]{2,1,0:T(8,128)(2,1)}, bf16[2,128,128]{2,1,0:T(8,128)(2,1)S(1)}, u32[]{:S(2)}, u32[]{:S(2)}) collective-permute-start(bf16[2,128,128]{2,1,0:T(8,128)(2,1)} %bitcast.36), channel_id=1, source_target_pairs={{0,3},{1,2},{2,1},{3,0},{4,7},{5,6},{6,5},{7,4},{8,11},{9,10},{10,... | collective-permute-start | bytes 196616 | tf_op jit(solution)/shard_map/ppermute | solution.py:20
  8.5 3.6 %collective-permute-start.4 = (bf16[2,128,128]{2,1,0:T(8,128)(2,1)}, bf16[2,128,128]{2,1,0:T(8,128)(2,1)S(1)}, u32[]{:S(2)}, u32[]{:S(2)}) collective-permute-start(bf16[2,128,128]{2,1,0:T(8,128)(2,1)} %bitcast.37), channel_id=1, source_target_pairs={{0,6},{1,7},{2,4},{3,5},{4,2},{5,3},{6,0},{7,1},{8,14},{9,15},{10,... | collective-permute-start | bytes 196616 | tf_op jit(solution)/shard_map/ppermute | solution.py:20
  12.1 0.9 %convert_reduce_fusion = s32[2,32]{1,0:T(2,128)S(1)} fusion(s32[2,32]{1,0:T(2,128)} %bitcast.47, pred[32,32]{1,0:T(8,128)(4,1)S(1)} %iota_compare_fusion.1), kind=kLoop, calls=%fused_computation.4 | loop fusion | flops 12224 | bytes 1536 | tf_op jit(solution)/shard_map/reduce_sum | solution.py:43
  13.0 0.8 select_reduce_fusion.floats
  13.8 0.7 fusion.7
  14.5 0.8 %select_reduce_fusion.2 = (s32[2,32]{1,0:T(2,128)S(1)}, s32[2,32]{1,0:T(2,128)S(1)}) fusion(s32[2,32]{1,0:T(2,128)S(1)} %fusion.7, s32[2,32]{1,0:T(2,128)S(1)} %convert_reduce_fusion, s32[2,32]{1,0:T(2,128)} %bitcast.48), kind=kLoop, calls=%fused_computation.2 | loop fusion | flops 10112 | bytes 1280 | tf_op jit(solution)/shard_map/reduce_sum | solution.py:47
  15.3 0.1 slice_compare_fusion
  15.4 0.1 pad_convert_fusion
  15.5 0.0 collective-permute-start.3
  15.5 0.8 collective-permute-start.2
  16.3 0.4 collective-permute-start.1
  16.7 4.2 %collective-permute-done.3.refs_3_ = bf16[2,128,128]{2,1,0:T(8,128)(2,1)S(1)} collective-permute-done((bf16[2,128,128]{2,1,0:T(8,128)(2,1)}, bf16[2,128,128]{2,1,0:T(8,128)(2,1)S(1)}, u32[]{:S(2)}, u32[]{:S(2)}) %collective-permute-start.3) | collective-permute-done | bytes 65568 | tf_op jit(solution)/shard_map/ppermute | solution.py:20
  21.0 0.1 collective-permute-done.2.refs_2_
  21.1 1.4 %copy-done = bf16[1,2,24,128,128]{4,3,2,1,0:T(8,128)(2,1)S(1)} copy-done((bf16[1,2,24,128,128]{4,3,2,1,0:T(8,128)(2,1)S(1)}, bf16[1,2,24,128,128]{4,3,2,1,0:T(8,128)(2,1)}, u32[]{:S(2)}) %copy-start) | copy-done | bytes 1572888
  22.5 0.8 %copy-done.1 = bf16[1,2,128,128]{3,2,1,0:T(8,128)(2,1)S(1)} copy-done((bf16[1,2,128,128]{3,2,1,0:T(8,128)(2,1)S(1)}, bf16[1,2,128,128]{3,2,1,0:T(8,128)(2,1)}, u32[]{:S(2)}) %copy-start.1) | copy-done | bytes 65560
  23.3 2.6 %first_image.1.refs_8_ = bf16[2,128,128]{2,1,0:T(8,128)(2,1)S(1)} custom-call(s32[2,3,32]{2,1,0:T(4,128)S(1)} %pad_add_fusion.ints, f32[2,32]{1,0:T(2,128)S(1)} %select_reduce_fusion.floats, bf16[2,24,128,128]{3,2,1,0:T(8,128)(2,1)S(1)} %bitcast.31, bf16[2,24,128,128]{3,2,1,0:T(8,128)(2,1)S(1)} %collective-permute-done.right, ...), custom_call_target="tpu_custom_call" | custom-call | tf_op jit(solution)/shard_map/first_image/pallas_call | solution.py:201
  25.9 0.0 copy-start.3
  25.9 3.3 %collective-permute-start.14 = (bf16[2,128,128]{2,1,0:T(8,128)(2,1)S(1)}, bf16[2,128,128]{2,1,0:T(8,128)(2,1)S(1)}, u32[]{:S(2)}, u32[]{:S(2)}) collective-permute-start(bf16[2,128,128]{2,1,0:T(8,128)(2,1)S(1)} %first_image.1.refs_8_), channel_id=1, source_target_pairs={{0,7},{1,6},{2,5},{3,4},{4,3},{5,2},{6,1},{7,0},{8,15},{9,14},{10,... | collective-permute-start | bytes 196616 | tf_op jit(solution)/shard_map/ppermute | solution.py:20
  29.2 0.1 collective-permute-start.13
  29.4 1.9 %collective-permute-start.12 = (bf16[2,128,128]{2,1,0:T(8,128)(2,1)S(1)}, bf16[2,128,128]{2,1,0:T(8,128)(2,1)S(1)}, u32[]{:S(2)}, u32[]{:S(2)}) collective-permute-start(bf16[2,128,128]{2,1,0:T(8,128)(2,1)S(1)} %first_image.1.refs_8_), channel_id=1, source_target_pairs={{0,3},{1,2},{2,1},{3,0},{4,7},{5,6},{6,5},{7,4},{8,11},{9,10},{10,... | collective-permute-start | bytes 196616 | tf_op jit(solution)/shard_map/ppermute | solution.py:20
  31.3 3.2 %collective-permute-start.11 = (bf16[2,128,128]{2,1,0:T(8,128)(2,1)S(1)}, bf16[2,128,128]{2,1,0:T(8,128)(2,1)S(1)}, u32[]{:S(2)}, u32[]{:S(2)}) collective-permute-start(bf16[2,128,128]{2,1,0:T(8,128)(2,1)S(1)} %first_image.1.refs_8_), channel_id=1, source_target_pairs={{0,6},{1,7},{2,4},{3,5},{4,2},{5,3},{6,0},{7,1},{8,14},{9,15},{10,... | collective-permute-start | bytes 196616 | tf_op jit(solution)/shard_map/ppermute | solution.py:20
  34.5 1.2 %collective-permute-start.9 = (bf16[2,128,128]{2,1,0:T(8,128)(2,1)S(1)}, bf16[2,128,128]{2,1,0:T(8,128)(2,1)S(1)}, u32[]{:S(2)}, u32[]{:S(2)}) collective-permute-start(bf16[2,128,128]{2,1,0:T(8,128)(2,1)S(1)} %first_image.1.refs_8_), channel_id=1, source_target_pairs={{0,2},{1,3},{2,0},{3,1},{4,6},{5,7},{6,4},{7,5},{8,10},{9,11},{10,... | collective-permute-start | bytes 196616 | tf_op jit(solution)/shard_map/ppermute | solution.py:20
  35.7 1.8 %collective-permute-done.13.refs_14_ = bf16[2,128,128]{2,1,0:T(8,128)(2,1)S(1)} collective-permute-done((bf16[2,128,128]{2,1,0:T(8,128)(2,1)S(1)}, bf16[2,128,128]{2,1,0:T(8,128)(2,1)S(1)}, u32[]{:S(2)}, u32[]{:S(2)}) %collective-permute-start.13) | collective-permute-done | bytes 65568 | tf_op jit(solution)/shard_map/ppermute | solution.py:20
  37.5 1.0 %collective-permute-start.8 = (bf16[2,128,128]{2,1,0:T(8,128)(2,1)S(1)}, bf16[2,128,128]{2,1,0:T(8,128)(2,1)S(1)}, u32[]{:S(2)}, u32[]{:S(2)}) collective-permute-start(bf16[2,128,128]{2,1,0:T(8,128)(2,1)S(1)} %first_image.1.refs_8_), channel_id=1, source_target_pairs={{0,1},{1,0},{2,3},{3,2},{4,5},{5,4},{6,7},{7,6},{8,9},{9,8},{10,11... | collective-permute-start | bytes 196616 | tf_op jit(solution)/shard_map/ppermute | solution.py:20
  38.5 1.3 %collective-permute-done.10.refs_11_ = bf16[2,128,128]{2,1,0:T(8,128)(2,1)S(1)} collective-permute-done((bf16[2,128,128]{2,1,0:T(8,128)(2,1)S(1)}, bf16[2,128,128]{2,1,0:T(8,128)(2,1)S(1)}, u32[]{:S(2)}, u32[]{:S(2)}) %collective-permute-start.10) | collective-permute-done | bytes 65568 | tf_op jit(solution)/shard_map/ppermute | solution.py:20
  39.9 1.9 %collective-permute-done.8.refs_9_ = bf16[2,128,128]{2,1,0:T(8,128)(2,1)S(1)} collective-permute-done((bf16[2,128,128]{2,1,0:T(8,128)(2,1)S(1)}, bf16[2,128,128]{2,1,0:T(8,128)(2,1)S(1)}, u32[]{:S(2)}, u32[]{:S(2)}) %collective-permute-start.8) | collective-permute-done | bytes 65568 | tf_op jit(solution)/shard_map/ppermute | solution.py:20
  41.7 3.4 %middle_image.1 = (f32[1,1]{1,0:T(1,128)}, f32[16,128,128]{2,1,0:T(8,128)S(1)}, bf16[2,128,128]{2,1,0:T(8,128)(2,1)S(1)}) custom-call(s32[2,3,32]{2,1,0:T(4,128)S(1)} %pad_add_fusion.ints, f32[2,32]{1,0:T(2,128)S(1)} %select_reduce_fusion.floats, bf16[2,24,128,128]{3,2,1,0:T(8,128)(2,1)S(1)} %bitcast.32, ...), custom_call_target="tpu_custom_call" | custom-call | tf_op jit(solution)/shard_map/middle_image/pallas_call | solution.py:213
  45.1 2.5 %collective-permute-start.21 = (bf16[2,128,128]{2,1,0:T(8,128)(2,1)S(1)}, bf16[2,128,128]{2,1,0:T(8,128)(2,1)S(1)}, u32[]{:S(2)}, u32[]{:S(2)}) collective-permute-start(bf16[2,128,128]{2,1,0:T(8,128)(2,1)S(1)} %get-tuple-element.12.refs_1_), channel_id=1, source_target_pairs={{0,7},{1,6},{2,5},{3,4},{4,3},{5,2},{6,1},{7,0},{8,15},{9,14},{10,... | collective-permute-start | bytes 196616 | tf_op jit(solution)/shard_map/ppermute | solution.py:20
  47.6 3.3 %collective-permute-start.19 = (bf16[2,128,128]{2,1,0:T(8,128)(2,1)S(1)}, bf16[2,128,128]{2,1,0:T(8,128)(2,1)S(1)}, u32[]{:S(2)}, u32[]{:S(2)}) collective-permute-start(bf16[2,128,128]{2,1,0:T(8,128)(2,1)S(1)} %get-tuple-element.12.refs_1_), channel_id=1, source_target_pairs={{0,3},{1,2},{2,1},{3,0},{4,7},{5,6},{6,5},{7,4},{8,11},{9,10},{10,... | collective-permute-start | bytes 196616 | tf_op jit(solution)/shard_map/ppermute | solution.py:20
  50.9 1.9 %collective-permute-start.18 = (bf16[2,128,128]{2,1,0:T(8,128)(2,1)S(1)}, bf16[2,128,128]{2,1,0:T(8,128)(2,1)S(1)}, u32[]{:S(2)}, u32[]{:S(2)}) collective-permute-start(bf16[2,128,128]{2,1,0:T(8,128)(2,1)S(1)} %get-tuple-element.12.refs_1_), channel_id=1, source_target_pairs={{0,6},{1,7},{2,4},{3,5},{4,2},{5,3},{6,0},{7,1},{8,14},{9,15},{10,... | collective-permute-start | bytes 196616 | tf_op jit(solution)/shard_map/ppermute | solution.py:20
  52.9 2.4 %collective-permute-start.16 = (bf16[2,128,128]{2,1,0:T(8,128)(2,1)S(1)}, bf16[2,128,128]{2,1,0:T(8,128)(2,1)S(1)}, u32[]{:S(2)}, u32[]{:S(2)}) collective-permute-start(bf16[2,128,128]{2,1,0:T(8,128)(2,1)S(1)} %get-tuple-element.12.refs_1_), channel_id=1, source_target_pairs={{0,2},{1,3},{2,0},{3,1},{4,6},{5,7},{6,4},{7,5},{8,10},{9,11},{10,... | collective-permute-start | bytes 196616 | tf_op jit(solution)/shard_map/ppermute | solution.py:20
  55.3 1.0 %collective-permute-start.15 = (bf16[2,128,128]{2,1,0:T(8,128)(2,1)S(1)}, bf16[2,128,128]{2,1,0:T(8,128)(2,1)S(1)}, u32[]{:S(2)}, u32[]{:S(2)}) collective-permute-start(bf16[2,128,128]{2,1,0:T(8,128)(2,1)S(1)} %get-tuple-element.12.refs_1_), channel_id=1, source_target_pairs={{0,1},{1,0},{2,3},{3,2},{4,5},{5,4},{6,7},{7,6},{8,9},{9,8},{10,11... | collective-permute-start | bytes 196616 | tf_op jit(solution)/shard_map/ppermute | solution.py:20
  56.3 0.7 collective-permute-done.18.refs_5_
  57.0 1.4 %collective-permute-done.17.refs_4_ = bf16[2,128,128]{2,1,0:T(8,128)(2,1)S(1)} collective-permute-done((bf16[2,128,128]{2,1,0:T(8,128)(2,1)S(1)}, bf16[2,128,128]{2,1,0:T(8,128)(2,1)S(1)}, u32[]{:S(2)}, u32[]{:S(2)}) %collective-permute-start.17) | collective-permute-done | bytes 65568 | tf_op jit(solution)/shard_map/ppermute | solution.py:20
  58.4 1.2 %collective-permute-done.15.refs_2_ = bf16[2,128,128]{2,1,0:T(8,128)(2,1)S(1)} collective-permute-done((bf16[2,128,128]{2,1,0:T(8,128)(2,1)S(1)}, bf16[2,128,128]{2,1,0:T(8,128)(2,1)S(1)}, u32[]{:S(2)}, u32[]{:S(2)}) %collective-permute-start.15) | collective-permute-done | bytes 65568 | tf_op jit(solution)/shard_map/ppermute | solution.py:20
  59.6 3.4 %last_image.1 = (f32[1,1]{1,0:T(1,128)}, f32[2,128,128]{2,1,0:T(8,128)S(1)}, bf16[2,128,128]{2,1,0:T(8,128)(2,1)S(1)}, f32[1,8,128]{2,1,0:T(8,128)S(1)}) custom-call(s32[2,3,32]{2,1,0:T(4,128)S(1)} %pad_add_fusion.ints, f32[2,32]{1,0:T(2,128)S(1)} %select_reduce_fusion.floats, s32[2]{0:T(128)S(1)} %bitcast.43, bf16[2,24,128,128]{3,2,1,0:T(8,128)(2,1)S(1)} %bitcast.33, ...), custom_call_target="tpu_custom_call" | custom-call | tf_op jit(solution)/shard_map/last_image/pallas_call | solution.py:225
  63.0 2.6 %collective-permute-start.28 = (f32[1,8,128]{2,1,0:T(8,128)S(1)}, f32[1,8,128]{2,1,0:T(8,128)S(1)}, u32[]{:S(2)}, u32[]{:S(2)}) collective-permute-start(f32[1,8,128]{2,1,0:T(8,128)S(1)} %get-tuple-element.15.refs_0_), channel_id=1, source_target_pairs={{0,7},{1,6},{2,5},{3,4},{4,3},{5,2},{6,1},{7,0},{8,15},{9,14},{10,... | collective-permute-start | bytes 12296 | tf_op jit(solution)/shard_map/ppermute | solution.py:20
  65.6 3.2 %collective-permute-start.26 = (f32[1,8,128]{2,1,0:T(8,128)S(1)}, f32[1,8,128]{2,1,0:T(8,128)S(1)}, u32[]{:S(2)}, u32[]{:S(2)}) collective-permute-start(f32[1,8,128]{2,1,0:T(8,128)S(1)} %get-tuple-element.15.refs_0_), channel_id=1, source_target_pairs={{0,3},{1,2},{2,1},{3,0},{4,7},{5,6},{6,5},{7,4},{8,11},{9,10},{10,... | collective-permute-start | bytes 12296 | tf_op jit(solution)/shard_map/ppermute | solution.py:20
  68.8 2.1 %collective-permute-start.25 = (f32[1,8,128]{2,1,0:T(8,128)S(1)}, f32[1,8,128]{2,1,0:T(8,128)S(1)}, u32[]{:S(2)}, u32[]{:S(2)}) collective-permute-start(f32[1,8,128]{2,1,0:T(8,128)S(1)} %get-tuple-element.15.refs_0_), channel_id=1, source_target_pairs={{0,6},{1,7},{2,4},{3,5},{4,2},{5,3},{6,0},{7,1},{8,14},{9,15},{10,... | collective-permute-start | bytes 12296 | tf_op jit(solution)/shard_map/ppermute | solution.py:20
  70.9 2.3 %collective-permute-start.23 = (f32[1,8,128]{2,1,0:T(8,128)S(1)}, f32[1,8,128]{2,1,0:T(8,128)S(1)}, u32[]{:S(2)}, u32[]{:S(2)}) collective-permute-start(f32[1,8,128]{2,1,0:T(8,128)S(1)} %get-tuple-element.15.refs_0_), channel_id=1, source_target_pairs={{0,2},{1,3},{2,0},{3,1},{4,6},{5,7},{6,4},{7,5},{8,10},{9,11},{10,... | collective-permute-start | bytes 12296 | tf_op jit(solution)/shard_map/ppermute | solution.py:20
  73.2 1.0 %collective-permute-start.22 = (f32[1,8,128]{2,1,0:T(8,128)S(1)}, f32[1,8,128]{2,1,0:T(8,128)S(1)}, u32[]{:S(2)}, u32[]{:S(2)}) collective-permute-start(f32[1,8,128]{2,1,0:T(8,128)S(1)} %get-tuple-element.15.refs_0_), channel_id=1, source_target_pairs={{0,1},{1,0},{2,3},{3,2},{4,5},{5,4},{6,7},{7,6},{8,9},{9,8},{10,11... | collective-permute-start | bytes 12296 | tf_op jit(solution)/shard_map/ppermute | solution.py:20
  74.2 1.2 %collective-permute-done.24.refs_3_ = f32[1,8,128]{2,1,0:T(8,128)S(1)} collective-permute-done((f32[1,8,128]{2,1,0:T(8,128)S(1)}, f32[1,8,128]{2,1,0:T(8,128)S(1)}, u32[]{:S(2)}, u32[]{:S(2)}) %collective-permute-start.24) | collective-permute-done | bytes 4128 | tf_op jit(solution)/shard_map/ppermute | solution.py:20
  75.4 1.4 %collective-permute-done.22.refs_1_ = f32[1,8,128]{2,1,0:T(8,128)S(1)} collective-permute-done((f32[1,8,128]{2,1,0:T(8,128)S(1)}, f32[1,8,128]{2,1,0:T(8,128)S(1)}, u32[]{:S(2)}, u32[]{:S(2)}) %collective-permute-start.22) | collective-permute-done | bytes 4128 | tf_op jit(solution)/shard_map/ppermute | solution.py:20
  76.8 1.2 %finish.1 = (f32[1,128]{1,0:T(1,128)S(1)}, bf16[2,128,128]{2,1,0:T(8,128)(2,1)}) custom-call(s32[2]{0:T(128)S(1)} %bitcast.44, f32[2,128,128]{2,1,0:T(8,128)S(1)} %get-tuple-element.13.own, bf16[2,128,128]{2,1,0:T(8,128)(2,1)S(1)} %get-tuple-element.14.image, f32[1,8,128]{2,1,0:T(8,128)S(1)} %get-tuple-element.15.refs_0_, ...), custom_call_target="tpu_custom_call" | custom-call | tf_op jit(solution)/shard_map/finish/pallas_call | solution.py:241
  78.0 1.9 %pad_maximum_fusion = f32[1,3]{1,0:T(1,128)} fusion(f32[1,1]{1,0:T(1,128)S(1)} %bitcast.45, f32[1,1]{1,0:T(1,128)} %get-tuple-element.18, f32[1,1]{1,0:T(1,128)} %get-tuple-element.17), kind=kLoop, calls=%fused_computation.31 | loop fusion | flops 6 | bytes 24 | tf_op jit(solution)/shard_map/concatenate | solution.py:250
  (31 shorter events, 0.1 us)
Async XLA Ops:
  0.6 20.4 %collective-permute-start = (bf16[2,24,128,128]{3,2,1,0:T(8,128)(2,1)}, bf16[2,24,128,128]{3,2,1,0:T(8,128)(2,1)S(1)}, u32[]{:S(2)}, u32[]{:S(2)}) collective-permute-start(bf16[2,24,128,128]{3,2,1,0:T(8,128)(2,1)} %bitcast.52), channel_id=1, source_target_pairs={{0,8},{8,0},{1,9},{9,1},{2,10},{10,2},{3,11},{11,3},{4,12},{12,4},... | collective-permute-start | bytes 4718600 | tf_op jit(solution)/shard_map/ppermute | solution.py:186
  1.1 14.3 %collective-permute-start.7 = (bf16[2,128,128]{2,1,0:T(8,128)(2,1)}, bf16[2,128,128]{2,1,0:T(8,128)(2,1)S(1)}, u32[]{:S(2)}, u32[]{:S(2)}) collective-permute-start(bf16[2,128,128]{2,1,0:T(8,128)(2,1)} %bitcast.34), channel_id=1, source_target_pairs={{0,7},{1,6},{2,5},{3,4},{4,3},{5,2},{6,1},{7,0},{8,15},{9,14},{10,... | collective-permute-start | bytes 196616 | tf_op jit(solution)/shard_map/ppermute | solution.py:20
  6.8 8.7 %collective-permute-start.6 = (bf16[2,128,128]{2,1,0:T(8,128)(2,1)}, bf16[2,128,128]{2,1,0:T(8,128)(2,1)S(1)}, u32[]{:S(2)}, u32[]{:S(2)}) collective-permute-start(bf16[2,128,128]{2,1,0:T(8,128)(2,1)} %bitcast.35), channel_id=1, source_target_pairs={{0,5},{1,4},{2,7},{3,6},{4,1},{5,0},{6,3},{7,2},{8,13},{9,12},{10,... | collective-permute-start | bytes 196616 | tf_op jit(solution)/shard_map/ppermute | solution.py:20
  6.8 9.5 %collective-permute-start.5 = (bf16[2,128,128]{2,1,0:T(8,128)(2,1)}, bf16[2,128,128]{2,1,0:T(8,128)(2,1)S(1)}, u32[]{:S(2)}, u32[]{:S(2)}) collective-permute-start(bf16[2,128,128]{2,1,0:T(8,128)(2,1)} %bitcast.36), channel_id=1, source_target_pairs={{0,3},{1,2},{2,1},{3,0},{4,7},{5,6},{6,5},{7,4},{8,11},{9,10},{10,... | collective-permute-start | bytes 196616 | tf_op jit(solution)/shard_map/ppermute | solution.py:20
  8.5 8.3 %collective-permute-start.4 = (bf16[2,128,128]{2,1,0:T(8,128)(2,1)}, bf16[2,128,128]{2,1,0:T(8,128)(2,1)S(1)}, u32[]{:S(2)}, u32[]{:S(2)}) collective-permute-start(bf16[2,128,128]{2,1,0:T(8,128)(2,1)} %bitcast.37), channel_id=1, source_target_pairs={{0,6},{1,7},{2,4},{3,5},{4,2},{5,3},{6,0},{7,1},{8,14},{9,15},{10,... | collective-permute-start | bytes 196616 | tf_op jit(solution)/shard_map/ppermute | solution.py:20
  15.5 5.5 %collective-permute-start.3 = (bf16[2,128,128]{2,1,0:T(8,128)(2,1)}, bf16[2,128,128]{2,1,0:T(8,128)(2,1)S(1)}, u32[]{:S(2)}, u32[]{:S(2)}) collective-permute-start(bf16[2,128,128]{2,1,0:T(8,128)(2,1)} %bitcast.38), channel_id=1, source_target_pairs={{0,4},{1,5},{2,6},{3,7},{4,0},{5,1},{6,2},{7,3},{8,12},{9,13},{10,... | collective-permute-start | bytes 196616 | tf_op jit(solution)/shard_map/ppermute | solution.py:20
  15.5 5.5 %collective-permute-start.2 = (bf16[2,128,128]{2,1,0:T(8,128)(2,1)}, bf16[2,128,128]{2,1,0:T(8,128)(2,1)S(1)}, u32[]{:S(2)}, u32[]{:S(2)}) collective-permute-start(bf16[2,128,128]{2,1,0:T(8,128)(2,1)} %bitcast.39), channel_id=1, source_target_pairs={{0,2},{1,3},{2,0},{3,1},{4,6},{5,7},{6,4},{7,5},{8,10},{9,11},{10,... | collective-permute-start | bytes 196616 | tf_op jit(solution)/shard_map/ppermute | solution.py:20
  16.3 4.8 %collective-permute-start.1 = (bf16[2,128,128]{2,1,0:T(8,128)(2,1)}, bf16[2,128,128]{2,1,0:T(8,128)(2,1)S(1)}, u32[]{:S(2)}, u32[]{:S(2)}) collective-permute-start(bf16[2,128,128]{2,1,0:T(8,128)(2,1)} %bitcast.40), channel_id=1, source_target_pairs={{0,1},{1,0},{2,3},{3,2},{4,5},{5,4},{6,7},{7,6},{8,9},{9,8},{10,11... | collective-permute-start | bytes 196616 | tf_op jit(solution)/shard_map/ppermute | solution.py:20
  21.1 1.4 %copy-start = (bf16[1,2,24,128,128]{4,3,2,1,0:T(8,128)(2,1)S(1)}, bf16[1,2,24,128,128]{4,3,2,1,0:T(8,128)(2,1)}, u32[]{:S(2)}) copy-start(bf16[1,2,24,128,128]{4,3,2,1,0:T(8,128)(2,1)} %param.8) | copy-start | bytes 4718596
  22.5 0.8 %copy-start.1 = (bf16[1,2,128,128]{3,2,1,0:T(8,128)(2,1)S(1)}, bf16[1,2,128,128]{3,2,1,0:T(8,128)(2,1)}, u32[]{:S(2)}) copy-start(bf16[1,2,128,128]{3,2,1,0:T(8,128)(2,1)} %param.7) | copy-start | bytes 196612
  23.3 18.4 %copy-start.2 = (bf16[1,2,128,128]{3,2,1,0:T(8,128)(2,1)S(1)}, bf16[1,2,128,128]{3,2,1,0:T(8,128)(2,1)}, u32[]{:S(2)}) copy-start(bf16[1,2,128,128]{3,2,1,0:T(8,128)(2,1)} %param.7) | copy-start | bytes 196612
  25.9 33.7 %copy-start.3 = (s32[1,2]{1,0:T(1,128)S(1)}, s32[1,2]{1,0:T(1,128)}, u32[]{:S(2)}) copy-start(s32[1,2]{1,0:T(1,128)} %param.13) | copy-start | bytes 28
  25.9 8.6 %collective-permute-start.14 = (bf16[2,128,128]{2,1,0:T(8,128)(2,1)S(1)}, bf16[2,128,128]{2,1,0:T(8,128)(2,1)S(1)}, u32[]{:S(2)}, u32[]{:S(2)}) collective-permute-start(bf16[2,128,128]{2,1,0:T(8,128)(2,1)S(1)} %first_image.1.refs_8_), channel_id=1, source_target_pairs={{0,7},{1,6},{2,5},{3,4},{4,3},{5,2},{6,1},{7,0},{8,15},{9,14},{10,... | collective-permute-start | bytes 196616 | tf_op jit(solution)/shard_map/ppermute | solution.py:20
  29.2 8.2 %collective-permute-start.13 = (bf16[2,128,128]{2,1,0:T(8,128)(2,1)S(1)}, bf16[2,128,128]{2,1,0:T(8,128)(2,1)S(1)}, u32[]{:S(2)}, u32[]{:S(2)}) collective-permute-start(bf16[2,128,128]{2,1,0:T(8,128)(2,1)S(1)} %first_image.1.refs_8_), channel_id=1, source_target_pairs={{0,5},{1,4},{2,7},{3,6},{4,1},{5,0},{6,3},{7,2},{8,13},{9,12},{10,... | collective-permute-start | bytes 196616 | tf_op jit(solution)/shard_map/ppermute | solution.py:20
  29.4 9.1 %collective-permute-start.12 = (bf16[2,128,128]{2,1,0:T(8,128)(2,1)S(1)}, bf16[2,128,128]{2,1,0:T(8,128)(2,1)S(1)}, u32[]{:S(2)}, u32[]{:S(2)}) collective-permute-start(bf16[2,128,128]{2,1,0:T(8,128)(2,1)S(1)} %first_image.1.refs_8_), channel_id=1, source_target_pairs={{0,3},{1,2},{2,1},{3,0},{4,7},{5,6},{6,5},{7,4},{8,11},{9,10},{10,... | collective-permute-start | bytes 196616 | tf_op jit(solution)/shard_map/ppermute | solution.py:20
  31.3 7.2 %collective-permute-start.11 = (bf16[2,128,128]{2,1,0:T(8,128)(2,1)S(1)}, bf16[2,128,128]{2,1,0:T(8,128)(2,1)S(1)}, u32[]{:S(2)}, u32[]{:S(2)}) collective-permute-start(bf16[2,128,128]{2,1,0:T(8,128)(2,1)S(1)} %first_image.1.refs_8_), channel_id=1, source_target_pairs={{0,6},{1,7},{2,4},{3,5},{4,2},{5,3},{6,0},{7,1},{8,14},{9,15},{10,... | collective-permute-start | bytes 196616 | tf_op jit(solution)/shard_map/ppermute | solution.py:20
  34.5 5.3 %collective-permute-start.10 = (bf16[2,128,128]{2,1,0:T(8,128)(2,1)S(1)}, bf16[2,128,128]{2,1,0:T(8,128)(2,1)S(1)}, u32[]{:S(2)}, u32[]{:S(2)}) collective-permute-start(bf16[2,128,128]{2,1,0:T(8,128)(2,1)S(1)} %first_image.1.refs_8_), channel_id=1, source_target_pairs={{0,4},{1,5},{2,6},{3,7},{4,0},{5,1},{6,2},{7,3},{8,12},{9,13},{10,... | collective-permute-start | bytes 196616 | tf_op jit(solution)/shard_map/ppermute | solution.py:20
  34.5 5.3 %collective-permute-start.9 = (bf16[2,128,128]{2,1,0:T(8,128)(2,1)S(1)}, bf16[2,128,128]{2,1,0:T(8,128)(2,1)S(1)}, u32[]{:S(2)}, u32[]{:S(2)}) collective-permute-start(bf16[2,128,128]{2,1,0:T(8,128)(2,1)S(1)} %first_image.1.refs_8_), channel_id=1, source_target_pairs={{0,2},{1,3},{2,0},{3,1},{4,6},{5,7},{6,4},{7,5},{8,10},{9,11},{10,... | collective-permute-start | bytes 196616 | tf_op jit(solution)/shard_map/ppermute | solution.py:20
  37.5 4.3 %collective-permute-start.8 = (bf16[2,128,128]{2,1,0:T(8,128)(2,1)S(1)}, bf16[2,128,128]{2,1,0:T(8,128)(2,1)S(1)}, u32[]{:S(2)}, u32[]{:S(2)}) collective-permute-start(bf16[2,128,128]{2,1,0:T(8,128)(2,1)S(1)} %first_image.1.refs_8_), channel_id=1, source_target_pairs={{0,1},{1,0},{2,3},{3,2},{4,5},{5,4},{6,7},{7,6},{8,9},{9,8},{10,11... | collective-permute-start | bytes 196616 | tf_op jit(solution)/shard_map/ppermute | solution.py:20
  45.1 7.8 %collective-permute-start.21 = (bf16[2,128,128]{2,1,0:T(8,128)(2,1)S(1)}, bf16[2,128,128]{2,1,0:T(8,128)(2,1)S(1)}, u32[]{:S(2)}, u32[]{:S(2)}) collective-permute-start(bf16[2,128,128]{2,1,0:T(8,128)(2,1)S(1)} %get-tuple-element.12.refs_1_), channel_id=1, source_target_pairs={{0,7},{1,6},{2,5},{3,4},{4,3},{5,2},{6,1},{7,0},{8,15},{9,14},{10,... | collective-permute-start | bytes 196616 | tf_op jit(solution)/shard_map/ppermute | solution.py:20
  47.6 7.7 %collective-permute-start.20 = (bf16[2,128,128]{2,1,0:T(8,128)(2,1)S(1)}, bf16[2,128,128]{2,1,0:T(8,128)(2,1)S(1)}, u32[]{:S(2)}, u32[]{:S(2)}) collective-permute-start(bf16[2,128,128]{2,1,0:T(8,128)(2,1)S(1)} %get-tuple-element.12.refs_1_), channel_id=1, source_target_pairs={{0,5},{1,4},{2,7},{3,6},{4,1},{5,0},{6,3},{7,2},{8,13},{9,12},{10,... | collective-permute-start | bytes 196616 | tf_op jit(solution)/shard_map/ppermute | solution.py:20
  47.6 8.7 %collective-permute-start.19 = (bf16[2,128,128]{2,1,0:T(8,128)(2,1)S(1)}, bf16[2,128,128]{2,1,0:T(8,128)(2,1)S(1)}, u32[]{:S(2)}, u32[]{:S(2)}) collective-permute-start(bf16[2,128,128]{2,1,0:T(8,128)(2,1)S(1)} %get-tuple-element.12.refs_1_), channel_id=1, source_target_pairs={{0,3},{1,2},{2,1},{3,0},{4,7},{5,6},{6,5},{7,4},{8,11},{9,10},{10,... | collective-permute-start | bytes 196616 | tf_op jit(solution)/shard_map/ppermute | solution.py:20
  50.9 6.1 %collective-permute-start.18 = (bf16[2,128,128]{2,1,0:T(8,128)(2,1)S(1)}, bf16[2,128,128]{2,1,0:T(8,128)(2,1)S(1)}, u32[]{:S(2)}, u32[]{:S(2)}) collective-permute-start(bf16[2,128,128]{2,1,0:T(8,128)(2,1)S(1)} %get-tuple-element.12.refs_1_), channel_id=1, source_target_pairs={{0,6},{1,7},{2,4},{3,5},{4,2},{5,3},{6,0},{7,1},{8,14},{9,15},{10,... | collective-permute-start | bytes 196616 | tf_op jit(solution)/shard_map/ppermute | solution.py:20
  52.9 5.5 %collective-permute-start.17 = (bf16[2,128,128]{2,1,0:T(8,128)(2,1)S(1)}, bf16[2,128,128]{2,1,0:T(8,128)(2,1)S(1)}, u32[]{:S(2)}, u32[]{:S(2)}) collective-permute-start(bf16[2,128,128]{2,1,0:T(8,128)(2,1)S(1)} %get-tuple-element.12.refs_1_), channel_id=1, source_target_pairs={{0,4},{1,5},{2,6},{3,7},{4,0},{5,1},{6,2},{7,3},{8,12},{9,13},{10,... | collective-permute-start | bytes 196616 | tf_op jit(solution)/shard_map/ppermute | solution.py:20
  52.9 5.5 %collective-permute-start.16 = (bf16[2,128,128]{2,1,0:T(8,128)(2,1)S(1)}, bf16[2,128,128]{2,1,0:T(8,128)(2,1)S(1)}, u32[]{:S(2)}, u32[]{:S(2)}) collective-permute-start(bf16[2,128,128]{2,1,0:T(8,128)(2,1)S(1)} %get-tuple-element.12.refs_1_), channel_id=1, source_target_pairs={{0,2},{1,3},{2,0},{3,1},{4,6},{5,7},{6,4},{7,5},{8,10},{9,11},{10,... | collective-permute-start | bytes 196616 | tf_op jit(solution)/shard_map/ppermute | solution.py:20
  55.3 4.3 %collective-permute-start.15 = (bf16[2,128,128]{2,1,0:T(8,128)(2,1)S(1)}, bf16[2,128,128]{2,1,0:T(8,128)(2,1)S(1)}, u32[]{:S(2)}, u32[]{:S(2)}) collective-permute-start(bf16[2,128,128]{2,1,0:T(8,128)(2,1)S(1)} %get-tuple-element.12.refs_1_), channel_id=1, source_target_pairs={{0,1},{1,0},{2,3},{3,2},{4,5},{5,4},{6,7},{7,6},{8,9},{9,8},{10,11... | collective-permute-start | bytes 196616 | tf_op jit(solution)/shard_map/ppermute | solution.py:20
  63.0 7.9 %collective-permute-start.28 = (f32[1,8,128]{2,1,0:T(8,128)S(1)}, f32[1,8,128]{2,1,0:T(8,128)S(1)}, u32[]{:S(2)}, u32[]{:S(2)}) collective-permute-start(f32[1,8,128]{2,1,0:T(8,128)S(1)} %get-tuple-element.15.refs_0_), channel_id=1, source_target_pairs={{0,7},{1,6},{2,5},{3,4},{4,3},{5,2},{6,1},{7,0},{8,15},{9,14},{10,... | collective-permute-start | bytes 12296 | tf_op jit(solution)/shard_map/ppermute | solution.py:20
  65.6 7.6 %collective-permute-start.27 = (f32[1,8,128]{2,1,0:T(8,128)S(1)}, f32[1,8,128]{2,1,0:T(8,128)S(1)}, u32[]{:S(2)}, u32[]{:S(2)}) collective-permute-start(f32[1,8,128]{2,1,0:T(8,128)S(1)} %get-tuple-element.15.refs_0_), channel_id=1, source_target_pairs={{0,5},{1,4},{2,7},{3,6},{4,1},{5,0},{6,3},{7,2},{8,13},{9,12},{10,... | collective-permute-start | bytes 12296 | tf_op jit(solution)/shard_map/ppermute | solution.py:20
  65.6 8.6 %collective-permute-start.26 = (f32[1,8,128]{2,1,0:T(8,128)S(1)}, f32[1,8,128]{2,1,0:T(8,128)S(1)}, u32[]{:S(2)}, u32[]{:S(2)}) collective-permute-start(f32[1,8,128]{2,1,0:T(8,128)S(1)} %get-tuple-element.15.refs_0_), channel_id=1, source_target_pairs={{0,3},{1,2},{2,1},{3,0},{4,7},{5,6},{6,5},{7,4},{8,11},{9,10},{10,... | collective-permute-start | bytes 12296 | tf_op jit(solution)/shard_map/ppermute | solution.py:20
  68.8 5.4 %collective-permute-start.25 = (f32[1,8,128]{2,1,0:T(8,128)S(1)}, f32[1,8,128]{2,1,0:T(8,128)S(1)}, u32[]{:S(2)}, u32[]{:S(2)}) collective-permute-start(f32[1,8,128]{2,1,0:T(8,128)S(1)} %get-tuple-element.15.refs_0_), channel_id=1, source_target_pairs={{0,6},{1,7},{2,4},{3,5},{4,2},{5,3},{6,0},{7,1},{8,14},{9,15},{10,... | collective-permute-start | bytes 12296 | tf_op jit(solution)/shard_map/ppermute | solution.py:20
  70.9 4.5 %collective-permute-start.24 = (f32[1,8,128]{2,1,0:T(8,128)S(1)}, f32[1,8,128]{2,1,0:T(8,128)S(1)}, u32[]{:S(2)}, u32[]{:S(2)}) collective-permute-start(f32[1,8,128]{2,1,0:T(8,128)S(1)} %get-tuple-element.15.refs_0_), channel_id=1, source_target_pairs={{0,4},{1,5},{2,6},{3,7},{4,0},{5,1},{6,2},{7,3},{8,12},{9,13},{10,... | collective-permute-start | bytes 12296 | tf_op jit(solution)/shard_map/ppermute | solution.py:20
  70.9 4.5 %collective-permute-start.23 = (f32[1,8,128]{2,1,0:T(8,128)S(1)}, f32[1,8,128]{2,1,0:T(8,128)S(1)}, u32[]{:S(2)}, u32[]{:S(2)}) collective-permute-start(f32[1,8,128]{2,1,0:T(8,128)S(1)} %get-tuple-element.15.refs_0_), channel_id=1, source_target_pairs={{0,2},{1,3},{2,0},{3,1},{4,6},{5,7},{6,4},{7,5},{8,10},{9,11},{10,... | collective-permute-start | bytes 12296 | tf_op jit(solution)/shard_map/ppermute | solution.py:20
  73.2 3.6 %collective-permute-start.22 = (f32[1,8,128]{2,1,0:T(8,128)S(1)}, f32[1,8,128]{2,1,0:T(8,128)S(1)}, u32[]{:S(2)}, u32[]{:S(2)}) collective-permute-start(f32[1,8,128]{2,1,0:T(8,128)S(1)} %get-tuple-element.15.refs_0_), channel_id=1, source_target_pairs={{0,1},{1,0},{2,3},{3,2},{4,5},{5,4},{6,7},{7,6},{8,9},{9,8},{10,11... | collective-permute-start | bytes 12296 | tf_op jit(solution)/shard_map/ppermute | solution.py:20

commit v2 on v1

--- a/solution.py
+++ b/solution.py
@@ -12,7 +12,8 @@
 EPSILON = 1e-06
 SMEM = pl.BlockSpec(memory_space=pltpu.SMEM)
 VMEM = pl.BlockSpec(memory_space=pltpu.VMEM)
-NEAR = (0, 1, 2, 4, 6, 3, 5, 7)
+ANY = pl.BlockSpec(memory_space=pl.ANY)
+APART = (0, 4, 3, 7, 2, 6, 1, 5)
 
 
 def hop(block, distance):
@@ -21,40 +22,71 @@
 
 
 def gather(block):
-    if lax.axis_size("sec") != len(NEAR):
+    if lax.axis_size("sec") != len(APART):
         return [lax.all_gather(block, "sec", axis=0, tiled=True)]
-    return [block] + [hop(block, distance) for distance in NEAR[1:]]
-
-
-def slots(sector, local_count):
-    if lax.axis_size("sec") != len(NEAR):
+    both = jnp.concatenate([block, hop(block, 4)])
+    return [both] + [hop(both, distance) for distance in (3, 2, 1)]
+
+
+def slot(sector, blocks, devices, here):
+    if devices != len(APART):
         return sector
-    place = sorted(range(len(NEAR)), key=lambda position: NEAR[position])
-    apart = (sector // local_count) ^ lax.axis_index("sec")
-    found = sum(jnp.where(apart == d, place[d], 0) for d in range(len(NEAR)))
-    return found * local_count + sector % local_count
-
-
-def pair_table(sources, channels, couplings, local_count):
-    k = jnp.arange(sources.shape[1], dtype=jnp.int32)
-    before = (channels[:, None, :] < channels[:, :, None]) | (
-        (channels[:, None, :] == channels[:, :, None]) & (k[None, None, :] < k[None, :, None])
-    )
-    rank = jnp.sum(before.astype(jnp.int32), axis=2)
-    chosen = rank[:, None, :] == k[None, :, None]
-
-    def ordered(values):
-        return jnp.sum(jnp.where(chosen, values[:, None, :], jnp.zeros((), values.dtype)), axis=2)
-
-    channel = ordered(channels)
-    same = jnp.concatenate(
-        [jnp.zeros_like(channel[:, :1]), (channel[:, 1:] == channel[:, :-1]).astype(jnp.int32)], axis=1
-    )
-    ints = jnp.stack([ordered(slots(sources, local_count)), channel, same], axis=1)
-    return ints, ordered(couplings)
-
-
-def apply_operator(ints, floats, state, left, right, mixed, image):
+    apart = lax.div(sector, blocks) ^ here
+    place = jnp.int32(0)
+    for position in range(1, devices):
+        place = jnp.where(apart == APART[position], position, place)
+    return place * blocks + lax.rem(sector, blocks)
+
+
+def table_kernel(width, devices, here, sources, channels, couplings, ints, floats, starts):
+    blocks, pairs = sources.shape
+    for t in range(blocks):
+
+        def clear(w, carry):
+            starts[w] = 0
+            return carry
+
+        def count(k, carry):
+            starts[channels[t, k] + 1] += 1
+            return carry
+
+        def add(w, total):
+            total += starts[w]
+            starts[w] = total
+            return total
+
+        def put(k, carry):
+            channel = channels[t, k]
+            to = starts[channel]
+            starts[channel] = to + 1
+            ints[t, 0, to] = slot(sources[t, k], blocks, devices, here[0])
+            ints[t, 1, to] = channel
+            floats[t, to] = couplings[t, k]
+            return carry
+
+        def compare(k, carry):
+            ints[t, 2, k] = (ints[t, 1, k] == ints[t, 1, k - 1]).astype(jnp.int32)
+            return carry
+
+        lax.fori_loop(0, width + 1, clear, 0)
+        lax.fori_loop(0, pairs, count, 0)
+        lax.fori_loop(0, width + 1, add, jnp.int32(0))
+        lax.fori_loop(0, pairs, put, 0)
+        ints[t, 2, 0] = 0
+        lax.fori_loop(1, pairs, compare, 0)
+
+
+def fetch(sources, targets, semaphores):
+    copies = [
+        pltpu.make_async_copy(source, target, semaphores.at[at])
+        for at, (source, target) in enumerate(zip(sources, targets))
+    ]
+    for copy in copies:
+        copy.start()
+    return copies
+
+
+def apply_operator(ints, floats, state, copies, left, right, mixed, image):
     blocks, width = left.shape[0], left.shape[1]
     pairs = floats.shape[1]
     mixed[...] = jnp.zeros_like(mixed)
@@ -64,6 +96,8 @@
             term = floats[t, k] * state[ints[t, 0, k]]
             total = term + jnp.where(ints[t, 2, k] == 1, total, 0.0)
             mixed[t, ints[t, 1, k]] = total.astype(jnp.bfloat16)
+    for copy in copies:
+        copy.wait()
     for t in range(blocks):
         result = jnp.zeros(image.shape[1:], jnp.float32)
         for w in range(0, width, 2):
@@ -88,10 +122,11 @@
         at += size
 
 
-def first_kernel(count, ints, floats, left, right, *refs):
-    pieces, (image, state, mixed) = refs[:count], refs[count:]
+def first_kernel(count, ints, floats, *refs):
+    environment, pieces, (image, state, mixed, left, right, semaphores) = refs[:2], refs[2 : 2 + count], refs[2 + count :]
+    copies = fetch(environment, (left, right), semaphores)
     spread(pieces, state)
-    apply_operator(ints, floats, state, left, right, mixed, image)
+    apply_operator(ints, floats, state, copies, left, right, mixed, image)
 
 
 def rayleigh_update(before, images, after):
@@ -117,18 +152,20 @@
     return energy
 
 
-def middle_kernel(states, count, ints, floats, left, right, *refs):
-    before, images = refs[:states], refs[states : states + count]
-    energy, state, image, mixed = refs[states + count :]
-    energy[0, 0] = rayleigh_update(before, images, state)
-    apply_operator(ints, floats, state, left, right, mixed, image)
-
-
-def last_kernel(states, count, ints, floats, ranks, left, right, *refs):
-    before, images = refs[:states], refs[states : states + count]
-    energy, own, image, sums, state, mixed = refs[states + count :]
-    energy[0, 0] = rayleigh_update(before, images, state)
-    apply_operator(ints, floats, state, left, right, mixed, image)
+def middle_kernel(states, count, ints, floats, *refs):
+    environment, before, images = refs[:2], refs[2 : 2 + states], refs[2 + states : 2 + states + count]
+    energy, state, image, mixed, left, right, semaphores = refs[2 + states + count :]
+    copies = fetch(environment, (left, right), semaphores)
+    energy[...] = jnp.full(energy.shape, rayleigh_update(before, images, state))
+    apply_operator(ints, floats, state, copies, left, right, mixed, image)
+
+
+def last_kernel(states, count, ints, floats, ranks, *refs):
+    environment, before, images = refs[:2], refs[2 : 2 + states], refs[2 + states : 2 + states + count]
+    energy, own, image, sums, state, mixed, left, right, semaphores = refs[2 + states + count :]
+    copies = fetch(environment, (left, right), semaphores)
+    energy[...] = jnp.full(energy.shape, rayleigh_update(before, images, state))
+    apply_operator(ints, floats, state, copies, left, right, mixed, image)
     blocks, size = image.shape[0], image.shape[1]
     own[...] = state[:blocks]
     intersection = jnp.zeros((size, size), jnp.float32)
@@ -158,8 +195,8 @@
     sums[...] = result
 
 
-def finish_kernel(count, entries, ranks, own, image, *refs):
-    gathered, (energy, kept) = refs[:count], refs[count:]
+def finish_kernel(steps, count, entries, ranks, own, image, *refs):
+    earlier, gathered, (energies, kept) = refs[:steps], refs[steps : steps + count], refs[steps + count :]
     rows = []
     for piece in gathered:
         rows += [piece[s] for s in range(piece.shape[0])]
@@ -170,7 +207,11 @@
     for row in rows:
         shift = STEP * (total - row[2:3, :])
         kept_sq += row[3:4, :] + 2.0 * shift * row[4:5, :] + shift * shift * row[5:6, :]
-    energy[...] = jnp.broadcast_to(total, energy.shape)
+    column = lax.broadcasted_iota(jnp.int32, total.shape, 1)
+    listed = total
+    for step, energy in enumerate(earlier):
+        listed = jnp.where(column == step, energy[...], listed)
+    energies[...] = listed[:, : steps + 1]
     growth = 1.0 + STEP * total
     scale = 1.0 / jnp.sqrt(jnp.maximum(kept_sq, 0.0) / entries + EPSILON)
     size = image.shape[1]
@@ -189,33 +230,51 @@
     sectors = blocks * lax.axis_size("sec")
     entries = float(sectors * size * size)
     ranks = kept_rank[0]
-    ints, floats = pair_table(sources[0], channels[0], couplings[0], blocks)
+    devices = lax.axis_size("sec")
+    pairs = sources.shape[2]
+    params = pltpu.CompilerParams(vmem_limit_bytes=32 * 2**20)
+    ints, floats = pl.pallas_call(
+        functools.partial(table_kernel, width, devices),
+        out_shape=(
+            jax.ShapeDtypeStruct((blocks, 3, pairs), jnp.int32),
+            jax.ShapeDtypeStruct((blocks, pairs), jnp.float32),
+        ),
+        in_specs=[SMEM] * 4,
+        out_specs=(SMEM, SMEM),
+        scratch_shapes=[pltpu.SMEM((width + 1,), jnp.int32)],
+        compiler_params=params,
+        name="pair_table",
+    )(lax.axis_index("sec").reshape(1), sources[0], channels[0], couplings[0])
 
     own_type = jax.ShapeDtypeStruct((blocks, size, size), jnp.bfloat16)
-    number = jax.ShapeDtypeStruct((1, 1), jnp.float32)
+    number = jax.ShapeDtypeStruct((1, 128), jnp.float32)
     whole = (sectors, size, size)
-    mixed = pltpu.VMEM((blocks, width, size, size), jnp.bfloat16)
-    params = pltpu.CompilerParams(vmem_limit_bytes=24 * 2**20)
+    scratch = [
+        pltpu.VMEM(left.shape, jnp.bfloat16),
+        pltpu.VMEM(left.shape, jnp.bfloat16),
+        pltpu.VMEM(left.shape, jnp.bfloat16),
+        pltpu.SemaphoreType.DMA((2,)),
+    ]
 
     states = gather(start)
     image = pl.pallas_call(
         functools.partial(first_kernel, len(states)),
         out_shape=own_type,
-        in_specs=[SMEM, SMEM] + [VMEM] * (2 + len(states)),
+        in_specs=[SMEM, SMEM, ANY, ANY] + [VMEM] * len(states),
         out_specs=VMEM,
-        scratch_shapes=[pltpu.VMEM(whole, jnp.float32), mixed],
+        scratch_shapes=[pltpu.VMEM(whole, jnp.float32)] + scratch,
         compiler_params=params,
         name="first_image",
     )(ints, floats, left, right, *states)
     energies = []
-    for iteration in range(1, ITERS - 1):
+    for _ in range(1, ITERS - 1):
         images = gather(image)
         energy, state, image = pl.pallas_call(
             functools.partial(middle_kernel, len(states), len(images)),
             out_shape=(number, jax.ShapeDtypeStruct(whole, jnp.float32), own_type),
-            in_specs=[SMEM, SMEM] + [VMEM] * (2 + len(states) + len(images)),
-            out_specs=(SMEM, VMEM, VMEM),
-            scratch_shapes=[mixed],
+            in_specs=[SMEM, SMEM, ANY, ANY] + [VMEM] * (len(states) + len(images)),
+            out_specs=(VMEM, VMEM, VMEM),
+            scratch_shapes=scratch,
             compiler_params=params,
             name="middle_image",
         )(ints, floats, left, right, *states, *images)
@@ -230,24 +289,23 @@
             own_type,
             jax.ShapeDtypeStruct((1, 8, 128), jnp.float32),
         ),
-        in_specs=[SMEM, SMEM, SMEM] + [VMEM] * (2 + len(states) + len(images)),
-        out_specs=(SMEM, VMEM, VMEM, VMEM),
-        scratch_shapes=[pltpu.VMEM(whole, jnp.float32), mixed],
+        in_specs=[SMEM, SMEM, SMEM, ANY, ANY] + [VMEM] * (len(states) + len(images)),
+        out_specs=(VMEM, VMEM, VMEM, VMEM),
+        scratch_shapes=[pltpu.VMEM(whole, jnp.float32)] + scratch,
         compiler_params=params,
         name="last_image",
     )(ints, floats, ranks, left, right, *states, *images)
     energies.append(energy)
     gathered = gather(sums)
-    energy, kept = pl.pallas_call(
-        functools.partial(finish_kernel, len(gathered), entries),
-        out_shape=(jax.ShapeDtypeStruct((1, 128), jnp.float32), own_type),
-        in_specs=[SMEM] + [VMEM] * (2 + len(gathered)),
+    energies, kept = pl.pallas_call(
+        functools.partial(finish_kernel, len(energies), len(gathered), entries),
+        out_shape=(jax.ShapeDtypeStruct((1, ITERS), jnp.float32), own_type),
+        in_specs=[SMEM] + [VMEM] * (2 + len(energies) + len(gathered)),
         out_specs=(VMEM, VMEM),
         compiler_params=params,
         name="finish",
-    )(ranks, own, image, *gathered)
-    energies.append(energy[:, :1])
-    return kept[None], jnp.concatenate(energies, axis=1)
+    )(ranks, own, image, *energies, *gathered)
+    return kept[None], energies
 
 
 def solution(mesh):

time: 80.2 us -> 71.6 us (0.89)
  starting transfers between devices: 45.8 us -> 27.4 us
  waiting for transfers between devices: 15.2 us -> 23.7 us
  Pallas kernels: 10.6 us -> 15.2 us
  other arithmetic: 5.28 us -> 0.87 us
  local copies, waits for them, and re-layouts: 2.26 us -> 3.47 us
    ppermute x28 -> x16, starting transfers between devices: 45.3 us -> 26.8 us  [hop(): return lax.ppermute(block, 'sec', [(a, a ^ distance) for a in range(count)])]
    ppermute x28 -> x16, waiting for transfers between devices: 15.2 us -> 23.7 us  [hop(): return lax.ppermute(block, 'sec', [(a, a ^ distance) for a in range(count)])]
    pallas_call x1 -> x2, Pallas kernels: 1.23 us -> 5.53 us  [the longest x1 4.3 us: local(): pl.pallas_call(functools.partial(table_kernel, width, devices), out_shape...]
    reduce_sum x3 -> x0, other arithmetic: 2.53 us -> none  [the longest x2 1.6 us: ordered(): jnp.sum(jnp.where(chosen, values[:, None, :], jnp.zeros((), values.dtype)...]
    unnamed x8 -> x12, local copies, waits for them, and re-layouts: 2.26 us -> 3.45 us
    concatenate x1 -> x2, other arithmetic: 1.88 us -> 0.87 us  [gather(): both = jnp.concatenate([block, hop(block, 4)])]
  transfers between devices with their start and end apart: 29 -> 17, of which waited for: 10 -> 13; matrix products, arithmetic and copies ran while one was open for 4% -> 1% of each run, Pallas kernels for 0% -> 6%
where the time goes in v2:
time: 71.6 us; the launch traced here: 71.3 us
  starting transfers between devices  27.4 us (38%)
  waiting for transfers between devices  23.7 us (33%)
  Pallas kernels  15.2 us (21%)
  local copies, waits for them, and re-layouts  3.47 us (5%)
  other arithmetic  0.87 us (1%)
  between operations  0.74 us (1%)
    ppermute x16, starting transfers between devices, hop(): return lax.ppermute(block, 'sec', [(a, a ^ distance) for a in range(count)])  26.8 us
    ppermute x16, waiting for transfers between devices, hop(): return lax.ppermute(block, 'sec', [(a, a ^ distance) for a in range(count)])  23.7 us
    pallas_call x1, Pallas kernels, local(): pl.pallas_call(functools.partial(table_kernel, width, devices), out_shape...  4.3 us
    pallas_call x1, Pallas kernels, local(): pl.pallas_call(functools.partial(last_kernel, len(states), len(images)),...  3.59 us
    unnamed x12, local copies, waits for them, and re-layouts  3.45 us
    pallas_call x1, Pallas kernels, local(): pl.pallas_call(functools.partial(middle_kernel, len(states), len(images))...  3.26 us
    pallas_call x1, Pallas kernels, local(): pl.pallas_call(functools.partial(first_kernel, len(states)), out_shape=ow...  2.84 us
  transfers between devices with their start and end apart: 17, of which 13 were waited for; matrix products, arithmetic and copies ran while one was open for 1% of the time, Pallas kernels for 6%

profile of v2, /device:TPU:0, one launch (start us, length us, event | category | flops | bytes accessed | tf_op | source)
XLA Modules:
  0.0 71.3 jit_solution(5267013886963897946)
XLA Ops:
  0.6 0.5 collective-permute-start
  1.1 3.7 %collective-permute-start.1 = (bf16[2,128,128]{2,1,0:T(8,128)(2,1)}, bf16[2,128,128]{2,1,0:T(8,128)(2,1)S(1)}, u32[]{:S(2)}, u32[]{:S(2)}) collective-permute-start(bf16[2,128,128]{2,1,0:T(8,128)(2,1)} %bitcast.17), channel_id=1, source_target_pairs={{0,4},{1,5},{2,6},{3,7},{4,0},{5,1},{6,2},{7,3},{8,12},{9,13},{10,... | collective-permute-start | bytes 196616 | tf_op jit(solution)/shard_map/ppermute | solution.py:21
  4.8 4.3 %collective-permute-done.1 = bf16[2,128,128]{2,1,0:T(8,128)(2,1)S(1)} collective-permute-done((bf16[2,128,128]{2,1,0:T(8,128)(2,1)}, bf16[2,128,128]{2,1,0:T(8,128)(2,1)S(1)}, u32[]{:S(2)}, u32[]{:S(2)}) %collective-permute-start.1) | collective-permute-done | bytes 65568 | tf_op jit(solution)/shard_map/ppermute | solution.py:21
  9.1 0.9 %pad_maximum_fusion.refs_2_ = bf16[4,128,128]{2,1,0:T(8,128)(2,1)S(1)} fusion(bf16[2,128,128]{2,1,0:T(8,128)(2,1)S(1)} %collective-permute-done.1, bf16[2,128,128]{2,1,0:T(8,128)(2,1)} %bitcast.18), kind=kLoop, calls=%fused_computation | loop fusion | flops 65536 | bytes 262144 | tf_op jit(solution)/shard_map/concatenate | solution.py:27
  10.0 1.7 %collective-permute-start.4 = (bf16[4,128,128]{2,1,0:T(8,128)(2,1)S(1)}, bf16[4,128,128]{2,1,0:T(8,128)(2,1)S(1)}, u32[]{:S(2)}, u32[]{:S(2)}) collective-permute-start(bf16[4,128,128]{2,1,0:T(8,128)(2,1)S(1)} %pad_maximum_fusion.refs_2_), channel_id=1, source_target_pairs={{0,1},{1,0},{2,3},{3,2},{4,5},{5,4},{6,7},{7,6},{8,9},{9,8},{10,11... | collective-permute-start | bytes 393224 | tf_op jit(solution)/shard_map/ppermute | solution.py:21
  11.6 0.8 %collective-permute-start.3 = (bf16[4,128,128]{2,1,0:T(8,128)(2,1)S(1)}, bf16[4,128,128]{2,1,0:T(8,128)(2,1)S(1)}, u32[]{:S(2)}, u32[]{:S(2)}) collective-permute-start(bf16[4,128,128]{2,1,0:T(8,128)(2,1)S(1)} %pad_maximum_fusion.refs_2_), channel_id=1, source_target_pairs={{0,2},{1,3},{2,0},{3,1},{4,6},{5,7},{6,4},{7,5},{8,10},{9,11},{10,... | collective-permute-start | bytes 393224 | tf_op jit(solution)/shard_map/ppermute | solution.py:21
  12.4 1.1 %collective-permute-start.2 = (bf16[4,128,128]{2,1,0:T(8,128)(2,1)S(1)}, bf16[4,128,128]{2,1,0:T(8,128)(2,1)S(1)}, u32[]{:S(2)}, u32[]{:S(2)}) collective-permute-start(bf16[4,128,128]{2,1,0:T(8,128)(2,1)S(1)} %pad_maximum_fusion.refs_2_), channel_id=1, source_target_pairs={{0,3},{1,2},{2,1},{3,0},{4,7},{5,6},{6,5},{7,4},{8,11},{9,10},{10,... | collective-permute-start | bytes 393224 | tf_op jit(solution)/shard_map/ppermute | solution.py:21
  13.5 0.0 copy-start.2
  13.5 0.7 copy-done.2
  14.2 0.7 copy-done.3
  14.9 0.7 copy-done.4
  15.6 4.3 %pair_table.1 = (s32[2,3,32]{2,1,0:T(4,128)S(1)}, f32[2,32]{1,0:T(2,128)S(1)}) custom-call(s32[1]{0:T(128)} %bitcast.1.here, s32[2,32]{1,0:T(2,128)S(1)} %bitcast.14, s32[2,32]{1,0:T(2,128)S(1)} %bitcast.15, f32[2,32]{1,0:T(2,128)S(1)} %bitcast.16), custom_call_target="tpu_custom_call" | custom-call | tf_op jit(solution)/shard_map/pair_table/pallas_call | solution.py:236
  19.9 0.0 collective-permute-done.4.refs_5_
  19.9 0.0 collective-permute-done.3.refs_4_
  19.9 0.0 collective-permute-done.2.refs_3_
  19.9 0.0 collective-permute-done.refs_1_
  19.9 0.0 copy-start
  19.9 1.4 %copy-done = bf16[1,2,24,128,128]{4,3,2,1,0:T(8,128)(2,1)S(1)} copy-done((bf16[1,2,24,128,128]{4,3,2,1,0:T(8,128)(2,1)S(1)}, bf16[1,2,24,128,128]{4,3,2,1,0:T(8,128)(2,1)}, u32[]{:S(2)}) %copy-start) | copy-done | bytes 1572888
  21.3 2.8 %first_image.1 = bf16[2,128,128]{2,1,0:T(8,128)(2,1)S(1)} custom-call(s32[2,3,32]{2,1,0:T(4,128)S(1)} %get-tuple-element.13.ints, f32[2,32]{1,0:T(2,128)S(1)} %get-tuple-element.14.floats, bf16[2,24,128,128]{3,2,1,0:T(8,128)(2,1)S(1)} %bitcast.9, bf16[2,24,128,128]{3,2,1,0:T(8,128)(2,1)S(1)} %collective-permute-done.refs_1_, ...), custom_call_target="tpu_custom_call" | custom-call | tf_op jit(solution)/shard_map/first_image/pallas_call | solution.py:260
  24.2 2.2 %collective-permute-start.5 = (bf16[2,128,128]{2,1,0:T(8,128)(2,1)S(1)}, bf16[2,128,128]{2,1,0:T(8,128)(2,1)S(1)}, u32[]{:S(2)}, u32[]{:S(2)}) collective-permute-start(bf16[2,128,128]{2,1,0:T(8,128)(2,1)S(1)} %first_image.1), channel_id=1, source_target_pairs={{0,4},{1,5},{2,6},{3,7},{4,0},{5,1},{6,2},{7,3},{8,12},{9,13},{10,... | collective-permute-start | bytes 196616 | tf_op jit(solution)/shard_map/ppermute | solution.py:21
  26.4 3.0 %collective-permute-done.5 = bf16[2,128,128]{2,1,0:T(8,128)(2,1)S(1)} collective-permute-done((bf16[2,128,128]{2,1,0:T(8,128)(2,1)S(1)}, bf16[2,128,128]{2,1,0:T(8,128)(2,1)S(1)}, u32[]{:S(2)}, u32[]{:S(2)}) %collective-permute-start.5) | collective-permute-done | bytes 65568 | tf_op jit(solution)/shard_map/ppermute | solution.py:21
  29.4 0.0 copy-start.1
  29.4 2.3 %collective-permute-start.8 = (bf16[4,128,128]{2,1,0:T(8,128)(2,1)S(1)}, bf16[4,128,128]{2,1,0:T(8,128)(2,1)S(1)}, u32[]{:S(2)}, u32[]{:S(2)}) collective-permute-start(bf16[4,128,128]{2,1,0:T(8,128)(2,1)S(1)} %pad_maximum_fusion.1.refs_6_), channel_id=1, source_target_pairs={{0,1},{1,0},{2,3},{3,2},{4,5},{5,4},{6,7},{7,6},{8,9},{9,8},{10,11... | collective-permute-start | bytes 393224 | tf_op jit(solution)/shard_map/ppermute | solution.py:21
  31.8 0.5 collective-permute-start.7
  32.3 1.0 %collective-permute-start.6 = (bf16[4,128,128]{2,1,0:T(8,128)(2,1)S(1)}, bf16[4,128,128]{2,1,0:T(8,128)(2,1)S(1)}, u32[]{:S(2)}, u32[]{:S(2)}) collective-permute-start(bf16[4,128,128]{2,1,0:T(8,128)(2,1)S(1)} %pad_maximum_fusion.1.refs_6_), channel_id=1, source_target_pairs={{0,3},{1,2},{2,1},{3,0},{4,7},{5,6},{6,5},{7,4},{8,11},{9,10},{10,... | collective-permute-start | bytes 393224 | tf_op jit(solution)/shard_map/ppermute | solution.py:21
  33.3 2.8 %collective-permute-done.8.refs_9_ = bf16[4,128,128]{2,1,0:T(8,128)(2,1)S(1)} collective-permute-done((bf16[4,128,128]{2,1,0:T(8,128)(2,1)S(1)}, bf16[4,128,128]{2,1,0:T(8,128)(2,1)S(1)}, u32[]{:S(2)}, u32[]{:S(2)}) %collective-permute-start.8) | collective-permute-done | bytes 131104 | tf_op jit(solution)/shard_map/ppermute | solution.py:21
  36.1 0.6 collective-permute-done.7.refs_8_
  36.8 1.4 %collective-permute-done.6.refs_7_ = bf16[4,128,128]{2,1,0:T(8,128)(2,1)S(1)} collective-permute-done((bf16[4,128,128]{2,1,0:T(8,128)(2,1)S(1)}, bf16[4,128,128]{2,1,0:T(8,128)(2,1)S(1)}, u32[]{:S(2)}, u32[]{:S(2)}) %collective-permute-start.6) | collective-permute-done | bytes 131104 | tf_op jit(solution)/shard_map/ppermute | solution.py:21
  38.2 3.3 %middle_image.1 = (f32[1,128]{1,0:T(1,128)S(1)}, f32[16,128,128]{2,1,0:T(8,128)S(1)}, bf16[2,128,128]{2,1,0:T(8,128)(2,1)S(1)}) custom-call(s32[2,3,32]{2,1,0:T(4,128)S(1)} %get-tuple-element.13.ints, f32[2,32]{1,0:T(2,128)S(1)} %get-tuple-element.14.floats, bf16[2,24,128,128]{3,2,1,0:T(8,128)(2,1)S(1)} %bitcast.10, ...), custom_call_target="tpu_custom_call" | custom-call | tf_op jit(solution)/shard_map/middle_image/pallas_call | solution.py:272
  41.5 3.0 %collective-permute-start.9 = (bf16[2,128,128]{2,1,0:T(8,128)(2,1)S(1)}, bf16[2,128,128]{2,1,0:T(8,128)(2,1)S(1)}, u32[]{:S(2)}, u32[]{:S(2)}) collective-permute-start(bf16[2,128,128]{2,1,0:T(8,128)(2,1)S(1)} %get-tuple-element.16), channel_id=1, source_target_pairs={{0,4},{1,5},{2,6},{3,7},{4,0},{5,1},{6,2},{7,3},{8,12},{9,13},{10,... | collective-permute-start | bytes 196616 | tf_op jit(solution)/shard_map/ppermute | solution.py:21
  44.5 2.4 %collective-permute-done.9 = bf16[2,128,128]{2,1,0:T(8,128)(2,1)S(1)} collective-permute-done((bf16[2,128,128]{2,1,0:T(8,128)(2,1)S(1)}, bf16[2,128,128]{2,1,0:T(8,128)(2,1)S(1)}, u32[]{:S(2)}, u32[]{:S(2)}) %collective-permute-start.9) | collective-permute-done | bytes 65568 | tf_op jit(solution)/shard_map/ppermute | solution.py:21
  46.9 2.1 %collective-permute-start.12 = (bf16[4,128,128]{2,1,0:T(8,128)(2,1)S(1)}, bf16[4,128,128]{2,1,0:T(8,128)(2,1)S(1)}, u32[]{:S(2)}, u32[]{:S(2)}) collective-permute-start(bf16[4,128,128]{2,1,0:T(8,128)(2,1)S(1)} %constant_dynamic-update-slice_fusion.refs_3_), channel_id=1, source_target_pairs={{0,1},{1,0},{2,3},{3,2},{4,5},{5,4},{6,7},{7,6},{8,9},{9,8},{10,11... | collective-permute-start | bytes 393224 | tf_op jit(solution)/shard_map/ppermute | solution.py:21
  49.0 0.0 collective-permute-start.11
  49.0 1.5 %collective-permute-start.10 = (bf16[4,128,128]{2,1,0:T(8,128)(2,1)S(1)}, bf16[4,128,128]{2,1,0:T(8,128)(2,1)S(1)}, u32[]{:S(2)}, u32[]{:S(2)}) collective-permute-start(bf16[4,128,128]{2,1,0:T(8,128)(2,1)S(1)} %constant_dynamic-update-slice_fusion.refs_3_), channel_id=1, source_target_pairs={{0,3},{1,2},{2,1},{3,0},{4,7},{5,6},{6,5},{7,4},{8,11},{9,10},{10,... | collective-permute-start | bytes 393224 | tf_op jit(solution)/shard_map/ppermute | solution.py:21
  50.6 1.8 %collective-permute-done.12.refs_6_ = bf16[4,128,128]{2,1,0:T(8,128)(2,1)S(1)} collective-permute-done((bf16[4,128,128]{2,1,0:T(8,128)(2,1)S(1)}, bf16[4,128,128]{2,1,0:T(8,128)(2,1)S(1)}, u32[]{:S(2)}, u32[]{:S(2)}) %collective-permute-start.12) | collective-permute-done | bytes 131104 | tf_op jit(solution)/shard_map/ppermute | solution.py:21
  52.3 1.7 %collective-permute-done.11.refs_5_ = bf16[4,128,128]{2,1,0:T(8,128)(2,1)S(1)} collective-permute-done((bf16[4,128,128]{2,1,0:T(8,128)(2,1)S(1)}, bf16[4,128,128]{2,1,0:T(8,128)(2,1)S(1)}, u32[]{:S(2)}, u32[]{:S(2)}) %collective-permute-start.11) | collective-permute-done | bytes 131104 | tf_op jit(solution)/shard_map/ppermute | solution.py:21
  54.0 0.9 %collective-permute-done.10.refs_4_ = bf16[4,128,128]{2,1,0:T(8,128)(2,1)S(1)} collective-permute-done((bf16[4,128,128]{2,1,0:T(8,128)(2,1)S(1)}, bf16[4,128,128]{2,1,0:T(8,128)(2,1)S(1)}, u32[]{:S(2)}, u32[]{:S(2)}) %collective-permute-start.10) | collective-permute-done | bytes 131104 | tf_op jit(solution)/shard_map/ppermute | solution.py:21
  54.9 0.0 copy-done.1
  54.9 3.6 %last_image.1 = (f32[1,128]{1,0:T(1,128)S(1)}, f32[2,128,128]{2,1,0:T(8,128)S(1)}, bf16[2,128,128]{2,1,0:T(8,128)(2,1)S(1)}, f32[1,8,128]{2,1,0:T(8,128)S(1)}) custom-call(s32[2,3,32]{2,1,0:T(4,128)S(1)} %get-tuple-element.13.ints, f32[2,32]{1,0:T(2,128)S(1)} %get-tuple-element.14.floats, s32[2]{0:T(128)S(1)} %bitcast.12, ...), custom_call_target="tpu_custom_call" | custom-call | tf_op jit(solution)/shard_map/last_image/pallas_call | solution.py:284
  58.5 3.4 %collective-permute-start.13 = (f32[1,8,128]{2,1,0:T(8,128)S(1)}, f32[1,8,128]{2,1,0:T(8,128)S(1)}, u32[]{:S(2)}, u32[]{:S(2)}) collective-permute-start(f32[1,8,128]{2,1,0:T(8,128)S(1)} %get-tuple-element.21), channel_id=1, source_target_pairs={{0,4},{1,5},{2,6},{3,7},{4,0},{5,1},{6,2},{7,3},{8,12},{9,13},{10,... | collective-permute-start | bytes 12296 | tf_op jit(solution)/shard_map/ppermute | solution.py:21
  61.9 1.6 %collective-permute-done.13 = f32[1,8,128]{2,1,0:T(8,128)S(1)} collective-permute-done((f32[1,8,128]{2,1,0:T(8,128)S(1)}, f32[1,8,128]{2,1,0:T(8,128)S(1)}, u32[]{:S(2)}, u32[]{:S(2)}) %collective-permute-start.13) | collective-permute-done | bytes 4128 | tf_op jit(solution)/shard_map/ppermute | solution.py:21
  63.5 1.6 %collective-permute-start.16 = (f32[2,8,128]{2,1,0:T(8,128)S(1)}, f32[2,8,128]{2,1,0:T(8,128)S(1)}, u32[]{:S(2)}, u32[]{:S(2)}) collective-permute-start(f32[2,8,128]{2,1,0:T(8,128)S(1)} %constant_dynamic-update-slice_fusion.2.refs_2_), channel_id=1, source_target_pairs={{0,1},{1,0},{2,3},{3,2},{4,5},{5,4},{6,7},{7,6},{8,9},{9,8},{10,11... | collective-permute-start | bytes 24584 | tf_op jit(solution)/shard_map/ppermute | solution.py:21
  65.0 0.5 collective-permute-start.15
  65.5 1.4 %collective-permute-start.14 = (f32[2,8,128]{2,1,0:T(8,128)S(1)}, f32[2,8,128]{2,1,0:T(8,128)S(1)}, u32[]{:S(2)}, u32[]{:S(2)}) collective-permute-start(f32[2,8,128]{2,1,0:T(8,128)S(1)} %constant_dynamic-update-slice_fusion.2.refs_2_), channel_id=1, source_target_pairs={{0,3},{1,2},{2,1},{3,0},{4,7},{5,6},{6,5},{7,4},{8,11},{9,10},{10,... | collective-permute-start | bytes 24584 | tf_op jit(solution)/shard_map/ppermute | solution.py:21
  67.0 0.2 collective-permute-done.16.refs_5_
  67.1 1.6 %collective-permute-done.15.refs_4_ = f32[2,8,128]{2,1,0:T(8,128)S(1)} collective-permute-done((f32[2,8,128]{2,1,0:T(8,128)S(1)}, f32[2,8,128]{2,1,0:T(8,128)S(1)}, u32[]{:S(2)}, u32[]{:S(2)}) %collective-permute-start.15) | collective-permute-done | bytes 8224 | tf_op jit(solution)/shard_map/ppermute | solution.py:21
  68.7 1.4 %collective-permute-done.14.refs_3_ = f32[2,8,128]{2,1,0:T(8,128)S(1)} collective-permute-done((f32[2,8,128]{2,1,0:T(8,128)S(1)}, f32[2,8,128]{2,1,0:T(8,128)S(1)}, u32[]{:S(2)}, u32[]{:S(2)}) %collective-permute-start.14) | collective-permute-done | bytes 8224 | tf_op jit(solution)/shard_map/ppermute | solution.py:21
  70.1 1.2 %finish.1 = (f32[1,3]{1,0:T(1,128)}, bf16[2,128,128]{2,1,0:T(8,128)(2,1)}) custom-call(s32[2]{0:T(128)S(1)} %bitcast.13, f32[2,128,128]{2,1,0:T(8,128)S(1)} %get-tuple-element.17.own, bf16[2,128,128]{2,1,0:T(8,128)(2,1)S(1)} %get-tuple-element.18.image, f32[1,128]{1,0:T(1,128)S(1)} %get-tuple-element.19.refs_0_, f32[1,128]{1,0:T(1,128)S(1)} %get-tuple-element.20.refs_1_, ...), custom_call_target="tpu_custom_call" | custom-call | tf_op jit(solution)/shard_map/finish/pallas_call | solution.py:300
  (7 shorter events, 0.0 us)
Async XLA Ops:
  0.6 19.3 %collective-permute-start = (bf16[2,24,128,128]{3,2,1,0:T(8,128)(2,1)}, bf16[2,24,128,128]{3,2,1,0:T(8,128)(2,1)S(1)}, u32[]{:S(2)}, u32[]{:S(2)}) collective-permute-start(bf16[2,24,128,128]{3,2,1,0:T(8,128)(2,1)} %bitcast.19), channel_id=1, source_target_pairs={{0,8},{8,0},{1,9},{9,1},{2,10},{10,2},{3,11},{11,3},{4,12},{12,4},... | collective-permute-start | bytes 4718600 | tf_op jit(solution)/shard_map/ppermute | solution.py:227
  1.1 8.0 %collective-permute-start.1 = (bf16[2,128,128]{2,1,0:T(8,128)(2,1)}, bf16[2,128,128]{2,1,0:T(8,128)(2,1)S(1)}, u32[]{:S(2)}, u32[]{:S(2)}) collective-permute-start(bf16[2,128,128]{2,1,0:T(8,128)(2,1)} %bitcast.17), channel_id=1, source_target_pairs={{0,4},{1,5},{2,6},{3,7},{4,0},{5,1},{6,2},{7,3},{8,12},{9,13},{10,... | collective-permute-start | bytes 196616 | tf_op jit(solution)/shard_map/ppermute | solution.py:21
  10.0 9.9 %collective-permute-start.4 = (bf16[4,128,128]{2,1,0:T(8,128)(2,1)S(1)}, bf16[4,128,128]{2,1,0:T(8,128)(2,1)S(1)}, u32[]{:S(2)}, u32[]{:S(2)}) collective-permute-start(bf16[4,128,128]{2,1,0:T(8,128)(2,1)S(1)} %pad_maximum_fusion.refs_2_), channel_id=1, source_target_pairs={{0,1},{1,0},{2,3},{3,2},{4,5},{5,4},{6,7},{7,6},{8,9},{9,8},{10,11... | collective-permute-start | bytes 393224 | tf_op jit(solution)/shard_map/ppermute | solution.py:21
  11.6 8.3 %collective-permute-start.3 = (bf16[4,128,128]{2,1,0:T(8,128)(2,1)S(1)}, bf16[4,128,128]{2,1,0:T(8,128)(2,1)S(1)}, u32[]{:S(2)}, u32[]{:S(2)}) collective-permute-start(bf16[4,128,128]{2,1,0:T(8,128)(2,1)S(1)} %pad_maximum_fusion.refs_2_), channel_id=1, source_target_pairs={{0,2},{1,3},{2,0},{3,1},{4,6},{5,7},{6,4},{7,5},{8,10},{9,11},{10,... | collective-permute-start | bytes 393224 | tf_op jit(solution)/shard_map/ppermute | solution.py:21
  12.4 7.5 %collective-permute-start.2 = (bf16[4,128,128]{2,1,0:T(8,128)(2,1)S(1)}, bf16[4,128,128]{2,1,0:T(8,128)(2,1)S(1)}, u32[]{:S(2)}, u32[]{:S(2)}) collective-permute-start(bf16[4,128,128]{2,1,0:T(8,128)(2,1)S(1)} %pad_maximum_fusion.refs_2_), channel_id=1, source_target_pairs={{0,3},{1,2},{2,1},{3,0},{4,7},{5,6},{6,5},{7,4},{8,11},{9,10},{10,... | collective-permute-start | bytes 393224 | tf_op jit(solution)/shard_map/ppermute | solution.py:21
  13.5 0.7 copy-start.2
  14.2 0.7 copy-start.3
  14.9 0.7 copy-start.4
  19.9 1.4 %copy-start = (bf16[1,2,24,128,128]{4,3,2,1,0:T(8,128)(2,1)S(1)}, bf16[1,2,24,128,128]{4,3,2,1,0:T(8,128)(2,1)}, u32[]{:S(2)}) copy-start(bf16[1,2,24,128,128]{4,3,2,1,0:T(8,128)(2,1)} %param.8) | copy-start | bytes 4718596
  24.2 5.2 %collective-permute-start.5 = (bf16[2,128,128]{2,1,0:T(8,128)(2,1)S(1)}, bf16[2,128,128]{2,1,0:T(8,128)(2,1)S(1)}, u32[]{:S(2)}, u32[]{:S(2)}) collective-permute-start(bf16[2,128,128]{2,1,0:T(8,128)(2,1)S(1)} %first_image.1), channel_id=1, source_target_pairs={{0,4},{1,5},{2,6},{3,7},{4,0},{5,1},{6,2},{7,3},{8,12},{9,13},{10,... | collective-permute-start | bytes 196616 | tf_op jit(solution)/shard_map/ppermute | solution.py:21
  29.4 25.5 %copy-start.1 = (s32[1,2]{1,0:T(1,128)S(1)}, s32[1,2]{1,0:T(1,128)}, u32[]{:S(2)}) copy-start(s32[1,2]{1,0:T(1,128)} %param.13) | copy-start | bytes 28
  29.4 6.7 %collective-permute-start.8 = (bf16[4,128,128]{2,1,0:T(8,128)(2,1)S(1)}, bf16[4,128,128]{2,1,0:T(8,128)(2,1)S(1)}, u32[]{:S(2)}, u32[]{:S(2)}) collective-permute-start(bf16[4,128,128]{2,1,0:T(8,128)(2,1)S(1)} %pad_maximum_fusion.1.refs_6_), channel_id=1, source_target_pairs={{0,1},{1,0},{2,3},{3,2},{4,5},{5,4},{6,7},{7,6},{8,9},{9,8},{10,11... | collective-permute-start | bytes 393224 | tf_op jit(solution)/shard_map/ppermute | solution.py:21
  31.8 5.0 %collective-permute-start.7 = (bf16[4,128,128]{2,1,0:T(8,128)(2,1)S(1)}, bf16[4,128,128]{2,1,0:T(8,128)(2,1)S(1)}, u32[]{:S(2)}, u32[]{:S(2)}) collective-permute-start(bf16[4,128,128]{2,1,0:T(8,128)(2,1)S(1)} %pad_maximum_fusion.1.refs_6_), channel_id=1, source_target_pairs={{0,2},{1,3},{2,0},{3,1},{4,6},{5,7},{6,4},{7,5},{8,10},{9,11},{10,... | collective-permute-start | bytes 393224 | tf_op jit(solution)/shard_map/ppermute | solution.py:21
  32.3 5.9 %collective-permute-start.6 = (bf16[4,128,128]{2,1,0:T(8,128)(2,1)S(1)}, bf16[4,128,128]{2,1,0:T(8,128)(2,1)S(1)}, u32[]{:S(2)}, u32[]{:S(2)}) collective-permute-start(bf16[4,128,128]{2,1,0:T(8,128)(2,1)S(1)} %pad_maximum_fusion.1.refs_6_), channel_id=1, source_target_pairs={{0,3},{1,2},{2,1},{3,0},{4,7},{5,6},{6,5},{7,4},{8,11},{9,10},{10,... | collective-permute-start | bytes 393224 | tf_op jit(solution)/shard_map/ppermute | solution.py:21
  41.5 5.4 %collective-permute-start.9 = (bf16[2,128,128]{2,1,0:T(8,128)(2,1)S(1)}, bf16[2,128,128]{2,1,0:T(8,128)(2,1)S(1)}, u32[]{:S(2)}, u32[]{:S(2)}) collective-permute-start(bf16[2,128,128]{2,1,0:T(8,128)(2,1)S(1)} %get-tuple-element.16), channel_id=1, source_target_pairs={{0,4},{1,5},{2,6},{3,7},{4,0},{5,1},{6,2},{7,3},{8,12},{9,13},{10,... | collective-permute-start | bytes 196616 | tf_op jit(solution)/shard_map/ppermute | solution.py:21
  46.9 5.4 %collective-permute-start.12 = (bf16[4,128,128]{2,1,0:T(8,128)(2,1)S(1)}, bf16[4,128,128]{2,1,0:T(8,128)(2,1)S(1)}, u32[]{:S(2)}, u32[]{:S(2)}) collective-permute-start(bf16[4,128,128]{2,1,0:T(8,128)(2,1)S(1)} %constant_dynamic-update-slice_fusion.refs_3_), channel_id=1, source_target_pairs={{0,1},{1,0},{2,3},{3,2},{4,5},{5,4},{6,7},{7,6},{8,9},{9,8},{10,11... | collective-permute-start | bytes 393224 | tf_op jit(solution)/shard_map/ppermute | solution.py:21
  49.0 5.0 %collective-permute-start.11 = (bf16[4,128,128]{2,1,0:T(8,128)(2,1)S(1)}, bf16[4,128,128]{2,1,0:T(8,128)(2,1)S(1)}, u32[]{:S(2)}, u32[]{:S(2)}) collective-permute-start(bf16[4,128,128]{2,1,0:T(8,128)(2,1)S(1)} %constant_dynamic-update-slice_fusion.refs_3_), channel_id=1, source_target_pairs={{0,2},{1,3},{2,0},{3,1},{4,6},{5,7},{6,4},{7,5},{8,10},{9,11},{10,... | collective-permute-start | bytes 393224 | tf_op jit(solution)/shard_map/ppermute | solution.py:21
  49.0 5.9 %collective-permute-start.10 = (bf16[4,128,128]{2,1,0:T(8,128)(2,1)S(1)}, bf16[4,128,128]{2,1,0:T(8,128)(2,1)S(1)}, u32[]{:S(2)}, u32[]{:S(2)}) collective-permute-start(bf16[4,128,128]{2,1,0:T(8,128)(2,1)S(1)} %constant_dynamic-update-slice_fusion.refs_3_), channel_id=1, source_target_pairs={{0,3},{1,2},{2,1},{3,0},{4,7},{5,6},{6,5},{7,4},{8,11},{9,10},{10,... | collective-permute-start | bytes 393224 | tf_op jit(solution)/shard_map/ppermute | solution.py:21
  58.5 5.0 %collective-permute-start.13 = (f32[1,8,128]{2,1,0:T(8,128)S(1)}, f32[1,8,128]{2,1,0:T(8,128)S(1)}, u32[]{:S(2)}, u32[]{:S(2)}) collective-permute-start(f32[1,8,128]{2,1,0:T(8,128)S(1)} %get-tuple-element.21), channel_id=1, source_target_pairs={{0,4},{1,5},{2,6},{3,7},{4,0},{5,1},{6,2},{7,3},{8,12},{9,13},{10,... | collective-permute-start | bytes 12296 | tf_op jit(solution)/shard_map/ppermute | solution.py:21
  63.5 3.7 %collective-permute-start.16 = (f32[2,8,128]{2,1,0:T(8,128)S(1)}, f32[2,8,128]{2,1,0:T(8,128)S(1)}, u32[]{:S(2)}, u32[]{:S(2)}) collective-permute-start(f32[2,8,128]{2,1,0:T(8,128)S(1)} %constant_dynamic-update-slice_fusion.2.refs_2_), channel_id=1, source_target_pairs={{0,1},{1,0},{2,3},{3,2},{4,5},{5,4},{6,7},{7,6},{8,9},{9,8},{10,11... | collective-permute-start | bytes 24584 | tf_op jit(solution)/shard_map/ppermute | solution.py:21
  65.0 3.7 %collective-permute-start.15 = (f32[2,8,128]{2,1,0:T(8,128)S(1)}, f32[2,8,128]{2,1,0:T(8,128)S(1)}, u32[]{:S(2)}, u32[]{:S(2)}) collective-permute-start(f32[2,8,128]{2,1,0:T(8,128)S(1)} %constant_dynamic-update-slice_fusion.2.refs_2_), channel_id=1, source_target_pairs={{0,2},{1,3},{2,0},{3,1},{4,6},{5,7},{6,4},{7,5},{8,10},{9,11},{10,... | collective-permute-start | bytes 24584 | tf_op jit(solution)/shard_map/ppermute | solution.py:21
  65.5 4.5 %collective-permute-start.14 = (f32[2,8,128]{2,1,0:T(8,128)S(1)}, f32[2,8,128]{2,1,0:T(8,128)S(1)}, u32[]{:S(2)}, u32[]{:S(2)}) collective-permute-start(f32[2,8,128]{2,1,0:T(8,128)S(1)} %constant_dynamic-update-slice_fusion.2.refs_2_), channel_id=1, source_target_pairs={{0,3},{1,2},{2,1},{3,0},{4,7},{5,6},{6,5},{7,4},{8,11},{9,10},{10,... | collective-permute-start | bytes 24584 | tf_op jit(solution)/shard_map/ppermute | solution.py:21

commit v3 on v2

v3 whole, which is shorter than its diff:
```python
import functools

import jax
import jax.numpy as jnp
from jax import lax
from jax.experimental import pallas as pl
from jax.experimental.pallas import tpu as pltpu
from jax.sharding import PartitionSpec as P

ITERS = 3
STEP = 0.5
EPSILON = 1e-06
SMEM = pl.BlockSpec(memory_space=pltpu.SMEM)
VMEM = pl.BlockSpec(memory_space=pltpu.VMEM)
ANY = pl.BlockSpec(memory_space=pl.ANY)
HBM = pl.BlockSpec(memory_space=pltpu.HBM)
APART = (0, 4, 1, 2, 3, 7, 6, 5)


def hop(block, distance):
    count = lax.axis_size("sec")
    return lax.ppermute(block, "sec", [(a, a ^ distance) for a in range(count)])


def gather(block):
    if lax.axis_size("sec") != len(APART):
        return [lax.all_gather(block, "sec", axis=0, tiled=True)]
    relayed = hop(block, 4)
    near = [hop(block, distance) for distance in (1, 2, 3)]
    return [block, relayed] + near + [hop(relayed, distance) for distance in (3, 2, 1)]


def gather_small(block):
    if lax.axis_size("sec") != len(APART):
        return [lax.all_gather(block, "sec", axis=0, tiled=True)]
    line = jnp.concatenate([block] + [hop(block, distance) for distance in (2, 4, 6)])
    return [line, hop(line, 1)]


def slot(sector, blocks, devices, here):
    if devices != len(APART):
        return sector
    apart = lax.div(sector, blocks) ^ here
    place = jnp.int32(0)
    for position in range(1, devices):
        place = jnp.where(apart == APART[position], position, place)
    return place * blocks + lax.rem(sector, blocks)


def prepare_kernel(devices, *refs):
    arguments, left, (codes, floats, near), scratch = refs[:3], refs[3], refs[4:7], refs[7:]
    sources, channels, couplings, starts, semaphores = scratch
    copies = fetch((*arguments, left), (sources, channels, couplings, near), semaphores)
    blocks, pairs = sources.shape
    width = near.shape[1]
    here = lax.axis_index("sec")
    seen = 1 << 16
    for w in range(width + 1):
        for t in range(blocks):
            starts[t, w] = 0
    for copy in copies[:3]:
        copy.wait()

    def count(k, carry):
        for t in range(blocks):
            starts[t, channels[t, k] + 1] += 1
        return carry

    def add(w, totals):
        totals = tuple(totals[t] + starts[t, w] for t in range(blocks))
        for t in range(blocks):
            starts[t, w] = totals[t]
        return totals

    def put(k, carry):
        for t in range(blocks):
            channel = channels[t, k]
            mark = starts[t, channel]
            to = mark & (seen - 1)
            starts[t, channel] = (to + 1) | seen
            same = lax.shift_right_logical(mark, 16)
            code = slot(sources[t, k], blocks, devices, here)
            codes[t, to] = (code << 16) | (channel << 1) | same
            floats[t, to] = couplings[t, k]
        return carry

    lax.fori_loop(0, pairs, count, 0, unroll=4)
    lax.fori_loop(0, width + 1, add, (jnp.int32(0),) * blocks, unroll=5)
    lax.fori_loop(0, pairs, put, 0, unroll=2)
    copies[3].wait()


def fetch(sources, targets, semaphores):
    copies = [
        pltpu.make_async_copy(source, target, semaphores.at[at])
        for at, (source, target) in enumerate(zip(sources, targets))
    ]
    for copy in copies:
        copy.start()
    return copies


def apply_operator(copies, codes, floats, state, left, right, mixed, image):
    blocks, width = left.shape[0], left.shape[1]
    pairs = floats.shape[1]
    for t in range(blocks):
        mixed[t][...] = jnp.zeros_like(mixed[t])
    for copy in copies:
        copy.wait()
    for t in range(blocks):
        total = jnp.zeros(state.shape[1:], jnp.float32)
        for k in range(pairs):
            code = codes[t, k]
            term = floats[t, k] * state[lax.shift_right_logical(code, 16)]
            total = term + jnp.where((code & 1) == 1, total, 0.0)
            mixed[t][lax.shift_right_logical(code, 1) & 0x7FFF] = total.astype(jnp.bfloat16)
    for t in range(blocks):
        result = jnp.zeros(image.shape[1:], jnp.float32)
        for w in range(0, width, 2):
            halves = [
                jnp.dot(left[t, v], mixed[t][v], preferred_element_type=jnp.float32).astype(jnp.bfloat16)
                for v in (w, w + 1)
            ]
            result += lax.dot_general(
                jnp.concatenate(halves, axis=1),
                jnp.concatenate([right[t, w], right[t, w + 1]], axis=1),
                (((1,), (1,)), ((), ())),
                preferred_element_type=jnp.float32,
            )
        image[t] = result.astype(jnp.bfloat16)


def spread(pieces, target):
    at = 0
    for piece in pieces:
        size = piece.shape[0]
        target[at : at + size] = piece[...].astype(jnp.float32)
        at += size


def first_kernel(count, codes, floats, left, right, *refs):
    pieces, (image, state, codes_here, floats_here, semaphores, *mixed) = refs[:count], refs[count:]
    copies = fetch((codes, floats), (codes_here, floats_here), semaphores)
    spread(pieces, state)
    apply_operator(copies, codes_here, floats_here, state, left, right, mixed, image)


def rayleigh_update(before, images, after):
    shape = before[0].shape[1:]
    intersection = jnp.zeros(shape, jnp.float32)
    squares = jnp.zeros(shape, jnp.float32)
    at = 0
    flat = []
    for piece in before:
        flat += [(piece, s) for s in range(piece.shape[0])]
    pictures = []
    for piece in images:
        pictures += [(piece, s) for s in range(piece.shape[0])]
    for (piece, s), (picture, p) in zip(flat, pictures):
        value = piece[s].astype(jnp.float32)
        intersection += value * picture[p].astype(jnp.float32)
        squares += value * value
    energy = jnp.sum(intersection) / jnp.sum(squares)
    growth = 1.0 + STEP * energy
    for (piece, s), (picture, p) in zip(flat, pictures):
        after[at] = growth * piece[s].astype(jnp.float32) - STEP * picture[p].astype(jnp.float32)
        at += 1
    return energy


def middle_kernel(states, count, codes, floats, left, right, *refs):
    before, images = refs[:states], refs[states : states + count]
    energy, state, image, codes_here, floats_here, semaphores, *mixed = refs[states + count :]
    copies = fetch((codes, floats), (codes_here, floats_here), semaphores)
    energy[...] = jnp.full(energy.shape, rayleigh_update(before, images, state))
    apply_operator(copies, codes_here, floats_here, state, left, right, mixed, image)


def last_kernel(states, count, codes, floats, ranks, left, right, *refs):
    before, images = refs[:states], refs[states : states + count]
    energy, own, image, sums, state, codes_here, floats_here, ranks_here, semaphores, *mixed = refs[states + count :]
    copies = fetch((codes, floats, ranks), (codes_here, floats_here, ranks_here), semaphores)
    energy[...] = jnp.full(energy.shape, rayleigh_update(before, images, state))
    apply_operator(copies, codes_here, floats_here, state, left, right, mixed, image)
    blocks, size = image.shape[0], image.shape[1]
    intersection = jnp.zeros((size, size), jnp.float32)
    squares = jnp.zeros((size, size), jnp.float32)
    for t in range(blocks):
        value = state[t]
        intersection += value * image[t].astype(jnp.float32)
        squares += value * value
    intersection, squares = jnp.sum(intersection), jnp.sum(squares)
    here = jnp.where(squares > 1e-30, intersection / jnp.maximum(squares, 1e-30), 0.0)
    growth = 1.0 + STEP * here
    column = lax.broadcasted_iota(jnp.int32, (size, size), 1)
    dd = jnp.zeros((size, size), jnp.float32)
    dc = jnp.zeros((size, size), jnp.float32)
    cc = jnp.zeros((size, size), jnp.float32)
    for t in range(blocks):
        keep = column < ranks_here[0, t]
        value = jnp.where(keep, state[t], 0.0)
        picture = jnp.where(keep, image[t].astype(jnp.float32), 0.0)
        own[t] = value
        image[t] = picture.astype(jnp.bfloat16)
        moved = growth * value - STEP * picture
        dd += moved * moved
        dc += moved * value
        cc += value * value
    row = lax.broadcasted_iota(jnp.int32, sums.shape, 1)
    result = jnp.zeros(sums.shape, jnp.float32)
    for at, number in enumerate([intersection, squares, here, jnp.sum(dd), jnp.sum(dc), jnp.sum(cc)]):
        result = jnp.where(row == at, number, result)
    sums[...] = result


def finish_kernel(steps, count, entries, own, image, *refs):
    earlier, gathered, (energies, kept) = refs[:steps], refs[steps : steps + count], refs[steps + count :]
    rows = []
    for piece in gathered:
        rows += [piece[s] for s in range(piece.shape[0])]
    intersection = sum(row[0:1, :] for row in rows)
    squares = sum(row[1:2, :] for row in rows)
    total = intersection / squares
    kept_sq = jnp.zeros_like(total)
    for row in rows:
        shift = STEP * (total - row[2:3, :])
        kept_sq += row[3:4, :] + 2.0 * shift * row[4:5, :] + shift * shift * row[5:6, :]
    column = lax.broadcasted_iota(jnp.int32, total.shape, 1)
    listed = total
    for step, energy in enumerate(earlier):
        listed = jnp.where(column == step, energy[...], listed)
    energies[...] = listed[:, : steps + 1]
    growth = 1.0 + STEP * total
    scale = 1.0 / jnp.sqrt(jnp.maximum(kept_sq, 0.0) / entries + EPSILON)
    for t in range(image.shape[0]):
        kept[t] = ((growth * own[t] - STEP * image[t].astype(jnp.float32)) * scale).astype(jnp.bfloat16)


def local(initial_state, left_blocks, right_blocks, sources, channels, couplings, kept_rank):
    start = initial_state[0]
    left = left_blocks[0]
    right = lax.ppermute(right_blocks[0], "seg", [(0, 1), (1, 0)])
    blocks, size = start.shape[0], start.shape[1]
    width = left.shape[1]
    sectors = blocks * lax.axis_size("sec")
    entries = float(sectors * size * size)
    devices = lax.axis_size("sec")
    pairs = sources.shape[2]
    params = pltpu.CompilerParams(vmem_limit_bytes=32 * 2**20)
    ints = jax.ShapeDtypeStruct((blocks, pairs), jnp.int32)
    floats = jax.ShapeDtypeStruct((blocks, pairs), jnp.float32)
    codes, couplings, left = pl.pallas_call(
        functools.partial(prepare_kernel, devices),
        out_shape=(ints, floats, jax.ShapeDtypeStruct(left.shape, left.dtype)),
        in_specs=[HBM] * 4,
        out_specs=(SMEM, SMEM, VMEM),
        scratch_shapes=[
            pltpu.SMEM(ints.shape, jnp.int32),
            pltpu.SMEM(ints.shape, jnp.int32),
            pltpu.SMEM(ints.shape, jnp.float32),
            pltpu.SMEM((blocks, width + 1), jnp.int32),
            pltpu.SemaphoreType.DMA((4,)),
        ],
        compiler_params=params,
        name="prepare",
    )(sources[0], channels[0], couplings[0], left)

    own_type = jax.ShapeDtypeStruct((blocks, size, size), jnp.bfloat16)
    number = jax.ShapeDtypeStruct((1, 128), jnp.float32)
    whole = (sectors, size, size)
    tables = [pltpu.SMEM(ints.shape, jnp.int32), pltpu.SMEM(floats.shape, jnp.float32)]
    mixed = [pltpu.VMEM((width, size, size), jnp.bfloat16)] * blocks

    states = gather(start)
    image = pl.pallas_call(
        functools.partial(first_kernel, len(states)),
        out_shape=own_type,
        in_specs=[ANY, ANY] + [VMEM] * (2 + len(states)),
        out_specs=VMEM,
        scratch_shapes=[pltpu.VMEM(whole, jnp.float32), *tables, pltpu.SemaphoreType.DMA((2,)), *mixed],
        compiler_params=params,
        name="first_image",
    )(codes, couplings, left, right, *states)
    energies = []
    for _ in range(1, ITERS - 1):
        images = gather(image)
        energy, state, image = pl.pallas_call(
            functools.partial(middle_kernel, len(states), len(images)),
            out_shape=(number, jax.ShapeDtypeStruct(whole, jnp.float32), own_type),
            in_specs=[ANY, ANY] + [VMEM] * (2 + len(states) + len(images)),
            out_specs=(VMEM, VMEM, VMEM),
            scratch_shapes=[*tables, pltpu.SemaphoreType.DMA((2,)), *mixed],
            compiler_params=params,
            name="middle_image",
        )(codes, couplings, left, right, *states, *images)
        states = [state]
        energies.append(energy)
    images = gather(image)
    energy, own, image, sums = pl.pallas_call(
        functools.partial(last_kernel, len(states), len(images)),
        out_shape=(
            number,
            jax.ShapeDtypeStruct((blocks, size, size), jnp.float32),
            own_type,
            jax.ShapeDtypeStruct((1, 8, 128), jnp.float32),
        ),
        in_specs=[ANY, ANY, ANY] + [VMEM] * (2 + len(states) + len(images)),
        out_specs=(VMEM, VMEM, VMEM, VMEM),
        scratch_shapes=[
            pltpu.VMEM(whole, jnp.float32),
            *tables,
            pltpu.SMEM((1, blocks), jnp.int32),
            pltpu.SemaphoreType.DMA((3,)),
            *mixed,
        ],
        compiler_params=params,
        name="last_image",
    )(codes, couplings, kept_rank, left, right, *states, *images)
    energies.append(energy)
    gathered = gather_small(sums)
    energies, kept = pl.pallas_call(
        functools.partial(finish_kernel, len(energies), len(gathered), entries),
        out_shape=(jax.ShapeDtypeStruct((1, ITERS), jnp.float32), own_type),
        in_specs=[VMEM] * (2 + len(energies) + len(gathered)),
        out_specs=(VMEM, VMEM),
        compiler_params=params,
        name="finish",
    )(own, image, *energies, *gathered)
    return kept[None], energies


def solution(mesh):
    return jax.shard_map(
        local,
        mesh=mesh,
        in_specs=(
            P(("parts", "seg"), "sec", None, None),
            P(("parts", "seg"), "sec", None, None, None),
            P(("parts", "seg"), "sec", None, None, None),
            P(("parts", "seg"), "sec", None),
            P(("parts", "seg"), "sec", None),
            P(("parts", "seg"), "sec", None),
            P(("parts", "seg"), "sec"),
        ),
        out_specs=(P(("parts", "seg"), "sec", None, None), P(("parts", "seg"), None)),
        check_vma=False,
    )
```

time: 71.6 us -> 65.2 us (0.911)
  waiting for transfers between devices: 23.7 us -> 14.4 us
  starting transfers between devices: 27.4 us -> 35.4 us
  Pallas kernels: 15.2 us -> 10.9 us
  other arithmetic: 0.87 us -> 0 us
    ppermute x16 -> x25, waiting for transfers between devices: 23.7 us -> 14.4 us  [hop(): return lax.ppermute(block, 'sec', [(a, a ^ distance) for a in range(count)])]
    ppermute x16 -> x25, starting transfers between devices: 26.8 us -> 34.9 us  [hop(): return lax.ppermute(block, 'sec', [(a, a ^ distance) for a in range(count)])]
    pallas_call x1, Pallas kernels: 4.3 us -> 2.64 us  [local(): pl.pallas_call(functools.partial(prepare_kernel, devices), out_shape=(int...]
    concatenate x2 -> x0, other arithmetic: 0.87 us -> none  [gather(): both = jnp.concatenate([block, hop(block, 4)])]
    pallas_call x1, Pallas kernels: 3.59 us -> 2.76 us  [local(): pl.pallas_call(functools.partial(last_kernel, len(states), len(images)),...]
    unnamed x12 -> x15, local copies, waits for them, and re-layouts: 3.45 us -> 3.46 us
  transfers between devices with their start and end apart: 17 -> 26, of which waited for: 13 -> 14; matrix products, arithmetic and copies ran while one was open for 1% -> 0% of each run, Pallas kernels for 6% -> 4%
where the time goes in v3:
time: 65.2 us; the launch traced here: 65 us
  starting transfers between devices  35.4 us (54%)
  waiting for transfers between devices  14.4 us (22%)
  Pallas kernels  10.9 us (17%)
  local copies, waits for them, and re-layouts  3.46 us (5%)
  between operations  0.75 us (1%)
    ppermute x25, starting transfers between devices, hop(): return lax.ppermute(block, 'sec', [(a, a ^ distance) for a in range(count)])  34.9 us
    ppermute x25, waiting for transfers between devices, hop(): return lax.ppermute(block, 'sec', [(a, a ^ distance) for a in range(count)])  14.4 us
    unnamed x15, local copies, waits for them, and re-layouts  3.46 us
    pallas_call x1, Pallas kernels, local(): pl.pallas_call(functools.partial(last_kernel, len(states), len(images)),...  2.76 us
    pallas_call x1, Pallas kernels, local(): pl.pallas_call(functools.partial(prepare_kernel, devices), out_shape=(int...  2.64 us
    pallas_call x1, Pallas kernels, local(): pl.pallas_call(functools.partial(middle_kernel, len(states), len(images))...  2.57 us
    pallas_call x1, Pallas kernels, local(): pl.pallas_call(functools.partial(first_kernel, len(states)), out_shape=ow...  2.27 us
  transfers between devices with their start and end apart: 26, of which 14 were waited for; matrix products, arithmetic and copies ran while one was open for 0% of the time, Pallas kernels for 4%

profile of v3, /device:TPU:0, one launch (start us, length us, event | category | flops | bytes accessed | tf_op | source)
XLA Modules:
  0.0 65.0 jit_solution(12560551972460170517)
XLA Ops:
  0.6 0.5 collective-permute-start
  1.1 3.7 %collective-permute-start.1 = (bf16[2,128,128]{2,1,0:T(8,128)(2,1)}, bf16[2,128,128]{2,1,0:T(8,128)(2,1)S(1)}, u32[]{:S(2)}, u32[]{:S(2)}) collective-permute-start(bf16[2,128,128]{2,1,0:T(8,128)(2,1)} %bitcast.8), channel_id=1, source_target_pairs={{0,4},{1,5},{2,6},{3,7},{4,0},{5,1},{6,2},{7,3},{8,12},{9,13},{10,... | collective-permute-start | bytes 196616 | tf_op jit(solution)/shard_map/ppermute | solution.py:22
  4.8 2.5 %collective-permute-start.4 = (bf16[2,128,128]{2,1,0:T(8,128)(2,1)}, bf16[2,128,128]{2,1,0:T(8,128)(2,1)S(1)}, u32[]{:S(2)}, u32[]{:S(2)}) collective-permute-start(bf16[2,128,128]{2,1,0:T(8,128)(2,1)} %bitcast.9), channel_id=1, source_target_pairs={{0,3},{1,2},{2,1},{3,0},{4,7},{5,6},{6,5},{7,4},{8,11},{9,10},{10,... | collective-permute-start | bytes 196616 | tf_op jit(solution)/shard_map/ppermute | solution.py:22
  7.3 0.4 collective-permute-start.3
  7.8 0.5 collective-permute-start.2
  8.3 0.7 %collective-permute-done.1.refs_1_ = bf16[2,128,128]{2,1,0:T(8,128)(2,1)S(1)} collective-permute-done((bf16[2,128,128]{2,1,0:T(8,128)(2,1)}, bf16[2,128,128]{2,1,0:T(8,128)(2,1)S(1)}, u32[]{:S(2)}, u32[]{:S(2)}) %collective-permute-start.1) | collective-permute-done | bytes 65568 | tf_op jit(solution)/shard_map/ppermute | solution.py:22
  9.0 1.6 %collective-permute-start.7 = (bf16[2,128,128]{2,1,0:T(8,128)(2,1)S(1)}, bf16[2,128,128]{2,1,0:T(8,128)(2,1)S(1)}, u32[]{:S(2)}, u32[]{:S(2)}) collective-permute-start(bf16[2,128,128]{2,1,0:T(8,128)(2,1)S(1)} %collective-permute-done.1.refs_1_), channel_id=1, source_target_pairs={{0,1},{1,0},{2,3},{3,2},{4,5},{5,4},{6,7},{7,6},{8,9},{9,8},{10,11... | collective-permute-start | bytes 196616 | tf_op jit(solution)/shard_map/ppermute | solution.py:22
  10.6 0.3 collective-permute-done.4.refs_4_
  10.9 1.5 %collective-permute-start.6 = (bf16[2,128,128]{2,1,0:T(8,128)(2,1)S(1)}, bf16[2,128,128]{2,1,0:T(8,128)(2,1)S(1)}, u32[]{:S(2)}, u32[]{:S(2)}) collective-permute-start(bf16[2,128,128]{2,1,0:T(8,128)(2,1)S(1)} %collective-permute-done.1.refs_1_), channel_id=1, source_target_pairs={{0,2},{1,3},{2,0},{3,1},{4,6},{5,7},{6,4},{7,5},{8,10},{9,11},{10,... | collective-permute-start | bytes 196616 | tf_op jit(solution)/shard_map/ppermute | solution.py:22
  12.4 1.1 %collective-permute-start.5 = (bf16[2,128,128]{2,1,0:T(8,128)(2,1)S(1)}, bf16[2,128,128]{2,1,0:T(8,128)(2,1)S(1)}, u32[]{:S(2)}, u32[]{:S(2)}) collective-permute-start(bf16[2,128,128]{2,1,0:T(8,128)(2,1)S(1)} %collective-permute-done.1.refs_1_), channel_id=1, source_target_pairs={{0,3},{1,2},{2,1},{3,0},{4,7},{5,6},{6,5},{7,4},{8,11},{9,10},{10,... | collective-permute-start | bytes 196616 | tf_op jit(solution)/shard_map/ppermute | solution.py:22
  13.5 1.4 %copy-done = bf16[1,2,24,128,128]{4,3,2,1,0:T(8,128)(2,1)S(1)} copy-done((bf16[1,2,24,128,128]{4,3,2,1,0:T(8,128)(2,1)S(1)}, bf16[1,2,24,128,128]{4,3,2,1,0:T(8,128)(2,1)}, u32[]{:S(2)}) %copy-start) | copy-done | bytes 1572888
  14.9 0.7 %copy-done.2 = s32[1,2,32]{2,1,0:T(2,128)S(1)} copy-done((s32[1,2,32]{2,1,0:T(2,128)S(1)}, s32[1,2,32]{2,1,0:T(2,128)}, u32[]{:S(2)}) %copy-start.2) | copy-done | bytes 280
  15.6 0.7 %copy-done.3 = s32[1,2,32]{2,1,0:T(2,128)S(1)} copy-done((s32[1,2,32]{2,1,0:T(2,128)S(1)}, s32[1,2,32]{2,1,0:T(2,128)}, u32[]{:S(2)}) %copy-start.3) | copy-done | bytes 280
  16.3 0.7 %copy-done.4 = f32[1,2,32]{2,1,0:T(2,128)S(1)} copy-done((f32[1,2,32]{2,1,0:T(2,128)S(1)}, f32[1,2,32]{2,1,0:T(2,128)}, u32[]{:S(2)}) %copy-start.4) | copy-done | bytes 280
  17.0 2.6 %prepare.1 = (s32[2,32]{1,0:T(2,128)S(1)}, f32[2,32]{1,0:T(2,128)S(1)}, bf16[2,24,128,128]{3,2,1,0:T(8,128)(2,1)S(1)}) custom-call(s32[2,32]{1,0:T(2,128)S(1)} %bitcast.14, s32[2,32]{1,0:T(2,128)S(1)} %bitcast.15, f32[2,32]{1,0:T(2,128)S(1)} %bitcast.16, bf16[2,24,128,128]{3,2,1,0:T(8,128)(2,1)S(1)} %bitcast.7), custom_call_target="tpu_custom_call" | custom-call | tf_op jit(solution)/shard_map/prepare/pallas_call | solution.py:252
  19.7 2.3 %first_image.1.refs_8_ = bf16[2,128,128]{2,1,0:T(8,128)(2,1)S(1)} custom-call(s32[2,32]{1,0:T(2,128)S(1)} %get-tuple-element.14.codes, f32[2,32]{1,0:T(2,128)S(1)} %get-tuple-element.15.floats, bf16[2,24,128,128]{3,2,1,0:T(8,128)(2,1)S(1)} %get-tuple-element.16.left, bf16[2,24,128,128]{3,2,1,0:T(8,128)(2,1)S(1)} %collective-permute-done.right, ...), custom_call_target="tpu_custom_call" | custom-call | tf_op jit(solution)/shard_map/first_image/pallas_call | solution.py:275
  22.0 1.6 %collective-permute-start.8 = (bf16[2,128,128]{2,1,0:T(8,128)(2,1)S(1)}, bf16[2,128,128]{2,1,0:T(8,128)(2,1)S(1)}, u32[]{:S(2)}, u32[]{:S(2)}) collective-permute-start(bf16[2,128,128]{2,1,0:T(8,128)(2,1)S(1)} %first_image.1.refs_8_), channel_id=1, source_target_pairs={{0,4},{1,5},{2,6},{3,7},{4,0},{5,1},{6,2},{7,3},{8,12},{9,13},{10,... | collective-permute-start | bytes 196616 | tf_op jit(solution)/shard_map/ppermute | solution.py:22
  23.6 2.7 %collective-permute-start.11 = (bf16[2,128,128]{2,1,0:T(8,128)(2,1)S(1)}, bf16[2,128,128]{2,1,0:T(8,128)(2,1)S(1)}, u32[]{:S(2)}, u32[]{:S(2)}) collective-permute-start(bf16[2,128,128]{2,1,0:T(8,128)(2,1)S(1)} %first_image.1.refs_8_), channel_id=1, source_target_pairs={{0,3},{1,2},{2,1},{3,0},{4,7},{5,6},{6,5},{7,4},{8,11},{9,10},{10,... | collective-permute-start | bytes 196616 | tf_op jit(solution)/shard_map/ppermute | solution.py:22
  26.4 0.7 %collective-permute-start.9 = (bf16[2,128,128]{2,1,0:T(8,128)(2,1)S(1)}, bf16[2,128,128]{2,1,0:T(8,128)(2,1)S(1)}, u32[]{:S(2)}, u32[]{:S(2)}) collective-permute-start(bf16[2,128,128]{2,1,0:T(8,128)(2,1)S(1)} %first_image.1.refs_8_), channel_id=1, source_target_pairs={{0,1},{1,0},{2,3},{3,2},{4,5},{5,4},{6,7},{7,6},{8,9},{9,8},{10,11... | collective-permute-start | bytes 196616 | tf_op jit(solution)/shard_map/ppermute | solution.py:22
  27.1 0.2 collective-permute-done.8.refs_9_
  27.3 1.1 %collective-permute-start.14 = (bf16[2,128,128]{2,1,0:T(8,128)(2,1)S(1)}, bf16[2,128,128]{2,1,0:T(8,128)(2,1)S(1)}, u32[]{:S(2)}, u32[]{:S(2)}) collective-permute-start(bf16[2,128,128]{2,1,0:T(8,128)(2,1)S(1)} %collective-permute-done.8.refs_9_), channel_id=1, source_target_pairs={{0,1},{1,0},{2,3},{3,2},{4,5},{5,4},{6,7},{7,6},{8,9},{9,8},{10,11... | collective-permute-start | bytes 196616 | tf_op jit(solution)/shard_map/ppermute | solution.py:22
  28.4 2.0 %collective-permute-start.13 = (bf16[2,128,128]{2,1,0:T(8,128)(2,1)S(1)}, bf16[2,128,128]{2,1,0:T(8,128)(2,1)S(1)}, u32[]{:S(2)}, u32[]{:S(2)}) collective-permute-start(bf16[2,128,128]{2,1,0:T(8,128)(2,1)S(1)} %collective-permute-done.8.refs_9_), channel_id=1, source_target_pairs={{0,2},{1,3},{2,0},{3,1},{4,6},{5,7},{6,4},{7,5},{8,10},{9,11},{10,... | collective-permute-start | bytes 196616 | tf_op jit(solution)/shard_map/ppermute | solution.py:22
  30.4 1.2 %collective-permute-start.12 = (bf16[2,128,128]{2,1,0:T(8,128)(2,1)S(1)}, bf16[2,128,128]{2,1,0:T(8,128)(2,1)S(1)}, u32[]{:S(2)}, u32[]{:S(2)}) collective-permute-start(bf16[2,128,128]{2,1,0:T(8,128)(2,1)S(1)} %collective-permute-done.8.refs_9_), channel_id=1, source_target_pairs={{0,3},{1,2},{2,1},{3,0},{4,7},{5,6},{6,5},{7,4},{8,11},{9,10},{10,... | collective-permute-start | bytes 196616 | tf_op jit(solution)/shard_map/ppermute | solution.py:22
  31.6 0.7 %collective-permute-done.14.refs_15_ = bf16[2,128,128]{2,1,0:T(8,128)(2,1)S(1)} collective-permute-done((bf16[2,128,128]{2,1,0:T(8,128)(2,1)S(1)}, bf16[2,128,128]{2,1,0:T(8,128)(2,1)S(1)}, u32[]{:S(2)}, u32[]{:S(2)}) %collective-permute-start.14) | collective-permute-done | bytes 65568 | tf_op jit(solution)/shard_map/ppermute | solution.py:22
  32.3 0.4 collective-permute-done.13.refs_14_
  32.7 2.9 %collective-permute-done.12.refs_13_ = bf16[2,128,128]{2,1,0:T(8,128)(2,1)S(1)} collective-permute-done((bf16[2,128,128]{2,1,0:T(8,128)(2,1)S(1)}, bf16[2,128,128]{2,1,0:T(8,128)(2,1)S(1)}, u32[]{:S(2)}, u32[]{:S(2)}) %collective-permute-start.12) | collective-permute-done | bytes 65568 | tf_op jit(solution)/shard_map/ppermute | solution.py:22
  35.5 2.6 %middle_image.1 = (f32[1,128]{1,0:T(1,128)S(1)}, f32[16,128,128]{2,1,0:T(8,128)S(1)}, bf16[2,128,128]{2,1,0:T(8,128)(2,1)S(1)}) custom-call(s32[2,32]{1,0:T(2,128)S(1)} %get-tuple-element.14.codes, f32[2,32]{1,0:T(2,128)S(1)} %get-tuple-element.15.floats, bf16[2,24,128,128]{3,2,1,0:T(8,128)(2,1)S(1)} %get-tuple-element.16.left, ...), custom_call_target="tpu_custom_call" | custom-call | tf_op jit(solution)/shard_map/middle_image/pallas_call | solution.py:287
  38.1 2.3 %collective-permute-start.15 = (bf16[2,128,128]{2,1,0:T(8,128)(2,1)S(1)}, bf16[2,128,128]{2,1,0:T(8,128)(2,1)S(1)}, u32[]{:S(2)}, u32[]{:S(2)}) collective-permute-start(bf16[2,128,128]{2,1,0:T(8,128)(2,1)S(1)} %get-tuple-element.18.refs_1_), channel_id=1, source_target_pairs={{0,4},{1,5},{2,6},{3,7},{4,0},{5,1},{6,2},{7,3},{8,12},{9,13},{10,... | collective-permute-start | bytes 196616 | tf_op jit(solution)/shard_map/ppermute | solution.py:22
  40.4 0.7 %collective-permute-start.18 = (bf16[2,128,128]{2,1,0:T(8,128)(2,1)S(1)}, bf16[2,128,128]{2,1,0:T(8,128)(2,1)S(1)}, u32[]{:S(2)}, u32[]{:S(2)}) collective-permute-start(bf16[2,128,128]{2,1,0:T(8,128)(2,1)S(1)} %get-tuple-element.18.refs_1_), channel_id=1, source_target_pairs={{0,3},{1,2},{2,1},{3,0},{4,7},{5,6},{6,5},{7,4},{8,11},{9,10},{10,... | collective-permute-start | bytes 196616 | tf_op jit(solution)/shard_map/ppermute | solution.py:22
  41.1 1.2 %collective-permute-start.17 = (bf16[2,128,128]{2,1,0:T(8,128)(2,1)S(1)}, bf16[2,128,128]{2,1,0:T(8,128)(2,1)S(1)}, u32[]{:S(2)}, u32[]{:S(2)}) collective-permute-start(bf16[2,128,128]{2,1,0:T(8,128)(2,1)S(1)} %get-tuple-element.18.refs_1_), channel_id=1, source_target_pairs={{0,2},{1,3},{2,0},{3,1},{4,6},{5,7},{6,4},{7,5},{8,10},{9,11},{10,... | collective-permute-start | bytes 196616 | tf_op jit(solution)/shard_map/ppermute | solution.py:22
  42.3 1.6 %collective-permute-start.16 = (bf16[2,128,128]{2,1,0:T(8,128)(2,1)S(1)}, bf16[2,128,128]{2,1,0:T(8,128)(2,1)S(1)}, u32[]{:S(2)}, u32[]{:S(2)}) collective-permute-start(bf16[2,128,128]{2,1,0:T(8,128)(2,1)S(1)} %get-tuple-element.18.refs_1_), channel_id=1, source_target_pairs={{0,1},{1,0},{2,3},{3,2},{4,5},{5,4},{6,7},{7,6},{8,9},{9,8},{10,11... | collective-permute-start | bytes 196616 | tf_op jit(solution)/shard_map/ppermute | solution.py:22
  43.9 0.2 collective-permute-done.15.refs_2_
  44.1 0.9 %collective-permute-start.21 = (bf16[2,128,128]{2,1,0:T(8,128)(2,1)S(1)}, bf16[2,128,128]{2,1,0:T(8,128)(2,1)S(1)}, u32[]{:S(2)}, u32[]{:S(2)}) collective-permute-start(bf16[2,128,128]{2,1,0:T(8,128)(2,1)S(1)} %collective-permute-done.15.refs_2_), channel_id=1, source_target_pairs={{0,1},{1,0},{2,3},{3,2},{4,5},{5,4},{6,7},{7,6},{8,9},{9,8},{10,11... | collective-permute-start | bytes 196616 | tf_op jit(solution)/shard_map/ppermute | solution.py:22
  45.0 0.2 collective-permute-start.20
  45.2 0.6 collective-permute-done.18.refs_5_
  45.8 1.8 %collective-permute-start.19 = (bf16[2,128,128]{2,1,0:T(8,128)(2,1)S(1)}, bf16[2,128,128]{2,1,0:T(8,128)(2,1)S(1)}, u32[]{:S(2)}, u32[]{:S(2)}) collective-permute-start(bf16[2,128,128]{2,1,0:T(8,128)(2,1)S(1)} %collective-permute-done.15.refs_2_), channel_id=1, source_target_pairs={{0,3},{1,2},{2,1},{3,0},{4,7},{5,6},{6,5},{7,4},{8,11},{9,10},{10,... | collective-permute-start | bytes 196616 | tf_op jit(solution)/shard_map/ppermute | solution.py:22
  47.6 0.8 %collective-permute-done.21.refs_8_ = bf16[2,128,128]{2,1,0:T(8,128)(2,1)S(1)} collective-permute-done((bf16[2,128,128]{2,1,0:T(8,128)(2,1)S(1)}, bf16[2,128,128]{2,1,0:T(8,128)(2,1)S(1)}, u32[]{:S(2)}, u32[]{:S(2)}) %collective-permute-start.21) | collective-permute-done | bytes 65568 | tf_op jit(solution)/shard_map/ppermute | solution.py:22
  48.4 0.9 %collective-permute-done.20.refs_7_ = bf16[2,128,128]{2,1,0:T(8,128)(2,1)S(1)} collective-permute-done((bf16[2,128,128]{2,1,0:T(8,128)(2,1)S(1)}, bf16[2,128,128]{2,1,0:T(8,128)(2,1)S(1)}, u32[]{:S(2)}, u32[]{:S(2)}) %collective-permute-start.20) | collective-permute-done | bytes 65568 | tf_op jit(solution)/shard_map/ppermute | solution.py:22
  49.3 1.7 %collective-permute-done.19.refs_6_ = bf16[2,128,128]{2,1,0:T(8,128)(2,1)S(1)} collective-permute-done((bf16[2,128,128]{2,1,0:T(8,128)(2,1)S(1)}, bf16[2,128,128]{2,1,0:T(8,128)(2,1)S(1)}, u32[]{:S(2)}, u32[]{:S(2)}) %collective-permute-start.19) | collective-permute-done | bytes 65568 | tf_op jit(solution)/shard_map/ppermute | solution.py:22
  51.0 2.8 %last_image.1 = (f32[1,128]{1,0:T(1,128)S(1)}, f32[2,128,128]{2,1,0:T(8,128)S(1)}, bf16[2,128,128]{2,1,0:T(8,128)(2,1)S(1)}, f32[1,8,128]{2,1,0:T(8,128)S(1)}) custom-call(s32[2,32]{1,0:T(2,128)S(1)} %get-tuple-element.14.codes, f32[2,32]{1,0:T(2,128)S(1)} %get-tuple-element.15.floats, s32[1,2]{1,0:T(1,128)S(1)} %copy-done.5, ...), custom_call_target="tpu_custom_call" | custom-call | tf_op jit(solution)/shard_map/last_image/pallas_call | solution.py:299
  53.8 2.3 %collective-permute-start.24 = (f32[1,8,128]{2,1,0:T(8,128)S(1)}, f32[1,8,128]{2,1,0:T(8,128)S(1)}, u32[]{:S(2)}, u32[]{:S(2)}) collective-permute-start(f32[1,8,128]{2,1,0:T(8,128)S(1)} %get-tuple-element.23), channel_id=1, source_target_pairs={{0,6},{1,7},{2,4},{3,5},{4,2},{5,3},{6,0},{7,1},{8,14},{9,15},{10,... | collective-permute-start | bytes 12296 | tf_op jit(solution)/shard_map/ppermute | solution.py:22
  56.0 0.5 collective-permute-start.23
  56.5 1.7 %collective-permute-start.22 = (f32[1,8,128]{2,1,0:T(8,128)S(1)}, f32[1,8,128]{2,1,0:T(8,128)S(1)}, u32[]{:S(2)}, u32[]{:S(2)}) collective-permute-start(f32[1,8,128]{2,1,0:T(8,128)S(1)} %get-tuple-element.23), channel_id=1, source_target_pairs={{0,2},{1,3},{2,0},{3,1},{4,6},{5,7},{6,4},{7,5},{8,10},{9,11},{10,... | collective-permute-start | bytes 12296 | tf_op jit(solution)/shard_map/ppermute | solution.py:22
  58.2 1.9 %collective-permute-done.22 = f32[1,8,128]{2,1,0:T(8,128)S(1)} collective-permute-done((f32[1,8,128]{2,1,0:T(8,128)S(1)}, f32[1,8,128]{2,1,0:T(8,128)S(1)}, u32[]{:S(2)}, u32[]{:S(2)}) %collective-permute-start.22) | collective-permute-done | bytes 4128 | tf_op jit(solution)/shard_map/ppermute | solution.py:22
  60.1 0.4 collective-permute-done.23
  60.5 1.1 %collective-permute-start.25 = (f32[4,8,128]{2,1,0:T(8,128)S(1)}, f32[4,8,128]{2,1,0:T(8,128)S(1)}, u32[]{:S(2)}, u32[]{:S(2)}) collective-permute-start(f32[4,8,128]{2,1,0:T(8,128)S(1)} %constant_dynamic-update-slice_fusion.refs_2_), channel_id=1, source_target_pairs={{0,1},{1,0},{2,3},{3,2},{4,5},{5,4},{6,7},{7,6},{8,9},{9,8},{10,11... | collective-permute-start | bytes 49160 | tf_op jit(solution)/shard_map/ppermute | solution.py:22
  61.6 2.7 %collective-permute-done.25.refs_3_ = f32[4,8,128]{2,1,0:T(8,128)S(1)} collective-permute-done((f32[4,8,128]{2,1,0:T(8,128)S(1)}, f32[4,8,128]{2,1,0:T(8,128)S(1)}, u32[]{:S(2)}, u32[]{:S(2)}) %collective-permute-start.25) | collective-permute-done | bytes 16416 | tf_op jit(solution)/shard_map/ppermute | solution.py:22
  64.3 0.7 %finish.1 = (f32[1,3]{1,0:T(1,128)}, bf16[2,128,128]{2,1,0:T(8,128)(2,1)}) custom-call(f32[2,128,128]{2,1,0:T(8,128)S(1)} %get-tuple-element.19.own, bf16[2,128,128]{2,1,0:T(8,128)(2,1)S(1)} %get-tuple-element.20.image, f32[1,128]{1,0:T(1,128)S(1)} %get-tuple-element.21.refs_0_, f32[1,128]{1,0:T(1,128)S(1)} %get-tuple-element.22.refs_1_, ...), custom_call_target="tpu_custom_call" | custom-call | tf_op jit(solution)/shard_map/finish/pallas_call | solution.py:321
  (25 shorter events, 0.1 us)
Async XLA Ops:
  0.6 19.0 %collective-permute-start = (bf16[2,24,128,128]{3,2,1,0:T(8,128)(2,1)}, bf16[2,24,128,128]{3,2,1,0:T(8,128)(2,1)S(1)}, u32[]{:S(2)}, u32[]{:S(2)}) collective-permute-start(bf16[2,24,128,128]{3,2,1,0:T(8,128)(2,1)} %bitcast.17), channel_id=1, source_target_pairs={{0,8},{8,0},{1,9},{9,1},{2,10},{10,2},{3,11},{11,3},{4,12},{12,4},... | collective-permute-start | bytes 4718600 | tf_op jit(solution)/shard_map/ppermute | solution.py:242
  1.1 7.9 %collective-permute-start.1 = (bf16[2,128,128]{2,1,0:T(8,128)(2,1)}, bf16[2,128,128]{2,1,0:T(8,128)(2,1)S(1)}, u32[]{:S(2)}, u32[]{:S(2)}) collective-permute-start(bf16[2,128,128]{2,1,0:T(8,128)(2,1)} %bitcast.8), channel_id=1, source_target_pairs={{0,4},{1,5},{2,6},{3,7},{4,0},{5,1},{6,2},{7,3},{8,12},{9,13},{10,... | collective-permute-start | bytes 196616 | tf_op jit(solution)/shard_map/ppermute | solution.py:22
  4.8 6.1 %collective-permute-start.4 = (bf16[2,128,128]{2,1,0:T(8,128)(2,1)}, bf16[2,128,128]{2,1,0:T(8,128)(2,1)S(1)}, u32[]{:S(2)}, u32[]{:S(2)}) collective-permute-start(bf16[2,128,128]{2,1,0:T(8,128)(2,1)} %bitcast.9), channel_id=1, source_target_pairs={{0,3},{1,2},{2,1},{3,0},{4,7},{5,6},{6,5},{7,4},{8,11},{9,10},{10,... | collective-permute-start | bytes 196616 | tf_op jit(solution)/shard_map/ppermute | solution.py:22
  7.3 5.1 %collective-permute-start.3 = (bf16[2,128,128]{2,1,0:T(8,128)(2,1)}, bf16[2,128,128]{2,1,0:T(8,128)(2,1)S(1)}, u32[]{:S(2)}, u32[]{:S(2)}) collective-permute-start(bf16[2,128,128]{2,1,0:T(8,128)(2,1)} %bitcast.10), channel_id=1, source_target_pairs={{0,2},{1,3},{2,0},{3,1},{4,6},{5,7},{6,4},{7,5},{8,10},{9,11},{10,... | collective-permute-start | bytes 196616 | tf_op jit(solution)/shard_map/ppermute | solution.py:22
  7.8 11.8 %collective-permute-start.2 = (bf16[2,128,128]{2,1,0:T(8,128)(2,1)}, bf16[2,128,128]{2,1,0:T(8,128)(2,1)S(1)}, u32[]{:S(2)}, u32[]{:S(2)}) collective-permute-start(bf16[2,128,128]{2,1,0:T(8,128)(2,1)} %bitcast.11), channel_id=1, source_target_pairs={{0,1},{1,0},{2,3},{3,2},{4,5},{5,4},{6,7},{7,6},{8,9},{9,8},{10,11... | collective-permute-start | bytes 196616 | tf_op jit(solution)/shard_map/ppermute | solution.py:22
  9.0 10.6 %collective-permute-start.7 = (bf16[2,128,128]{2,1,0:T(8,128)(2,1)S(1)}, bf16[2,128,128]{2,1,0:T(8,128)(2,1)S(1)}, u32[]{:S(2)}, u32[]{:S(2)}) collective-permute-start(bf16[2,128,128]{2,1,0:T(8,128)(2,1)S(1)} %collective-permute-done.1.refs_1_), channel_id=1, source_target_pairs={{0,1},{1,0},{2,3},{3,2},{4,5},{5,4},{6,7},{7,6},{8,9},{9,8},{10,11... | collective-permute-start | bytes 196616 | tf_op jit(solution)/shard_map/ppermute | solution.py:22
  10.9 8.7 %collective-permute-start.6 = (bf16[2,128,128]{2,1,0:T(8,128)(2,1)S(1)}, bf16[2,128,128]{2,1,0:T(8,128)(2,1)S(1)}, u32[]{:S(2)}, u32[]{:S(2)}) collective-permute-start(bf16[2,128,128]{2,1,0:T(8,128)(2,1)S(1)} %collective-permute-done.1.refs_1_), channel_id=1, source_target_pairs={{0,2},{1,3},{2,0},{3,1},{4,6},{5,7},{6,4},{7,5},{8,10},{9,11},{10,... | collective-permute-start | bytes 196616 | tf_op jit(solution)/shard_map/ppermute | solution.py:22
  12.4 7.2 %collective-permute-start.5 = (bf16[2,128,128]{2,1,0:T(8,128)(2,1)S(1)}, bf16[2,128,128]{2,1,0:T(8,128)(2,1)S(1)}, u32[]{:S(2)}, u32[]{:S(2)}) collective-permute-start(bf16[2,128,128]{2,1,0:T(8,128)(2,1)S(1)} %collective-permute-done.1.refs_1_), channel_id=1, source_target_pairs={{0,3},{1,2},{2,1},{3,0},{4,7},{5,6},{6,5},{7,4},{8,11},{9,10},{10,... | collective-permute-start | bytes 196616 | tf_op jit(solution)/shard_map/ppermute | solution.py:22
  13.5 1.4 %copy-start = (bf16[1,2,24,128,128]{4,3,2,1,0:T(8,128)(2,1)S(1)}, bf16[1,2,24,128,128]{4,3,2,1,0:T(8,128)(2,1)}, u32[]{:S(2)}) copy-start(bf16[1,2,24,128,128]{4,3,2,1,0:T(8,128)(2,1)} %param.8) | copy-start | bytes 4718596
  14.9 0.7 %copy-start.2 = (s32[1,2,32]{2,1,0:T(2,128)S(1)}, s32[1,2,32]{2,1,0:T(2,128)}, u32[]{:S(2)}) copy-start(s32[1,2,32]{2,1,0:T(2,128)} %param.10) | copy-start | bytes 772
  15.6 0.7 %copy-start.3 = (s32[1,2,32]{2,1,0:T(2,128)S(1)}, s32[1,2,32]{2,1,0:T(2,128)}, u32[]{:S(2)}) copy-start(s32[1,2,32]{2,1,0:T(2,128)} %param.11) | copy-start | bytes 772
  16.3 0.7 %copy-start.4 = (f32[1,2,32]{2,1,0:T(2,128)S(1)}, f32[1,2,32]{2,1,0:T(2,128)}, u32[]{:S(2)}) copy-start(f32[1,2,32]{2,1,0:T(2,128)} %param.12) | copy-start | bytes 772
  17.0 2.7 %copy-start.1 = (bf16[1,2,128,128]{3,2,1,0:T(8,128)(2,1)S(1)}, bf16[1,2,128,128]{3,2,1,0:T(8,128)(2,1)}, u32[]{:S(2)}) copy-start(bf16[1,2,128,128]{3,2,1,0:T(8,128)(2,1)} %param.7) | copy-start | bytes 196612
  22.0 29.0 %copy-start.5 = (s32[1,2]{1,0:T(1,128)S(1)}, s32[1,2]{1,0:T(1,128)}, u32[]{:S(2)}) copy-start(s32[1,2]{1,0:T(1,128)} %ranks.1) | copy-start | bytes 28
  22.0 5.3 %collective-permute-start.8 = (bf16[2,128,128]{2,1,0:T(8,128)(2,1)S(1)}, bf16[2,128,128]{2,1,0:T(8,128)(2,1)S(1)}, u32[]{:S(2)}, u32[]{:S(2)}) collective-permute-start(bf16[2,128,128]{2,1,0:T(8,128)(2,1)S(1)} %first_image.1.refs_8_), channel_id=1, source_target_pairs={{0,4},{1,5},{2,6},{3,7},{4,0},{5,1},{6,2},{7,3},{8,12},{9,13},{10,... | collective-permute-start | bytes 196616 | tf_op jit(solution)/shard_map/ppermute | solution.py:22
  23.6 6.8 %collective-permute-start.11 = (bf16[2,128,128]{2,1,0:T(8,128)(2,1)S(1)}, bf16[2,128,128]{2,1,0:T(8,128)(2,1)S(1)}, u32[]{:S(2)}, u32[]{:S(2)}) collective-permute-start(bf16[2,128,128]{2,1,0:T(8,128)(2,1)S(1)} %first_image.1.refs_8_), channel_id=1, source_target_pairs={{0,3},{1,2},{2,1},{3,0},{4,7},{5,6},{6,5},{7,4},{8,11},{9,10},{10,... | collective-permute-start | bytes 196616 | tf_op jit(solution)/shard_map/ppermute | solution.py:22
  26.3 5.3 %collective-permute-start.10 = (bf16[2,128,128]{2,1,0:T(8,128)(2,1)S(1)}, bf16[2,128,128]{2,1,0:T(8,128)(2,1)S(1)}, u32[]{:S(2)}, u32[]{:S(2)}) collective-permute-start(bf16[2,128,128]{2,1,0:T(8,128)(2,1)S(1)} %first_image.1.refs_8_), channel_id=1, source_target_pairs={{0,2},{1,3},{2,0},{3,1},{4,6},{5,7},{6,4},{7,5},{8,10},{9,11},{10,... | collective-permute-start | bytes 196616 | tf_op jit(solution)/shard_map/ppermute | solution.py:22
  26.4 5.2 %collective-permute-start.9 = (bf16[2,128,128]{2,1,0:T(8,128)(2,1)S(1)}, bf16[2,128,128]{2,1,0:T(8,128)(2,1)S(1)}, u32[]{:S(2)}, u32[]{:S(2)}) collective-permute-start(bf16[2,128,128]{2,1,0:T(8,128)(2,1)S(1)} %first_image.1.refs_8_), channel_id=1, source_target_pairs={{0,1},{1,0},{2,3},{3,2},{4,5},{5,4},{6,7},{7,6},{8,9},{9,8},{10,11... | collective-permute-start | bytes 196616 | tf_op jit(solution)/shard_map/ppermute | solution.py:22
  27.3 5.0 %collective-permute-start.14 = (bf16[2,128,128]{2,1,0:T(8,128)(2,1)S(1)}, bf16[2,128,128]{2,1,0:T(8,128)(2,1)S(1)}, u32[]{:S(2)}, u32[]{:S(2)}) collective-permute-start(bf16[2,128,128]{2,1,0:T(8,128)(2,1)S(1)} %collective-permute-done.8.refs_9_), channel_id=1, source_target_pairs={{0,1},{1,0},{2,3},{3,2},{4,5},{5,4},{6,7},{7,6},{8,9},{9,8},{10,11... | collective-permute-start | bytes 196616 | tf_op jit(solution)/shard_map/ppermute | solution.py:22
  28.4 4.3 %collective-permute-start.13 = (bf16[2,128,128]{2,1,0:T(8,128)(2,1)S(1)}, bf16[2,128,128]{2,1,0:T(8,128)(2,1)S(1)}, u32[]{:S(2)}, u32[]{:S(2)}) collective-permute-start(bf16[2,128,128]{2,1,0:T(8,128)(2,1)S(1)} %collective-permute-done.8.refs_9_), channel_id=1, source_target_pairs={{0,2},{1,3},{2,0},{3,1},{4,6},{5,7},{6,4},{7,5},{8,10},{9,11},{10,... | collective-permute-start | bytes 196616 | tf_op jit(solution)/shard_map/ppermute | solution.py:22
  30.4 5.2 %collective-permute-start.12 = (bf16[2,128,128]{2,1,0:T(8,128)(2,1)S(1)}, bf16[2,128,128]{2,1,0:T(8,128)(2,1)S(1)}, u32[]{:S(2)}, u32[]{:S(2)}) collective-permute-start(bf16[2,128,128]{2,1,0:T(8,128)(2,1)S(1)} %collective-permute-done.8.refs_9_), channel_id=1, source_target_pairs={{0,3},{1,2},{2,1},{3,0},{4,7},{5,6},{6,5},{7,4},{8,11},{9,10},{10,... | collective-permute-start | bytes 196616 | tf_op jit(solution)/shard_map/ppermute | solution.py:22
  38.1 6.0 %collective-permute-start.15 = (bf16[2,128,128]{2,1,0:T(8,128)(2,1)S(1)}, bf16[2,128,128]{2,1,0:T(8,128)(2,1)S(1)}, u32[]{:S(2)}, u32[]{:S(2)}) collective-permute-start(bf16[2,128,128]{2,1,0:T(8,128)(2,1)S(1)} %get-tuple-element.18.refs_1_), channel_id=1, source_target_pairs={{0,4},{1,5},{2,6},{3,7},{4,0},{5,1},{6,2},{7,3},{8,12},{9,13},{10,... | collective-permute-start | bytes 196616 | tf_op jit(solution)/shard_map/ppermute | solution.py:22
  40.4 5.4 %collective-permute-start.18 = (bf16[2,128,128]{2,1,0:T(8,128)(2,1)S(1)}, bf16[2,128,128]{2,1,0:T(8,128)(2,1)S(1)}, u32[]{:S(2)}, u32[]{:S(2)}) collective-permute-start(bf16[2,128,128]{2,1,0:T(8,128)(2,1)S(1)} %get-tuple-element.18.refs_1_), channel_id=1, source_target_pairs={{0,3},{1,2},{2,1},{3,0},{4,7},{5,6},{6,5},{7,4},{8,11},{9,10},{10,... | collective-permute-start | bytes 196616 | tf_op jit(solution)/shard_map/ppermute | solution.py:22
  41.1 6.5 %collective-permute-start.17 = (bf16[2,128,128]{2,1,0:T(8,128)(2,1)S(1)}, bf16[2,128,128]{2,1,0:T(8,128)(2,1)S(1)}, u32[]{:S(2)}, u32[]{:S(2)}) collective-permute-start(bf16[2,128,128]{2,1,0:T(8,128)(2,1)S(1)} %get-tuple-element.18.refs_1_), channel_id=1, source_target_pairs={{0,2},{1,3},{2,0},{3,1},{4,6},{5,7},{6,4},{7,5},{8,10},{9,11},{10,... | collective-permute-start | bytes 196616 | tf_op jit(solution)/shard_map/ppermute | solution.py:22
  42.3 5.4 %collective-permute-start.16 = (bf16[2,128,128]{2,1,0:T(8,128)(2,1)S(1)}, bf16[2,128,128]{2,1,0:T(8,128)(2,1)S(1)}, u32[]{:S(2)}, u32[]{:S(2)}) collective-permute-start(bf16[2,128,128]{2,1,0:T(8,128)(2,1)S(1)} %get-tuple-element.18.refs_1_), channel_id=1, source_target_pairs={{0,1},{1,0},{2,3},{3,2},{4,5},{5,4},{6,7},{7,6},{8,9},{9,8},{10,11... | collective-permute-start | bytes 196616 | tf_op jit(solution)/shard_map/ppermute | solution.py:22
  44.1 4.3 %collective-permute-start.21 = (bf16[2,128,128]{2,1,0:T(8,128)(2,1)S(1)}, bf16[2,128,128]{2,1,0:T(8,128)(2,1)S(1)}, u32[]{:S(2)}, u32[]{:S(2)}) collective-permute-start(bf16[2,128,128]{2,1,0:T(8,128)(2,1)S(1)} %collective-permute-done.15.refs_2_), channel_id=1, source_target_pairs={{0,1},{1,0},{2,3},{3,2},{4,5},{5,4},{6,7},{7,6},{8,9},{9,8},{10,11... | collective-permute-start | bytes 196616 | tf_op jit(solution)/shard_map/ppermute | solution.py:22
  45.0 4.3 %collective-permute-start.20 = (bf16[2,128,128]{2,1,0:T(8,128)(2,1)S(1)}, bf16[2,128,128]{2,1,0:T(8,128)(2,1)S(1)}, u32[]{:S(2)}, u32[]{:S(2)}) collective-permute-start(bf16[2,128,128]{2,1,0:T(8,128)(2,1)S(1)} %collective-permute-done.15.refs_2_), channel_id=1, source_target_pairs={{0,2},{1,3},{2,0},{3,1},{4,6},{5,7},{6,4},{7,5},{8,10},{9,11},{10,... | collective-permute-start | bytes 196616 | tf_op jit(solution)/shard_map/ppermute | solution.py:22
  45.8 5.2 %collective-permute-start.19 = (bf16[2,128,128]{2,1,0:T(8,128)(2,1)S(1)}, bf16[2,128,128]{2,1,0:T(8,128)(2,1)S(1)}, u32[]{:S(2)}, u32[]{:S(2)}) collective-permute-start(bf16[2,128,128]{2,1,0:T(8,128)(2,1)S(1)} %collective-permute-done.15.refs_2_), channel_id=1, source_target_pairs={{0,3},{1,2},{2,1},{3,0},{4,7},{5,6},{6,5},{7,4},{8,11},{9,10},{10,... | collective-permute-start | bytes 196616 | tf_op jit(solution)/shard_map/ppermute | solution.py:22
  53.8 6.8 %collective-permute-start.24 = (f32[1,8,128]{2,1,0:T(8,128)S(1)}, f32[1,8,128]{2,1,0:T(8,128)S(1)}, u32[]{:S(2)}, u32[]{:S(2)}) collective-permute-start(f32[1,8,128]{2,1,0:T(8,128)S(1)} %get-tuple-element.23), channel_id=1, source_target_pairs={{0,6},{1,7},{2,4},{3,5},{4,2},{5,3},{6,0},{7,1},{8,14},{9,15},{10,... | collective-permute-start | bytes 12296 | tf_op jit(solution)/shard_map/ppermute | solution.py:22
  56.0 4.5 %collective-permute-start.23 = (f32[1,8,128]{2,1,0:T(8,128)S(1)}, f32[1,8,128]{2,1,0:T(8,128)S(1)}, u32[]{:S(2)}, u32[]{:S(2)}) collective-permute-start(f32[1,8,128]{2,1,0:T(8,128)S(1)} %get-tuple-element.23), channel_id=1, source_target_pairs={{0,4},{1,5},{2,6},{3,7},{4,0},{5,1},{6,2},{7,3},{8,12},{9,13},{10,... | collective-permute-start | bytes 12296 | tf_op jit(solution)/shard_map/ppermute | solution.py:22
  56.5 3.6 %collective-permute-start.22 = (f32[1,8,128]{2,1,0:T(8,128)S(1)}, f32[1,8,128]{2,1,0:T(8,128)S(1)}, u32[]{:S(2)}, u32[]{:S(2)}) collective-permute-start(f32[1,8,128]{2,1,0:T(8,128)S(1)} %get-tuple-element.23), channel_id=1, source_target_pairs={{0,2},{1,3},{2,0},{3,1},{4,6},{5,7},{6,4},{7,5},{8,10},{9,11},{10,... | collective-permute-start | bytes 12296 | tf_op jit(solution)/shard_map/ppermute | solution.py:22
  60.5 3.8 %collective-permute-start.25 = (f32[4,8,128]{2,1,0:T(8,128)S(1)}, f32[4,8,128]{2,1,0:T(8,128)S(1)}, u32[]{:S(2)}, u32[]{:S(2)}) collective-permute-start(f32[4,8,128]{2,1,0:T(8,128)S(1)} %constant_dynamic-update-slice_fusion.refs_2_), channel_id=1, source_target_pairs={{0,1},{1,0},{2,3},{3,2},{4,5},{5,4},{6,7},{7,6},{8,9},{9,8},{10,11... | collective-permute-start | bytes 49160 | tf_op jit(solution)/shard_map/ppermute | solution.py:22

commit v4 on v3

--- a/solution.py
+++ b/solution.py
@@ -14,7 +14,7 @@
 VMEM = pl.BlockSpec(memory_space=pltpu.VMEM)
 ANY = pl.BlockSpec(memory_space=pl.ANY)
 HBM = pl.BlockSpec(memory_space=pltpu.HBM)
-APART = (0, 4, 1, 2, 3, 7, 6, 5)
+APART = (0, 4, 1, 2, 3, 5, 6, 7)
 
 
 def hop(block, distance):
@@ -27,14 +27,7 @@
         return [lax.all_gather(block, "sec", axis=0, tiled=True)]
     relayed = hop(block, 4)
     near = [hop(block, distance) for distance in (1, 2, 3)]
-    return [block, relayed] + near + [hop(relayed, distance) for distance in (3, 2, 1)]
-
-
-def gather_small(block):
-    if lax.axis_size("sec") != len(APART):
-        return [lax.all_gather(block, "sec", axis=0, tiled=True)]
-    line = jnp.concatenate([block] + [hop(block, distance) for distance in (2, 4, 6)])
-    return [line, hop(line, 1)]
+    return [block, relayed] + near + [hop(relayed, distance) for distance in (1, 2, 3)]
 
 
 def slot(sector, blocks, devices, here):
@@ -213,11 +206,9 @@
     sums[...] = result
 
 
-def finish_kernel(steps, count, entries, own, image, *refs):
-    earlier, gathered, (energies, kept) = refs[:steps], refs[steps : steps + count], refs[steps + count :]
-    rows = []
-    for piece in gathered:
-        rows += [piece[s] for s in range(piece.shape[0])]
+def finish_kernel(steps, entries, own, image, gathered, *refs):
+    earlier, (energies, kept) = refs[:steps], refs[steps:]
+    rows = [gathered[device] for device in range(gathered.shape[0])]
     intersection = sum(row[0:1, :] for row in rows)
     squares = sum(row[1:2, :] for row in rows)
     total = intersection / squares
@@ -263,7 +254,7 @@
         ],
         compiler_params=params,
         name="prepare",
-    )(sources[0], channels[0], couplings[0], left)
+    )(*(pltpu.with_memory_space_constraint(block, pltpu.HBM) for block in (sources[0], channels[0], couplings[0], left)))
 
     own_type = jax.ShapeDtypeStruct((blocks, size, size), jnp.bfloat16)
     number = jax.ShapeDtypeStruct((1, 128), jnp.float32)
@@ -302,7 +293,7 @@
             number,
             jax.ShapeDtypeStruct((blocks, size, size), jnp.float32),
             own_type,
-            jax.ShapeDtypeStruct((1, 8, 128), jnp.float32),
+            jax.ShapeDtypeStruct((devices, 8, 128), jnp.float32),
         ),
         in_specs=[ANY, ANY, ANY] + [VMEM] * (2 + len(states) + len(images)),
         out_specs=(VMEM, VMEM, VMEM, VMEM),
@@ -317,15 +308,15 @@
         name="last_image",
     )(codes, couplings, kept_rank, left, right, *states, *images)
     energies.append(energy)
-    gathered = gather_small(sums)
+    gathered = lax.all_to_all(sums, "sec", 0, 0)
     energies, kept = pl.pallas_call(
-        functools.partial(finish_kernel, len(energies), len(gathered), entries),
+        functools.partial(finish_kernel, len(energies), entries),
         out_shape=(jax.ShapeDtypeStruct((1, ITERS), jnp.float32), own_type),
-        in_specs=[VMEM] * (2 + len(energies) + len(gathered)),
+        in_specs=[VMEM] * (3 + len(energies)),
         out_specs=(VMEM, VMEM),
         compiler_params=params,
         name="finish",
-    )(own, image, *energies, *gathered)
+    )(own, image, gathered, *energies)
     return kept[None], energies
 
 

time: 65.2 us -> 61.3 us (0.940)
  blocking collectives: 0 us -> 11.2 us
  waiting for transfers between devices: 14.4 us -> 7.61 us
  starting transfers between devices: 35.4 us -> 30.5 us
  local copies, waits for them, and re-layouts: 3.46 us -> 0.01 us
    all_to_all x0 -> x1, blocking collectives: none -> 11.2 us  [local(): gathered = lax.all_to_all(sums, 'sec', 0, 0)]
    ppermute x25 -> x21, waiting for transfers between devices: 14.4 us -> 7.6 us  [hop(): return lax.ppermute(block, 'sec', [(a, a ^ distance) for a in range(count)])]
    ppermute x25 -> x21, starting transfers between devices: 34.9 us -> 30 us  [hop(): return lax.ppermute(block, 'sec', [(a, a ^ distance) for a in range(count)])]
    unnamed x15 -> x4, local copies, waits for them, and re-layouts: 3.46 us -> 0.01 us
  transfers between devices with their start and end apart: 26 -> 22, of which waited for: 14 -> 9; matrix products, arithmetic and copies ran while one was open for 0% -> 0% of each run, Pallas kernels for 4% -> 5%
where the time goes in v4:
time: 61.3 us; the launch traced here: 61.1 us
  starting transfers between devices  30.5 us (50%)
  blocking collectives  11.2 us (18%)
  Pallas kernels  11.1 us (18%)
  waiting for transfers between devices  7.61 us (12%)
  between operations  0.75 us (1%)
    ppermute x21, starting transfers between devices, hop(): return lax.ppermute(block, 'sec', [(a, a ^ distance) for a in range(count)])  30 us
    all_to_all x1, blocking collectives, local(): gathered = lax.all_to_all(sums, 'sec', 0, 0)  11.2 us
    ppermute x21, waiting for transfers between devices, hop(): return lax.ppermute(block, 'sec', [(a, a ^ distance) for a in range(count)])  7.6 us
    pallas_call x1, Pallas kernels, local(): pl.pallas_call(functools.partial(prepare_kernel, devices), out_shape=(int...  2.78 us
    pallas_call x1, Pallas kernels, local(): pl.pallas_call(functools.partial(last_kernel, len(states), len(images)),...  2.77 us
    pallas_call x1, Pallas kernels, local(): pl.pallas_call(functools.partial(middle_kernel, len(states), len(images))...  2.55 us
    pallas_call x1, Pallas kernels, local(): pl.pallas_call(functools.partial(first_kernel, len(states)), out_shape=ow...  2.27 us
  transfers between devices with their start and end apart: 22, of which 9 were waited for; matrix products, arithmetic and copies ran while one was open for 0% of the time, Pallas kernels for 5%

profile of v4, /device:TPU:0, one launch (start us, length us, event | category | flops | bytes accessed | tf_op | source)
XLA Modules:
  0.0 61.1 jit_solution(7180307185974765750)
XLA Ops:
  0.6 0.5 collective-permute-start
  1.2 3.7 %collective-permute-start.1 = (bf16[2,128,128]{2,1,0:T(8,128)(2,1)}, bf16[2,128,128]{2,1,0:T(8,128)(2,1)S(1)}, u32[]{:S(2)}, u32[]{:S(2)}) collective-permute-start(bf16[2,128,128]{2,1,0:T(8,128)(2,1)} %bitcast.7), channel_id=1, source_target_pairs={{0,4},{1,5},{2,6},{3,7},{4,0},{5,1},{6,2},{7,3},{8,12},{9,13},{10,... | collective-permute-start | bytes 196616 | tf_op jit(solution)/shard_map/ppermute | solution.py:22
  4.8 2.5 %collective-permute-start.4 = (bf16[2,128,128]{2,1,0:T(8,128)(2,1)}, bf16[2,128,128]{2,1,0:T(8,128)(2,1)S(1)}, u32[]{:S(2)}, u32[]{:S(2)}) collective-permute-start(bf16[2,128,128]{2,1,0:T(8,128)(2,1)} %bitcast.8), channel_id=1, source_target_pairs={{0,3},{1,2},{2,1},{3,0},{4,7},{5,6},{6,5},{7,4},{8,11},{9,10},{10,... | collective-permute-start | bytes 196616 | tf_op jit(solution)/shard_map/ppermute | solution.py:22
  7.4 0.4 collective-permute-start.3
  7.8 0.5 collective-permute-start.2
  8.3 0.7 %collective-permute-done.1.refs_1_ = bf16[2,128,128]{2,1,0:T(8,128)(2,1)S(1)} collective-permute-done((bf16[2,128,128]{2,1,0:T(8,128)(2,1)}, bf16[2,128,128]{2,1,0:T(8,128)(2,1)S(1)}, u32[]{:S(2)}, u32[]{:S(2)}) %collective-permute-start.1) | collective-permute-done | bytes 65568 | tf_op jit(solution)/shard_map/ppermute | solution.py:22
  9.0 1.9 %collective-permute-start.7 = (bf16[2,128,128]{2,1,0:T(8,128)(2,1)S(1)}, bf16[2,128,128]{2,1,0:T(8,128)(2,1)S(1)}, u32[]{:S(2)}, u32[]{:S(2)}) collective-permute-start(bf16[2,128,128]{2,1,0:T(8,128)(2,1)S(1)} %collective-permute-done.1.refs_1_), channel_id=1, source_target_pairs={{0,3},{1,2},{2,1},{3,0},{4,7},{5,6},{6,5},{7,4},{8,11},{9,10},{10,... | collective-permute-start | bytes 196616 | tf_op jit(solution)/shard_map/ppermute | solution.py:22
  11.0 0.0 collective-permute-done.4.refs_4_
  11.0 1.5 %collective-permute-start.6 = (bf16[2,128,128]{2,1,0:T(8,128)(2,1)S(1)}, bf16[2,128,128]{2,1,0:T(8,128)(2,1)S(1)}, u32[]{:S(2)}, u32[]{:S(2)}) collective-permute-start(bf16[2,128,128]{2,1,0:T(8,128)(2,1)S(1)} %collective-permute-done.1.refs_1_), channel_id=1, source_target_pairs={{0,2},{1,3},{2,0},{3,1},{4,6},{5,7},{6,4},{7,5},{8,10},{9,11},{10,... | collective-permute-start | bytes 196616 | tf_op jit(solution)/shard_map/ppermute | solution.py:22
  12.4 0.0 collective-permute-done.3.refs_3_
  12.5 1.4 %collective-permute-start.5 = (bf16[2,128,128]{2,1,0:T(8,128)(2,1)S(1)}, bf16[2,128,128]{2,1,0:T(8,128)(2,1)S(1)}, u32[]{:S(2)}, u32[]{:S(2)}) collective-permute-start(bf16[2,128,128]{2,1,0:T(8,128)(2,1)S(1)} %collective-permute-done.1.refs_1_), channel_id=1, source_target_pairs={{0,1},{1,0},{2,3},{3,2},{4,5},{5,4},{6,7},{7,6},{8,9},{9,8},{10,11... | collective-permute-start | bytes 196616 | tf_op jit(solution)/shard_map/ppermute | solution.py:22
  13.9 2.8 %prepare.1 = (s32[2,32]{1,0:T(2,128)S(1)}, f32[2,32]{1,0:T(2,128)S(1)}, bf16[2,24,128,128]{3,2,1,0:T(8,128)(2,1)S(1)}) custom-call(s32[2,32]{1,0:T(2,128)} %bitcast.14, s32[2,32]{1,0:T(2,128)} %bitcast.15, f32[2,32]{1,0:T(2,128)} %bitcast.16, bf16[2,24,128,128]{3,2,1,0:T(8,128)(2,1)} %bitcast.13), custom_call_target="tpu_custom_call" | custom-call | tf_op jit(solution)/shard_map/prepare/pallas_call | solution.py:243
  16.7 0.0 collective-permute-done.7.refs_7_
  16.7 0.0 collective-permute-done.6.refs_6_
  16.7 0.0 collective-permute-done.5.refs_5_
  16.7 0.0 collective-permute-done.right
  16.8 2.3 %first_image.1.refs_8_ = bf16[2,128,128]{2,1,0:T(8,128)(2,1)S(1)} custom-call(s32[2,32]{1,0:T(2,128)S(1)} %get-tuple-element.14.codes, f32[2,32]{1,0:T(2,128)S(1)} %get-tuple-element.15.floats, bf16[2,24,128,128]{3,2,1,0:T(8,128)(2,1)S(1)} %get-tuple-element.16.left, bf16[2,24,128,128]{3,2,1,0:T(8,128)(2,1)S(1)} %collective-permute-done.right, ...), custom_call_target="tpu_custom_call" | custom-call | tf_op jit(solution)/shard_map/first_image/pallas_call | solution.py:266
  19.0 0.0 copy-start.1
  19.1 2.0 %collective-permute-start.8 = (bf16[2,128,128]{2,1,0:T(8,128)(2,1)S(1)}, bf16[2,128,128]{2,1,0:T(8,128)(2,1)S(1)}, u32[]{:S(2)}, u32[]{:S(2)}) collective-permute-start(bf16[2,128,128]{2,1,0:T(8,128)(2,1)S(1)} %first_image.1.refs_8_), channel_id=1, source_target_pairs={{0,4},{1,5},{2,6},{3,7},{4,0},{5,1},{6,2},{7,3},{8,12},{9,13},{10,... | collective-permute-start | bytes 196616 | tf_op jit(solution)/shard_map/ppermute | solution.py:22
  21.0 2.0 %collective-permute-start.11 = (bf16[2,128,128]{2,1,0:T(8,128)(2,1)S(1)}, bf16[2,128,128]{2,1,0:T(8,128)(2,1)S(1)}, u32[]{:S(2)}, u32[]{:S(2)}) collective-permute-start(bf16[2,128,128]{2,1,0:T(8,128)(2,1)S(1)} %first_image.1.refs_8_), channel_id=1, source_target_pairs={{0,3},{1,2},{2,1},{3,0},{4,7},{5,6},{6,5},{7,4},{8,11},{9,10},{10,... | collective-permute-start | bytes 196616 | tf_op jit(solution)/shard_map/ppermute | solution.py:22
  23.0 0.7 %collective-permute-start.10 = (bf16[2,128,128]{2,1,0:T(8,128)(2,1)S(1)}, bf16[2,128,128]{2,1,0:T(8,128)(2,1)S(1)}, u32[]{:S(2)}, u32[]{:S(2)}) collective-permute-start(bf16[2,128,128]{2,1,0:T(8,128)(2,1)S(1)} %first_image.1.refs_8_), channel_id=1, source_target_pairs={{0,2},{1,3},{2,0},{3,1},{4,6},{5,7},{6,4},{7,5},{8,10},{9,11},{10,... | collective-permute-start | bytes 196616 | tf_op jit(solution)/shard_map/ppermute | solution.py:22
  23.7 0.8 %collective-permute-start.9 = (bf16[2,128,128]{2,1,0:T(8,128)(2,1)S(1)}, bf16[2,128,128]{2,1,0:T(8,128)(2,1)S(1)}, u32[]{:S(2)}, u32[]{:S(2)}) collective-permute-start(bf16[2,128,128]{2,1,0:T(8,128)(2,1)S(1)} %first_image.1.refs_8_), channel_id=1, source_target_pairs={{0,1},{1,0},{2,3},{3,2},{4,5},{5,4},{6,7},{7,6},{8,9},{9,8},{10,11... | collective-permute-start | bytes 196616 | tf_op jit(solution)/shard_map/ppermute | solution.py:22
  24.5 0.2 collective-permute-done.8.refs_9_
  24.7 1.8 %collective-permute-start.14 = (bf16[2,128,128]{2,1,0:T(8,128)(2,1)S(1)}, bf16[2,128,128]{2,1,0:T(8,128)(2,1)S(1)}, u32[]{:S(2)}, u32[]{:S(2)}) collective-permute-start(bf16[2,128,128]{2,1,0:T(8,128)(2,1)S(1)} %collective-permute-done.8.refs_9_), channel_id=1, source_target_pairs={{0,3},{1,2},{2,1},{3,0},{4,7},{5,6},{6,5},{7,4},{8,11},{9,10},{10,... | collective-permute-start | bytes 196616 | tf_op jit(solution)/shard_map/ppermute | solution.py:22
  26.5 1.0 %collective-permute-start.13 = (bf16[2,128,128]{2,1,0:T(8,128)(2,1)S(1)}, bf16[2,128,128]{2,1,0:T(8,128)(2,1)S(1)}, u32[]{:S(2)}, u32[]{:S(2)}) collective-permute-start(bf16[2,128,128]{2,1,0:T(8,128)(2,1)S(1)} %collective-permute-done.8.refs_9_), channel_id=1, source_target_pairs={{0,2},{1,3},{2,0},{3,1},{4,6},{5,7},{6,4},{7,5},{8,10},{9,11},{10,... | collective-permute-start | bytes 196616 | tf_op jit(solution)/shard_map/ppermute | solution.py:22
  27.6 0.0 collective-permute-done.11.refs_12_
  27.6 0.6 %collective-permute-start.12 = (bf16[2,128,128]{2,1,0:T(8,128)(2,1)S(1)}, bf16[2,128,128]{2,1,0:T(8,128)(2,1)S(1)}, u32[]{:S(2)}, u32[]{:S(2)}) collective-permute-start(bf16[2,128,128]{2,1,0:T(8,128)(2,1)S(1)} %collective-permute-done.8.refs_9_), channel_id=1, source_target_pairs={{0,1},{1,0},{2,3},{3,2},{4,5},{5,4},{6,7},{7,6},{8,9},{9,8},{10,11... | collective-permute-start | bytes 196616 | tf_op jit(solution)/shard_map/ppermute | solution.py:22
  28.2 0.0 collective-permute-done.10.refs_11_
  28.2 0.8 %collective-permute-done.9.refs_10_ = bf16[2,128,128]{2,1,0:T(8,128)(2,1)S(1)} collective-permute-done((bf16[2,128,128]{2,1,0:T(8,128)(2,1)S(1)}, bf16[2,128,128]{2,1,0:T(8,128)(2,1)S(1)}, u32[]{:S(2)}, u32[]{:S(2)}) %collective-permute-start.9) | collective-permute-done | bytes 65568 | tf_op jit(solution)/shard_map/ppermute | solution.py:22
  29.0 0.9 %collective-permute-done.14.refs_15_ = bf16[2,128,128]{2,1,0:T(8,128)(2,1)S(1)} collective-permute-done((bf16[2,128,128]{2,1,0:T(8,128)(2,1)S(1)}, bf16[2,128,128]{2,1,0:T(8,128)(2,1)S(1)}, u32[]{:S(2)}, u32[]{:S(2)}) %collective-permute-start.14) | collective-permute-done | bytes 65568 | tf_op jit(solution)/shard_map/ppermute | solution.py:22
  29.8 0.9 %collective-permute-done.13.refs_14_ = bf16[2,128,128]{2,1,0:T(8,128)(2,1)S(1)} collective-permute-done((bf16[2,128,128]{2,1,0:T(8,128)(2,1)S(1)}, bf16[2,128,128]{2,1,0:T(8,128)(2,1)S(1)}, u32[]{:S(2)}, u32[]{:S(2)}) %collective-permute-start.13) | collective-permute-done | bytes 65568 | tf_op jit(solution)/shard_map/ppermute | solution.py:22
  30.8 1.0 %collective-permute-done.12.refs_13_ = bf16[2,128,128]{2,1,0:T(8,128)(2,1)S(1)} collective-permute-done((bf16[2,128,128]{2,1,0:T(8,128)(2,1)S(1)}, bf16[2,128,128]{2,1,0:T(8,128)(2,1)S(1)}, u32[]{:S(2)}, u32[]{:S(2)}) %collective-permute-start.12) | collective-permute-done | bytes 65568 | tf_op jit(solution)/shard_map/ppermute | solution.py:22
  31.8 2.5 %middle_image.1 = (f32[1,128]{1,0:T(1,128)S(1)}, f32[16,128,128]{2,1,0:T(8,128)S(1)}, bf16[2,128,128]{2,1,0:T(8,128)(2,1)S(1)}) custom-call(s32[2,32]{1,0:T(2,128)S(1)} %get-tuple-element.14.codes, f32[2,32]{1,0:T(2,128)S(1)} %get-tuple-element.15.floats, bf16[2,24,128,128]{3,2,1,0:T(8,128)(2,1)S(1)} %get-tuple-element.16.left, ...), custom_call_target="tpu_custom_call" | custom-call | tf_op jit(solution)/shard_map/middle_image/pallas_call | solution.py:278
  34.4 2.1 %collective-permute-start.15 = (bf16[2,128,128]{2,1,0:T(8,128)(2,1)S(1)}, bf16[2,128,128]{2,1,0:T(8,128)(2,1)S(1)}, u32[]{:S(2)}, u32[]{:S(2)}) collective-permute-start(bf16[2,128,128]{2,1,0:T(8,128)(2,1)S(1)} %get-tuple-element.18.refs_1_), channel_id=1, source_target_pairs={{0,4},{1,5},{2,6},{3,7},{4,0},{5,1},{6,2},{7,3},{8,12},{9,13},{10,... | collective-permute-start | bytes 196616 | tf_op jit(solution)/shard_map/ppermute | solution.py:22
  36.5 1.9 %collective-permute-start.18 = (bf16[2,128,128]{2,1,0:T(8,128)(2,1)S(1)}, bf16[2,128,128]{2,1,0:T(8,128)(2,1)S(1)}, u32[]{:S(2)}, u32[]{:S(2)}) collective-permute-start(bf16[2,128,128]{2,1,0:T(8,128)(2,1)S(1)} %get-tuple-element.18.refs_1_), channel_id=1, source_target_pairs={{0,3},{1,2},{2,1},{3,0},{4,7},{5,6},{6,5},{7,4},{8,11},{9,10},{10,... | collective-permute-start | bytes 196616 | tf_op jit(solution)/shard_map/ppermute | solution.py:22
  38.4 0.3 collective-permute-start.17
  38.7 1.2 %collective-permute-start.16 = (bf16[2,128,128]{2,1,0:T(8,128)(2,1)S(1)}, bf16[2,128,128]{2,1,0:T(8,128)(2,1)S(1)}, u32[]{:S(2)}, u32[]{:S(2)}) collective-permute-start(bf16[2,128,128]{2,1,0:T(8,128)(2,1)S(1)} %get-tuple-element.18.refs_1_), channel_id=1, source_target_pairs={{0,1},{1,0},{2,3},{3,2},{4,5},{5,4},{6,7},{7,6},{8,9},{9,8},{10,11... | collective-permute-start | bytes 196616 | tf_op jit(solution)/shard_map/ppermute | solution.py:22
  40.0 0.0 collective-permute-done.15.refs_2_
  40.0 1.9 %collective-permute-start.21 = (bf16[2,128,128]{2,1,0:T(8,128)(2,1)S(1)}, bf16[2,128,128]{2,1,0:T(8,128)(2,1)S(1)}, u32[]{:S(2)}, u32[]{:S(2)}) collective-permute-start(bf16[2,128,128]{2,1,0:T(8,128)(2,1)S(1)} %collective-permute-done.15.refs_2_), channel_id=1, source_target_pairs={{0,3},{1,2},{2,1},{3,0},{4,7},{5,6},{6,5},{7,4},{8,11},{9,10},{10,... | collective-permute-start | bytes 196616 | tf_op jit(solution)/shard_map/ppermute | solution.py:22
  41.9 0.3 collective-permute-start.20
  42.2 1.2 %collective-permute-start.19 = (bf16[2,128,128]{2,1,0:T(8,128)(2,1)S(1)}, bf16[2,128,128]{2,1,0:T(8,128)(2,1)S(1)}, u32[]{:S(2)}, u32[]{:S(2)}) collective-permute-start(bf16[2,128,128]{2,1,0:T(8,128)(2,1)S(1)} %collective-permute-done.15.refs_2_), channel_id=1, source_target_pairs={{0,1},{1,0},{2,3},{3,2},{4,5},{5,4},{6,7},{7,6},{8,9},{9,8},{10,11... | collective-permute-start | bytes 196616 | tf_op jit(solution)/shard_map/ppermute | solution.py:22
  43.5 0.0 collective-permute-done.16.refs_3_
  43.5 1.7 %collective-permute-done.21.refs_8_ = bf16[2,128,128]{2,1,0:T(8,128)(2,1)S(1)} collective-permute-done((bf16[2,128,128]{2,1,0:T(8,128)(2,1)S(1)}, bf16[2,128,128]{2,1,0:T(8,128)(2,1)S(1)}, u32[]{:S(2)}, u32[]{:S(2)}) %collective-permute-start.21) | collective-permute-done | bytes 65568 | tf_op jit(solution)/shard_map/ppermute | solution.py:22
  45.1 1.0 %collective-permute-done.20.refs_7_ = bf16[2,128,128]{2,1,0:T(8,128)(2,1)S(1)} collective-permute-done((bf16[2,128,128]{2,1,0:T(8,128)(2,1)S(1)}, bf16[2,128,128]{2,1,0:T(8,128)(2,1)S(1)}, u32[]{:S(2)}, u32[]{:S(2)}) %collective-permute-start.20) | collective-permute-done | bytes 65568 | tf_op jit(solution)/shard_map/ppermute | solution.py:22
  46.2 0.3 collective-permute-done.19.refs_6_
  46.5 2.8 %last_image.1 = (f32[1,128]{1,0:T(1,128)S(1)}, f32[2,128,128]{2,1,0:T(8,128)S(1)}, bf16[2,128,128]{2,1,0:T(8,128)(2,1)S(1)}, f32[8,8,128]{2,1,0:T(8,128)S(1)}) custom-call(s32[2,32]{1,0:T(2,128)S(1)} %get-tuple-element.14.codes, f32[2,32]{1,0:T(2,128)S(1)} %get-tuple-element.15.floats, s32[1,2]{1,0:T(1,128)S(1)} %copy-done.1, ...), custom_call_target="tpu_custom_call" | custom-call | tf_op jit(solution)/shard_map/last_image/pallas_call | solution.py:290
  49.3 11.2 %all_to_all.5.gathered = f32[8,8,128]{2,1,0:T(8,128)S(1)} all-to-all(f32[8,8,128]{2,1,0:T(8,128)S(1)} %get-tuple-element.21), channel_id=1, replica_groups=mesh['parts'=2,'seg'=2,'sec'=8] {'sec'}, dimensions={0} | all-to-all | bytes 65536 | tf_op jit(solution)/shard_map/all_to_all | solution.py:311
  60.4 0.7 %finish.1 = (f32[1,3]{1,0:T(1,128)}, bf16[2,128,128]{2,1,0:T(8,128)(2,1)}) custom-call(f32[2,128,128]{2,1,0:T(8,128)S(1)} %get-tuple-element.19.own, bf16[2,128,128]{2,1,0:T(8,128)(2,1)S(1)} %get-tuple-element.20.image, f32[8,8,128]{2,1,0:T(8,128)S(1)} %all_to_all.5.gathered, f32[1,128]{1,0:T(1,128)S(1)} %get-tuple-element.22.refs_0_, ...), custom_call_target="tpu_custom_call" | custom-call | tf_op jit(solution)/shard_map/finish/pallas_call | solution.py:312
  (6 shorter events, 0.0 us)
Async XLA Ops:
  0.6 16.1 %copy-start = (bf16[1,2,128,128]{3,2,1,0:T(8,128)(2,1)S(1)}, bf16[1,2,128,128]{3,2,1,0:T(8,128)(2,1)}, u32[]{:S(2)}) copy-start(bf16[1,2,128,128]{3,2,1,0:T(8,128)(2,1)} %param.7) | copy-start | bytes 196612
  0.6 16.1 %collective-permute-start = (bf16[2,24,128,128]{3,2,1,0:T(8,128)(2,1)}, bf16[2,24,128,128]{3,2,1,0:T(8,128)(2,1)S(1)}, u32[]{:S(2)}, u32[]{:S(2)}) collective-permute-start(bf16[2,24,128,128]{3,2,1,0:T(8,128)(2,1)} %bitcast.17), channel_id=1, source_target_pairs={{0,8},{8,0},{1,9},{9,1},{2,10},{10,2},{3,11},{11,3},{4,12},{12,4},... | collective-permute-start | bytes 4718600 | tf_op jit(solution)/shard_map/ppermute | solution.py:233
  1.2 7.9 %collective-permute-start.1 = (bf16[2,128,128]{2,1,0:T(8,128)(2,1)}, bf16[2,128,128]{2,1,0:T(8,128)(2,1)S(1)}, u32[]{:S(2)}, u32[]{:S(2)}) collective-permute-start(bf16[2,128,128]{2,1,0:T(8,128)(2,1)} %bitcast.7), channel_id=1, source_target_pairs={{0,4},{1,5},{2,6},{3,7},{4,0},{5,1},{6,2},{7,3},{8,12},{9,13},{10,... | collective-permute-start | bytes 196616 | tf_op jit(solution)/shard_map/ppermute | solution.py:22
  4.8 6.2 %collective-permute-start.4 = (bf16[2,128,128]{2,1,0:T(8,128)(2,1)}, bf16[2,128,128]{2,1,0:T(8,128)(2,1)S(1)}, u32[]{:S(2)}, u32[]{:S(2)}) collective-permute-start(bf16[2,128,128]{2,1,0:T(8,128)(2,1)} %bitcast.8), channel_id=1, source_target_pairs={{0,3},{1,2},{2,1},{3,0},{4,7},{5,6},{6,5},{7,4},{8,11},{9,10},{10,... | collective-permute-start | bytes 196616 | tf_op jit(solution)/shard_map/ppermute | solution.py:22
  7.4 5.1 %collective-permute-start.3 = (bf16[2,128,128]{2,1,0:T(8,128)(2,1)}, bf16[2,128,128]{2,1,0:T(8,128)(2,1)S(1)}, u32[]{:S(2)}, u32[]{:S(2)}) collective-permute-start(bf16[2,128,128]{2,1,0:T(8,128)(2,1)} %bitcast.9), channel_id=1, source_target_pairs={{0,2},{1,3},{2,0},{3,1},{4,6},{5,7},{6,4},{7,5},{8,10},{9,11},{10,... | collective-permute-start | bytes 196616 | tf_op jit(solution)/shard_map/ppermute | solution.py:22
  7.8 8.9 %collective-permute-start.2 = (bf16[2,128,128]{2,1,0:T(8,128)(2,1)}, bf16[2,128,128]{2,1,0:T(8,128)(2,1)S(1)}, u32[]{:S(2)}, u32[]{:S(2)}) collective-permute-start(bf16[2,128,128]{2,1,0:T(8,128)(2,1)} %bitcast.10), channel_id=1, source_target_pairs={{0,1},{1,0},{2,3},{3,2},{4,5},{5,4},{6,7},{7,6},{8,9},{9,8},{10,11... | collective-permute-start | bytes 196616 | tf_op jit(solution)/shard_map/ppermute | solution.py:22
  9.0 7.7 %collective-permute-start.7 = (bf16[2,128,128]{2,1,0:T(8,128)(2,1)S(1)}, bf16[2,128,128]{2,1,0:T(8,128)(2,1)S(1)}, u32[]{:S(2)}, u32[]{:S(2)}) collective-permute-start(bf16[2,128,128]{2,1,0:T(8,128)(2,1)S(1)} %collective-permute-done.1.refs_1_), channel_id=1, source_target_pairs={{0,3},{1,2},{2,1},{3,0},{4,7},{5,6},{6,5},{7,4},{8,11},{9,10},{10,... | collective-permute-start | bytes 196616 | tf_op jit(solution)/shard_map/ppermute | solution.py:22
  11.0 5.7 %collective-permute-start.6 = (bf16[2,128,128]{2,1,0:T(8,128)(2,1)S(1)}, bf16[2,128,128]{2,1,0:T(8,128)(2,1)S(1)}, u32[]{:S(2)}, u32[]{:S(2)}) collective-permute-start(bf16[2,128,128]{2,1,0:T(8,128)(2,1)S(1)} %collective-permute-done.1.refs_1_), channel_id=1, source_target_pairs={{0,2},{1,3},{2,0},{3,1},{4,6},{5,7},{6,4},{7,5},{8,10},{9,11},{10,... | collective-permute-start | bytes 196616 | tf_op jit(solution)/shard_map/ppermute | solution.py:22
  12.5 4.3 %collective-permute-start.5 = (bf16[2,128,128]{2,1,0:T(8,128)(2,1)S(1)}, bf16[2,128,128]{2,1,0:T(8,128)(2,1)S(1)}, u32[]{:S(2)}, u32[]{:S(2)}) collective-permute-start(bf16[2,128,128]{2,1,0:T(8,128)(2,1)S(1)} %collective-permute-done.1.refs_1_), channel_id=1, source_target_pairs={{0,1},{1,0},{2,3},{3,2},{4,5},{5,4},{6,7},{7,6},{8,9},{9,8},{10,11... | collective-permute-start | bytes 196616 | tf_op jit(solution)/shard_map/ppermute | solution.py:22
  19.0 27.5 %copy-start.1 = (s32[1,2]{1,0:T(1,128)S(1)}, s32[1,2]{1,0:T(1,128)}, u32[]{:S(2)}) copy-start(s32[1,2]{1,0:T(1,128)} %ranks.1) | copy-start | bytes 28
  19.1 5.6 %collective-permute-start.8 = (bf16[2,128,128]{2,1,0:T(8,128)(2,1)S(1)}, bf16[2,128,128]{2,1,0:T(8,128)(2,1)S(1)}, u32[]{:S(2)}, u32[]{:S(2)}) collective-permute-start(bf16[2,128,128]{2,1,0:T(8,128)(2,1)S(1)} %first_image.1.refs_8_), channel_id=1, source_target_pairs={{0,4},{1,5},{2,6},{3,7},{4,0},{5,1},{6,2},{7,3},{8,12},{9,13},{10,... | collective-permute-start | bytes 196616 | tf_op jit(solution)/shard_map/ppermute | solution.py:22
  21.0 6.5 %collective-permute-start.11 = (bf16[2,128,128]{2,1,0:T(8,128)(2,1)S(1)}, bf16[2,128,128]{2,1,0:T(8,128)(2,1)S(1)}, u32[]{:S(2)}, u32[]{:S(2)}) collective-permute-start(bf16[2,128,128]{2,1,0:T(8,128)(2,1)S(1)} %first_image.1.refs_8_), channel_id=1, source_target_pairs={{0,3},{1,2},{2,1},{3,0},{4,7},{5,6},{6,5},{7,4},{8,11},{9,10},{10,... | collective-permute-start | bytes 196616 | tf_op jit(solution)/shard_map/ppermute | solution.py:22
  23.0 5.2 %collective-permute-start.10 = (bf16[2,128,128]{2,1,0:T(8,128)(2,1)S(1)}, bf16[2,128,128]{2,1,0:T(8,128)(2,1)S(1)}, u32[]{:S(2)}, u32[]{:S(2)}) collective-permute-start(bf16[2,128,128]{2,1,0:T(8,128)(2,1)S(1)} %first_image.1.refs_8_), channel_id=1, source_target_pairs={{0,2},{1,3},{2,0},{3,1},{4,6},{5,7},{6,4},{7,5},{8,10},{9,11},{10,... | collective-permute-start | bytes 196616 | tf_op jit(solution)/shard_map/ppermute | solution.py:22
  23.7 5.3 %collective-permute-start.9 = (bf16[2,128,128]{2,1,0:T(8,128)(2,1)S(1)}, bf16[2,128,128]{2,1,0:T(8,128)(2,1)S(1)}, u32[]{:S(2)}, u32[]{:S(2)}) collective-permute-start(bf16[2,128,128]{2,1,0:T(8,128)(2,1)S(1)} %first_image.1.refs_8_), channel_id=1, source_target_pairs={{0,1},{1,0},{2,3},{3,2},{4,5},{5,4},{6,7},{7,6},{8,9},{9,8},{10,11... | collective-permute-start | bytes 196616 | tf_op jit(solution)/shard_map/ppermute | solution.py:22
  24.7 5.2 %collective-permute-start.14 = (bf16[2,128,128]{2,1,0:T(8,128)(2,1)S(1)}, bf16[2,128,128]{2,1,0:T(8,128)(2,1)S(1)}, u32[]{:S(2)}, u32[]{:S(2)}) collective-permute-start(bf16[2,128,128]{2,1,0:T(8,128)(2,1)S(1)} %collective-permute-done.8.refs_9_), channel_id=1, source_target_pairs={{0,3},{1,2},{2,1},{3,0},{4,7},{5,6},{6,5},{7,4},{8,11},{9,10},{10,... | collective-permute-start | bytes 196616 | tf_op jit(solution)/shard_map/ppermute | solution.py:22
  26.5 4.3 %collective-permute-start.13 = (bf16[2,128,128]{2,1,0:T(8,128)(2,1)S(1)}, bf16[2,128,128]{2,1,0:T(8,128)(2,1)S(1)}, u32[]{:S(2)}, u32[]{:S(2)}) collective-permute-start(bf16[2,128,128]{2,1,0:T(8,128)(2,1)S(1)} %collective-permute-done.8.refs_9_), channel_id=1, source_target_pairs={{0,2},{1,3},{2,0},{3,1},{4,6},{5,7},{6,4},{7,5},{8,10},{9,11},{10,... | collective-permute-start | bytes 196616 | tf_op jit(solution)/shard_map/ppermute | solution.py:22
  27.6 4.3 %collective-permute-start.12 = (bf16[2,128,128]{2,1,0:T(8,128)(2,1)S(1)}, bf16[2,128,128]{2,1,0:T(8,128)(2,1)S(1)}, u32[]{:S(2)}, u32[]{:S(2)}) collective-permute-start(bf16[2,128,128]{2,1,0:T(8,128)(2,1)S(1)} %collective-permute-done.8.refs_9_), channel_id=1, source_target_pairs={{0,1},{1,0},{2,3},{3,2},{4,5},{5,4},{6,7},{7,6},{8,9},{9,8},{10,11... | collective-permute-start | bytes 196616 | tf_op jit(solution)/shard_map/ppermute | solution.py:22
  34.4 5.6 %collective-permute-start.15 = (bf16[2,128,128]{2,1,0:T(8,128)(2,1)S(1)}, bf16[2,128,128]{2,1,0:T(8,128)(2,1)S(1)}, u32[]{:S(2)}, u32[]{:S(2)}) collective-permute-start(bf16[2,128,128]{2,1,0:T(8,128)(2,1)S(1)} %get-tuple-element.18.refs_1_), channel_id=1, source_target_pairs={{0,4},{1,5},{2,6},{3,7},{4,0},{5,1},{6,2},{7,3},{8,12},{9,13},{10,... | collective-permute-start | bytes 196616 | tf_op jit(solution)/shard_map/ppermute | solution.py:22
  36.5 5.8 %collective-permute-start.18 = (bf16[2,128,128]{2,1,0:T(8,128)(2,1)S(1)}, bf16[2,128,128]{2,1,0:T(8,128)(2,1)S(1)}, u32[]{:S(2)}, u32[]{:S(2)}) collective-permute-start(bf16[2,128,128]{2,1,0:T(8,128)(2,1)S(1)} %get-tuple-element.18.refs_1_), channel_id=1, source_target_pairs={{0,3},{1,2},{2,1},{3,0},{4,7},{5,6},{6,5},{7,4},{8,11},{9,10},{10,... | collective-permute-start | bytes 196616 | tf_op jit(solution)/shard_map/ppermute | solution.py:22
  38.4 5.0 %collective-permute-start.17 = (bf16[2,128,128]{2,1,0:T(8,128)(2,1)S(1)}, bf16[2,128,128]{2,1,0:T(8,128)(2,1)S(1)}, u32[]{:S(2)}, u32[]{:S(2)}) collective-permute-start(bf16[2,128,128]{2,1,0:T(8,128)(2,1)S(1)} %get-tuple-element.18.refs_1_), channel_id=1, source_target_pairs={{0,2},{1,3},{2,0},{3,1},{4,6},{5,7},{6,4},{7,5},{8,10},{9,11},{10,... | collective-permute-start | bytes 196616 | tf_op jit(solution)/shard_map/ppermute | solution.py:22
  38.7 4.7 %collective-permute-start.16 = (bf16[2,128,128]{2,1,0:T(8,128)(2,1)S(1)}, bf16[2,128,128]{2,1,0:T(8,128)(2,1)S(1)}, u32[]{:S(2)}, u32[]{:S(2)}) collective-permute-start(bf16[2,128,128]{2,1,0:T(8,128)(2,1)S(1)} %get-tuple-element.18.refs_1_), channel_id=1, source_target_pairs={{0,1},{1,0},{2,3},{3,2},{4,5},{5,4},{6,7},{7,6},{8,9},{9,8},{10,11... | collective-permute-start | bytes 196616 | tf_op jit(solution)/shard_map/ppermute | solution.py:22
  40.0 5.2 %collective-permute-start.21 = (bf16[2,128,128]{2,1,0:T(8,128)(2,1)S(1)}, bf16[2,128,128]{2,1,0:T(8,128)(2,1)S(1)}, u32[]{:S(2)}, u32[]{:S(2)}) collective-permute-start(bf16[2,128,128]{2,1,0:T(8,128)(2,1)S(1)} %collective-permute-done.15.refs_2_), channel_id=1, source_target_pairs={{0,3},{1,2},{2,1},{3,0},{4,7},{5,6},{6,5},{7,4},{8,11},{9,10},{10,... | collective-permute-start | bytes 196616 | tf_op jit(solution)/shard_map/ppermute | solution.py:22
  41.9 4.3 %collective-permute-start.20 = (bf16[2,128,128]{2,1,0:T(8,128)(2,1)S(1)}, bf16[2,128,128]{2,1,0:T(8,128)(2,1)S(1)}, u32[]{:S(2)}, u32[]{:S(2)}) collective-permute-start(bf16[2,128,128]{2,1,0:T(8,128)(2,1)S(1)} %collective-permute-done.15.refs_2_), channel_id=1, source_target_pairs={{0,2},{1,3},{2,0},{3,1},{4,6},{5,7},{6,4},{7,5},{8,10},{9,11},{10,... | collective-permute-start | bytes 196616 | tf_op jit(solution)/shard_map/ppermute | solution.py:22
  42.2 4.3 %collective-permute-start.19 = (bf16[2,128,128]{2,1,0:T(8,128)(2,1)S(1)}, bf16[2,128,128]{2,1,0:T(8,128)(2,1)S(1)}, u32[]{:S(2)}, u32[]{:S(2)}) collective-permute-start(bf16[2,128,128]{2,1,0:T(8,128)(2,1)S(1)} %collective-permute-done.15.refs_2_), channel_id=1, source_target_pairs={{0,1},{1,0},{2,3},{3,2},{4,5},{5,4},{6,7},{7,6},{8,9},{9,8},{10,11... | collective-permute-start | bytes 196616 | tf_op jit(solution)/shard_map/ppermute | solution.py:22

commit v5 on v3

--- a/solution.py
+++ b/solution.py
@@ -14,7 +14,7 @@
 VMEM = pl.BlockSpec(memory_space=pltpu.VMEM)
 ANY = pl.BlockSpec(memory_space=pl.ANY)
 HBM = pl.BlockSpec(memory_space=pltpu.HBM)
-APART = (0, 4, 1, 2, 3, 7, 6, 5)
+APART = (0, 4, 1, 2, 3, 5, 6, 7)
 
 
 def hop(block, distance):
@@ -27,66 +27,62 @@
         return [lax.all_gather(block, "sec", axis=0, tiled=True)]
     relayed = hop(block, 4)
     near = [hop(block, distance) for distance in (1, 2, 3)]
-    return [block, relayed] + near + [hop(relayed, distance) for distance in (3, 2, 1)]
+    return [block, relayed] + near + [hop(relayed, distance) for distance in (1, 2, 3)]
+
+
+def cross(block, distance):
+    count = lax.axis_size("sec")
+    route = [(a, count + (a ^ distance)) for a in range(count)] + [(count + a, a ^ distance) for a in range(count)]
+    return lax.ppermute(block, ("seg", "sec"), route)
 
 
 def gather_small(block):
     if lax.axis_size("sec") != len(APART):
         return [lax.all_gather(block, "sec", axis=0, tiled=True)]
-    line = jnp.concatenate([block] + [hop(block, distance) for distance in (2, 4, 6)])
-    return [line, hop(line, 1)]
+    line = jnp.concatenate([cross(block, distance) for distance in (0, 1, 2, 3)])
+    return [cross(line, 0), cross(line, 4)]
 
 
 def slot(sector, blocks, devices, here):
     if devices != len(APART):
         return sector
-    apart = lax.div(sector, blocks) ^ here
-    place = jnp.int32(0)
+    owner = sum((sector >= blocks * device).astype(jnp.int32) for device in range(1, devices))
+    apart = owner ^ here
+    place = jnp.zeros_like(sector)
     for position in range(1, devices):
         place = jnp.where(apart == APART[position], position, place)
-    return place * blocks + lax.rem(sector, blocks)
+    return place * blocks + sector - owner * blocks
+
+
+def code_bits(width):
+    return (2 * width - 1).bit_length()
 
 
 def prepare_kernel(devices, *refs):
-    arguments, left, (codes, floats, near), scratch = refs[:3], refs[3], refs[4:7], refs[7:]
-    sources, channels, couplings, starts, semaphores = scratch
+    arguments, left, (codes, floats, near), (sources, channels, couplings, semaphores) = refs[:3], refs[3], refs[4:7], refs[7:]
     copies = fetch((*arguments, left), (sources, channels, couplings, near), semaphores)
     blocks, pairs = sources.shape
     width = near.shape[1]
     here = lax.axis_index("sec")
-    seen = 1 << 16
-    for w in range(width + 1):
-        for t in range(blocks):
-            starts[t, w] = 0
+    down = lax.broadcasted_iota(jnp.int32, (pairs, pairs), 0)
+    across = lax.broadcasted_iota(jnp.int32, (pairs, pairs), 1)
+
+    def column(row):
+        return jnp.sum(jnp.where(down == across, row, 0.0), axis=1, keepdims=True)
+
     for copy in copies[:3]:
         copy.wait()
-
-    def count(k, carry):
-        for t in range(blocks):
-            starts[t, channels[t, k] + 1] += 1
-        return carry
-
-    def add(w, totals):
-        totals = tuple(totals[t] + starts[t, w] for t in range(blocks))
-        for t in range(blocks):
-            starts[t, w] = totals[t]
-        return totals
-
-    def put(k, carry):
-        for t in range(blocks):
-            channel = channels[t, k]
-            mark = starts[t, channel]
-            to = mark & (seen - 1)
-            starts[t, channel] = (to + 1) | seen
-            same = lax.shift_right_logical(mark, 16)
-            code = slot(sources[t, k], blocks, devices, here)
-            codes[t, to] = (code << 16) | (channel << 1) | same
-            floats[t, to] = couplings[t, k]
-        return carry
-
-    lax.fori_loop(0, pairs, count, 0, unroll=4)
-    lax.fori_loop(0, width + 1, add, (jnp.int32(0),) * blocks, unroll=5)
-    lax.fori_loop(0, pairs, put, 0, unroll=2)
+    for t in range(blocks):
+        channel = channels[t : t + 1, :].astype(jnp.float32)
+        place = slot(sources[t : t + 1, :], blocks, devices, here).astype(jnp.float32)
+        mine = column(channel)
+        earlier = (channel == mine) & (across < down)
+        rank = jnp.sum(jnp.where((channel < mine) | earlier, 1.0, 0.0), axis=1, keepdims=True)
+        same = jnp.max(jnp.where(earlier, 1.0, 0.0), axis=1, keepdims=True)
+        code = column(place) * float(1 << code_bits(width)) + 2.0 * mine + same
+        chosen = rank == across.astype(jnp.float32)
+        codes[t : t + 1, :] = jnp.sum(jnp.where(chosen, code, 0.0), axis=0, keepdims=True).astype(jnp.int32)
+        floats[t : t + 1, :] = jnp.sum(jnp.where(chosen, column(couplings[t : t + 1, :]), 0.0), axis=0, keepdims=True)
     copies[3].wait()
 
 
@@ -100,20 +96,32 @@
     return copies
 
 
+def mixing(t, codes, floats, state, mixed):
+    pairs = floats.shape[1]
+    width, size = mixed[t].shape[0], mixed[t].shape[1]
+    bits = code_bits(width)
+    for first in range(0, size, size // 2):
+        rows = slice(first, first + size // 2)
+        total = jnp.zeros((size // 2, size), jnp.float32)
+        for k in range(pairs):
+            code = codes[t, k]
+            term = floats[t, k] * state[lax.shift_right_logical(code, bits), rows]
+            total = term + jnp.where((code & 1) == 1, total, 0.0)
+            channel = lax.shift_right_logical(code, 1) & ((1 << (bits - 1)) - 1)
+            mixed[t][channel, rows] = total.astype(jnp.bfloat16)
+            yield
+
+
 def apply_operator(copies, codes, floats, state, left, right, mixed, image):
     blocks, width = left.shape[0], left.shape[1]
-    pairs = floats.shape[1]
     for t in range(blocks):
         mixed[t][...] = jnp.zeros_like(mixed[t])
     for copy in copies:
         copy.wait()
-    for t in range(blocks):
-        total = jnp.zeros(state.shape[1:], jnp.float32)
-        for k in range(pairs):
-            code = codes[t, k]
-            term = floats[t, k] * state[lax.shift_right_logical(code, 16)]
-            total = term + jnp.where((code & 1) == 1, total, 0.0)
-            mixed[t][lax.shift_right_logical(code, 1) & 0x7FFF] = total.astype(jnp.bfloat16)
+    steps = [mixing(t, codes, floats, state, mixed) for t in range(blocks)]
+    for _ in steps[0]:
+        pass
+    share = -(-4 * floats.shape[1] // width)
     for t in range(blocks):
         result = jnp.zeros(image.shape[1:], jnp.float32)
         for w in range(0, width, 2):
@@ -127,7 +135,13 @@
                 (((1,), (1,)), ((), ())),
                 preferred_element_type=jnp.float32,
             )
+            if t + 1 < blocks:
+                for _ in range(share):
+                    next(steps[t + 1], None)
         image[t] = result.astype(jnp.bfloat16)
+        if t + 1 < blocks:
+            for _ in steps[t + 1]:
+                pass
 
 
 def spread(pieces, target):
@@ -160,7 +174,7 @@
         value = piece[s].astype(jnp.float32)
         intersection += value * picture[p].astype(jnp.float32)
         squares += value * value
-    energy = jnp.sum(intersection) / jnp.sum(squares)
+    energy = jnp.sum(intersection, keepdims=True) / jnp.sum(squares, keepdims=True)
     growth = 1.0 + STEP * energy
     for (piece, s), (picture, p) in zip(flat, pictures):
         after[at] = growth * piece[s].astype(jnp.float32) - STEP * picture[p].astype(jnp.float32)
@@ -172,7 +186,7 @@
     before, images = refs[:states], refs[states : states + count]
     energy, state, image, codes_here, floats_here, semaphores, *mixed = refs[states + count :]
     copies = fetch((codes, floats), (codes_here, floats_here), semaphores)
-    energy[...] = jnp.full(energy.shape, rayleigh_update(before, images, state))
+    energy[...] = jnp.broadcast_to(rayleigh_update(before, images, state), energy.shape)
     apply_operator(copies, codes_here, floats_here, state, left, right, mixed, image)
 
 
@@ -180,7 +194,7 @@
     before, images = refs[:states], refs[states : states + count]
     energy, own, image, sums, state, codes_here, floats_here, ranks_here, semaphores, *mixed = refs[states + count :]
     copies = fetch((codes, floats, ranks), (codes_here, floats_here, ranks_here), semaphores)
-    energy[...] = jnp.full(energy.shape, rayleigh_update(before, images, state))
+    energy[...] = jnp.broadcast_to(rayleigh_update(before, images, state), energy.shape)
     apply_operator(copies, codes_here, floats_here, state, left, right, mixed, image)
     blocks, size = image.shape[0], image.shape[1]
     intersection = jnp.zeros((size, size), jnp.float32)
@@ -189,7 +203,7 @@
         value = state[t]
         intersection += value * image[t].astype(jnp.float32)
         squares += value * value
-    intersection, squares = jnp.sum(intersection), jnp.sum(squares)
+    intersection, squares = jnp.sum(intersection, keepdims=True), jnp.sum(squares, keepdims=True)
     here = jnp.where(squares > 1e-30, intersection / jnp.maximum(squares, 1e-30), 0.0)
     growth = 1.0 + STEP * here
     column = lax.broadcasted_iota(jnp.int32, (size, size), 1)
@@ -206,18 +220,17 @@
         dd += moved * moved
         dc += moved * value
         cc += value * value
-    row = lax.broadcasted_iota(jnp.int32, sums.shape, 1)
-    result = jnp.zeros(sums.shape, jnp.float32)
-    for at, number in enumerate([intersection, squares, here, jnp.sum(dd), jnp.sum(dc), jnp.sum(cc)]):
+    row = lax.broadcasted_iota(jnp.int32, sums.shape[1:], 0)
+    result = jnp.zeros(sums.shape[1:], jnp.float32)
+    kept = [jnp.sum(value, keepdims=True) for value in (dd, dc, cc)]
+    for at, number in enumerate([intersection, squares, here, *kept]):
         result = jnp.where(row == at, number, result)
-    sums[...] = result
+    sums[...] = jnp.broadcast_to(result, sums.shape)
 
 
 def finish_kernel(steps, count, entries, own, image, *refs):
     earlier, gathered, (energies, kept) = refs[:steps], refs[steps : steps + count], refs[steps + count :]
-    rows = []
-    for piece in gathered:
-        rows += [piece[s] for s in range(piece.shape[0])]
+    rows = [piece[device] for piece in gathered for device in range(piece.shape[0])]
     intersection = sum(row[0:1, :] for row in rows)
     squares = sum(row[1:2, :] for row in rows)
     total = intersection / squares
@@ -253,17 +266,16 @@
         functools.partial(prepare_kernel, devices),
         out_shape=(ints, floats, jax.ShapeDtypeStruct(left.shape, left.dtype)),
         in_specs=[HBM] * 4,
-        out_specs=(SMEM, SMEM, VMEM),
+        out_specs=(VMEM, VMEM, VMEM),
         scratch_shapes=[
-            pltpu.SMEM(ints.shape, jnp.int32),
-            pltpu.SMEM(ints.shape, jnp.int32),
-            pltpu.SMEM(ints.shape, jnp.float32),
-            pltpu.SMEM((blocks, width + 1), jnp.int32),
+            pltpu.VMEM(ints.shape, jnp.int32),
+            pltpu.VMEM(ints.shape, jnp.int32),
+            pltpu.VMEM(ints.shape, jnp.float32),
             pltpu.SemaphoreType.DMA((4,)),
         ],
         compiler_params=params,
         name="prepare",
-    )(sources[0], channels[0], couplings[0], left)
+    )(*(pltpu.with_memory_space_constraint(block, pltpu.HBM) for block in (sources[0], channels[0], couplings[0], left)))
 
     own_type = jax.ShapeDtypeStruct((blocks, size, size), jnp.bfloat16)
     number = jax.ShapeDtypeStruct((1, 128), jnp.float32)

time: 65.2 us -> 59.9 us (0.919)
  local copies, waits for them, and re-layouts: 3.46 us -> 0.02 us
  waiting for transfers between devices: 14.4 us -> 12.7 us
  Pallas kernels: 10.9 us -> 9.72 us
  starting transfers between devices: 35.4 us -> 36.5 us
    ppermute x0 -> x6, starting transfers between devices: none -> 5.95 us  [cross(): return lax.ppermute(block, ('seg', 'sec'), route)]
    ppermute x25 -> x21, waiting for transfers between devices: 14.4 us -> 8.91 us  [hop(): return lax.ppermute(block, 'sec', [(a, a ^ distance) for a in range(count)])]
    ppermute x25 -> x21, starting transfers between devices: 34.9 us -> 30 us  [hop(): return lax.ppermute(block, 'sec', [(a, a ^ distance) for a in range(count)])]
    ppermute x0 -> x6, waiting for transfers between devices: none -> 3.77 us  [cross(): return lax.ppermute(block, ('seg', 'sec'), route)]
    unnamed x15 -> x7, local copies, waits for them, and re-layouts: 3.46 us -> 0.02 us
    pallas_call x1, Pallas kernels: 2.64 us -> 1.49 us  [local(): pl.pallas_call(functools.partial(prepare_kernel, devices), out_shape=(int...]
  transfers between devices with their start and end apart: 26 -> 28, of which waited for: 14 -> 12; matrix products, arithmetic and copies ran while one was open for 0% -> 0% of each run, Pallas kernels for 4% -> 2%
where the time goes in v5:
time: 59.9 us; the launch traced here: 59.7 us
  starting transfers between devices  36.5 us (61%)
  waiting for transfers between devices  12.7 us (21%)
  Pallas kernels  9.72 us (16%)
  between operations  0.74 us (1%)
    ppermute x21, starting transfers between devices, hop(): return lax.ppermute(block, 'sec', [(a, a ^ distance) for a in range(count)])  30 us
    ppermute x21, waiting for transfers between devices, hop(): return lax.ppermute(block, 'sec', [(a, a ^ distance) for a in range(count)])  8.91 us
    ppermute x6, starting transfers between devices, cross(): return lax.ppermute(block, ('seg', 'sec'), route)  5.95 us
    ppermute x6, waiting for transfers between devices, cross(): return lax.ppermute(block, ('seg', 'sec'), route)  3.77 us
    pallas_call x1, Pallas kernels, local(): pl.pallas_call(functools.partial(last_kernel, len(states), len(images)),...  2.7 us
    pallas_call x1, Pallas kernels, local(): pl.pallas_call(functools.partial(middle_kernel, len(states), len(images))...  2.57 us
    pallas_call x1, Pallas kernels, local(): pl.pallas_call(functools.partial(first_kernel, len(states)), out_shape=ow...  2.27 us
    pallas_call x1, Pallas kernels, local(): pl.pallas_call(functools.partial(prepare_kernel, devices), out_shape=(int...  1.49 us
  transfers between devices with their start and end apart: 28, of which 12 were waited for; matrix products, arithmetic and copies ran while one was open for 0% of the time, Pallas kernels for 2%

profile of v5, /device:TPU:0, one launch (start us, length us, event | category | flops | bytes accessed | tf_op | source)
XLA Modules:
  0.0 59.7 jit_solution(17683324877632287213)
XLA Ops:
  0.6 0.5 collective-permute-start
  1.2 3.7 %collective-permute-start.1 = (bf16[2,128,128]{2,1,0:T(8,128)(2,1)}, bf16[2,128,128]{2,1,0:T(8,128)(2,1)S(1)}, u32[]{:S(2)}, u32[]{:S(2)}) collective-permute-start(bf16[2,128,128]{2,1,0:T(8,128)(2,1)} %bitcast.7), channel_id=1, source_target_pairs={{0,4},{1,5},{2,6},{3,7},{4,0},{5,1},{6,2},{7,3},{8,12},{9,13},{10,... | collective-permute-start | bytes 196616 | tf_op jit(solution)/shard_map/ppermute | solution.py:22
  4.8 2.5 %collective-permute-start.4 = (bf16[2,128,128]{2,1,0:T(8,128)(2,1)}, bf16[2,128,128]{2,1,0:T(8,128)(2,1)S(1)}, u32[]{:S(2)}, u32[]{:S(2)}) collective-permute-start(bf16[2,128,128]{2,1,0:T(8,128)(2,1)} %bitcast.8), channel_id=1, source_target_pairs={{0,3},{1,2},{2,1},{3,0},{4,7},{5,6},{6,5},{7,4},{8,11},{9,10},{10,... | collective-permute-start | bytes 196616 | tf_op jit(solution)/shard_map/ppermute | solution.py:22
  7.4 0.4 collective-permute-start.3
  7.8 0.5 collective-permute-start.2
  8.3 0.7 %collective-permute-done.1.refs_1_ = bf16[2,128,128]{2,1,0:T(8,128)(2,1)S(1)} collective-permute-done((bf16[2,128,128]{2,1,0:T(8,128)(2,1)}, bf16[2,128,128]{2,1,0:T(8,128)(2,1)S(1)}, u32[]{:S(2)}, u32[]{:S(2)}) %collective-permute-start.1) | collective-permute-done | bytes 65568 | tf_op jit(solution)/shard_map/ppermute | solution.py:22
  9.0 1.9 %collective-permute-start.7 = (bf16[2,128,128]{2,1,0:T(8,128)(2,1)S(1)}, bf16[2,128,128]{2,1,0:T(8,128)(2,1)S(1)}, u32[]{:S(2)}, u32[]{:S(2)}) collective-permute-start(bf16[2,128,128]{2,1,0:T(8,128)(2,1)S(1)} %collective-permute-done.1.refs_1_), channel_id=1, source_target_pairs={{0,3},{1,2},{2,1},{3,0},{4,7},{5,6},{6,5},{7,4},{8,11},{9,10},{10,... | collective-permute-start | bytes 196616 | tf_op jit(solution)/shard_map/ppermute | solution.py:22
  11.0 1.5 %collective-permute-start.6 = (bf16[2,128,128]{2,1,0:T(8,128)(2,1)S(1)}, bf16[2,128,128]{2,1,0:T(8,128)(2,1)S(1)}, u32[]{:S(2)}, u32[]{:S(2)}) collective-permute-start(bf16[2,128,128]{2,1,0:T(8,128)(2,1)S(1)} %collective-permute-done.1.refs_1_), channel_id=1, source_target_pairs={{0,2},{1,3},{2,0},{3,1},{4,6},{5,7},{6,4},{7,5},{8,10},{9,11},{10,... | collective-permute-start | bytes 196616 | tf_op jit(solution)/shard_map/ppermute | solution.py:22
  12.4 0.0 collective-permute-done.3.refs_3_
  12.5 1.4 %collective-permute-start.5 = (bf16[2,128,128]{2,1,0:T(8,128)(2,1)S(1)}, bf16[2,128,128]{2,1,0:T(8,128)(2,1)S(1)}, u32[]{:S(2)}, u32[]{:S(2)}) collective-permute-start(bf16[2,128,128]{2,1,0:T(8,128)(2,1)S(1)} %collective-permute-done.1.refs_1_), channel_id=1, source_target_pairs={{0,1},{1,0},{2,3},{3,2},{4,5},{5,4},{6,7},{7,6},{8,9},{9,8},{10,11... | collective-permute-start | bytes 196616 | tf_op jit(solution)/shard_map/ppermute | solution.py:22
  13.9 1.5 %prepare.1 = (s32[2,32]{1,0:T(2,128)S(1)}, f32[2,32]{1,0:T(2,128)S(1)}, bf16[2,24,128,128]{3,2,1,0:T(8,128)(2,1)S(1)}) custom-call(s32[2,32]{1,0:T(2,128)} %bitcast.14, s32[2,32]{1,0:T(2,128)} %bitcast.15, f32[2,32]{1,0:T(2,128)} %bitcast.16, bf16[2,24,128,128]{3,2,1,0:T(8,128)(2,1)} %bitcast.13), custom_call_target="tpu_custom_call" | custom-call | tf_op jit(solution)/shard_map/prepare/pallas_call | solution.py:265
  15.4 0.0 collective-permute-done.6.refs_6_
  15.5 1.3 %collective-permute-done.5.refs_5_ = bf16[2,128,128]{2,1,0:T(8,128)(2,1)S(1)} collective-permute-done((bf16[2,128,128]{2,1,0:T(8,128)(2,1)S(1)}, bf16[2,128,128]{2,1,0:T(8,128)(2,1)S(1)}, u32[]{:S(2)}, u32[]{:S(2)}) %collective-permute-start.5) | collective-permute-done | bytes 65568 | tf_op jit(solution)/shard_map/ppermute | solution.py:22
  16.7 2.3 %first_image.1.refs_8_ = bf16[2,128,128]{2,1,0:T(8,128)(2,1)S(1)} custom-call(s32[2,32]{1,0:T(2,128)S(1)} %get-tuple-element.14.codes, f32[2,32]{1,0:T(2,128)S(1)} %get-tuple-element.15.floats, bf16[2,24,128,128]{3,2,1,0:T(8,128)(2,1)S(1)} %get-tuple-element.16.left, bf16[2,24,128,128]{3,2,1,0:T(8,128)(2,1)S(1)} %collective-permute-done.right, ...), custom_call_target="tpu_custom_call" | custom-call | tf_op jit(solution)/shard_map/first_image/pallas_call | solution.py:287
  19.0 0.0 copy-start.1
  19.0 2.0 %collective-permute-start.8 = (bf16[2,128,128]{2,1,0:T(8,128)(2,1)S(1)}, bf16[2,128,128]{2,1,0:T(8,128)(2,1)S(1)}, u32[]{:S(2)}, u32[]{:S(2)}) collective-permute-start(bf16[2,128,128]{2,1,0:T(8,128)(2,1)S(1)} %first_image.1.refs_8_), channel_id=1, source_target_pairs={{0,4},{1,5},{2,6},{3,7},{4,0},{5,1},{6,2},{7,3},{8,12},{9,13},{10,... | collective-permute-start | bytes 196616 | tf_op jit(solution)/shard_map/ppermute | solution.py:22
  21.0 2.0 %collective-permute-start.11 = (bf16[2,128,128]{2,1,0:T(8,128)(2,1)S(1)}, bf16[2,128,128]{2,1,0:T(8,128)(2,1)S(1)}, u32[]{:S(2)}, u32[]{:S(2)}) collective-permute-start(bf16[2,128,128]{2,1,0:T(8,128)(2,1)S(1)} %first_image.1.refs_8_), channel_id=1, source_target_pairs={{0,3},{1,2},{2,1},{3,0},{4,7},{5,6},{6,5},{7,4},{8,11},{9,10},{10,... | collective-permute-start | bytes 196616 | tf_op jit(solution)/shard_map/ppermute | solution.py:22
  23.0 0.7 %collective-permute-start.10 = (bf16[2,128,128]{2,1,0:T(8,128)(2,1)S(1)}, bf16[2,128,128]{2,1,0:T(8,128)(2,1)S(1)}, u32[]{:S(2)}, u32[]{:S(2)}) collective-permute-start(bf16[2,128,128]{2,1,0:T(8,128)(2,1)S(1)} %first_image.1.refs_8_), channel_id=1, source_target_pairs={{0,2},{1,3},{2,0},{3,1},{4,6},{5,7},{6,4},{7,5},{8,10},{9,11},{10,... | collective-permute-start | bytes 196616 | tf_op jit(solution)/shard_map/ppermute | solution.py:22
  23.7 0.8 %collective-permute-start.9 = (bf16[2,128,128]{2,1,0:T(8,128)(2,1)S(1)}, bf16[2,128,128]{2,1,0:T(8,128)(2,1)S(1)}, u32[]{:S(2)}, u32[]{:S(2)}) collective-permute-start(bf16[2,128,128]{2,1,0:T(8,128)(2,1)S(1)} %first_image.1.refs_8_), channel_id=1, source_target_pairs={{0,1},{1,0},{2,3},{3,2},{4,5},{5,4},{6,7},{7,6},{8,9},{9,8},{10,11... | collective-permute-start | bytes 196616 | tf_op jit(solution)/shard_map/ppermute | solution.py:22
  24.5 0.1 collective-permute-done.8.refs_9_
  24.6 1.9 %collective-permute-start.14 = (bf16[2,128,128]{2,1,0:T(8,128)(2,1)S(1)}, bf16[2,128,128]{2,1,0:T(8,128)(2,1)S(1)}, u32[]{:S(2)}, u32[]{:S(2)}) collective-permute-start(bf16[2,128,128]{2,1,0:T(8,128)(2,1)S(1)} %collective-permute-done.8.refs_9_), channel_id=1, source_target_pairs={{0,3},{1,2},{2,1},{3,0},{4,7},{5,6},{6,5},{7,4},{8,11},{9,10},{10,... | collective-permute-start | bytes 196616 | tf_op jit(solution)/shard_map/ppermute | solution.py:22
  26.5 1.1 %collective-permute-start.13 = (bf16[2,128,128]{2,1,0:T(8,128)(2,1)S(1)}, bf16[2,128,128]{2,1,0:T(8,128)(2,1)S(1)}, u32[]{:S(2)}, u32[]{:S(2)}) collective-permute-start(bf16[2,128,128]{2,1,0:T(8,128)(2,1)S(1)} %collective-permute-done.8.refs_9_), channel_id=1, source_target_pairs={{0,2},{1,3},{2,0},{3,1},{4,6},{5,7},{6,4},{7,5},{8,10},{9,11},{10,... | collective-permute-start | bytes 196616 | tf_op jit(solution)/shard_map/ppermute | solution.py:22
  27.6 0.5 collective-permute-start.12
  28.1 0.9 %collective-permute-done.9.refs_10_ = bf16[2,128,128]{2,1,0:T(8,128)(2,1)S(1)} collective-permute-done((bf16[2,128,128]{2,1,0:T(8,128)(2,1)S(1)}, bf16[2,128,128]{2,1,0:T(8,128)(2,1)S(1)}, u32[]{:S(2)}, u32[]{:S(2)}) %collective-permute-start.9) | collective-permute-done | bytes 65568 | tf_op jit(solution)/shard_map/ppermute | solution.py:22
  29.0 0.8 %collective-permute-done.14.refs_15_ = bf16[2,128,128]{2,1,0:T(8,128)(2,1)S(1)} collective-permute-done((bf16[2,128,128]{2,1,0:T(8,128)(2,1)S(1)}, bf16[2,128,128]{2,1,0:T(8,128)(2,1)S(1)}, u32[]{:S(2)}, u32[]{:S(2)}) %collective-permute-start.14) | collective-permute-done | bytes 65568 | tf_op jit(solution)/shard_map/ppermute | solution.py:22
  29.7 1.0 %collective-permute-done.13.refs_14_ = bf16[2,128,128]{2,1,0:T(8,128)(2,1)S(1)} collective-permute-done((bf16[2,128,128]{2,1,0:T(8,128)(2,1)S(1)}, bf16[2,128,128]{2,1,0:T(8,128)(2,1)S(1)}, u32[]{:S(2)}, u32[]{:S(2)}) %collective-permute-start.13) | collective-permute-done | bytes 65568 | tf_op jit(solution)/shard_map/ppermute | solution.py:22
  30.7 1.1 %collective-permute-done.12.refs_13_ = bf16[2,128,128]{2,1,0:T(8,128)(2,1)S(1)} collective-permute-done((bf16[2,128,128]{2,1,0:T(8,128)(2,1)S(1)}, bf16[2,128,128]{2,1,0:T(8,128)(2,1)S(1)}, u32[]{:S(2)}, u32[]{:S(2)}) %collective-permute-start.12) | collective-permute-done | bytes 65568 | tf_op jit(solution)/shard_map/ppermute | solution.py:22
  31.8 2.6 %middle_image.1 = (f32[1,128]{1,0:T(1,128)S(1)}, f32[16,128,128]{2,1,0:T(8,128)S(1)}, bf16[2,128,128]{2,1,0:T(8,128)(2,1)S(1)}) custom-call(s32[2,32]{1,0:T(2,128)S(1)} %get-tuple-element.14.codes, f32[2,32]{1,0:T(2,128)S(1)} %get-tuple-element.15.floats, bf16[2,24,128,128]{3,2,1,0:T(8,128)(2,1)S(1)} %get-tuple-element.16.left, ...), custom_call_target="tpu_custom_call" | custom-call | tf_op jit(solution)/shard_map/middle_image/pallas_call | solution.py:299
  34.4 2.1 %collective-permute-start.15 = (bf16[2,128,128]{2,1,0:T(8,128)(2,1)S(1)}, bf16[2,128,128]{2,1,0:T(8,128)(2,1)S(1)}, u32[]{:S(2)}, u32[]{:S(2)}) collective-permute-start(bf16[2,128,128]{2,1,0:T(8,128)(2,1)S(1)} %get-tuple-element.18.refs_1_), channel_id=1, source_target_pairs={{0,4},{1,5},{2,6},{3,7},{4,0},{5,1},{6,2},{7,3},{8,12},{9,13},{10,... | collective-permute-start | bytes 196616 | tf_op jit(solution)/shard_map/ppermute | solution.py:22
  36.5 1.9 %collective-permute-start.18 = (bf16[2,128,128]{2,1,0:T(8,128)(2,1)S(1)}, bf16[2,128,128]{2,1,0:T(8,128)(2,1)S(1)}, u32[]{:S(2)}, u32[]{:S(2)}) collective-permute-start(bf16[2,128,128]{2,1,0:T(8,128)(2,1)S(1)} %get-tuple-element.18.refs_1_), channel_id=1, source_target_pairs={{0,3},{1,2},{2,1},{3,0},{4,7},{5,6},{6,5},{7,4},{8,11},{9,10},{10,... | collective-permute-start | bytes 196616 | tf_op jit(solution)/shard_map/ppermute | solution.py:22
  38.4 0.3 collective-permute-start.17
  38.7 1.2 %collective-permute-start.16 = (bf16[2,128,128]{2,1,0:T(8,128)(2,1)S(1)}, bf16[2,128,128]{2,1,0:T(8,128)(2,1)S(1)}, u32[]{:S(2)}, u32[]{:S(2)}) collective-permute-start(bf16[2,128,128]{2,1,0:T(8,128)(2,1)S(1)} %get-tuple-element.18.refs_1_), channel_id=1, source_target_pairs={{0,1},{1,0},{2,3},{3,2},{4,5},{5,4},{6,7},{7,6},{8,9},{9,8},{10,11... | collective-permute-start | bytes 196616 | tf_op jit(solution)/shard_map/ppermute | solution.py:22
  40.0 2.2 %collective-permute-start.21 = (bf16[2,128,128]{2,1,0:T(8,128)(2,1)S(1)}, bf16[2,128,128]{2,1,0:T(8,128)(2,1)S(1)}, u32[]{:S(2)}, u32[]{:S(2)}) collective-permute-start(bf16[2,128,128]{2,1,0:T(8,128)(2,1)S(1)} %collective-permute-done.15.refs_2_), channel_id=1, source_target_pairs={{0,3},{1,2},{2,1},{3,0},{4,7},{5,6},{6,5},{7,4},{8,11},{9,10},{10,... | collective-permute-start | bytes 196616 | tf_op jit(solution)/shard_map/ppermute | solution.py:22
  42.2 0.1 collective-permute-start.20
  42.2 1.2 %collective-permute-start.19 = (bf16[2,128,128]{2,1,0:T(8,128)(2,1)S(1)}, bf16[2,128,128]{2,1,0:T(8,128)(2,1)S(1)}, u32[]{:S(2)}, u32[]{:S(2)}) collective-permute-start(bf16[2,128,128]{2,1,0:T(8,128)(2,1)S(1)} %collective-permute-done.15.refs_2_), channel_id=1, source_target_pairs={{0,1},{1,0},{2,3},{3,2},{4,5},{5,4},{6,7},{7,6},{8,9},{9,8},{10,11... | collective-permute-start | bytes 196616 | tf_op jit(solution)/shard_map/ppermute | solution.py:22
  43.5 1.7 %collective-permute-done.21.refs_8_ = bf16[2,128,128]{2,1,0:T(8,128)(2,1)S(1)} collective-permute-done((bf16[2,128,128]{2,1,0:T(8,128)(2,1)S(1)}, bf16[2,128,128]{2,1,0:T(8,128)(2,1)S(1)}, u32[]{:S(2)}, u32[]{:S(2)}) %collective-permute-start.21) | collective-permute-done | bytes 65568 | tf_op jit(solution)/shard_map/ppermute | solution.py:22
  45.1 1.3 %collective-permute-done.20.refs_7_ = bf16[2,128,128]{2,1,0:T(8,128)(2,1)S(1)} collective-permute-done((bf16[2,128,128]{2,1,0:T(8,128)(2,1)S(1)}, bf16[2,128,128]{2,1,0:T(8,128)(2,1)S(1)}, u32[]{:S(2)}, u32[]{:S(2)}) %collective-permute-start.20) | collective-permute-done | bytes 65568 | tf_op jit(solution)/shard_map/ppermute | solution.py:22
  46.4 0.1 collective-permute-done.19.refs_6_
  46.5 2.7 %last_image.1 = (f32[1,128]{1,0:T(1,128)S(1)}, f32[2,128,128]{2,1,0:T(8,128)S(1)}, bf16[2,128,128]{2,1,0:T(8,128)(2,1)S(1)}, f32[1,8,128]{2,1,0:T(8,128)S(1)}) custom-call(s32[2,32]{1,0:T(2,128)S(1)} %get-tuple-element.14.codes, f32[2,32]{1,0:T(2,128)S(1)} %get-tuple-element.15.floats, s32[1,2]{1,0:T(1,128)S(1)} %copy-done.1, ...), custom_call_target="tpu_custom_call" | custom-call | tf_op jit(solution)/shard_map/last_image/pallas_call | solution.py:311
  49.2 0.1 collective-permute-start.22
  49.3 1.9 %collective-permute-start.25 = (f32[1,8,128]{2,1,0:T(8,128)S(1)}, f32[1,8,128]{2,1,0:T(8,128)S(1)}, u32[]{:S(2)}, u32[]{:S(2)}) collective-permute-start(f32[1,8,128]{2,1,0:T(8,128)S(1)} %get-tuple-element.23), channel_id=1, source_target_pairs={{0,11},{1,10},{2,9},{3,8},{4,15},{5,14},{6,13},{7,12},{8,3},{9,2},... | collective-permute-start | bytes 12296 | tf_op jit(solution)/shard_map/ppermute | solution.py:36
  51.2 0.6 collective-permute-start.24
  51.8 0.8 %collective-permute-start.23 = (f32[1,8,128]{2,1,0:T(8,128)S(1)}, f32[1,8,128]{2,1,0:T(8,128)S(1)}, u32[]{:S(2)}, u32[]{:S(2)}) collective-permute-start(f32[1,8,128]{2,1,0:T(8,128)S(1)} %get-tuple-element.23), channel_id=1, source_target_pairs={{0,9},{1,8},{2,11},{3,10},{4,13},{5,12},{6,15},{7,14},{8,1},{9,0},... | collective-permute-start | bytes 12296 | tf_op jit(solution)/shard_map/ppermute | solution.py:36
  52.6 2.2 %collective-permute-done.23 = f32[1,8,128]{2,1,0:T(8,128)S(1)} collective-permute-done((f32[1,8,128]{2,1,0:T(8,128)S(1)}, f32[1,8,128]{2,1,0:T(8,128)S(1)}, u32[]{:S(2)}, u32[]{:S(2)}) %collective-permute-start.23) | collective-permute-done | bytes 4128 | tf_op jit(solution)/shard_map/ppermute | solution.py:36
  54.8 2.5 %collective-permute-start.27 = (f32[4,8,128]{2,1,0:T(8,128)S(1)}, f32[4,8,128]{2,1,0:T(8,128)S(1)}, u32[]{:S(2)}, u32[]{:S(2)}) collective-permute-start(f32[4,8,128]{2,1,0:T(8,128)S(1)} %constant_dynamic-update-slice_fusion), channel_id=1, source_target_pairs={{0,12},{1,13},{2,14},{3,15},{4,8},{5,9},{6,10},{7,11},{8,4},{9,5},... | collective-permute-start | bytes 49160 | tf_op jit(solution)/shard_map/ppermute | solution.py:36
  57.3 0.1 collective-permute-start.26
  57.4 1.6 %collective-permute-done.27.refs_3_ = f32[4,8,128]{2,1,0:T(8,128)S(1)} collective-permute-done((f32[4,8,128]{2,1,0:T(8,128)S(1)}, f32[4,8,128]{2,1,0:T(8,128)S(1)}, u32[]{:S(2)}, u32[]{:S(2)}) %collective-permute-start.27) | collective-permute-done | bytes 16416 | tf_op jit(solution)/shard_map/ppermute | solution.py:36
  59.0 0.7 %finish.1 = (f32[1,3]{1,0:T(1,128)}, bf16[2,128,128]{2,1,0:T(8,128)(2,1)}) custom-call(f32[2,128,128]{2,1,0:T(8,128)S(1)} %get-tuple-element.19.own, bf16[2,128,128]{2,1,0:T(8,128)(2,1)S(1)} %get-tuple-element.20.image, f32[1,128]{1,0:T(1,128)S(1)} %get-tuple-element.21.refs_0_, f32[1,128]{1,0:T(1,128)S(1)} %get-tuple-element.22.refs_1_, ...), custom_call_target="tpu_custom_call" | custom-call | tf_op jit(solution)/shard_map/finish/pallas_call | solution.py:333
  (21 shorter events, 0.1 us)
Async XLA Ops:
  0.6 16.1 %copy-start = (bf16[1,2,128,128]{3,2,1,0:T(8,128)(2,1)S(1)}, bf16[1,2,128,128]{3,2,1,0:T(8,128)(2,1)}, u32[]{:S(2)}) copy-start(bf16[1,2,128,128]{3,2,1,0:T(8,128)(2,1)} %param.7) | copy-start | bytes 196612
  0.6 16.1 %collective-permute-start = (bf16[2,24,128,128]{3,2,1,0:T(8,128)(2,1)}, bf16[2,24,128,128]{3,2,1,0:T(8,128)(2,1)S(1)}, u32[]{:S(2)}, u32[]{:S(2)}) collective-permute-start(bf16[2,24,128,128]{3,2,1,0:T(8,128)(2,1)} %bitcast.17), channel_id=1, source_target_pairs={{0,8},{8,0},{1,9},{9,1},{2,10},{10,2},{3,11},{11,3},{4,12},{12,4},... | collective-permute-start | bytes 4718600 | tf_op jit(solution)/shard_map/ppermute | solution.py:255
  1.2 7.9 %collective-permute-start.1 = (bf16[2,128,128]{2,1,0:T(8,128)(2,1)}, bf16[2,128,128]{2,1,0:T(8,128)(2,1)S(1)}, u32[]{:S(2)}, u32[]{:S(2)}) collective-permute-start(bf16[2,128,128]{2,1,0:T(8,128)(2,1)} %bitcast.7), channel_id=1, source_target_pairs={{0,4},{1,5},{2,6},{3,7},{4,0},{5,1},{6,2},{7,3},{8,12},{9,13},{10,... | collective-permute-start | bytes 196616 | tf_op jit(solution)/shard_map/ppermute | solution.py:22
  4.8 6.2 %collective-permute-start.4 = (bf16[2,128,128]{2,1,0:T(8,128)(2,1)}, bf16[2,128,128]{2,1,0:T(8,128)(2,1)S(1)}, u32[]{:S(2)}, u32[]{:S(2)}) collective-permute-start(bf16[2,128,128]{2,1,0:T(8,128)(2,1)} %bitcast.8), channel_id=1, source_target_pairs={{0,3},{1,2},{2,1},{3,0},{4,7},{5,6},{6,5},{7,4},{8,11},{9,10},{10,... | collective-permute-start | bytes 196616 | tf_op jit(solution)/shard_map/ppermute | solution.py:22
  7.4 5.1 %collective-permute-start.3 = (bf16[2,128,128]{2,1,0:T(8,128)(2,1)}, bf16[2,128,128]{2,1,0:T(8,128)(2,1)S(1)}, u32[]{:S(2)}, u32[]{:S(2)}) collective-permute-start(bf16[2,128,128]{2,1,0:T(8,128)(2,1)} %bitcast.9), channel_id=1, source_target_pairs={{0,2},{1,3},{2,0},{3,1},{4,6},{5,7},{6,4},{7,5},{8,10},{9,11},{10,... | collective-permute-start | bytes 196616 | tf_op jit(solution)/shard_map/ppermute | solution.py:22
  7.8 7.6 %collective-permute-start.2 = (bf16[2,128,128]{2,1,0:T(8,128)(2,1)}, bf16[2,128,128]{2,1,0:T(8,128)(2,1)S(1)}, u32[]{:S(2)}, u32[]{:S(2)}) collective-permute-start(bf16[2,128,128]{2,1,0:T(8,128)(2,1)} %bitcast.10), channel_id=1, source_target_pairs={{0,1},{1,0},{2,3},{3,2},{4,5},{5,4},{6,7},{7,6},{8,9},{9,8},{10,11... | collective-permute-start | bytes 196616 | tf_op jit(solution)/shard_map/ppermute | solution.py:22
  9.0 6.4 %collective-permute-start.7 = (bf16[2,128,128]{2,1,0:T(8,128)(2,1)S(1)}, bf16[2,128,128]{2,1,0:T(8,128)(2,1)S(1)}, u32[]{:S(2)}, u32[]{:S(2)}) collective-permute-start(bf16[2,128,128]{2,1,0:T(8,128)(2,1)S(1)} %collective-permute-done.1.refs_1_), channel_id=1, source_target_pairs={{0,3},{1,2},{2,1},{3,0},{4,7},{5,6},{6,5},{7,4},{8,11},{9,10},{10,... | collective-permute-start | bytes 196616 | tf_op jit(solution)/shard_map/ppermute | solution.py:22
  11.0 4.5 %collective-permute-start.6 = (bf16[2,128,128]{2,1,0:T(8,128)(2,1)S(1)}, bf16[2,128,128]{2,1,0:T(8,128)(2,1)S(1)}, u32[]{:S(2)}, u32[]{:S(2)}) collective-permute-start(bf16[2,128,128]{2,1,0:T(8,128)(2,1)S(1)} %collective-permute-done.1.refs_1_), channel_id=1, source_target_pairs={{0,2},{1,3},{2,0},{3,1},{4,6},{5,7},{6,4},{7,5},{8,10},{9,11},{10,... | collective-permute-start | bytes 196616 | tf_op jit(solution)/shard_map/ppermute | solution.py:22
  12.5 4.3 %collective-permute-start.5 = (bf16[2,128,128]{2,1,0:T(8,128)(2,1)S(1)}, bf16[2,128,128]{2,1,0:T(8,128)(2,1)S(1)}, u32[]{:S(2)}, u32[]{:S(2)}) collective-permute-start(bf16[2,128,128]{2,1,0:T(8,128)(2,1)S(1)} %collective-permute-done.1.refs_1_), channel_id=1, source_target_pairs={{0,1},{1,0},{2,3},{3,2},{4,5},{5,4},{6,7},{7,6},{8,9},{9,8},{10,11... | collective-permute-start | bytes 196616 | tf_op jit(solution)/shard_map/ppermute | solution.py:22
  19.0 27.5 %copy-start.1 = (s32[1,2]{1,0:T(1,128)S(1)}, s32[1,2]{1,0:T(1,128)}, u32[]{:S(2)}) copy-start(s32[1,2]{1,0:T(1,128)} %ranks.1) | copy-start | bytes 28
  19.0 5.5 %collective-permute-start.8 = (bf16[2,128,128]{2,1,0:T(8,128)(2,1)S(1)}, bf16[2,128,128]{2,1,0:T(8,128)(2,1)S(1)}, u32[]{:S(2)}, u32[]{:S(2)}) collective-permute-start(bf16[2,128,128]{2,1,0:T(8,128)(2,1)S(1)} %first_image.1.refs_8_), channel_id=1, source_target_pairs={{0,4},{1,5},{2,6},{3,7},{4,0},{5,1},{6,2},{7,3},{8,12},{9,13},{10,... | collective-permute-start | bytes 196616 | tf_op jit(solution)/shard_map/ppermute | solution.py:22
  21.0 6.5 %collective-permute-start.11 = (bf16[2,128,128]{2,1,0:T(8,128)(2,1)S(1)}, bf16[2,128,128]{2,1,0:T(8,128)(2,1)S(1)}, u32[]{:S(2)}, u32[]{:S(2)}) collective-permute-start(bf16[2,128,128]{2,1,0:T(8,128)(2,1)S(1)} %first_image.1.refs_8_), channel_id=1, source_target_pairs={{0,3},{1,2},{2,1},{3,0},{4,7},{5,6},{6,5},{7,4},{8,11},{9,10},{10,... | collective-permute-start | bytes 196616 | tf_op jit(solution)/shard_map/ppermute | solution.py:22
  23.0 5.1 %collective-permute-start.10 = (bf16[2,128,128]{2,1,0:T(8,128)(2,1)S(1)}, bf16[2,128,128]{2,1,0:T(8,128)(2,1)S(1)}, u32[]{:S(2)}, u32[]{:S(2)}) collective-permute-start(bf16[2,128,128]{2,1,0:T(8,128)(2,1)S(1)} %first_image.1.refs_8_), channel_id=1, source_target_pairs={{0,2},{1,3},{2,0},{3,1},{4,6},{5,7},{6,4},{7,5},{8,10},{9,11},{10,... | collective-permute-start | bytes 196616 | tf_op jit(solution)/shard_map/ppermute | solution.py:22
  23.7 5.3 %collective-permute-start.9 = (bf16[2,128,128]{2,1,0:T(8,128)(2,1)S(1)}, bf16[2,128,128]{2,1,0:T(8,128)(2,1)S(1)}, u32[]{:S(2)}, u32[]{:S(2)}) collective-permute-start(bf16[2,128,128]{2,1,0:T(8,128)(2,1)S(1)} %first_image.1.refs_8_), channel_id=1, source_target_pairs={{0,1},{1,0},{2,3},{3,2},{4,5},{5,4},{6,7},{7,6},{8,9},{9,8},{10,11... | collective-permute-start | bytes 196616 | tf_op jit(solution)/shard_map/ppermute | solution.py:22
  24.6 5.2 %collective-permute-start.14 = (bf16[2,128,128]{2,1,0:T(8,128)(2,1)S(1)}, bf16[2,128,128]{2,1,0:T(8,128)(2,1)S(1)}, u32[]{:S(2)}, u32[]{:S(2)}) collective-permute-start(bf16[2,128,128]{2,1,0:T(8,128)(2,1)S(1)} %collective-permute-done.8.refs_9_), channel_id=1, source_target_pairs={{0,3},{1,2},{2,1},{3,0},{4,7},{5,6},{6,5},{7,4},{8,11},{9,10},{10,... | collective-permute-start | bytes 196616 | tf_op jit(solution)/shard_map/ppermute | solution.py:22
  26.5 4.3 %collective-permute-start.13 = (bf16[2,128,128]{2,1,0:T(8,128)(2,1)S(1)}, bf16[2,128,128]{2,1,0:T(8,128)(2,1)S(1)}, u32[]{:S(2)}, u32[]{:S(2)}) collective-permute-start(bf16[2,128,128]{2,1,0:T(8,128)(2,1)S(1)} %collective-permute-done.8.refs_9_), channel_id=1, source_target_pairs={{0,2},{1,3},{2,0},{3,1},{4,6},{5,7},{6,4},{7,5},{8,10},{9,11},{10,... | collective-permute-start | bytes 196616 | tf_op jit(solution)/shard_map/ppermute | solution.py:22
  27.6 4.3 %collective-permute-start.12 = (bf16[2,128,128]{2,1,0:T(8,128)(2,1)S(1)}, bf16[2,128,128]{2,1,0:T(8,128)(2,1)S(1)}, u32[]{:S(2)}, u32[]{:S(2)}) collective-permute-start(bf16[2,128,128]{2,1,0:T(8,128)(2,1)S(1)} %collective-permute-done.8.refs_9_), channel_id=1, source_target_pairs={{0,1},{1,0},{2,3},{3,2},{4,5},{5,4},{6,7},{7,6},{8,9},{9,8},{10,11... | collective-permute-start | bytes 196616 | tf_op jit(solution)/shard_map/ppermute | solution.py:22
  34.4 5.6 %collective-permute-start.15 = (bf16[2,128,128]{2,1,0:T(8,128)(2,1)S(1)}, bf16[2,128,128]{2,1,0:T(8,128)(2,1)S(1)}, u32[]{:S(2)}, u32[]{:S(2)}) collective-permute-start(bf16[2,128,128]{2,1,0:T(8,128)(2,1)S(1)} %get-tuple-element.18.refs_1_), channel_id=1, source_target_pairs={{0,4},{1,5},{2,6},{3,7},{4,0},{5,1},{6,2},{7,3},{8,12},{9,13},{10,... | collective-permute-start | bytes 196616 | tf_op jit(solution)/shard_map/ppermute | solution.py:22
  36.5 5.8 %collective-permute-start.18 = (bf16[2,128,128]{2,1,0:T(8,128)(2,1)S(1)}, bf16[2,128,128]{2,1,0:T(8,128)(2,1)S(1)}, u32[]{:S(2)}, u32[]{:S(2)}) collective-permute-start(bf16[2,128,128]{2,1,0:T(8,128)(2,1)S(1)} %get-tuple-element.18.refs_1_), channel_id=1, source_target_pairs={{0,3},{1,2},{2,1},{3,0},{4,7},{5,6},{6,5},{7,4},{8,11},{9,10},{10,... | collective-permute-start | bytes 196616 | tf_op jit(solution)/shard_map/ppermute | solution.py:22
  38.4 5.0 %collective-permute-start.17 = (bf16[2,128,128]{2,1,0:T(8,128)(2,1)S(1)}, bf16[2,128,128]{2,1,0:T(8,128)(2,1)S(1)}, u32[]{:S(2)}, u32[]{:S(2)}) collective-permute-start(bf16[2,128,128]{2,1,0:T(8,128)(2,1)S(1)} %get-tuple-element.18.refs_1_), channel_id=1, source_target_pairs={{0,2},{1,3},{2,0},{3,1},{4,6},{5,7},{6,4},{7,5},{8,10},{9,11},{10,... | collective-permute-start | bytes 196616 | tf_op jit(solution)/shard_map/ppermute | solution.py:22
  38.7 4.7 %collective-permute-start.16 = (bf16[2,128,128]{2,1,0:T(8,128)(2,1)S(1)}, bf16[2,128,128]{2,1,0:T(8,128)(2,1)S(1)}, u32[]{:S(2)}, u32[]{:S(2)}) collective-permute-start(bf16[2,128,128]{2,1,0:T(8,128)(2,1)S(1)} %get-tuple-element.18.refs_1_), channel_id=1, source_target_pairs={{0,1},{1,0},{2,3},{3,2},{4,5},{5,4},{6,7},{7,6},{8,9},{9,8},{10,11... | collective-permute-start | bytes 196616 | tf_op jit(solution)/shard_map/ppermute | solution.py:22
  40.0 5.2 %collective-permute-start.21 = (bf16[2,128,128]{2,1,0:T(8,128)(2,1)S(1)}, bf16[2,128,128]{2,1,0:T(8,128)(2,1)S(1)}, u32[]{:S(2)}, u32[]{:S(2)}) collective-permute-start(bf16[2,128,128]{2,1,0:T(8,128)(2,1)S(1)} %collective-permute-done.15.refs_2_), channel_id=1, source_target_pairs={{0,3},{1,2},{2,1},{3,0},{4,7},{5,6},{6,5},{7,4},{8,11},{9,10},{10,... | collective-permute-start | bytes 196616 | tf_op jit(solution)/shard_map/ppermute | solution.py:22
  42.2 4.3 %collective-permute-start.20 = (bf16[2,128,128]{2,1,0:T(8,128)(2,1)S(1)}, bf16[2,128,128]{2,1,0:T(8,128)(2,1)S(1)}, u32[]{:S(2)}, u32[]{:S(2)}) collective-permute-start(bf16[2,128,128]{2,1,0:T(8,128)(2,1)S(1)} %collective-permute-done.15.refs_2_), channel_id=1, source_target_pairs={{0,2},{1,3},{2,0},{3,1},{4,6},{5,7},{6,4},{7,5},{8,10},{9,11},{10,... | collective-permute-start | bytes 196616 | tf_op jit(solution)/shard_map/ppermute | solution.py:22
  42.2 4.3 %collective-permute-start.19 = (bf16[2,128,128]{2,1,0:T(8,128)(2,1)S(1)}, bf16[2,128,128]{2,1,0:T(8,128)(2,1)S(1)}, u32[]{:S(2)}, u32[]{:S(2)}) collective-permute-start(bf16[2,128,128]{2,1,0:T(8,128)(2,1)S(1)} %collective-permute-done.15.refs_2_), channel_id=1, source_target_pairs={{0,1},{1,0},{2,3},{3,2},{4,5},{5,4},{6,7},{7,6},{8,9},{9,8},{10,11... | collective-permute-start | bytes 196616 | tf_op jit(solution)/shard_map/ppermute | solution.py:22
  49.2 3.4 %collective-permute-start.22 = (f32[1,8,128]{2,1,0:T(8,128)S(1)}, f32[1,8,128]{2,1,0:T(8,128)S(1)}, u32[]{:S(2)}, u32[]{:S(2)}) collective-permute-start(f32[1,8,128]{2,1,0:T(8,128)S(1)} %get-tuple-element.23), channel_id=1, source_target_pairs={{0,8},{1,9},{2,10},{3,11},{4,12},{5,13},{6,14},{7,15},{8,0},{9,1},... | collective-permute-start | bytes 12296 | tf_op jit(solution)/shard_map/ppermute | solution.py:36
  49.3 5.5 %collective-permute-start.25 = (f32[1,8,128]{2,1,0:T(8,128)S(1)}, f32[1,8,128]{2,1,0:T(8,128)S(1)}, u32[]{:S(2)}, u32[]{:S(2)}) collective-permute-start(f32[1,8,128]{2,1,0:T(8,128)S(1)} %get-tuple-element.23), channel_id=1, source_target_pairs={{0,11},{1,10},{2,9},{3,8},{4,15},{5,14},{6,13},{7,12},{8,3},{9,2},... | collective-permute-start | bytes 12296 | tf_op jit(solution)/shard_map/ppermute | solution.py:36
  51.2 3.6 %collective-permute-start.24 = (f32[1,8,128]{2,1,0:T(8,128)S(1)}, f32[1,8,128]{2,1,0:T(8,128)S(1)}, u32[]{:S(2)}, u32[]{:S(2)}) collective-permute-start(f32[1,8,128]{2,1,0:T(8,128)S(1)} %get-tuple-element.23), channel_id=1, source_target_pairs={{0,10},{1,11},{2,8},{3,9},{4,14},{5,15},{6,12},{7,13},{8,2},{9,3},... | collective-permute-start | bytes 12296 | tf_op jit(solution)/shard_map/ppermute | solution.py:36
  51.8 3.0 %collective-permute-start.23 = (f32[1,8,128]{2,1,0:T(8,128)S(1)}, f32[1,8,128]{2,1,0:T(8,128)S(1)}, u32[]{:S(2)}, u32[]{:S(2)}) collective-permute-start(f32[1,8,128]{2,1,0:T(8,128)S(1)} %get-tuple-element.23), channel_id=1, source_target_pairs={{0,9},{1,8},{2,11},{3,10},{4,13},{5,12},{6,15},{7,14},{8,1},{9,0},... | collective-permute-start | bytes 12296 | tf_op jit(solution)/shard_map/ppermute | solution.py:36
  54.8 4.1 %collective-permute-start.27 = (f32[4,8,128]{2,1,0:T(8,128)S(1)}, f32[4,8,128]{2,1,0:T(8,128)S(1)}, u32[]{:S(2)}, u32[]{:S(2)}) collective-permute-start(f32[4,8,128]{2,1,0:T(8,128)S(1)} %constant_dynamic-update-slice_fusion), channel_id=1, source_target_pairs={{0,12},{1,13},{2,14},{3,15},{4,8},{5,9},{6,10},{7,11},{8,4},{9,5},... | collective-permute-start | bytes 49160 | tf_op jit(solution)/shard_map/ppermute | solution.py:36
  57.3 1.6 %collective-permute-start.26 = (f32[4,8,128]{2,1,0:T(8,128)S(1)}, f32[4,8,128]{2,1,0:T(8,128)S(1)}, u32[]{:S(2)}, u32[]{:S(2)}) collective-permute-start(f32[4,8,128]{2,1,0:T(8,128)S(1)} %constant_dynamic-update-slice_fusion), channel_id=1, source_target_pairs={{0,8},{1,9},{2,10},{3,11},{4,12},{5,13},{6,14},{7,15},{8,0},{9,1},... | collective-permute-start | bytes 49160 | tf_op jit(solution)/shard_map/ppermute | solution.py:36

commit v6 on v5

--- a/solution.py
+++ b/solution.py
@@ -12,9 +12,8 @@
 EPSILON = 1e-06
 SMEM = pl.BlockSpec(memory_space=pltpu.SMEM)
 VMEM = pl.BlockSpec(memory_space=pltpu.VMEM)
-ANY = pl.BlockSpec(memory_space=pl.ANY)
 HBM = pl.BlockSpec(memory_space=pltpu.HBM)
-APART = (0, 4, 1, 2, 3, 5, 6, 7)
+APART = (0, 4, 3, 2, 1, 5, 6, 7)
 
 
 def hop(block, distance):
@@ -26,7 +25,7 @@
     if lax.axis_size("sec") != len(APART):
         return [lax.all_gather(block, "sec", axis=0, tiled=True)]
     relayed = hop(block, 4)
-    near = [hop(block, distance) for distance in (1, 2, 3)]
+    near = [hop(block, distance) for distance in (3, 2, 1)]
     return [block, relayed] + near + [hop(relayed, distance) for distance in (1, 2, 3)]
 
 
@@ -59,7 +58,7 @@
 
 
 def prepare_kernel(devices, *refs):
-    arguments, left, (codes, floats, near), (sources, channels, couplings, semaphores) = refs[:3], refs[3], refs[4:7], refs[7:]
+    arguments, left, (codes, factors, near), (sources, channels, couplings, semaphores) = refs[:3], refs[3], refs[4:7], refs[7:]
     copies = fetch((*arguments, left), (sources, channels, couplings, near), semaphores)
     blocks, pairs = sources.shape
     width = near.shape[1]
@@ -82,7 +81,7 @@
         code = column(place) * float(1 << code_bits(width)) + 2.0 * mine + same
         chosen = rank == across.astype(jnp.float32)
         codes[t : t + 1, :] = jnp.sum(jnp.where(chosen, code, 0.0), axis=0, keepdims=True).astype(jnp.int32)
-        floats[t : t + 1, :] = jnp.sum(jnp.where(chosen, column(couplings[t : t + 1, :]), 0.0), axis=0, keepdims=True)
+        factors[t : t + 1, :] = jnp.sum(jnp.where(chosen, column(couplings[t : t + 1, :]), 0.0), axis=0, keepdims=True)
     copies[3].wait()
 
 
@@ -96,32 +95,24 @@
     return copies
 
 
-def mixing(t, codes, floats, state, mixed):
-    pairs = floats.shape[1]
+def mixing(t, codes, factors, state, mixed):
+    pairs = factors.shape[1]
     width, size = mixed[t].shape[0], mixed[t].shape[1]
     bits = code_bits(width)
-    for first in range(0, size, size // 2):
-        rows = slice(first, first + size // 2)
-        total = jnp.zeros((size // 2, size), jnp.float32)
-        for k in range(pairs):
-            code = codes[t, k]
-            term = floats[t, k] * state[lax.shift_right_logical(code, bits), rows]
-            total = term + jnp.where((code & 1) == 1, total, 0.0)
-            channel = lax.shift_right_logical(code, 1) & ((1 << (bits - 1)) - 1)
-            mixed[t][channel, rows] = total.astype(jnp.bfloat16)
-            yield
-
-
-def apply_operator(copies, codes, floats, state, left, right, mixed, image):
+    total = jnp.zeros((size, size), jnp.float32)
+    for k in range(pairs):
+        code = codes[t, k]
+        term = factors[t, k] * state[lax.shift_right_logical(code, bits)]
+        total = term + jnp.where((code & 1) == 1, total, 0.0)
+        mixed[t][lax.shift_right_logical(code, 1) & ((1 << (bits - 1)) - 1)] = total.astype(jnp.bfloat16)
+
+
+def apply_operator(codes, factors, state, left, right, mixed, image):
     blocks, width = left.shape[0], left.shape[1]
     for t in range(blocks):
         mixed[t][...] = jnp.zeros_like(mixed[t])
-    for copy in copies:
-        copy.wait()
-    steps = [mixing(t, codes, floats, state, mixed) for t in range(blocks)]
-    for _ in steps[0]:
-        pass
-    share = -(-4 * floats.shape[1] // width)
+    for t in range(blocks):
+        mixing(t, codes, factors, state, mixed)
     for t in range(blocks):
         result = jnp.zeros(image.shape[1:], jnp.float32)
         for w in range(0, width, 2):
@@ -135,13 +126,7 @@
                 (((1,), (1,)), ((), ())),
                 preferred_element_type=jnp.float32,
             )
-            if t + 1 < blocks:
-                for _ in range(share):
-                    next(steps[t + 1], None)
         image[t] = result.astype(jnp.bfloat16)
-        if t + 1 < blocks:
-            for _ in steps[t + 1]:
-                pass
 
 
 def spread(pieces, target):
@@ -152,11 +137,10 @@
         at += size
 
 
-def first_kernel(count, codes, floats, left, right, *refs):
-    pieces, (image, state, codes_here, floats_here, semaphores, *mixed) = refs[:count], refs[count:]
-    copies = fetch((codes, floats), (codes_here, floats_here), semaphores)
+def first_kernel(count, codes, factors, left, right, *refs):
+    pieces, (image, state, *mixed) = refs[:count], refs[count:]
     spread(pieces, state)
-    apply_operator(copies, codes_here, floats_here, state, left, right, mixed, image)
+    apply_operator(codes[...], factors[...], state, left, right, mixed, image)
 
 
 def rayleigh_update(before, images, after):
@@ -182,20 +166,18 @@
     return energy
 
 
-def middle_kernel(states, count, codes, floats, left, right, *refs):
+def middle_kernel(states, count, codes, factors, left, right, *refs):
     before, images = refs[:states], refs[states : states + count]
-    energy, state, image, codes_here, floats_here, semaphores, *mixed = refs[states + count :]
-    copies = fetch((codes, floats), (codes_here, floats_here), semaphores)
+    energy, state, image, *mixed = refs[states + count :]
     energy[...] = jnp.broadcast_to(rayleigh_update(before, images, state), energy.shape)
-    apply_operator(copies, codes_here, floats_here, state, left, right, mixed, image)
-
-
-def last_kernel(states, count, codes, floats, ranks, left, right, *refs):
+    apply_operator(codes[...], factors[...], state, left, right, mixed, image)
+
+
+def last_kernel(states, count, codes, factors, ranks, left, right, *refs):
     before, images = refs[:states], refs[states : states + count]
-    energy, own, image, sums, state, codes_here, floats_here, ranks_here, semaphores, *mixed = refs[states + count :]
-    copies = fetch((codes, floats, ranks), (codes_here, floats_here, ranks_here), semaphores)
+    energy, own, image, sums, state, *mixed = refs[states + count :]
     energy[...] = jnp.broadcast_to(rayleigh_update(before, images, state), energy.shape)
-    apply_operator(copies, codes_here, floats_here, state, left, right, mixed, image)
+    apply_operator(codes[...], factors[...], state, left, right, mixed, image)
     blocks, size = image.shape[0], image.shape[1]
     intersection = jnp.zeros((size, size), jnp.float32)
     squares = jnp.zeros((size, size), jnp.float32)
@@ -211,7 +193,7 @@
     dc = jnp.zeros((size, size), jnp.float32)
     cc = jnp.zeros((size, size), jnp.float32)
     for t in range(blocks):
-        keep = column < ranks_here[0, t]
+        keep = column < ranks[0:1, t : t + 1]
         value = jnp.where(keep, state[t], 0.0)
         picture = jnp.where(keep, image[t].astype(jnp.float32), 0.0)
         own[t] = value
@@ -261,10 +243,10 @@
     pairs = sources.shape[2]
     params = pltpu.CompilerParams(vmem_limit_bytes=32 * 2**20)
     ints = jax.ShapeDtypeStruct((blocks, pairs), jnp.int32)
-    floats = jax.ShapeDtypeStruct((blocks, pairs), jnp.float32)
-    codes, couplings, left = pl.pallas_call(
+    factors = jax.ShapeDtypeStruct((blocks, pairs), jnp.float32)
+    codes, factors, left = pl.pallas_call(
         functools.partial(prepare_kernel, devices),
-        out_shape=(ints, floats, jax.ShapeDtypeStruct(left.shape, left.dtype)),
+        out_shape=(ints, factors, jax.ShapeDtypeStruct(left.shape, left.dtype)),
         in_specs=[HBM] * 4,
         out_specs=(VMEM, VMEM, VMEM),
         scratch_shapes=[
@@ -280,31 +262,30 @@
     own_type = jax.ShapeDtypeStruct((blocks, size, size), jnp.bfloat16)
     number = jax.ShapeDtypeStruct((1, 128), jnp.float32)
     whole = (sectors, size, size)
-    tables = [pltpu.SMEM(ints.shape, jnp.int32), pltpu.SMEM(floats.shape, jnp.float32)]
     mixed = [pltpu.VMEM((width, size, size), jnp.bfloat16)] * blocks
 
     states = gather(start)
     image = pl.pallas_call(
         functools.partial(first_kernel, len(states)),
         out_shape=own_type,
-        in_specs=[ANY, ANY] + [VMEM] * (2 + len(states)),
+        in_specs=[VMEM] * (4 + len(states)),
         out_specs=VMEM,
-        scratch_shapes=[pltpu.VMEM(whole, jnp.float32), *tables, pltpu.SemaphoreType.DMA((2,)), *mixed],
+        scratch_shapes=[pltpu.VMEM(whole, jnp.float32), *mixed],
         compiler_params=params,
         name="first_image",
-    )(codes, couplings, left, right, *states)
+    )(codes, factors, left, right, *states)
     energies = []
     for _ in range(1, ITERS - 1):
         images = gather(image)
         energy, state, image = pl.pallas_call(
             functools.partial(middle_kernel, len(states), len(images)),
             out_shape=(number, jax.ShapeDtypeStruct(whole, jnp.float32), own_type),
-            in_specs=[ANY, ANY] + [VMEM] * (2 + len(states) + len(images)),
+            in_specs=[VMEM] * (4 + len(states) + len(images)),
             out_specs=(VMEM, VMEM, VMEM),
-            scratch_shapes=[*tables, pltpu.SemaphoreType.DMA((2,)), *mixed],
+            scratch_shapes=mixed,
             compiler_params=params,
             name="middle_image",
-        )(codes, couplings, left, right, *states, *images)
+        )(codes, factors, left, right, *states, *images)
         states = [state]
         energies.append(energy)
     images = gather(image)
@@ -316,18 +297,15 @@
             own_type,
             jax.ShapeDtypeStruct((1, 8, 128), jnp.float32),
         ),
-        in_specs=[ANY, ANY, ANY] + [VMEM] * (2 + len(states) + len(images)),
+        in_specs=[VMEM] * (5 + len(states) + len(images)),
         out_specs=(VMEM, VMEM, VMEM, VMEM),
         scratch_shapes=[
             pltpu.VMEM(whole, jnp.float32),
-            *tables,
-            pltpu.SMEM((1, blocks), jnp.int32),
-            pltpu.SemaphoreType.DMA((3,)),
             *mixed,
         ],
         compiler_params=params,
         name="last_image",
-    )(codes, couplings, kept_rank, left, right, *states, *images)
+    )(codes, factors, kept_rank, left, right, *states, *images)
     energies.append(energy)
     gathered = gather_small(sums)
     energies, kept = pl.pallas_call(

time: 59.9 us -> 58.7 us (0.980)
  starting transfers between devices: 36.5 us -> 35.5 us
    ppermute x21, starting transfers between devices: 30 us -> 29.3 us  [hop(): return lax.ppermute(block, 'sec', [(a, a ^ distance) for a in range(count)])]
    ppermute x21, waiting for transfers between devices: 8.91 us -> 9.51 us  [hop(): return lax.ppermute(block, 'sec', [(a, a ^ distance) for a in range(count)])]
  transfers between devices with their start and end apart: 28 -> 28, of which waited for: 12 -> 12; matrix products, arithmetic and copies ran while one was open for 0% -> 0% of each run, Pallas kernels for 2% -> 3%
where the time goes in v6:
time: 58.7 us; the launch traced here: 58.6 us
  starting transfers between devices  35.5 us (60%)
  waiting for transfers between devices  13.2 us (22%)
  Pallas kernels  9.15 us (16%)
  between operations  0.73 us (1%)
    ppermute x21, starting transfers between devices, hop(): return lax.ppermute(block, 'sec', [(a, a ^ distance) for a in range(count)])  29.3 us
    ppermute x21, waiting for transfers between devices, hop(): return lax.ppermute(block, 'sec', [(a, a ^ distance) for a in range(count)])  9.51 us
    ppermute x6, starting transfers between devices, cross(): return lax.ppermute(block, ('seg', 'sec'), route)  5.65 us
    ppermute x6, waiting for transfers between devices, cross(): return lax.ppermute(block, ('seg', 'sec'), route)  3.71 us
    pallas_call x1, Pallas kernels, local(): pl.pallas_call(functools.partial(last_kernel, len(states), len(images)),...  2.62 us
    pallas_call x1, Pallas kernels, local(): pl.pallas_call(functools.partial(middle_kernel, len(states), len(images))...  2.36 us
    pallas_call x1, Pallas kernels, local(): pl.pallas_call(functools.partial(first_kernel, len(states)), out_shape=ow...  1.99 us
    pallas_call x1, Pallas kernels, local(): pl.pallas_call(functools.partial(prepare_kernel, devices), out_shape=(int...  1.49 us
  transfers between devices with their start and end apart: 28, of which 12 were waited for; matrix products, arithmetic and copies ran while one was open for 0% of the time, Pallas kernels for 3%

profile of v6, /device:TPU:0, one launch (start us, length us, event | category | flops | bytes accessed | tf_op | source)
XLA Modules:
  0.0 58.6 jit_solution(15241366317555329549)
XLA Ops:
  0.6 0.5 collective-permute-start
  1.2 3.7 %collective-permute-start.1 = (bf16[2,128,128]{2,1,0:T(8,128)(2,1)}, bf16[2,128,128]{2,1,0:T(8,128)(2,1)S(1)}, u32[]{:S(2)}, u32[]{:S(2)}) collective-permute-start(bf16[2,128,128]{2,1,0:T(8,128)(2,1)} %bitcast.7), channel_id=1, source_target_pairs={{0,4},{1,5},{2,6},{3,7},{4,0},{5,1},{6,2},{7,3},{8,12},{9,13},{10,... | collective-permute-start | bytes 196616 | tf_op jit(solution)/shard_map/ppermute | solution.py:21
  4.8 1.5 %collective-permute-start.4 = (bf16[2,128,128]{2,1,0:T(8,128)(2,1)}, bf16[2,128,128]{2,1,0:T(8,128)(2,1)S(1)}, u32[]{:S(2)}, u32[]{:S(2)}) collective-permute-start(bf16[2,128,128]{2,1,0:T(8,128)(2,1)} %bitcast.8), channel_id=1, source_target_pairs={{0,1},{1,0},{2,3},{3,2},{4,5},{5,4},{6,7},{7,6},{8,9},{9,8},{10,11... | collective-permute-start | bytes 196616 | tf_op jit(solution)/shard_map/ppermute | solution.py:21
  6.3 1.6 %collective-permute-start.3 = (bf16[2,128,128]{2,1,0:T(8,128)(2,1)}, bf16[2,128,128]{2,1,0:T(8,128)(2,1)S(1)}, u32[]{:S(2)}, u32[]{:S(2)}) collective-permute-start(bf16[2,128,128]{2,1,0:T(8,128)(2,1)} %bitcast.9), channel_id=1, source_target_pairs={{0,2},{1,3},{2,0},{3,1},{4,6},{5,7},{6,4},{7,5},{8,10},{9,11},{10,... | collective-permute-start | bytes 196616 | tf_op jit(solution)/shard_map/ppermute | solution.py:21
  7.9 0.4 collective-permute-start.2
  8.3 0.8 %collective-permute-done.1.refs_1_ = bf16[2,128,128]{2,1,0:T(8,128)(2,1)S(1)} collective-permute-done((bf16[2,128,128]{2,1,0:T(8,128)(2,1)}, bf16[2,128,128]{2,1,0:T(8,128)(2,1)S(1)}, u32[]{:S(2)}, u32[]{:S(2)}) %collective-permute-start.1) | collective-permute-done | bytes 65568 | tf_op jit(solution)/shard_map/ppermute | solution.py:21
  9.1 1.8 %collective-permute-start.7 = (bf16[2,128,128]{2,1,0:T(8,128)(2,1)S(1)}, bf16[2,128,128]{2,1,0:T(8,128)(2,1)S(1)}, u32[]{:S(2)}, u32[]{:S(2)}) collective-permute-start(bf16[2,128,128]{2,1,0:T(8,128)(2,1)S(1)} %collective-permute-done.1.refs_1_), channel_id=1, source_target_pairs={{0,3},{1,2},{2,1},{3,0},{4,7},{5,6},{6,5},{7,4},{8,11},{9,10},{10,... | collective-permute-start | bytes 196616 | tf_op jit(solution)/shard_map/ppermute | solution.py:21
  11.0 0.0 collective-permute-done.4.refs_4_
  11.0 1.1 %collective-permute-start.6 = (bf16[2,128,128]{2,1,0:T(8,128)(2,1)S(1)}, bf16[2,128,128]{2,1,0:T(8,128)(2,1)S(1)}, u32[]{:S(2)}, u32[]{:S(2)}) collective-permute-start(bf16[2,128,128]{2,1,0:T(8,128)(2,1)S(1)} %collective-permute-done.1.refs_1_), channel_id=1, source_target_pairs={{0,2},{1,3},{2,0},{3,1},{4,6},{5,7},{6,4},{7,5},{8,10},{9,11},{10,... | collective-permute-start | bytes 196616 | tf_op jit(solution)/shard_map/ppermute | solution.py:21
  12.1 0.0 collective-permute-done.3.refs_3_
  12.1 0.5 collective-permute-start.5
  12.6 1.5 %prepare.1 = (s32[2,32]{1,0:T(2,128)S(1)}, f32[2,32]{1,0:T(2,128)S(1)}, bf16[2,24,128,128]{3,2,1,0:T(8,128)(2,1)S(1)}) custom-call(s32[2,32]{1,0:T(2,128)} %bitcast.14, s32[2,32]{1,0:T(2,128)} %bitcast.15, f32[2,32]{1,0:T(2,128)} %bitcast.16, bf16[2,24,128,128]{3,2,1,0:T(8,128)(2,1)} %bitcast.13), custom_call_target="tpu_custom_call" | custom-call | tf_op jit(solution)/shard_map/prepare/pallas_call | solution.py:247
  14.1 0.7 %collective-permute-done.7.refs_7_ = bf16[2,128,128]{2,1,0:T(8,128)(2,1)S(1)} collective-permute-done((bf16[2,128,128]{2,1,0:T(8,128)(2,1)S(1)}, bf16[2,128,128]{2,1,0:T(8,128)(2,1)S(1)}, u32[]{:S(2)}, u32[]{:S(2)}) %collective-permute-start.7) | collective-permute-done | bytes 65568 | tf_op jit(solution)/shard_map/ppermute | solution.py:21
  14.8 0.6 %collective-permute-done.6.refs_6_ = bf16[2,128,128]{2,1,0:T(8,128)(2,1)S(1)} collective-permute-done((bf16[2,128,128]{2,1,0:T(8,128)(2,1)S(1)}, bf16[2,128,128]{2,1,0:T(8,128)(2,1)S(1)}, u32[]{:S(2)}, u32[]{:S(2)}) %collective-permute-start.6) | collective-permute-done | bytes 65568 | tf_op jit(solution)/shard_map/ppermute | solution.py:21
  15.5 0.9 %collective-permute-done.5.refs_5_ = bf16[2,128,128]{2,1,0:T(8,128)(2,1)S(1)} collective-permute-done((bf16[2,128,128]{2,1,0:T(8,128)(2,1)S(1)}, bf16[2,128,128]{2,1,0:T(8,128)(2,1)S(1)}, u32[]{:S(2)}, u32[]{:S(2)}) %collective-permute-start.5) | collective-permute-done | bytes 65568 | tf_op jit(solution)/shard_map/ppermute | solution.py:21
  16.4 2.0 %first_image.1.refs_8_ = bf16[2,128,128]{2,1,0:T(8,128)(2,1)S(1)} custom-call(s32[2,32]{1,0:T(2,128)S(1)} %get-tuple-element.14.codes, f32[2,32]{1,0:T(2,128)S(1)} %get-tuple-element.15.factors, bf16[2,24,128,128]{3,2,1,0:T(8,128)(2,1)S(1)} %get-tuple-element.16.left, bf16[2,24,128,128]{3,2,1,0:T(8,128)(2,1)S(1)} %collective-permute-done.right, ...), custom_call_target="tpu_custom_call" | custom-call | tf_op jit(solution)/shard_map/first_image/pallas_call | solution.py:268
  18.4 0.0 copy-start.1
  18.4 2.4 %collective-permute-start.8 = (bf16[2,128,128]{2,1,0:T(8,128)(2,1)S(1)}, bf16[2,128,128]{2,1,0:T(8,128)(2,1)S(1)}, u32[]{:S(2)}, u32[]{:S(2)}) collective-permute-start(bf16[2,128,128]{2,1,0:T(8,128)(2,1)S(1)} %first_image.1.refs_8_), channel_id=1, source_target_pairs={{0,4},{1,5},{2,6},{3,7},{4,0},{5,1},{6,2},{7,3},{8,12},{9,13},{10,... | collective-permute-start | bytes 196616 | tf_op jit(solution)/shard_map/ppermute | solution.py:21
  20.7 0.5 collective-permute-start.11
  21.2 2.0 %collective-permute-start.10 = (bf16[2,128,128]{2,1,0:T(8,128)(2,1)S(1)}, bf16[2,128,128]{2,1,0:T(8,128)(2,1)S(1)}, u32[]{:S(2)}, u32[]{:S(2)}) collective-permute-start(bf16[2,128,128]{2,1,0:T(8,128)(2,1)S(1)} %first_image.1.refs_8_), channel_id=1, source_target_pairs={{0,2},{1,3},{2,0},{3,1},{4,6},{5,7},{6,4},{7,5},{8,10},{9,11},{10,... | collective-permute-start | bytes 196616 | tf_op jit(solution)/shard_map/ppermute | solution.py:21
  23.3 1.0 %collective-permute-start.9 = (bf16[2,128,128]{2,1,0:T(8,128)(2,1)S(1)}, bf16[2,128,128]{2,1,0:T(8,128)(2,1)S(1)}, u32[]{:S(2)}, u32[]{:S(2)}) collective-permute-start(bf16[2,128,128]{2,1,0:T(8,128)(2,1)S(1)} %first_image.1.refs_8_), channel_id=1, source_target_pairs={{0,3},{1,2},{2,1},{3,0},{4,7},{5,6},{6,5},{7,4},{8,11},{9,10},{10,... | collective-permute-start | bytes 196616 | tf_op jit(solution)/shard_map/ppermute | solution.py:21
  24.2 2.0 %collective-permute-start.14 = (bf16[2,128,128]{2,1,0:T(8,128)(2,1)S(1)}, bf16[2,128,128]{2,1,0:T(8,128)(2,1)S(1)}, u32[]{:S(2)}, u32[]{:S(2)}) collective-permute-start(bf16[2,128,128]{2,1,0:T(8,128)(2,1)S(1)} %collective-permute-done.8.refs_9_), channel_id=1, source_target_pairs={{0,3},{1,2},{2,1},{3,0},{4,7},{5,6},{6,5},{7,4},{8,11},{9,10},{10,... | collective-permute-start | bytes 196616 | tf_op jit(solution)/shard_map/ppermute | solution.py:21
  26.2 0.0 collective-permute-start.13
  26.2 1.5 %collective-permute-start.12 = (bf16[2,128,128]{2,1,0:T(8,128)(2,1)S(1)}, bf16[2,128,128]{2,1,0:T(8,128)(2,1)S(1)}, u32[]{:S(2)}, u32[]{:S(2)}) collective-permute-start(bf16[2,128,128]{2,1,0:T(8,128)(2,1)S(1)} %collective-permute-done.8.refs_9_), channel_id=1, source_target_pairs={{0,1},{1,0},{2,3},{3,2},{4,5},{5,4},{6,7},{7,6},{8,9},{9,8},{10,11... | collective-permute-start | bytes 196616 | tf_op jit(solution)/shard_map/ppermute | solution.py:21
  27.7 1.0 %collective-permute-done.9.refs_10_ = bf16[2,128,128]{2,1,0:T(8,128)(2,1)S(1)} collective-permute-done((bf16[2,128,128]{2,1,0:T(8,128)(2,1)S(1)}, bf16[2,128,128]{2,1,0:T(8,128)(2,1)S(1)}, u32[]{:S(2)}, u32[]{:S(2)}) %collective-permute-start.9) | collective-permute-done | bytes 65568 | tf_op jit(solution)/shard_map/ppermute | solution.py:21
  28.7 0.7 %collective-permute-done.14.refs_15_ = bf16[2,128,128]{2,1,0:T(8,128)(2,1)S(1)} collective-permute-done((bf16[2,128,128]{2,1,0:T(8,128)(2,1)S(1)}, bf16[2,128,128]{2,1,0:T(8,128)(2,1)S(1)}, u32[]{:S(2)}, u32[]{:S(2)}) %collective-permute-start.14) | collective-permute-done | bytes 65568 | tf_op jit(solution)/shard_map/ppermute | solution.py:21
  29.4 1.1 %collective-permute-done.13.refs_14_ = bf16[2,128,128]{2,1,0:T(8,128)(2,1)S(1)} collective-permute-done((bf16[2,128,128]{2,1,0:T(8,128)(2,1)S(1)}, bf16[2,128,128]{2,1,0:T(8,128)(2,1)S(1)}, u32[]{:S(2)}, u32[]{:S(2)}) %collective-permute-start.13) | collective-permute-done | bytes 65568 | tf_op jit(solution)/shard_map/ppermute | solution.py:21
  30.5 0.0 collective-permute-done.12.refs_13_
  30.5 2.4 %middle_image.1 = (f32[1,128]{1,0:T(1,128)S(1)}, f32[16,128,128]{2,1,0:T(8,128)S(1)}, bf16[2,128,128]{2,1,0:T(8,128)(2,1)S(1)}) custom-call(s32[2,32]{1,0:T(2,128)S(1)} %get-tuple-element.14.codes, f32[2,32]{1,0:T(2,128)S(1)} %get-tuple-element.15.factors, bf16[2,24,128,128]{3,2,1,0:T(8,128)(2,1)S(1)} %get-tuple-element.16.left, ...), custom_call_target="tpu_custom_call" | custom-call | tf_op jit(solution)/shard_map/middle_image/pallas_call | solution.py:280
  32.8 2.2 %collective-permute-start.15 = (bf16[2,128,128]{2,1,0:T(8,128)(2,1)S(1)}, bf16[2,128,128]{2,1,0:T(8,128)(2,1)S(1)}, u32[]{:S(2)}, u32[]{:S(2)}) collective-permute-start(bf16[2,128,128]{2,1,0:T(8,128)(2,1)S(1)} %get-tuple-element.18.refs_1_), channel_id=1, source_target_pairs={{0,4},{1,5},{2,6},{3,7},{4,0},{5,1},{6,2},{7,3},{8,12},{9,13},{10,... | collective-permute-start | bytes 196616 | tf_op jit(solution)/shard_map/ppermute | solution.py:21
  35.0 1.6 %collective-permute-start.18 = (bf16[2,128,128]{2,1,0:T(8,128)(2,1)S(1)}, bf16[2,128,128]{2,1,0:T(8,128)(2,1)S(1)}, u32[]{:S(2)}, u32[]{:S(2)}) collective-permute-start(bf16[2,128,128]{2,1,0:T(8,128)(2,1)S(1)} %get-tuple-element.18.refs_1_), channel_id=1, source_target_pairs={{0,1},{1,0},{2,3},{3,2},{4,5},{5,4},{6,7},{7,6},{8,9},{9,8},{10,11... | collective-permute-start | bytes 196616 | tf_op jit(solution)/shard_map/ppermute | solution.py:21
  36.6 1.9 %collective-permute-start.17 = (bf16[2,128,128]{2,1,0:T(8,128)(2,1)S(1)}, bf16[2,128,128]{2,1,0:T(8,128)(2,1)S(1)}, u32[]{:S(2)}, u32[]{:S(2)}) collective-permute-start(bf16[2,128,128]{2,1,0:T(8,128)(2,1)S(1)} %get-tuple-element.18.refs_1_), channel_id=1, source_target_pairs={{0,2},{1,3},{2,0},{3,1},{4,6},{5,7},{6,4},{7,5},{8,10},{9,11},{10,... | collective-permute-start | bytes 196616 | tf_op jit(solution)/shard_map/ppermute | solution.py:21
  38.5 3.1 %collective-permute-start.21 = (bf16[2,128,128]{2,1,0:T(8,128)(2,1)S(1)}, bf16[2,128,128]{2,1,0:T(8,128)(2,1)S(1)}, u32[]{:S(2)}, u32[]{:S(2)}) collective-permute-start(bf16[2,128,128]{2,1,0:T(8,128)(2,1)S(1)} %collective-permute-done.15.refs_2_), channel_id=1, source_target_pairs={{0,3},{1,2},{2,1},{3,0},{4,7},{5,6},{6,5},{7,4},{8,11},{9,10},{10,... | collective-permute-start | bytes 196616 | tf_op jit(solution)/shard_map/ppermute | solution.py:21
  41.6 0.6 collective-permute-start.19
  42.2 1.5 %collective-permute-done.16.refs_3_ = bf16[2,128,128]{2,1,0:T(8,128)(2,1)S(1)} collective-permute-done((bf16[2,128,128]{2,1,0:T(8,128)(2,1)S(1)}, bf16[2,128,128]{2,1,0:T(8,128)(2,1)S(1)}, u32[]{:S(2)}, u32[]{:S(2)}) %collective-permute-start.16) | collective-permute-done | bytes 65568 | tf_op jit(solution)/shard_map/ppermute | solution.py:21
  43.7 0.7 %collective-permute-done.21.refs_8_ = bf16[2,128,128]{2,1,0:T(8,128)(2,1)S(1)} collective-permute-done((bf16[2,128,128]{2,1,0:T(8,128)(2,1)S(1)}, bf16[2,128,128]{2,1,0:T(8,128)(2,1)S(1)}, u32[]{:S(2)}, u32[]{:S(2)}) %collective-permute-start.21) | collective-permute-done | bytes 65568 | tf_op jit(solution)/shard_map/ppermute | solution.py:21
  44.4 1.5 %collective-permute-done.20.refs_7_ = bf16[2,128,128]{2,1,0:T(8,128)(2,1)S(1)} collective-permute-done((bf16[2,128,128]{2,1,0:T(8,128)(2,1)S(1)}, bf16[2,128,128]{2,1,0:T(8,128)(2,1)S(1)}, u32[]{:S(2)}, u32[]{:S(2)}) %collective-permute-start.20) | collective-permute-done | bytes 65568 | tf_op jit(solution)/shard_map/ppermute | solution.py:21
  45.9 0.0 collective-permute-done.19.refs_6_
  45.9 2.6 %last_image.1 = (f32[1,128]{1,0:T(1,128)S(1)}, f32[2,128,128]{2,1,0:T(8,128)S(1)}, bf16[2,128,128]{2,1,0:T(8,128)(2,1)S(1)}, f32[1,8,128]{2,1,0:T(8,128)S(1)}) custom-call(s32[2,32]{1,0:T(2,128)S(1)} %get-tuple-element.14.codes, f32[2,32]{1,0:T(2,128)S(1)} %get-tuple-element.15.factors, s32[1,2]{1,0:T(1,128)S(1)} %copy-done.1, ...), custom_call_target="tpu_custom_call" | custom-call | tf_op jit(solution)/shard_map/last_image/pallas_call | solution.py:292
  48.5 0.1 collective-permute-start.22
  48.6 2.0 %collective-permute-start.25 = (f32[1,8,128]{2,1,0:T(8,128)S(1)}, f32[1,8,128]{2,1,0:T(8,128)S(1)}, u32[]{:S(2)}, u32[]{:S(2)}) collective-permute-start(f32[1,8,128]{2,1,0:T(8,128)S(1)} %get-tuple-element.23), channel_id=1, source_target_pairs={{0,11},{1,10},{2,9},{3,8},{4,15},{5,14},{6,13},{7,12},{8,3},{9,2},... | collective-permute-start | bytes 12296 | tf_op jit(solution)/shard_map/ppermute | solution.py:35
  50.6 0.2 collective-permute-start.24
  50.7 1.2 %collective-permute-start.23 = (f32[1,8,128]{2,1,0:T(8,128)S(1)}, f32[1,8,128]{2,1,0:T(8,128)S(1)}, u32[]{:S(2)}, u32[]{:S(2)}) collective-permute-start(f32[1,8,128]{2,1,0:T(8,128)S(1)} %get-tuple-element.23), channel_id=1, source_target_pairs={{0,9},{1,8},{2,11},{3,10},{4,13},{5,12},{6,15},{7,14},{8,1},{9,0},... | collective-permute-start | bytes 12296 | tf_op jit(solution)/shard_map/ppermute | solution.py:35
  51.9 1.8 %collective-permute-done.23 = f32[1,8,128]{2,1,0:T(8,128)S(1)} collective-permute-done((f32[1,8,128]{2,1,0:T(8,128)S(1)}, f32[1,8,128]{2,1,0:T(8,128)S(1)}, u32[]{:S(2)}, u32[]{:S(2)}) %collective-permute-start.23) | collective-permute-done | bytes 4128 | tf_op jit(solution)/shard_map/ppermute | solution.py:35
  53.8 1.9 %collective-permute-start.27 = (f32[4,8,128]{2,1,0:T(8,128)S(1)}, f32[4,8,128]{2,1,0:T(8,128)S(1)}, u32[]{:S(2)}, u32[]{:S(2)}) collective-permute-start(f32[4,8,128]{2,1,0:T(8,128)S(1)} %constant_dynamic-update-slice_fusion), channel_id=1, source_target_pairs={{0,12},{1,13},{2,14},{3,15},{4,8},{5,9},{6,10},{7,11},{8,4},{9,5},... | collective-permute-start | bytes 49160 | tf_op jit(solution)/shard_map/ppermute | solution.py:35
  55.7 0.4 collective-permute-start.26
  56.0 1.9 %collective-permute-done.27.refs_3_ = f32[4,8,128]{2,1,0:T(8,128)S(1)} collective-permute-done((f32[4,8,128]{2,1,0:T(8,128)S(1)}, f32[4,8,128]{2,1,0:T(8,128)S(1)}, u32[]{:S(2)}, u32[]{:S(2)}) %collective-permute-start.27) | collective-permute-done | bytes 16416 | tf_op jit(solution)/shard_map/ppermute | solution.py:35
  57.9 0.7 %finish.1 = (f32[1,3]{1,0:T(1,128)}, bf16[2,128,128]{2,1,0:T(8,128)(2,1)}) custom-call(f32[2,128,128]{2,1,0:T(8,128)S(1)} %get-tuple-element.19.own, bf16[2,128,128]{2,1,0:T(8,128)(2,1)S(1)} %get-tuple-element.20.image, f32[1,128]{1,0:T(1,128)S(1)} %get-tuple-element.21.refs_0_, f32[1,128]{1,0:T(1,128)S(1)} %get-tuple-element.22.refs_1_, ...), custom_call_target="tpu_custom_call" | custom-call | tf_op jit(solution)/shard_map/finish/pallas_call | solution.py:311
  (21 shorter events, 0.1 us)
Async XLA Ops:
  0.6 15.7 %copy-start = (bf16[1,2,128,128]{3,2,1,0:T(8,128)(2,1)S(1)}, bf16[1,2,128,128]{3,2,1,0:T(8,128)(2,1)}, u32[]{:S(2)}) copy-start(bf16[1,2,128,128]{3,2,1,0:T(8,128)(2,1)} %param.7) | copy-start | bytes 196612
  0.6 15.7 %collective-permute-start = (bf16[2,24,128,128]{3,2,1,0:T(8,128)(2,1)}, bf16[2,24,128,128]{3,2,1,0:T(8,128)(2,1)S(1)}, u32[]{:S(2)}, u32[]{:S(2)}) collective-permute-start(bf16[2,24,128,128]{3,2,1,0:T(8,128)(2,1)} %bitcast.17), channel_id=1, source_target_pairs={{0,8},{8,0},{1,9},{9,1},{2,10},{10,2},{3,11},{11,3},{4,12},{12,4},... | collective-permute-start | bytes 4718600 | tf_op jit(solution)/shard_map/ppermute | solution.py:237
  1.2 8.0 %collective-permute-start.1 = (bf16[2,128,128]{2,1,0:T(8,128)(2,1)}, bf16[2,128,128]{2,1,0:T(8,128)(2,1)S(1)}, u32[]{:S(2)}, u32[]{:S(2)}) collective-permute-start(bf16[2,128,128]{2,1,0:T(8,128)(2,1)} %bitcast.7), channel_id=1, source_target_pairs={{0,4},{1,5},{2,6},{3,7},{4,0},{5,1},{6,2},{7,3},{8,12},{9,13},{10,... | collective-permute-start | bytes 196616 | tf_op jit(solution)/shard_map/ppermute | solution.py:21
  4.8 6.1 %collective-permute-start.4 = (bf16[2,128,128]{2,1,0:T(8,128)(2,1)}, bf16[2,128,128]{2,1,0:T(8,128)(2,1)S(1)}, u32[]{:S(2)}, u32[]{:S(2)}) collective-permute-start(bf16[2,128,128]{2,1,0:T(8,128)(2,1)} %bitcast.8), channel_id=1, source_target_pairs={{0,1},{1,0},{2,3},{3,2},{4,5},{5,4},{6,7},{7,6},{8,9},{9,8},{10,11... | collective-permute-start | bytes 196616 | tf_op jit(solution)/shard_map/ppermute | solution.py:21
  6.3 5.7 %collective-permute-start.3 = (bf16[2,128,128]{2,1,0:T(8,128)(2,1)}, bf16[2,128,128]{2,1,0:T(8,128)(2,1)S(1)}, u32[]{:S(2)}, u32[]{:S(2)}) collective-permute-start(bf16[2,128,128]{2,1,0:T(8,128)(2,1)} %bitcast.9), channel_id=1, source_target_pairs={{0,2},{1,3},{2,0},{3,1},{4,6},{5,7},{6,4},{7,5},{8,10},{9,11},{10,... | collective-permute-start | bytes 196616 | tf_op jit(solution)/shard_map/ppermute | solution.py:21
  7.9 6.2 %collective-permute-start.2 = (bf16[2,128,128]{2,1,0:T(8,128)(2,1)}, bf16[2,128,128]{2,1,0:T(8,128)(2,1)S(1)}, u32[]{:S(2)}, u32[]{:S(2)}) collective-permute-start(bf16[2,128,128]{2,1,0:T(8,128)(2,1)} %bitcast.10), channel_id=1, source_target_pairs={{0,3},{1,2},{2,1},{3,0},{4,7},{5,6},{6,5},{7,4},{8,11},{9,10},{10,... | collective-permute-start | bytes 196616 | tf_op jit(solution)/shard_map/ppermute | solution.py:21
  9.1 5.7 %collective-permute-start.7 = (bf16[2,128,128]{2,1,0:T(8,128)(2,1)S(1)}, bf16[2,128,128]{2,1,0:T(8,128)(2,1)S(1)}, u32[]{:S(2)}, u32[]{:S(2)}) collective-permute-start(bf16[2,128,128]{2,1,0:T(8,128)(2,1)S(1)} %collective-permute-done.1.refs_1_), channel_id=1, source_target_pairs={{0,3},{1,2},{2,1},{3,0},{4,7},{5,6},{6,5},{7,4},{8,11},{9,10},{10,... | collective-permute-start | bytes 196616 | tf_op jit(solution)/shard_map/ppermute | solution.py:21
  11.0 4.5 %collective-permute-start.6 = (bf16[2,128,128]{2,1,0:T(8,128)(2,1)S(1)}, bf16[2,128,128]{2,1,0:T(8,128)(2,1)S(1)}, u32[]{:S(2)}, u32[]{:S(2)}) collective-permute-start(bf16[2,128,128]{2,1,0:T(8,128)(2,1)S(1)} %collective-permute-done.1.refs_1_), channel_id=1, source_target_pairs={{0,2},{1,3},{2,0},{3,1},{4,6},{5,7},{6,4},{7,5},{8,10},{9,11},{10,... | collective-permute-start | bytes 196616 | tf_op jit(solution)/shard_map/ppermute | solution.py:21
  12.1 4.3 %collective-permute-start.5 = (bf16[2,128,128]{2,1,0:T(8,128)(2,1)S(1)}, bf16[2,128,128]{2,1,0:T(8,128)(2,1)S(1)}, u32[]{:S(2)}, u32[]{:S(2)}) collective-permute-start(bf16[2,128,128]{2,1,0:T(8,128)(2,1)S(1)} %collective-permute-done.1.refs_1_), channel_id=1, source_target_pairs={{0,1},{1,0},{2,3},{3,2},{4,5},{5,4},{6,7},{7,6},{8,9},{9,8},{10,11... | collective-permute-start | bytes 196616 | tf_op jit(solution)/shard_map/ppermute | solution.py:21
  18.4 27.5 %copy-start.1 = (s32[1,2]{1,0:T(1,128)S(1)}, s32[1,2]{1,0:T(1,128)}, u32[]{:S(2)}) copy-start(s32[1,2]{1,0:T(1,128)} %ranks.1) | copy-start | bytes 28
  18.4 5.8 %collective-permute-start.8 = (bf16[2,128,128]{2,1,0:T(8,128)(2,1)S(1)}, bf16[2,128,128]{2,1,0:T(8,128)(2,1)S(1)}, u32[]{:S(2)}, u32[]{:S(2)}) collective-permute-start(bf16[2,128,128]{2,1,0:T(8,128)(2,1)S(1)} %first_image.1.refs_8_), channel_id=1, source_target_pairs={{0,4},{1,5},{2,6},{3,7},{4,0},{5,1},{6,2},{7,3},{8,12},{9,13},{10,... | collective-permute-start | bytes 196616 | tf_op jit(solution)/shard_map/ppermute | solution.py:21
  20.7 5.5 %collective-permute-start.11 = (bf16[2,128,128]{2,1,0:T(8,128)(2,1)S(1)}, bf16[2,128,128]{2,1,0:T(8,128)(2,1)S(1)}, u32[]{:S(2)}, u32[]{:S(2)}) collective-permute-start(bf16[2,128,128]{2,1,0:T(8,128)(2,1)S(1)} %first_image.1.refs_8_), channel_id=1, source_target_pairs={{0,1},{1,0},{2,3},{3,2},{4,5},{5,4},{6,7},{7,6},{8,9},{9,8},{10,11... | collective-permute-start | bytes 196616 | tf_op jit(solution)/shard_map/ppermute | solution.py:21
  21.2 6.5 %collective-permute-start.10 = (bf16[2,128,128]{2,1,0:T(8,128)(2,1)S(1)}, bf16[2,128,128]{2,1,0:T(8,128)(2,1)S(1)}, u32[]{:S(2)}, u32[]{:S(2)}) collective-permute-start(bf16[2,128,128]{2,1,0:T(8,128)(2,1)S(1)} %first_image.1.refs_8_), channel_id=1, source_target_pairs={{0,2},{1,3},{2,0},{3,1},{4,6},{5,7},{6,4},{7,5},{8,10},{9,11},{10,... | collective-permute-start | bytes 196616 | tf_op jit(solution)/shard_map/ppermute | solution.py:21
  23.3 5.4 %collective-permute-start.9 = (bf16[2,128,128]{2,1,0:T(8,128)(2,1)S(1)}, bf16[2,128,128]{2,1,0:T(8,128)(2,1)S(1)}, u32[]{:S(2)}, u32[]{:S(2)}) collective-permute-start(bf16[2,128,128]{2,1,0:T(8,128)(2,1)S(1)} %first_image.1.refs_8_), channel_id=1, source_target_pairs={{0,3},{1,2},{2,1},{3,0},{4,7},{5,6},{6,5},{7,4},{8,11},{9,10},{10,... | collective-permute-start | bytes 196616 | tf_op jit(solution)/shard_map/ppermute | solution.py:21
  24.2 5.2 %collective-permute-start.14 = (bf16[2,128,128]{2,1,0:T(8,128)(2,1)S(1)}, bf16[2,128,128]{2,1,0:T(8,128)(2,1)S(1)}, u32[]{:S(2)}, u32[]{:S(2)}) collective-permute-start(bf16[2,128,128]{2,1,0:T(8,128)(2,1)S(1)} %collective-permute-done.8.refs_9_), channel_id=1, source_target_pairs={{0,3},{1,2},{2,1},{3,0},{4,7},{5,6},{6,5},{7,4},{8,11},{9,10},{10,... | collective-permute-start | bytes 196616 | tf_op jit(solution)/shard_map/ppermute | solution.py:21
  26.2 4.3 %collective-permute-start.13 = (bf16[2,128,128]{2,1,0:T(8,128)(2,1)S(1)}, bf16[2,128,128]{2,1,0:T(8,128)(2,1)S(1)}, u32[]{:S(2)}, u32[]{:S(2)}) collective-permute-start(bf16[2,128,128]{2,1,0:T(8,128)(2,1)S(1)} %collective-permute-done.8.refs_9_), channel_id=1, source_target_pairs={{0,2},{1,3},{2,0},{3,1},{4,6},{5,7},{6,4},{7,5},{8,10},{9,11},{10,... | collective-permute-start | bytes 196616 | tf_op jit(solution)/shard_map/ppermute | solution.py:21
  26.2 4.3 %collective-permute-start.12 = (bf16[2,128,128]{2,1,0:T(8,128)(2,1)S(1)}, bf16[2,128,128]{2,1,0:T(8,128)(2,1)S(1)}, u32[]{:S(2)}, u32[]{:S(2)}) collective-permute-start(bf16[2,128,128]{2,1,0:T(8,128)(2,1)S(1)} %collective-permute-done.8.refs_9_), channel_id=1, source_target_pairs={{0,1},{1,0},{2,3},{3,2},{4,5},{5,4},{6,7},{7,6},{8,9},{9,8},{10,11... | collective-permute-start | bytes 196616 | tf_op jit(solution)/shard_map/ppermute | solution.py:21
  32.8 5.7 %collective-permute-start.15 = (bf16[2,128,128]{2,1,0:T(8,128)(2,1)S(1)}, bf16[2,128,128]{2,1,0:T(8,128)(2,1)S(1)}, u32[]{:S(2)}, u32[]{:S(2)}) collective-permute-start(bf16[2,128,128]{2,1,0:T(8,128)(2,1)S(1)} %get-tuple-element.18.refs_1_), channel_id=1, source_target_pairs={{0,4},{1,5},{2,6},{3,7},{4,0},{5,1},{6,2},{7,3},{8,12},{9,13},{10,... | collective-permute-start | bytes 196616 | tf_op jit(solution)/shard_map/ppermute | solution.py:21
  35.0 6.6 %collective-permute-start.18 = (bf16[2,128,128]{2,1,0:T(8,128)(2,1)S(1)}, bf16[2,128,128]{2,1,0:T(8,128)(2,1)S(1)}, u32[]{:S(2)}, u32[]{:S(2)}) collective-permute-start(bf16[2,128,128]{2,1,0:T(8,128)(2,1)S(1)} %get-tuple-element.18.refs_1_), channel_id=1, source_target_pairs={{0,1},{1,0},{2,3},{3,2},{4,5},{5,4},{6,7},{7,6},{8,9},{9,8},{10,11... | collective-permute-start | bytes 196616 | tf_op jit(solution)/shard_map/ppermute | solution.py:21
  36.6 5.6 %collective-permute-start.17 = (bf16[2,128,128]{2,1,0:T(8,128)(2,1)S(1)}, bf16[2,128,128]{2,1,0:T(8,128)(2,1)S(1)}, u32[]{:S(2)}, u32[]{:S(2)}) collective-permute-start(bf16[2,128,128]{2,1,0:T(8,128)(2,1)S(1)} %get-tuple-element.18.refs_1_), channel_id=1, source_target_pairs={{0,2},{1,3},{2,0},{3,1},{4,6},{5,7},{6,4},{7,5},{8,10},{9,11},{10,... | collective-permute-start | bytes 196616 | tf_op jit(solution)/shard_map/ppermute | solution.py:21
  38.5 5.2 %collective-permute-start.16 = (bf16[2,128,128]{2,1,0:T(8,128)(2,1)S(1)}, bf16[2,128,128]{2,1,0:T(8,128)(2,1)S(1)}, u32[]{:S(2)}, u32[]{:S(2)}) collective-permute-start(bf16[2,128,128]{2,1,0:T(8,128)(2,1)S(1)} %get-tuple-element.18.refs_1_), channel_id=1, source_target_pairs={{0,3},{1,2},{2,1},{3,0},{4,7},{5,6},{6,5},{7,4},{8,11},{9,10},{10,... | collective-permute-start | bytes 196616 | tf_op jit(solution)/shard_map/ppermute | solution.py:21
  38.5 5.9 %collective-permute-start.21 = (bf16[2,128,128]{2,1,0:T(8,128)(2,1)S(1)}, bf16[2,128,128]{2,1,0:T(8,128)(2,1)S(1)}, u32[]{:S(2)}, u32[]{:S(2)}) collective-permute-start(bf16[2,128,128]{2,1,0:T(8,128)(2,1)S(1)} %collective-permute-done.15.refs_2_), channel_id=1, source_target_pairs={{0,3},{1,2},{2,1},{3,0},{4,7},{5,6},{6,5},{7,4},{8,11},{9,10},{10,... | collective-permute-start | bytes 196616 | tf_op jit(solution)/shard_map/ppermute | solution.py:21
  41.6 4.3 %collective-permute-start.20 = (bf16[2,128,128]{2,1,0:T(8,128)(2,1)S(1)}, bf16[2,128,128]{2,1,0:T(8,128)(2,1)S(1)}, u32[]{:S(2)}, u32[]{:S(2)}) collective-permute-start(bf16[2,128,128]{2,1,0:T(8,128)(2,1)S(1)} %collective-permute-done.15.refs_2_), channel_id=1, source_target_pairs={{0,2},{1,3},{2,0},{3,1},{4,6},{5,7},{6,4},{7,5},{8,10},{9,11},{10,... | collective-permute-start | bytes 196616 | tf_op jit(solution)/shard_map/ppermute | solution.py:21
  41.6 4.3 %collective-permute-start.19 = (bf16[2,128,128]{2,1,0:T(8,128)(2,1)S(1)}, bf16[2,128,128]{2,1,0:T(8,128)(2,1)S(1)}, u32[]{:S(2)}, u32[]{:S(2)}) collective-permute-start(bf16[2,128,128]{2,1,0:T(8,128)(2,1)S(1)} %collective-permute-done.15.refs_2_), channel_id=1, source_target_pairs={{0,1},{1,0},{2,3},{3,2},{4,5},{5,4},{6,7},{7,6},{8,9},{9,8},{10,11... | collective-permute-start | bytes 196616 | tf_op jit(solution)/shard_map/ppermute | solution.py:21
  48.5 3.4 %collective-permute-start.22 = (f32[1,8,128]{2,1,0:T(8,128)S(1)}, f32[1,8,128]{2,1,0:T(8,128)S(1)}, u32[]{:S(2)}, u32[]{:S(2)}) collective-permute-start(f32[1,8,128]{2,1,0:T(8,128)S(1)} %get-tuple-element.23), channel_id=1, source_target_pairs={{0,8},{1,9},{2,10},{3,11},{4,12},{5,13},{6,14},{7,15},{8,0},{9,1},... | collective-permute-start | bytes 12296 | tf_op jit(solution)/shard_map/ppermute | solution.py:35
  48.6 5.2 %collective-permute-start.25 = (f32[1,8,128]{2,1,0:T(8,128)S(1)}, f32[1,8,128]{2,1,0:T(8,128)S(1)}, u32[]{:S(2)}, u32[]{:S(2)}) collective-permute-start(f32[1,8,128]{2,1,0:T(8,128)S(1)} %get-tuple-element.23), channel_id=1, source_target_pairs={{0,11},{1,10},{2,9},{3,8},{4,15},{5,14},{6,13},{7,12},{8,3},{9,2},... | collective-permute-start | bytes 12296 | tf_op jit(solution)/shard_map/ppermute | solution.py:35
  50.6 3.2 %collective-permute-start.24 = (f32[1,8,128]{2,1,0:T(8,128)S(1)}, f32[1,8,128]{2,1,0:T(8,128)S(1)}, u32[]{:S(2)}, u32[]{:S(2)}) collective-permute-start(f32[1,8,128]{2,1,0:T(8,128)S(1)} %get-tuple-element.23), channel_id=1, source_target_pairs={{0,10},{1,11},{2,8},{3,9},{4,14},{5,15},{6,12},{7,13},{8,2},{9,3},... | collective-permute-start | bytes 12296 | tf_op jit(solution)/shard_map/ppermute | solution.py:35
  50.7 3.0 %collective-permute-start.23 = (f32[1,8,128]{2,1,0:T(8,128)S(1)}, f32[1,8,128]{2,1,0:T(8,128)S(1)}, u32[]{:S(2)}, u32[]{:S(2)}) collective-permute-start(f32[1,8,128]{2,1,0:T(8,128)S(1)} %get-tuple-element.23), channel_id=1, source_target_pairs={{0,9},{1,8},{2,11},{3,10},{4,13},{5,12},{6,15},{7,14},{8,1},{9,0},... | collective-permute-start | bytes 12296 | tf_op jit(solution)/shard_map/ppermute | solution.py:35
  53.8 4.1 %collective-permute-start.27 = (f32[4,8,128]{2,1,0:T(8,128)S(1)}, f32[4,8,128]{2,1,0:T(8,128)S(1)}, u32[]{:S(2)}, u32[]{:S(2)}) collective-permute-start(f32[4,8,128]{2,1,0:T(8,128)S(1)} %constant_dynamic-update-slice_fusion), channel_id=1, source_target_pairs={{0,12},{1,13},{2,14},{3,15},{4,8},{5,9},{6,10},{7,11},{8,4},{9,5},... | collective-permute-start | bytes 49160 | tf_op jit(solution)/shard_map/ppermute | solution.py:35
  55.7 2.2 %collective-permute-start.26 = (f32[4,8,128]{2,1,0:T(8,128)S(1)}, f32[4,8,128]{2,1,0:T(8,128)S(1)}, u32[]{:S(2)}, u32[]{:S(2)}) collective-permute-start(f32[4,8,128]{2,1,0:T(8,128)S(1)} %constant_dynamic-update-slice_fusion), channel_id=1, source_target_pairs={{0,8},{1,9},{2,10},{3,11},{4,12},{5,13},{6,14},{7,15},{8,0},{9,1},... | collective-permute-start | bytes 49160 | tf_op jit(solution)/shard_map/ppermute | solution.py:35

commit v7 on v6

--- a/solution.py
+++ b/solution.py
@@ -51,6 +51,10 @@
     for position in range(1, devices):
         place = jnp.where(apart == APART[position], position, place)
     return place * blocks + sector - owner * blocks
+
+
+def first_slot(blocks):
+    return 0 if lax.axis_size("sec") == len(APART) else lax.axis_index("sec") * blocks
 
 
 def code_bits(width):
@@ -179,10 +183,11 @@
     energy[...] = jnp.broadcast_to(rayleigh_update(before, images, state), energy.shape)
     apply_operator(codes[...], factors[...], state, left, right, mixed, image)
     blocks, size = image.shape[0], image.shape[1]
+    first = first_slot(blocks)
     intersection = jnp.zeros((size, size), jnp.float32)
     squares = jnp.zeros((size, size), jnp.float32)
     for t in range(blocks):
-        value = state[t]
+        value = state[first + t]
         intersection += value * image[t].astype(jnp.float32)
         squares += value * value
     intersection, squares = jnp.sum(intersection, keepdims=True), jnp.sum(squares, keepdims=True)
@@ -194,7 +199,7 @@
     cc = jnp.zeros((size, size), jnp.float32)
     for t in range(blocks):
         keep = column < ranks[0:1, t : t + 1]
-        value = jnp.where(keep, state[t], 0.0)
+        value = jnp.where(keep, state[first + t], 0.0)
         picture = jnp.where(keep, image[t].astype(jnp.float32), 0.0)
         own[t] = value
         image[t] = picture.astype(jnp.bfloat16)

time: 58.7 us -> 58.7 us (level)
  no operation moved by 1% of the time
where the time goes in v7:
time: 58.7 us; the launch traced here: 58.6 us
  starting transfers between devices  35.5 us (60%)
  waiting for transfers between devices  13.2 us (22%)
  Pallas kernels  9.15 us (16%)
  between operations  0.73 us (1%)
    ppermute x21, starting transfers between devices, hop(): return lax.ppermute(block, 'sec', [(a, a ^ distance) for a in range(count)])  29.3 us
    ppermute x21, waiting for transfers between devices, hop(): return lax.ppermute(block, 'sec', [(a, a ^ distance) for a in range(count)])  9.51 us
    ppermute x6, starting transfers between devices, cross(): return lax.ppermute(block, ('seg', 'sec'), route)  5.65 us
    ppermute x6, waiting for transfers between devices, cross(): return lax.ppermute(block, ('seg', 'sec'), route)  3.71 us
    pallas_call x1, Pallas kernels, local(): pl.pallas_call(functools.partial(last_kernel, len(states), len(images)),...  2.62 us
    pallas_call x1, Pallas kernels, local(): pl.pallas_call(functools.partial(middle_kernel, len(states), len(images))...  2.36 us
    pallas_call x1, Pallas kernels, local(): pl.pallas_call(functools.partial(first_kernel, len(states)), out_shape=ow...  1.99 us
    pallas_call x1, Pallas kernels, local(): pl.pallas_call(functools.partial(prepare_kernel, devices), out_shape=(int...  1.49 us
  transfers between devices with their start and end apart: 28, of which 12 were waited for; matrix products, arithmetic and copies ran while one was open for 0% of the time, Pallas kernels for 3%

profile of v7, /device:TPU:0, one launch (start us, length us, event | category | flops | bytes accessed | tf_op | source)
XLA Modules:
  0.0 58.6 jit_solution(15241366317555329549)
XLA Ops:
  0.6 0.5 collective-permute-start
  1.2 3.7 %collective-permute-start.1 = (bf16[2,128,128]{2,1,0:T(8,128)(2,1)}, bf16[2,128,128]{2,1,0:T(8,128)(2,1)S(1)}, u32[]{:S(2)}, u32[]{:S(2)}) collective-permute-start(bf16[2,128,128]{2,1,0:T(8,128)(2,1)} %bitcast.7), channel_id=1, source_target_pairs={{0,4},{1,5},{2,6},{3,7},{4,0},{5,1},{6,2},{7,3},{8,12},{9,13},{10,... | collective-permute-start | bytes 196616 | tf_op jit(solution)/shard_map/ppermute | solution.py:21
  4.8 1.5 %collective-permute-start.4 = (bf16[2,128,128]{2,1,0:T(8,128)(2,1)}, bf16[2,128,128]{2,1,0:T(8,128)(2,1)S(1)}, u32[]{:S(2)}, u32[]{:S(2)}) collective-permute-start(bf16[2,128,128]{2,1,0:T(8,128)(2,1)} %bitcast.8), channel_id=1, source_target_pairs={{0,1},{1,0},{2,3},{3,2},{4,5},{5,4},{6,7},{7,6},{8,9},{9,8},{10,11... | collective-permute-start | bytes 196616 | tf_op jit(solution)/shard_map/ppermute | solution.py:21
  6.3 1.6 %collective-permute-start.3 = (bf16[2,128,128]{2,1,0:T(8,128)(2,1)}, bf16[2,128,128]{2,1,0:T(8,128)(2,1)S(1)}, u32[]{:S(2)}, u32[]{:S(2)}) collective-permute-start(bf16[2,128,128]{2,1,0:T(8,128)(2,1)} %bitcast.9), channel_id=1, source_target_pairs={{0,2},{1,3},{2,0},{3,1},{4,6},{5,7},{6,4},{7,5},{8,10},{9,11},{10,... | collective-permute-start | bytes 196616 | tf_op jit(solution)/shard_map/ppermute | solution.py:21
  7.9 0.4 collective-permute-start.2
  8.3 0.8 %collective-permute-done.1.refs_1_ = bf16[2,128,128]{2,1,0:T(8,128)(2,1)S(1)} collective-permute-done((bf16[2,128,128]{2,1,0:T(8,128)(2,1)}, bf16[2,128,128]{2,1,0:T(8,128)(2,1)S(1)}, u32[]{:S(2)}, u32[]{:S(2)}) %collective-permute-start.1) | collective-permute-done | bytes 65568 | tf_op jit(solution)/shard_map/ppermute | solution.py:21
  9.1 1.8 %collective-permute-start.7 = (bf16[2,128,128]{2,1,0:T(8,128)(2,1)S(1)}, bf16[2,128,128]{2,1,0:T(8,128)(2,1)S(1)}, u32[]{:S(2)}, u32[]{:S(2)}) collective-permute-start(bf16[2,128,128]{2,1,0:T(8,128)(2,1)S(1)} %collective-permute-done.1.refs_1_), channel_id=1, source_target_pairs={{0,3},{1,2},{2,1},{3,0},{4,7},{5,6},{6,5},{7,4},{8,11},{9,10},{10,... | collective-permute-start | bytes 196616 | tf_op jit(solution)/shard_map/ppermute | solution.py:21
  11.0 0.0 collective-permute-done.4.refs_4_
  11.0 1.1 %collective-permute-start.6 = (bf16[2,128,128]{2,1,0:T(8,128)(2,1)S(1)}, bf16[2,128,128]{2,1,0:T(8,128)(2,1)S(1)}, u32[]{:S(2)}, u32[]{:S(2)}) collective-permute-start(bf16[2,128,128]{2,1,0:T(8,128)(2,1)S(1)} %collective-permute-done.1.refs_1_), channel_id=1, source_target_pairs={{0,2},{1,3},{2,0},{3,1},{4,6},{5,7},{6,4},{7,5},{8,10},{9,11},{10,... | collective-permute-start | bytes 196616 | tf_op jit(solution)/shard_map/ppermute | solution.py:21
  12.1 0.0 collective-permute-done.3.refs_3_
  12.1 0.5 collective-permute-start.5
  12.6 1.5 %prepare.1 = (s32[2,32]{1,0:T(2,128)S(1)}, f32[2,32]{1,0:T(2,128)S(1)}, bf16[2,24,128,128]{3,2,1,0:T(8,128)(2,1)S(1)}) custom-call(s32[2,32]{1,0:T(2,128)} %bitcast.14, s32[2,32]{1,0:T(2,128)} %bitcast.15, f32[2,32]{1,0:T(2,128)} %bitcast.16, bf16[2,24,128,128]{3,2,1,0:T(8,128)(2,1)} %bitcast.13), custom_call_target="tpu_custom_call" | custom-call | tf_op jit(solution)/shard_map/prepare/pallas_call | solution.py:252
  14.1 0.7 %collective-permute-done.7.refs_7_ = bf16[2,128,128]{2,1,0:T(8,128)(2,1)S(1)} collective-permute-done((bf16[2,128,128]{2,1,0:T(8,128)(2,1)S(1)}, bf16[2,128,128]{2,1,0:T(8,128)(2,1)S(1)}, u32[]{:S(2)}, u32[]{:S(2)}) %collective-permute-start.7) | collective-permute-done | bytes 65568 | tf_op jit(solution)/shard_map/ppermute | solution.py:21
  14.8 0.6 %collective-permute-done.6.refs_6_ = bf16[2,128,128]{2,1,0:T(8,128)(2,1)S(1)} collective-permute-done((bf16[2,128,128]{2,1,0:T(8,128)(2,1)S(1)}, bf16[2,128,128]{2,1,0:T(8,128)(2,1)S(1)}, u32[]{:S(2)}, u32[]{:S(2)}) %collective-permute-start.6) | collective-permute-done | bytes 65568 | tf_op jit(solution)/shard_map/ppermute | solution.py:21
  15.5 0.9 %collective-permute-done.5.refs_5_ = bf16[2,128,128]{2,1,0:T(8,128)(2,1)S(1)} collective-permute-done((bf16[2,128,128]{2,1,0:T(8,128)(2,1)S(1)}, bf16[2,128,128]{2,1,0:T(8,128)(2,1)S(1)}, u32[]{:S(2)}, u32[]{:S(2)}) %collective-permute-start.5) | collective-permute-done | bytes 65568 | tf_op jit(solution)/shard_map/ppermute | solution.py:21
  16.4 2.0 %first_image.1.refs_8_ = bf16[2,128,128]{2,1,0:T(8,128)(2,1)S(1)} custom-call(s32[2,32]{1,0:T(2,128)S(1)} %get-tuple-element.14.codes, f32[2,32]{1,0:T(2,128)S(1)} %get-tuple-element.15.factors, bf16[2,24,128,128]{3,2,1,0:T(8,128)(2,1)S(1)} %get-tuple-element.16.left, bf16[2,24,128,128]{3,2,1,0:T(8,128)(2,1)S(1)} %collective-permute-done.right, ...), custom_call_target="tpu_custom_call" | custom-call | tf_op jit(solution)/shard_map/first_image/pallas_call | solution.py:273
  18.4 0.0 copy-start.1
  18.4 2.4 %collective-permute-start.8 = (bf16[2,128,128]{2,1,0:T(8,128)(2,1)S(1)}, bf16[2,128,128]{2,1,0:T(8,128)(2,1)S(1)}, u32[]{:S(2)}, u32[]{:S(2)}) collective-permute-start(bf16[2,128,128]{2,1,0:T(8,128)(2,1)S(1)} %first_image.1.refs_8_), channel_id=1, source_target_pairs={{0,4},{1,5},{2,6},{3,7},{4,0},{5,1},{6,2},{7,3},{8,12},{9,13},{10,... | collective-permute-start | bytes 196616 | tf_op jit(solution)/shard_map/ppermute | solution.py:21
  20.7 0.5 collective-permute-start.11
  21.2 2.0 %collective-permute-start.10 = (bf16[2,128,128]{2,1,0:T(8,128)(2,1)S(1)}, bf16[2,128,128]{2,1,0:T(8,128)(2,1)S(1)}, u32[]{:S(2)}, u32[]{:S(2)}) collective-permute-start(bf16[2,128,128]{2,1,0:T(8,128)(2,1)S(1)} %first_image.1.refs_8_), channel_id=1, source_target_pairs={{0,2},{1,3},{2,0},{3,1},{4,6},{5,7},{6,4},{7,5},{8,10},{9,11},{10,... | collective-permute-start | bytes 196616 | tf_op jit(solution)/shard_map/ppermute | solution.py:21
  23.3 1.0 %collective-permute-start.9 = (bf16[2,128,128]{2,1,0:T(8,128)(2,1)S(1)}, bf16[2,128,128]{2,1,0:T(8,128)(2,1)S(1)}, u32[]{:S(2)}, u32[]{:S(2)}) collective-permute-start(bf16[2,128,128]{2,1,0:T(8,128)(2,1)S(1)} %first_image.1.refs_8_), channel_id=1, source_target_pairs={{0,3},{1,2},{2,1},{3,0},{4,7},{5,6},{6,5},{7,4},{8,11},{9,10},{10,... | collective-permute-start | bytes 196616 | tf_op jit(solution)/shard_map/ppermute | solution.py:21
  24.2 2.0 %collective-permute-start.14 = (bf16[2,128,128]{2,1,0:T(8,128)(2,1)S(1)}, bf16[2,128,128]{2,1,0:T(8,128)(2,1)S(1)}, u32[]{:S(2)}, u32[]{:S(2)}) collective-permute-start(bf16[2,128,128]{2,1,0:T(8,128)(2,1)S(1)} %collective-permute-done.8.refs_9_), channel_id=1, source_target_pairs={{0,3},{1,2},{2,1},{3,0},{4,7},{5,6},{6,5},{7,4},{8,11},{9,10},{10,... | collective-permute-start | bytes 196616 | tf_op jit(solution)/shard_map/ppermute | solution.py:21
  26.2 0.0 collective-permute-start.13
  26.2 1.5 %collective-permute-start.12 = (bf16[2,128,128]{2,1,0:T(8,128)(2,1)S(1)}, bf16[2,128,128]{2,1,0:T(8,128)(2,1)S(1)}, u32[]{:S(2)}, u32[]{:S(2)}) collective-permute-start(bf16[2,128,128]{2,1,0:T(8,128)(2,1)S(1)} %collective-permute-done.8.refs_9_), channel_id=1, source_target_pairs={{0,1},{1,0},{2,3},{3,2},{4,5},{5,4},{6,7},{7,6},{8,9},{9,8},{10,11... | collective-permute-start | bytes 196616 | tf_op jit(solution)/shard_map/ppermute | solution.py:21
  27.7 1.0 %collective-permute-done.9.refs_10_ = bf16[2,128,128]{2,1,0:T(8,128)(2,1)S(1)} collective-permute-done((bf16[2,128,128]{2,1,0:T(8,128)(2,1)S(1)}, bf16[2,128,128]{2,1,0:T(8,128)(2,1)S(1)}, u32[]{:S(2)}, u32[]{:S(2)}) %collective-permute-start.9) | collective-permute-done | bytes 65568 | tf_op jit(solution)/shard_map/ppermute | solution.py:21
  28.7 0.7 %collective-permute-done.14.refs_15_ = bf16[2,128,128]{2,1,0:T(8,128)(2,1)S(1)} collective-permute-done((bf16[2,128,128]{2,1,0:T(8,128)(2,1)S(1)}, bf16[2,128,128]{2,1,0:T(8,128)(2,1)S(1)}, u32[]{:S(2)}, u32[]{:S(2)}) %collective-permute-start.14) | collective-permute-done | bytes 65568 | tf_op jit(solution)/shard_map/ppermute | solution.py:21
  29.4 1.1 %collective-permute-done.13.refs_14_ = bf16[2,128,128]{2,1,0:T(8,128)(2,1)S(1)} collective-permute-done((bf16[2,128,128]{2,1,0:T(8,128)(2,1)S(1)}, bf16[2,128,128]{2,1,0:T(8,128)(2,1)S(1)}, u32[]{:S(2)}, u32[]{:S(2)}) %collective-permute-start.13) | collective-permute-done | bytes 65568 | tf_op jit(solution)/shard_map/ppermute | solution.py:21
  30.5 0.0 collective-permute-done.12.refs_13_
  30.5 2.4 %middle_image.1 = (f32[1,128]{1,0:T(1,128)S(1)}, f32[16,128,128]{2,1,0:T(8,128)S(1)}, bf16[2,128,128]{2,1,0:T(8,128)(2,1)S(1)}) custom-call(s32[2,32]{1,0:T(2,128)S(1)} %get-tuple-element.14.codes, f32[2,32]{1,0:T(2,128)S(1)} %get-tuple-element.15.factors, bf16[2,24,128,128]{3,2,1,0:T(8,128)(2,1)S(1)} %get-tuple-element.16.left, ...), custom_call_target="tpu_custom_call" | custom-call | tf_op jit(solution)/shard_map/middle_image/pallas_call | solution.py:285
  32.8 2.2 %collective-permute-start.15 = (bf16[2,128,128]{2,1,0:T(8,128)(2,1)S(1)}, bf16[2,128,128]{2,1,0:T(8,128)(2,1)S(1)}, u32[]{:S(2)}, u32[]{:S(2)}) collective-permute-start(bf16[2,128,128]{2,1,0:T(8,128)(2,1)S(1)} %get-tuple-element.18.refs_1_), channel_id=1, source_target_pairs={{0,4},{1,5},{2,6},{3,7},{4,0},{5,1},{6,2},{7,3},{8,12},{9,13},{10,... | collective-permute-start | bytes 196616 | tf_op jit(solution)/shard_map/ppermute | solution.py:21
  35.0 1.6 %collective-permute-start.18 = (bf16[2,128,128]{2,1,0:T(8,128)(2,1)S(1)}, bf16[2,128,128]{2,1,0:T(8,128)(2,1)S(1)}, u32[]{:S(2)}, u32[]{:S(2)}) collective-permute-start(bf16[2,128,128]{2,1,0:T(8,128)(2,1)S(1)} %get-tuple-element.18.refs_1_), channel_id=1, source_target_pairs={{0,1},{1,0},{2,3},{3,2},{4,5},{5,4},{6,7},{7,6},{8,9},{9,8},{10,11... | collective-permute-start | bytes 196616 | tf_op jit(solution)/shard_map/ppermute | solution.py:21
  36.6 1.9 %collective-permute-start.17 = (bf16[2,128,128]{2,1,0:T(8,128)(2,1)S(1)}, bf16[2,128,128]{2,1,0:T(8,128)(2,1)S(1)}, u32[]{:S(2)}, u32[]{:S(2)}) collective-permute-start(bf16[2,128,128]{2,1,0:T(8,128)(2,1)S(1)} %get-tuple-element.18.refs_1_), channel_id=1, source_target_pairs={{0,2},{1,3},{2,0},{3,1},{4,6},{5,7},{6,4},{7,5},{8,10},{9,11},{10,... | collective-permute-start | bytes 196616 | tf_op jit(solution)/shard_map/ppermute | solution.py:21
  38.5 3.1 %collective-permute-start.21 = (bf16[2,128,128]{2,1,0:T(8,128)(2,1)S(1)}, bf16[2,128,128]{2,1,0:T(8,128)(2,1)S(1)}, u32[]{:S(2)}, u32[]{:S(2)}) collective-permute-start(bf16[2,128,128]{2,1,0:T(8,128)(2,1)S(1)} %collective-permute-done.15.refs_2_), channel_id=1, source_target_pairs={{0,3},{1,2},{2,1},{3,0},{4,7},{5,6},{6,5},{7,4},{8,11},{9,10},{10,... | collective-permute-start | bytes 196616 | tf_op jit(solution)/shard_map/ppermute | solution.py:21
  41.6 0.6 collective-permute-start.19
  42.2 1.5 %collective-permute-done.16.refs_3_ = bf16[2,128,128]{2,1,0:T(8,128)(2,1)S(1)} collective-permute-done((bf16[2,128,128]{2,1,0:T(8,128)(2,1)S(1)}, bf16[2,128,128]{2,1,0:T(8,128)(2,1)S(1)}, u32[]{:S(2)}, u32[]{:S(2)}) %collective-permute-start.16) | collective-permute-done | bytes 65568 | tf_op jit(solution)/shard_map/ppermute | solution.py:21
  43.7 0.7 %collective-permute-done.21.refs_8_ = bf16[2,128,128]{2,1,0:T(8,128)(2,1)S(1)} collective-permute-done((bf16[2,128,128]{2,1,0:T(8,128)(2,1)S(1)}, bf16[2,128,128]{2,1,0:T(8,128)(2,1)S(1)}, u32[]{:S(2)}, u32[]{:S(2)}) %collective-permute-start.21) | collective-permute-done | bytes 65568 | tf_op jit(solution)/shard_map/ppermute | solution.py:21
  44.4 1.5 %collective-permute-done.20.refs_7_ = bf16[2,128,128]{2,1,0:T(8,128)(2,1)S(1)} collective-permute-done((bf16[2,128,128]{2,1,0:T(8,128)(2,1)S(1)}, bf16[2,128,128]{2,1,0:T(8,128)(2,1)S(1)}, u32[]{:S(2)}, u32[]{:S(2)}) %collective-permute-start.20) | collective-permute-done | bytes 65568 | tf_op jit(solution)/shard_map/ppermute | solution.py:21
  45.9 0.0 collective-permute-done.19.refs_6_
  45.9 2.6 %last_image.1 = (f32[1,128]{1,0:T(1,128)S(1)}, f32[2,128,128]{2,1,0:T(8,128)S(1)}, bf16[2,128,128]{2,1,0:T(8,128)(2,1)S(1)}, f32[1,8,128]{2,1,0:T(8,128)S(1)}) custom-call(s32[2,32]{1,0:T(2,128)S(1)} %get-tuple-element.14.codes, f32[2,32]{1,0:T(2,128)S(1)} %get-tuple-element.15.factors, s32[1,2]{1,0:T(1,128)S(1)} %copy-done.1, ...), custom_call_target="tpu_custom_call" | custom-call | tf_op jit(solution)/shard_map/last_image/pallas_call | solution.py:297
  48.5 0.1 collective-permute-start.22
  48.6 2.0 %collective-permute-start.25 = (f32[1,8,128]{2,1,0:T(8,128)S(1)}, f32[1,8,128]{2,1,0:T(8,128)S(1)}, u32[]{:S(2)}, u32[]{:S(2)}) collective-permute-start(f32[1,8,128]{2,1,0:T(8,128)S(1)} %get-tuple-element.23), channel_id=1, source_target_pairs={{0,11},{1,10},{2,9},{3,8},{4,15},{5,14},{6,13},{7,12},{8,3},{9,2},... | collective-permute-start | bytes 12296 | tf_op jit(solution)/shard_map/ppermute | solution.py:35
  50.6 0.2 collective-permute-start.24
  50.7 1.2 %collective-permute-start.23 = (f32[1,8,128]{2,1,0:T(8,128)S(1)}, f32[1,8,128]{2,1,0:T(8,128)S(1)}, u32[]{:S(2)}, u32[]{:S(2)}) collective-permute-start(f32[1,8,128]{2,1,0:T(8,128)S(1)} %get-tuple-element.23), channel_id=1, source_target_pairs={{0,9},{1,8},{2,11},{3,10},{4,13},{5,12},{6,15},{7,14},{8,1},{9,0},... | collective-permute-start | bytes 12296 | tf_op jit(solution)/shard_map/ppermute | solution.py:35
  51.9 1.8 %collective-permute-done.23 = f32[1,8,128]{2,1,0:T(8,128)S(1)} collective-permute-done((f32[1,8,128]{2,1,0:T(8,128)S(1)}, f32[1,8,128]{2,1,0:T(8,128)S(1)}, u32[]{:S(2)}, u32[]{:S(2)}) %collective-permute-start.23) | collective-permute-done | bytes 4128 | tf_op jit(solution)/shard_map/ppermute | solution.py:35
  53.8 1.9 %collective-permute-start.27 = (f32[4,8,128]{2,1,0:T(8,128)S(1)}, f32[4,8,128]{2,1,0:T(8,128)S(1)}, u32[]{:S(2)}, u32[]{:S(2)}) collective-permute-start(f32[4,8,128]{2,1,0:T(8,128)S(1)} %constant_dynamic-update-slice_fusion), channel_id=1, source_target_pairs={{0,12},{1,13},{2,14},{3,15},{4,8},{5,9},{6,10},{7,11},{8,4},{9,5},... | collective-permute-start | bytes 49160 | tf_op jit(solution)/shard_map/ppermute | solution.py:35
  55.7 0.4 collective-permute-start.26
  56.0 1.9 %collective-permute-done.27.refs_3_ = f32[4,8,128]{2,1,0:T(8,128)S(1)} collective-permute-done((f32[4,8,128]{2,1,0:T(8,128)S(1)}, f32[4,8,128]{2,1,0:T(8,128)S(1)}, u32[]{:S(2)}, u32[]{:S(2)}) %collective-permute-start.27) | collective-permute-done | bytes 16416 | tf_op jit(solution)/shard_map/ppermute | solution.py:35
  57.9 0.7 %finish.1 = (f32[1,3]{1,0:T(1,128)}, bf16[2,128,128]{2,1,0:T(8,128)(2,1)}) custom-call(f32[2,128,128]{2,1,0:T(8,128)S(1)} %get-tuple-element.19.own, bf16[2,128,128]{2,1,0:T(8,128)(2,1)S(1)} %get-tuple-element.20.image, f32[1,128]{1,0:T(1,128)S(1)} %get-tuple-element.21.refs_0_, f32[1,128]{1,0:T(1,128)S(1)} %get-tuple-element.22.refs_1_, ...), custom_call_target="tpu_custom_call" | custom-call | tf_op jit(solution)/shard_map/finish/pallas_call | solution.py:316
  (21 shorter events, 0.1 us)
Async XLA Ops:
  0.6 15.7 %copy-start = (bf16[1,2,128,128]{3,2,1,0:T(8,128)(2,1)S(1)}, bf16[1,2,128,128]{3,2,1,0:T(8,128)(2,1)}, u32[]{:S(2)}) copy-start(bf16[1,2,128,128]{3,2,1,0:T(8,128)(2,1)} %param.7) | copy-start | bytes 196612
  0.6 15.7 %collective-permute-start = (bf16[2,24,128,128]{3,2,1,0:T(8,128)(2,1)}, bf16[2,24,128,128]{3,2,1,0:T(8,128)(2,1)S(1)}, u32[]{:S(2)}, u32[]{:S(2)}) collective-permute-start(bf16[2,24,128,128]{3,2,1,0:T(8,128)(2,1)} %bitcast.17), channel_id=1, source_target_pairs={{0,8},{8,0},{1,9},{9,1},{2,10},{10,2},{3,11},{11,3},{4,12},{12,4},... | collective-permute-start | bytes 4718600 | tf_op jit(solution)/shard_map/ppermute | solution.py:242
  1.2 8.0 %collective-permute-start.1 = (bf16[2,128,128]{2,1,0:T(8,128)(2,1)}, bf16[2,128,128]{2,1,0:T(8,128)(2,1)S(1)}, u32[]{:S(2)}, u32[]{:S(2)}) collective-permute-start(bf16[2,128,128]{2,1,0:T(8,128)(2,1)} %bitcast.7), channel_id=1, source_target_pairs={{0,4},{1,5},{2,6},{3,7},{4,0},{5,1},{6,2},{7,3},{8,12},{9,13},{10,... | collective-permute-start | bytes 196616 | tf_op jit(solution)/shard_map/ppermute | solution.py:21
  4.8 6.1 %collective-permute-start.4 = (bf16[2,128,128]{2,1,0:T(8,128)(2,1)}, bf16[2,128,128]{2,1,0:T(8,128)(2,1)S(1)}, u32[]{:S(2)}, u32[]{:S(2)}) collective-permute-start(bf16[2,128,128]{2,1,0:T(8,128)(2,1)} %bitcast.8), channel_id=1, source_target_pairs={{0,1},{1,0},{2,3},{3,2},{4,5},{5,4},{6,7},{7,6},{8,9},{9,8},{10,11... | collective-permute-start | bytes 196616 | tf_op jit(solution)/shard_map/ppermute | solution.py:21
  6.3 5.7 %collective-permute-start.3 = (bf16[2,128,128]{2,1,0:T(8,128)(2,1)}, bf16[2,128,128]{2,1,0:T(8,128)(2,1)S(1)}, u32[]{:S(2)}, u32[]{:S(2)}) collective-permute-start(bf16[2,128,128]{2,1,0:T(8,128)(2,1)} %bitcast.9), channel_id=1, source_target_pairs={{0,2},{1,3},{2,0},{3,1},{4,6},{5,7},{6,4},{7,5},{8,10},{9,11},{10,... | collective-permute-start | bytes 196616 | tf_op jit(solution)/shard_map/ppermute | solution.py:21
  7.9 6.2 %collective-permute-start.2 = (bf16[2,128,128]{2,1,0:T(8,128)(2,1)}, bf16[2,128,128]{2,1,0:T(8,128)(2,1)S(1)}, u32[]{:S(2)}, u32[]{:S(2)}) collective-permute-start(bf16[2,128,128]{2,1,0:T(8,128)(2,1)} %bitcast.10), channel_id=1, source_target_pairs={{0,3},{1,2},{2,1},{3,0},{4,7},{5,6},{6,5},{7,4},{8,11},{9,10},{10,... | collective-permute-start | bytes 196616 | tf_op jit(solution)/shard_map/ppermute | solution.py:21
  9.1 5.7 %collective-permute-start.7 = (bf16[2,128,128]{2,1,0:T(8,128)(2,1)S(1)}, bf16[2,128,128]{2,1,0:T(8,128)(2,1)S(1)}, u32[]{:S(2)}, u32[]{:S(2)}) collective-permute-start(bf16[2,128,128]{2,1,0:T(8,128)(2,1)S(1)} %collective-permute-done.1.refs_1_), channel_id=1, source_target_pairs={{0,3},{1,2},{2,1},{3,0},{4,7},{5,6},{6,5},{7,4},{8,11},{9,10},{10,... | collective-permute-start | bytes 196616 | tf_op jit(solution)/shard_map/ppermute | solution.py:21
  11.0 4.5 %collective-permute-start.6 = (bf16[2,128,128]{2,1,0:T(8,128)(2,1)S(1)}, bf16[2,128,128]{2,1,0:T(8,128)(2,1)S(1)}, u32[]{:S(2)}, u32[]{:S(2)}) collective-permute-start(bf16[2,128,128]{2,1,0:T(8,128)(2,1)S(1)} %collective-permute-done.1.refs_1_), channel_id=1, source_target_pairs={{0,2},{1,3},{2,0},{3,1},{4,6},{5,7},{6,4},{7,5},{8,10},{9,11},{10,... | collective-permute-start | bytes 196616 | tf_op jit(solution)/shard_map/ppermute | solution.py:21
  12.1 4.3 %collective-permute-start.5 = (bf16[2,128,128]{2,1,0:T(8,128)(2,1)S(1)}, bf16[2,128,128]{2,1,0:T(8,128)(2,1)S(1)}, u32[]{:S(2)}, u32[]{:S(2)}) collective-permute-start(bf16[2,128,128]{2,1,0:T(8,128)(2,1)S(1)} %collective-permute-done.1.refs_1_), channel_id=1, source_target_pairs={{0,1},{1,0},{2,3},{3,2},{4,5},{5,4},{6,7},{7,6},{8,9},{9,8},{10,11... | collective-permute-start | bytes 196616 | tf_op jit(solution)/shard_map/ppermute | solution.py:21
  18.4 27.5 %copy-start.1 = (s32[1,2]{1,0:T(1,128)S(1)}, s32[1,2]{1,0:T(1,128)}, u32[]{:S(2)}) copy-start(s32[1,2]{1,0:T(1,128)} %ranks.1) | copy-start | bytes 28
  18.4 5.8 %collective-permute-start.8 = (bf16[2,128,128]{2,1,0:T(8,128)(2,1)S(1)}, bf16[2,128,128]{2,1,0:T(8,128)(2,1)S(1)}, u32[]{:S(2)}, u32[]{:S(2)}) collective-permute-start(bf16[2,128,128]{2,1,0:T(8,128)(2,1)S(1)} %first_image.1.refs_8_), channel_id=1, source_target_pairs={{0,4},{1,5},{2,6},{3,7},{4,0},{5,1},{6,2},{7,3},{8,12},{9,13},{10,... | collective-permute-start | bytes 196616 | tf_op jit(solution)/shard_map/ppermute | solution.py:21
  20.7 5.5 %collective-permute-start.11 = (bf16[2,128,128]{2,1,0:T(8,128)(2,1)S(1)}, bf16[2,128,128]{2,1,0:T(8,128)(2,1)S(1)}, u32[]{:S(2)}, u32[]{:S(2)}) collective-permute-start(bf16[2,128,128]{2,1,0:T(8,128)(2,1)S(1)} %first_image.1.refs_8_), channel_id=1, source_target_pairs={{0,1},{1,0},{2,3},{3,2},{4,5},{5,4},{6,7},{7,6},{8,9},{9,8},{10,11... | collective-permute-start | bytes 196616 | tf_op jit(solution)/shard_map/ppermute | solution.py:21
  21.2 6.5 %collective-permute-start.10 = (bf16[2,128,128]{2,1,0:T(8,128)(2,1)S(1)}, bf16[2,128,128]{2,1,0:T(8,128)(2,1)S(1)}, u32[]{:S(2)}, u32[]{:S(2)}) collective-permute-start(bf16[2,128,128]{2,1,0:T(8,128)(2,1)S(1)} %first_image.1.refs_8_), channel_id=1, source_target_pairs={{0,2},{1,3},{2,0},{3,1},{4,6},{5,7},{6,4},{7,5},{8,10},{9,11},{10,... | collective-permute-start | bytes 196616 | tf_op jit(solution)/shard_map/ppermute | solution.py:21
  23.3 5.4 %collective-permute-start.9 = (bf16[2,128,128]{2,1,0:T(8,128)(2,1)S(1)}, bf16[2,128,128]{2,1,0:T(8,128)(2,1)S(1)}, u32[]{:S(2)}, u32[]{:S(2)}) collective-permute-start(bf16[2,128,128]{2,1,0:T(8,128)(2,1)S(1)} %first_image.1.refs_8_), channel_id=1, source_target_pairs={{0,3},{1,2},{2,1},{3,0},{4,7},{5,6},{6,5},{7,4},{8,11},{9,10},{10,... | collective-permute-start | bytes 196616 | tf_op jit(solution)/shard_map/ppermute | solution.py:21
  24.2 5.2 %collective-permute-start.14 = (bf16[2,128,128]{2,1,0:T(8,128)(2,1)S(1)}, bf16[2,128,128]{2,1,0:T(8,128)(2,1)S(1)}, u32[]{:S(2)}, u32[]{:S(2)}) collective-permute-start(bf16[2,128,128]{2,1,0:T(8,128)(2,1)S(1)} %collective-permute-done.8.refs_9_), channel_id=1, source_target_pairs={{0,3},{1,2},{2,1},{3,0},{4,7},{5,6},{6,5},{7,4},{8,11},{9,10},{10,... | collective-permute-start | bytes 196616 | tf_op jit(solution)/shard_map/ppermute | solution.py:21
  26.2 4.3 %collective-permute-start.13 = (bf16[2,128,128]{2,1,0:T(8,128)(2,1)S(1)}, bf16[2,128,128]{2,1,0:T(8,128)(2,1)S(1)}, u32[]{:S(2)}, u32[]{:S(2)}) collective-permute-start(bf16[2,128,128]{2,1,0:T(8,128)(2,1)S(1)} %collective-permute-done.8.refs_9_), channel_id=1, source_target_pairs={{0,2},{1,3},{2,0},{3,1},{4,6},{5,7},{6,4},{7,5},{8,10},{9,11},{10,... | collective-permute-start | bytes 196616 | tf_op jit(solution)/shard_map/ppermute | solution.py:21
  26.2 4.3 %collective-permute-start.12 = (bf16[2,128,128]{2,1,0:T(8,128)(2,1)S(1)}, bf16[2,128,128]{2,1,0:T(8,128)(2,1)S(1)}, u32[]{:S(2)}, u32[]{:S(2)}) collective-permute-start(bf16[2,128,128]{2,1,0:T(8,128)(2,1)S(1)} %collective-permute-done.8.refs_9_), channel_id=1, source_target_pairs={{0,1},{1,0},{2,3},{3,2},{4,5},{5,4},{6,7},{7,6},{8,9},{9,8},{10,11... | collective-permute-start | bytes 196616 | tf_op jit(solution)/shard_map/ppermute | solution.py:21
  32.8 5.7 %collective-permute-start.15 = (bf16[2,128,128]{2,1,0:T(8,128)(2,1)S(1)}, bf16[2,128,128]{2,1,0:T(8,128)(2,1)S(1)}, u32[]{:S(2)}, u32[]{:S(2)}) collective-permute-start(bf16[2,128,128]{2,1,0:T(8,128)(2,1)S(1)} %get-tuple-element.18.refs_1_), channel_id=1, source_target_pairs={{0,4},{1,5},{2,6},{3,7},{4,0},{5,1},{6,2},{7,3},{8,12},{9,13},{10,... | collective-permute-start | bytes 196616 | tf_op jit(solution)/shard_map/ppermute | solution.py:21
  35.0 6.6 %collective-permute-start.18 = (bf16[2,128,128]{2,1,0:T(8,128)(2,1)S(1)}, bf16[2,128,128]{2,1,0:T(8,128)(2,1)S(1)}, u32[]{:S(2)}, u32[]{:S(2)}) collective-permute-start(bf16[2,128,128]{2,1,0:T(8,128)(2,1)S(1)} %get-tuple-element.18.refs_1_), channel_id=1, source_target_pairs={{0,1},{1,0},{2,3},{3,2},{4,5},{5,4},{6,7},{7,6},{8,9},{9,8},{10,11... | collective-permute-start | bytes 196616 | tf_op jit(solution)/shard_map/ppermute | solution.py:21
  36.6 5.6 %collective-permute-start.17 = (bf16[2,128,128]{2,1,0:T(8,128)(2,1)S(1)}, bf16[2,128,128]{2,1,0:T(8,128)(2,1)S(1)}, u32[]{:S(2)}, u32[]{:S(2)}) collective-permute-start(bf16[2,128,128]{2,1,0:T(8,128)(2,1)S(1)} %get-tuple-element.18.refs_1_), channel_id=1, source_target_pairs={{0,2},{1,3},{2,0},{3,1},{4,6},{5,7},{6,4},{7,5},{8,10},{9,11},{10,... | collective-permute-start | bytes 196616 | tf_op jit(solution)/shard_map/ppermute | solution.py:21
  38.5 5.2 %collective-permute-start.16 = (bf16[2,128,128]{2,1,0:T(8,128)(2,1)S(1)}, bf16[2,128,128]{2,1,0:T(8,128)(2,1)S(1)}, u32[]{:S(2)}, u32[]{:S(2)}) collective-permute-start(bf16[2,128,128]{2,1,0:T(8,128)(2,1)S(1)} %get-tuple-element.18.refs_1_), channel_id=1, source_target_pairs={{0,3},{1,2},{2,1},{3,0},{4,7},{5,6},{6,5},{7,4},{8,11},{9,10},{10,... | collective-permute-start | bytes 196616 | tf_op jit(solution)/shard_map/ppermute | solution.py:21
  38.5 5.9 %collective-permute-start.21 = (bf16[2,128,128]{2,1,0:T(8,128)(2,1)S(1)}, bf16[2,128,128]{2,1,0:T(8,128)(2,1)S(1)}, u32[]{:S(2)}, u32[]{:S(2)}) collective-permute-start(bf16[2,128,128]{2,1,0:T(8,128)(2,1)S(1)} %collective-permute-done.15.refs_2_), channel_id=1, source_target_pairs={{0,3},{1,2},{2,1},{3,0},{4,7},{5,6},{6,5},{7,4},{8,11},{9,10},{10,... | collective-permute-start | bytes 196616 | tf_op jit(solution)/shard_map/ppermute | solution.py:21
  41.6 4.3 %collective-permute-start.20 = (bf16[2,128,128]{2,1,0:T(8,128)(2,1)S(1)}, bf16[2,128,128]{2,1,0:T(8,128)(2,1)S(1)}, u32[]{:S(2)}, u32[]{:S(2)}) collective-permute-start(bf16[2,128,128]{2,1,0:T(8,128)(2,1)S(1)} %collective-permute-done.15.refs_2_), channel_id=1, source_target_pairs={{0,2},{1,3},{2,0},{3,1},{4,6},{5,7},{6,4},{7,5},{8,10},{9,11},{10,... | collective-permute-start | bytes 196616 | tf_op jit(solution)/shard_map/ppermute | solution.py:21
  41.6 4.3 %collective-permute-start.19 = (bf16[2,128,128]{2,1,0:T(8,128)(2,1)S(1)}, bf16[2,128,128]{2,1,0:T(8,128)(2,1)S(1)}, u32[]{:S(2)}, u32[]{:S(2)}) collective-permute-start(bf16[2,128,128]{2,1,0:T(8,128)(2,1)S(1)} %collective-permute-done.15.refs_2_), channel_id=1, source_target_pairs={{0,1},{1,0},{2,3},{3,2},{4,5},{5,4},{6,7},{7,6},{8,9},{9,8},{10,11... | collective-permute-start | bytes 196616 | tf_op jit(solution)/shard_map/ppermute | solution.py:21
  48.5 3.4 %collective-permute-start.22 = (f32[1,8,128]{2,1,0:T(8,128)S(1)}, f32[1,8,128]{2,1,0:T(8,128)S(1)}, u32[]{:S(2)}, u32[]{:S(2)}) collective-permute-start(f32[1,8,128]{2,1,0:T(8,128)S(1)} %get-tuple-element.23), channel_id=1, source_target_pairs={{0,8},{1,9},{2,10},{3,11},{4,12},{5,13},{6,14},{7,15},{8,0},{9,1},... | collective-permute-start | bytes 12296 | tf_op jit(solution)/shard_map/ppermute | solution.py:35
  48.6 5.2 %collective-permute-start.25 = (f32[1,8,128]{2,1,0:T(8,128)S(1)}, f32[1,8,128]{2,1,0:T(8,128)S(1)}, u32[]{:S(2)}, u32[]{:S(2)}) collective-permute-start(f32[1,8,128]{2,1,0:T(8,128)S(1)} %get-tuple-element.23), channel_id=1, source_target_pairs={{0,11},{1,10},{2,9},{3,8},{4,15},{5,14},{6,13},{7,12},{8,3},{9,2},... | collective-permute-start | bytes 12296 | tf_op jit(solution)/shard_map/ppermute | solution.py:35
  50.6 3.2 %collective-permute-start.24 = (f32[1,8,128]{2,1,0:T(8,128)S(1)}, f32[1,8,128]{2,1,0:T(8,128)S(1)}, u32[]{:S(2)}, u32[]{:S(2)}) collective-permute-start(f32[1,8,128]{2,1,0:T(8,128)S(1)} %get-tuple-element.23), channel_id=1, source_target_pairs={{0,10},{1,11},{2,8},{3,9},{4,14},{5,15},{6,12},{7,13},{8,2},{9,3},... | collective-permute-start | bytes 12296 | tf_op jit(solution)/shard_map/ppermute | solution.py:35
  50.7 3.0 %collective-permute-start.23 = (f32[1,8,128]{2,1,0:T(8,128)S(1)}, f32[1,8,128]{2,1,0:T(8,128)S(1)}, u32[]{:S(2)}, u32[]{:S(2)}) collective-permute-start(f32[1,8,128]{2,1,0:T(8,128)S(1)} %get-tuple-element.23), channel_id=1, source_target_pairs={{0,9},{1,8},{2,11},{3,10},{4,13},{5,12},{6,15},{7,14},{8,1},{9,0},... | collective-permute-start | bytes 12296 | tf_op jit(solution)/shard_map/ppermute | solution.py:35
  53.8 4.1 %collective-permute-start.27 = (f32[4,8,128]{2,1,0:T(8,128)S(1)}, f32[4,8,128]{2,1,0:T(8,128)S(1)}, u32[]{:S(2)}, u32[]{:S(2)}) collective-permute-start(f32[4,8,128]{2,1,0:T(8,128)S(1)} %constant_dynamic-update-slice_fusion), channel_id=1, source_target_pairs={{0,12},{1,13},{2,14},{3,15},{4,8},{5,9},{6,10},{7,11},{8,4},{9,5},... | collective-permute-start | bytes 49160 | tf_op jit(solution)/shard_map/ppermute | solution.py:35
  55.7 2.2 %collective-permute-start.26 = (f32[4,8,128]{2,1,0:T(8,128)S(1)}, f32[4,8,128]{2,1,0:T(8,128)S(1)}, u32[]{:S(2)}, u32[]{:S(2)}) collective-permute-start(f32[4,8,128]{2,1,0:T(8,128)S(1)} %constant_dynamic-update-slice_fusion), channel_id=1, source_target_pairs={{0,8},{1,9},{2,10},{3,11},{4,12},{5,13},{6,14},{7,15},{8,0},{9,1},... | collective-permute-start | bytes 49160 | tf_op jit(solution)/shard_map/ppermute | solution.py:35

commit v8 on v7

--- a/solution.py
+++ b/solution.py
@@ -224,7 +224,7 @@
     kept_sq = jnp.zeros_like(total)
     for row in rows:
         shift = STEP * (total - row[2:3, :])
-        kept_sq += row[3:4, :] + 2.0 * shift * row[4:5, :] + shift * shift * row[5:6, :]
+        kept_sq += row[3:4, :] + shift * (2.0 * row[4:5, :] + shift * row[5:6, :])
     column = lax.broadcasted_iota(jnp.int32, total.shape, 1)
     listed = total
     for step, energy in enumerate(earlier):

time: 58.7 us -> 58.7 us (level)
  no operation moved by 1% of the time
where the time goes in v8:
time: 58.7 us; the launch traced here: 58.6 us
  starting transfers between devices  35.5 us (60%)
  waiting for transfers between devices  13.2 us (22%)
  Pallas kernels  9.16 us (16%)
  between operations  0.73 us (1%)
    ppermute x21, starting transfers between devices, hop(): return lax.ppermute(block, 'sec', [(a, a ^ distance) for a in range(count)])  29.3 us
    ppermute x21, waiting for transfers between devices, hop(): return lax.ppermute(block, 'sec', [(a, a ^ distance) for a in range(count)])  9.51 us
    ppermute x6, starting transfers between devices, cross(): return lax.ppermute(block, ('seg', 'sec'), route)  5.65 us
    ppermute x6, waiting for transfers between devices, cross(): return lax.ppermute(block, ('seg', 'sec'), route)  3.71 us
    pallas_call x1, Pallas kernels, local(): pl.pallas_call(functools.partial(last_kernel, len(states), len(images)),...  2.62 us
    pallas_call x1, Pallas kernels, local(): pl.pallas_call(functools.partial(middle_kernel, len(states), len(images))...  2.36 us
    pallas_call x1, Pallas kernels, local(): pl.pallas_call(functools.partial(first_kernel, len(states)), out_shape=ow...  1.99 us
    pallas_call x1, Pallas kernels, local(): pl.pallas_call(functools.partial(prepare_kernel, devices), out_shape=(int...  1.49 us
  transfers between devices with their start and end apart: 28, of which 12 were waited for; matrix products, arithmetic and copies ran while one was open for 0% of the time, Pallas kernels for 3%

profile of v8, /device:TPU:0, one launch (start us, length us, event | category | flops | bytes accessed | tf_op | source)
XLA Modules:
  0.0 58.6 jit_solution(501932268893212035)
XLA Ops:
  0.6 0.5 collective-permute-start
  1.2 3.7 %collective-permute-start.1 = (bf16[2,128,128]{2,1,0:T(8,128)(2,1)}, bf16[2,128,128]{2,1,0:T(8,128)(2,1)S(1)}, u32[]{:S(2)}, u32[]{:S(2)}) collective-permute-start(bf16[2,128,128]{2,1,0:T(8,128)(2,1)} %bitcast.7), channel_id=1, source_target_pairs={{0,4},{1,5},{2,6},{3,7},{4,0},{5,1},{6,2},{7,3},{8,12},{9,13},{10,... | collective-permute-start | bytes 196616 | tf_op jit(solution)/shard_map/ppermute | solution.py:21
  4.8 1.5 %collective-permute-start.4 = (bf16[2,128,128]{2,1,0:T(8,128)(2,1)}, bf16[2,128,128]{2,1,0:T(8,128)(2,1)S(1)}, u32[]{:S(2)}, u32[]{:S(2)}) collective-permute-start(bf16[2,128,128]{2,1,0:T(8,128)(2,1)} %bitcast.8), channel_id=1, source_target_pairs={{0,1},{1,0},{2,3},{3,2},{4,5},{5,4},{6,7},{7,6},{8,9},{9,8},{10,11... | collective-permute-start | bytes 196616 | tf_op jit(solution)/shard_map/ppermute | solution.py:21
  6.3 1.6 %collective-permute-start.3 = (bf16[2,128,128]{2,1,0:T(8,128)(2,1)}, bf16[2,128,128]{2,1,0:T(8,128)(2,1)S(1)}, u32[]{:S(2)}, u32[]{:S(2)}) collective-permute-start(bf16[2,128,128]{2,1,0:T(8,128)(2,1)} %bitcast.9), channel_id=1, source_target_pairs={{0,2},{1,3},{2,0},{3,1},{4,6},{5,7},{6,4},{7,5},{8,10},{9,11},{10,... | collective-permute-start | bytes 196616 | tf_op jit(solution)/shard_map/ppermute | solution.py:21
  7.9 0.4 collective-permute-start.2
  8.3 0.8 %collective-permute-done.1.refs_1_ = bf16[2,128,128]{2,1,0:T(8,128)(2,1)S(1)} collective-permute-done((bf16[2,128,128]{2,1,0:T(8,128)(2,1)}, bf16[2,128,128]{2,1,0:T(8,128)(2,1)S(1)}, u32[]{:S(2)}, u32[]{:S(2)}) %collective-permute-start.1) | collective-permute-done | bytes 65568 | tf_op jit(solution)/shard_map/ppermute | solution.py:21
  9.1 1.8 %collective-permute-start.7 = (bf16[2,128,128]{2,1,0:T(8,128)(2,1)S(1)}, bf16[2,128,128]{2,1,0:T(8,128)(2,1)S(1)}, u32[]{:S(2)}, u32[]{:S(2)}) collective-permute-start(bf16[2,128,128]{2,1,0:T(8,128)(2,1)S(1)} %collective-permute-done.1.refs_1_), channel_id=1, source_target_pairs={{0,3},{1,2},{2,1},{3,0},{4,7},{5,6},{6,5},{7,4},{8,11},{9,10},{10,... | collective-permute-start | bytes 196616 | tf_op jit(solution)/shard_map/ppermute | solution.py:21
  11.0 0.0 collective-permute-done.4.refs_4_
  11.0 1.1 %collective-permute-start.6 = (bf16[2,128,128]{2,1,0:T(8,128)(2,1)S(1)}, bf16[2,128,128]{2,1,0:T(8,128)(2,1)S(1)}, u32[]{:S(2)}, u32[]{:S(2)}) collective-permute-start(bf16[2,128,128]{2,1,0:T(8,128)(2,1)S(1)} %collective-permute-done.1.refs_1_), channel_id=1, source_target_pairs={{0,2},{1,3},{2,0},{3,1},{4,6},{5,7},{6,4},{7,5},{8,10},{9,11},{10,... | collective-permute-start | bytes 196616 | tf_op jit(solution)/shard_map/ppermute | solution.py:21
  12.1 0.0 collective-permute-done.3.refs_3_
  12.1 0.5 collective-permute-start.5
  12.6 1.5 %prepare.1 = (s32[2,32]{1,0:T(2,128)S(1)}, f32[2,32]{1,0:T(2,128)S(1)}, bf16[2,24,128,128]{3,2,1,0:T(8,128)(2,1)S(1)}) custom-call(s32[2,32]{1,0:T(2,128)} %bitcast.14, s32[2,32]{1,0:T(2,128)} %bitcast.15, f32[2,32]{1,0:T(2,128)} %bitcast.16, bf16[2,24,128,128]{3,2,1,0:T(8,128)(2,1)} %bitcast.13), custom_call_target="tpu_custom_call" | custom-call | tf_op jit(solution)/shard_map/prepare/pallas_call | solution.py:252
  14.1 0.7 %collective-permute-done.7.refs_7_ = bf16[2,128,128]{2,1,0:T(8,128)(2,1)S(1)} collective-permute-done((bf16[2,128,128]{2,1,0:T(8,128)(2,1)S(1)}, bf16[2,128,128]{2,1,0:T(8,128)(2,1)S(1)}, u32[]{:S(2)}, u32[]{:S(2)}) %collective-permute-start.7) | collective-permute-done | bytes 65568 | tf_op jit(solution)/shard_map/ppermute | solution.py:21
  14.8 0.6 %collective-permute-done.6.refs_6_ = bf16[2,128,128]{2,1,0:T(8,128)(2,1)S(1)} collective-permute-done((bf16[2,128,128]{2,1,0:T(8,128)(2,1)S(1)}, bf16[2,128,128]{2,1,0:T(8,128)(2,1)S(1)}, u32[]{:S(2)}, u32[]{:S(2)}) %collective-permute-start.6) | collective-permute-done | bytes 65568 | tf_op jit(solution)/shard_map/ppermute | solution.py:21
  15.5 0.9 %collective-permute-done.5.refs_5_ = bf16[2,128,128]{2,1,0:T(8,128)(2,1)S(1)} collective-permute-done((bf16[2,128,128]{2,1,0:T(8,128)(2,1)S(1)}, bf16[2,128,128]{2,1,0:T(8,128)(2,1)S(1)}, u32[]{:S(2)}, u32[]{:S(2)}) %collective-permute-start.5) | collective-permute-done | bytes 65568 | tf_op jit(solution)/shard_map/ppermute | solution.py:21
  16.4 2.0 %first_image.1.refs_8_ = bf16[2,128,128]{2,1,0:T(8,128)(2,1)S(1)} custom-call(s32[2,32]{1,0:T(2,128)S(1)} %get-tuple-element.14.codes, f32[2,32]{1,0:T(2,128)S(1)} %get-tuple-element.15.factors, bf16[2,24,128,128]{3,2,1,0:T(8,128)(2,1)S(1)} %get-tuple-element.16.left, bf16[2,24,128,128]{3,2,1,0:T(8,128)(2,1)S(1)} %collective-permute-done.right, ...), custom_call_target="tpu_custom_call" | custom-call | tf_op jit(solution)/shard_map/first_image/pallas_call | solution.py:273
  18.4 0.0 copy-start.1
  18.4 2.4 %collective-permute-start.8 = (bf16[2,128,128]{2,1,0:T(8,128)(2,1)S(1)}, bf16[2,128,128]{2,1,0:T(8,128)(2,1)S(1)}, u32[]{:S(2)}, u32[]{:S(2)}) collective-permute-start(bf16[2,128,128]{2,1,0:T(8,128)(2,1)S(1)} %first_image.1.refs_8_), channel_id=1, source_target_pairs={{0,4},{1,5},{2,6},{3,7},{4,0},{5,1},{6,2},{7,3},{8,12},{9,13},{10,... | collective-permute-start | bytes 196616 | tf_op jit(solution)/shard_map/ppermute | solution.py:21
  20.7 0.5 collective-permute-start.11
  21.2 2.0 %collective-permute-start.10 = (bf16[2,128,128]{2,1,0:T(8,128)(2,1)S(1)}, bf16[2,128,128]{2,1,0:T(8,128)(2,1)S(1)}, u32[]{:S(2)}, u32[]{:S(2)}) collective-permute-start(bf16[2,128,128]{2,1,0:T(8,128)(2,1)S(1)} %first_image.1.refs_8_), channel_id=1, source_target_pairs={{0,2},{1,3},{2,0},{3,1},{4,6},{5,7},{6,4},{7,5},{8,10},{9,11},{10,... | collective-permute-start | bytes 196616 | tf_op jit(solution)/shard_map/ppermute | solution.py:21
  23.3 1.0 %collective-permute-start.9 = (bf16[2,128,128]{2,1,0:T(8,128)(2,1)S(1)}, bf16[2,128,128]{2,1,0:T(8,128)(2,1)S(1)}, u32[]{:S(2)}, u32[]{:S(2)}) collective-permute-start(bf16[2,128,128]{2,1,0:T(8,128)(2,1)S(1)} %first_image.1.refs_8_), channel_id=1, source_target_pairs={{0,3},{1,2},{2,1},{3,0},{4,7},{5,6},{6,5},{7,4},{8,11},{9,10},{10,... | collective-permute-start | bytes 196616 | tf_op jit(solution)/shard_map/ppermute | solution.py:21
  24.2 2.0 %collective-permute-start.14 = (bf16[2,128,128]{2,1,0:T(8,128)(2,1)S(1)}, bf16[2,128,128]{2,1,0:T(8,128)(2,1)S(1)}, u32[]{:S(2)}, u32[]{:S(2)}) collective-permute-start(bf16[2,128,128]{2,1,0:T(8,128)(2,1)S(1)} %collective-permute-done.8.refs_9_), channel_id=1, source_target_pairs={{0,3},{1,2},{2,1},{3,0},{4,7},{5,6},{6,5},{7,4},{8,11},{9,10},{10,... | collective-permute-start | bytes 196616 | tf_op jit(solution)/shard_map/ppermute | solution.py:21
  26.2 0.0 collective-permute-start.13
  26.2 1.5 %collective-permute-start.12 = (bf16[2,128,128]{2,1,0:T(8,128)(2,1)S(1)}, bf16[2,128,128]{2,1,0:T(8,128)(2,1)S(1)}, u32[]{:S(2)}, u32[]{:S(2)}) collective-permute-start(bf16[2,128,128]{2,1,0:T(8,128)(2,1)S(1)} %collective-permute-done.8.refs_9_), channel_id=1, source_target_pairs={{0,1},{1,0},{2,3},{3,2},{4,5},{5,4},{6,7},{7,6},{8,9},{9,8},{10,11... | collective-permute-start | bytes 196616 | tf_op jit(solution)/shard_map/ppermute | solution.py:21
  27.7 1.0 %collective-permute-done.9.refs_10_ = bf16[2,128,128]{2,1,0:T(8,128)(2,1)S(1)} collective-permute-done((bf16[2,128,128]{2,1,0:T(8,128)(2,1)S(1)}, bf16[2,128,128]{2,1,0:T(8,128)(2,1)S(1)}, u32[]{:S(2)}, u32[]{:S(2)}) %collective-permute-start.9) | collective-permute-done | bytes 65568 | tf_op jit(solution)/shard_map/ppermute | solution.py:21
  28.7 0.7 %collective-permute-done.14.refs_15_ = bf16[2,128,128]{2,1,0:T(8,128)(2,1)S(1)} collective-permute-done((bf16[2,128,128]{2,1,0:T(8,128)(2,1)S(1)}, bf16[2,128,128]{2,1,0:T(8,128)(2,1)S(1)}, u32[]{:S(2)}, u32[]{:S(2)}) %collective-permute-start.14) | collective-permute-done | bytes 65568 | tf_op jit(solution)/shard_map/ppermute | solution.py:21
  29.4 1.1 %collective-permute-done.13.refs_14_ = bf16[2,128,128]{2,1,0:T(8,128)(2,1)S(1)} collective-permute-done((bf16[2,128,128]{2,1,0:T(8,128)(2,1)S(1)}, bf16[2,128,128]{2,1,0:T(8,128)(2,1)S(1)}, u32[]{:S(2)}, u32[]{:S(2)}) %collective-permute-start.13) | collective-permute-done | bytes 65568 | tf_op jit(solution)/shard_map/ppermute | solution.py:21
  30.5 0.0 collective-permute-done.12.refs_13_
  30.5 2.4 %middle_image.1 = (f32[1,128]{1,0:T(1,128)S(1)}, f32[16,128,128]{2,1,0:T(8,128)S(1)}, bf16[2,128,128]{2,1,0:T(8,128)(2,1)S(1)}) custom-call(s32[2,32]{1,0:T(2,128)S(1)} %get-tuple-element.14.codes, f32[2,32]{1,0:T(2,128)S(1)} %get-tuple-element.15.factors, bf16[2,24,128,128]{3,2,1,0:T(8,128)(2,1)S(1)} %get-tuple-element.16.left, ...), custom_call_target="tpu_custom_call" | custom-call | tf_op jit(solution)/shard_map/middle_image/pallas_call | solution.py:285
  32.8 2.2 %collective-permute-start.15 = (bf16[2,128,128]{2,1,0:T(8,128)(2,1)S(1)}, bf16[2,128,128]{2,1,0:T(8,128)(2,1)S(1)}, u32[]{:S(2)}, u32[]{:S(2)}) collective-permute-start(bf16[2,128,128]{2,1,0:T(8,128)(2,1)S(1)} %get-tuple-element.18.refs_1_), channel_id=1, source_target_pairs={{0,4},{1,5},{2,6},{3,7},{4,0},{5,1},{6,2},{7,3},{8,12},{9,13},{10,... | collective-permute-start | bytes 196616 | tf_op jit(solution)/shard_map/ppermute | solution.py:21
  35.0 1.6 %collective-permute-start.18 = (bf16[2,128,128]{2,1,0:T(8,128)(2,1)S(1)}, bf16[2,128,128]{2,1,0:T(8,128)(2,1)S(1)}, u32[]{:S(2)}, u32[]{:S(2)}) collective-permute-start(bf16[2,128,128]{2,1,0:T(8,128)(2,1)S(1)} %get-tuple-element.18.refs_1_), channel_id=1, source_target_pairs={{0,1},{1,0},{2,3},{3,2},{4,5},{5,4},{6,7},{7,6},{8,9},{9,8},{10,11... | collective-permute-start | bytes 196616 | tf_op jit(solution)/shard_map/ppermute | solution.py:21
  36.6 1.9 %collective-permute-start.17 = (bf16[2,128,128]{2,1,0:T(8,128)(2,1)S(1)}, bf16[2,128,128]{2,1,0:T(8,128)(2,1)S(1)}, u32[]{:S(2)}, u32[]{:S(2)}) collective-permute-start(bf16[2,128,128]{2,1,0:T(8,128)(2,1)S(1)} %get-tuple-element.18.refs_1_), channel_id=1, source_target_pairs={{0,2},{1,3},{2,0},{3,1},{4,6},{5,7},{6,4},{7,5},{8,10},{9,11},{10,... | collective-permute-start | bytes 196616 | tf_op jit(solution)/shard_map/ppermute | solution.py:21
  38.5 3.1 %collective-permute-start.21 = (bf16[2,128,128]{2,1,0:T(8,128)(2,1)S(1)}, bf16[2,128,128]{2,1,0:T(8,128)(2,1)S(1)}, u32[]{:S(2)}, u32[]{:S(2)}) collective-permute-start(bf16[2,128,128]{2,1,0:T(8,128)(2,1)S(1)} %collective-permute-done.15.refs_2_), channel_id=1, source_target_pairs={{0,3},{1,2},{2,1},{3,0},{4,7},{5,6},{6,5},{7,4},{8,11},{9,10},{10,... | collective-permute-start | bytes 196616 | tf_op jit(solution)/shard_map/ppermute | solution.py:21
  41.6 0.6 collective-permute-start.19
  42.2 1.5 %collective-permute-done.16.refs_3_ = bf16[2,128,128]{2,1,0:T(8,128)(2,1)S(1)} collective-permute-done((bf16[2,128,128]{2,1,0:T(8,128)(2,1)S(1)}, bf16[2,128,128]{2,1,0:T(8,128)(2,1)S(1)}, u32[]{:S(2)}, u32[]{:S(2)}) %collective-permute-start.16) | collective-permute-done | bytes 65568 | tf_op jit(solution)/shard_map/ppermute | solution.py:21
  43.7 0.7 %collective-permute-done.21.refs_8_ = bf16[2,128,128]{2,1,0:T(8,128)(2,1)S(1)} collective-permute-done((bf16[2,128,128]{2,1,0:T(8,128)(2,1)S(1)}, bf16[2,128,128]{2,1,0:T(8,128)(2,1)S(1)}, u32[]{:S(2)}, u32[]{:S(2)}) %collective-permute-start.21) | collective-permute-done | bytes 65568 | tf_op jit(solution)/shard_map/ppermute | solution.py:21
  44.4 1.5 %collective-permute-done.20.refs_7_ = bf16[2,128,128]{2,1,0:T(8,128)(2,1)S(1)} collective-permute-done((bf16[2,128,128]{2,1,0:T(8,128)(2,1)S(1)}, bf16[2,128,128]{2,1,0:T(8,128)(2,1)S(1)}, u32[]{:S(2)}, u32[]{:S(2)}) %collective-permute-start.20) | collective-permute-done | bytes 65568 | tf_op jit(solution)/shard_map/ppermute | solution.py:21
  45.9 0.0 collective-permute-done.19.refs_6_
  45.9 2.6 %last_image.1 = (f32[1,128]{1,0:T(1,128)S(1)}, f32[2,128,128]{2,1,0:T(8,128)S(1)}, bf16[2,128,128]{2,1,0:T(8,128)(2,1)S(1)}, f32[1,8,128]{2,1,0:T(8,128)S(1)}) custom-call(s32[2,32]{1,0:T(2,128)S(1)} %get-tuple-element.14.codes, f32[2,32]{1,0:T(2,128)S(1)} %get-tuple-element.15.factors, s32[1,2]{1,0:T(1,128)S(1)} %copy-done.1, ...), custom_call_target="tpu_custom_call" | custom-call | tf_op jit(solution)/shard_map/last_image/pallas_call | solution.py:297
  48.5 0.1 collective-permute-start.22
  48.6 2.0 %collective-permute-start.25 = (f32[1,8,128]{2,1,0:T(8,128)S(1)}, f32[1,8,128]{2,1,0:T(8,128)S(1)}, u32[]{:S(2)}, u32[]{:S(2)}) collective-permute-start(f32[1,8,128]{2,1,0:T(8,128)S(1)} %get-tuple-element.23), channel_id=1, source_target_pairs={{0,11},{1,10},{2,9},{3,8},{4,15},{5,14},{6,13},{7,12},{8,3},{9,2},... | collective-permute-start | bytes 12296 | tf_op jit(solution)/shard_map/ppermute | solution.py:35
  50.6 0.2 collective-permute-start.24
  50.7 1.2 %collective-permute-start.23 = (f32[1,8,128]{2,1,0:T(8,128)S(1)}, f32[1,8,128]{2,1,0:T(8,128)S(1)}, u32[]{:S(2)}, u32[]{:S(2)}) collective-permute-start(f32[1,8,128]{2,1,0:T(8,128)S(1)} %get-tuple-element.23), channel_id=1, source_target_pairs={{0,9},{1,8},{2,11},{3,10},{4,13},{5,12},{6,15},{7,14},{8,1},{9,0},... | collective-permute-start | bytes 12296 | tf_op jit(solution)/shard_map/ppermute | solution.py:35
  51.9 1.8 %collective-permute-done.23 = f32[1,8,128]{2,1,0:T(8,128)S(1)} collective-permute-done((f32[1,8,128]{2,1,0:T(8,128)S(1)}, f32[1,8,128]{2,1,0:T(8,128)S(1)}, u32[]{:S(2)}, u32[]{:S(2)}) %collective-permute-start.23) | collective-permute-done | bytes 4128 | tf_op jit(solution)/shard_map/ppermute | solution.py:35
  53.8 1.9 %collective-permute-start.27 = (f32[4,8,128]{2,1,0:T(8,128)S(1)}, f32[4,8,128]{2,1,0:T(8,128)S(1)}, u32[]{:S(2)}, u32[]{:S(2)}) collective-permute-start(f32[4,8,128]{2,1,0:T(8,128)S(1)} %constant_dynamic-update-slice_fusion), channel_id=1, source_target_pairs={{0,12},{1,13},{2,14},{3,15},{4,8},{5,9},{6,10},{7,11},{8,4},{9,5},... | collective-permute-start | bytes 49160 | tf_op jit(solution)/shard_map/ppermute | solution.py:35
  55.7 0.4 collective-permute-start.26
  56.0 1.9 %collective-permute-done.27.refs_3_ = f32[4,8,128]{2,1,0:T(8,128)S(1)} collective-permute-done((f32[4,8,128]{2,1,0:T(8,128)S(1)}, f32[4,8,128]{2,1,0:T(8,128)S(1)}, u32[]{:S(2)}, u32[]{:S(2)}) %collective-permute-start.27) | collective-permute-done | bytes 16416 | tf_op jit(solution)/shard_map/ppermute | solution.py:35
  57.9 0.7 %finish.1 = (f32[1,3]{1,0:T(1,128)}, bf16[2,128,128]{2,1,0:T(8,128)(2,1)}) custom-call(f32[2,128,128]{2,1,0:T(8,128)S(1)} %get-tuple-element.19.own, bf16[2,128,128]{2,1,0:T(8,128)(2,1)S(1)} %get-tuple-element.20.image, f32[1,128]{1,0:T(1,128)S(1)} %get-tuple-element.21.refs_0_, f32[1,128]{1,0:T(1,128)S(1)} %get-tuple-element.22.refs_1_, ...), custom_call_target="tpu_custom_call" | custom-call | tf_op jit(solution)/shard_map/finish/pallas_call | solution.py:316
  (21 shorter events, 0.1 us)
Async XLA Ops:
  0.6 15.7 %copy-start = (bf16[1,2,128,128]{3,2,1,0:T(8,128)(2,1)S(1)}, bf16[1,2,128,128]{3,2,1,0:T(8,128)(2,1)}, u32[]{:S(2)}) copy-start(bf16[1,2,128,128]{3,2,1,0:T(8,128)(2,1)} %param.7) | copy-start | bytes 196612
  0.6 15.7 %collective-permute-start = (bf16[2,24,128,128]{3,2,1,0:T(8,128)(2,1)}, bf16[2,24,128,128]{3,2,1,0:T(8,128)(2,1)S(1)}, u32[]{:S(2)}, u32[]{:S(2)}) collective-permute-start(bf16[2,24,128,128]{3,2,1,0:T(8,128)(2,1)} %bitcast.17), channel_id=1, source_target_pairs={{0,8},{8,0},{1,9},{9,1},{2,10},{10,2},{3,11},{11,3},{4,12},{12,4},... | collective-permute-start | bytes 4718600 | tf_op jit(solution)/shard_map/ppermute | solution.py:242
  1.2 8.0 %collective-permute-start.1 = (bf16[2,128,128]{2,1,0:T(8,128)(2,1)}, bf16[2,128,128]{2,1,0:T(8,128)(2,1)S(1)}, u32[]{:S(2)}, u32[]{:S(2)}) collective-permute-start(bf16[2,128,128]{2,1,0:T(8,128)(2,1)} %bitcast.7), channel_id=1, source_target_pairs={{0,4},{1,5},{2,6},{3,7},{4,0},{5,1},{6,2},{7,3},{8,12},{9,13},{10,... | collective-permute-start | bytes 196616 | tf_op jit(solution)/shard_map/ppermute | solution.py:21
  4.8 6.1 %collective-permute-start.4 = (bf16[2,128,128]{2,1,0:T(8,128)(2,1)}, bf16[2,128,128]{2,1,0:T(8,128)(2,1)S(1)}, u32[]{:S(2)}, u32[]{:S(2)}) collective-permute-start(bf16[2,128,128]{2,1,0:T(8,128)(2,1)} %bitcast.8), channel_id=1, source_target_pairs={{0,1},{1,0},{2,3},{3,2},{4,5},{5,4},{6,7},{7,6},{8,9},{9,8},{10,11... | collective-permute-start | bytes 196616 | tf_op jit(solution)/shard_map/ppermute | solution.py:21
  6.3 5.7 %collective-permute-start.3 = (bf16[2,128,128]{2,1,0:T(8,128)(2,1)}, bf16[2,128,128]{2,1,0:T(8,128)(2,1)S(1)}, u32[]{:S(2)}, u32[]{:S(2)}) collective-permute-start(bf16[2,128,128]{2,1,0:T(8,128)(2,1)} %bitcast.9), channel_id=1, source_target_pairs={{0,2},{1,3},{2,0},{3,1},{4,6},{5,7},{6,4},{7,5},{8,10},{9,11},{10,... | collective-permute-start | bytes 196616 | tf_op jit(solution)/shard_map/ppermute | solution.py:21
  7.9 6.2 %collective-permute-start.2 = (bf16[2,128,128]{2,1,0:T(8,128)(2,1)}, bf16[2,128,128]{2,1,0:T(8,128)(2,1)S(1)}, u32[]{:S(2)}, u32[]{:S(2)}) collective-permute-start(bf16[2,128,128]{2,1,0:T(8,128)(2,1)} %bitcast.10), channel_id=1, source_target_pairs={{0,3},{1,2},{2,1},{3,0},{4,7},{5,6},{6,5},{7,4},{8,11},{9,10},{10,... | collective-permute-start | bytes 196616 | tf_op jit(solution)/shard_map/ppermute | solution.py:21
  9.1 5.7 %collective-permute-start.7 = (bf16[2,128,128]{2,1,0:T(8,128)(2,1)S(1)}, bf16[2,128,128]{2,1,0:T(8,128)(2,1)S(1)}, u32[]{:S(2)}, u32[]{:S(2)}) collective-permute-start(bf16[2,128,128]{2,1,0:T(8,128)(2,1)S(1)} %collective-permute-done.1.refs_1_), channel_id=1, source_target_pairs={{0,3},{1,2},{2,1},{3,0},{4,7},{5,6},{6,5},{7,4},{8,11},{9,10},{10,... | collective-permute-start | bytes 196616 | tf_op jit(solution)/shard_map/ppermute | solution.py:21
  11.0 4.5 %collective-permute-start.6 = (bf16[2,128,128]{2,1,0:T(8,128)(2,1)S(1)}, bf16[2,128,128]{2,1,0:T(8,128)(2,1)S(1)}, u32[]{:S(2)}, u32[]{:S(2)}) collective-permute-start(bf16[2,128,128]{2,1,0:T(8,128)(2,1)S(1)} %collective-permute-done.1.refs_1_), channel_id=1, source_target_pairs={{0,2},{1,3},{2,0},{3,1},{4,6},{5,7},{6,4},{7,5},{8,10},{9,11},{10,... | collective-permute-start | bytes 196616 | tf_op jit(solution)/shard_map/ppermute | solution.py:21
  12.1 4.3 %collective-permute-start.5 = (bf16[2,128,128]{2,1,0:T(8,128)(2,1)S(1)}, bf16[2,128,128]{2,1,0:T(8,128)(2,1)S(1)}, u32[]{:S(2)}, u32[]{:S(2)}) collective-permute-start(bf16[2,128,128]{2,1,0:T(8,128)(2,1)S(1)} %collective-permute-done.1.refs_1_), channel_id=1, source_target_pairs={{0,1},{1,0},{2,3},{3,2},{4,5},{5,4},{6,7},{7,6},{8,9},{9,8},{10,11... | collective-permute-start | bytes 196616 | tf_op jit(solution)/shard_map/ppermute | solution.py:21
  18.4 27.5 %copy-start.1 = (s32[1,2]{1,0:T(1,128)S(1)}, s32[1,2]{1,0:T(1,128)}, u32[]{:S(2)}) copy-start(s32[1,2]{1,0:T(1,128)} %ranks.1) | copy-start | bytes 28
  18.4 5.8 %collective-permute-start.8 = (bf16[2,128,128]{2,1,0:T(8,128)(2,1)S(1)}, bf16[2,128,128]{2,1,0:T(8,128)(2,1)S(1)}, u32[]{:S(2)}, u32[]{:S(2)}) collective-permute-start(bf16[2,128,128]{2,1,0:T(8,128)(2,1)S(1)} %first_image.1.refs_8_), channel_id=1, source_target_pairs={{0,4},{1,5},{2,6},{3,7},{4,0},{5,1},{6,2},{7,3},{8,12},{9,13},{10,... | collective-permute-start | bytes 196616 | tf_op jit(solution)/shard_map/ppermute | solution.py:21
  20.7 5.5 %collective-permute-start.11 = (bf16[2,128,128]{2,1,0:T(8,128)(2,1)S(1)}, bf16[2,128,128]{2,1,0:T(8,128)(2,1)S(1)}, u32[]{:S(2)}, u32[]{:S(2)}) collective-permute-start(bf16[2,128,128]{2,1,0:T(8,128)(2,1)S(1)} %first_image.1.refs_8_), channel_id=1, source_target_pairs={{0,1},{1,0},{2,3},{3,2},{4,5},{5,4},{6,7},{7,6},{8,9},{9,8},{10,11... | collective-permute-start | bytes 196616 | tf_op jit(solution)/shard_map/ppermute | solution.py:21
  21.2 6.5 %collective-permute-start.10 = (bf16[2,128,128]{2,1,0:T(8,128)(2,1)S(1)}, bf16[2,128,128]{2,1,0:T(8,128)(2,1)S(1)}, u32[]{:S(2)}, u32[]{:S(2)}) collective-permute-start(bf16[2,128,128]{2,1,0:T(8,128)(2,1)S(1)} %first_image.1.refs_8_), channel_id=1, source_target_pairs={{0,2},{1,3},{2,0},{3,1},{4,6},{5,7},{6,4},{7,5},{8,10},{9,11},{10,... | collective-permute-start | bytes 196616 | tf_op jit(solution)/shard_map/ppermute | solution.py:21
  23.3 5.4 %collective-permute-start.9 = (bf16[2,128,128]{2,1,0:T(8,128)(2,1)S(1)}, bf16[2,128,128]{2,1,0:T(8,128)(2,1)S(1)}, u32[]{:S(2)}, u32[]{:S(2)}) collective-permute-start(bf16[2,128,128]{2,1,0:T(8,128)(2,1)S(1)} %first_image.1.refs_8_), channel_id=1, source_target_pairs={{0,3},{1,2},{2,1},{3,0},{4,7},{5,6},{6,5},{7,4},{8,11},{9,10},{10,... | collective-permute-start | bytes 196616 | tf_op jit(solution)/shard_map/ppermute | solution.py:21
  24.2 5.2 %collective-permute-start.14 = (bf16[2,128,128]{2,1,0:T(8,128)(2,1)S(1)}, bf16[2,128,128]{2,1,0:T(8,128)(2,1)S(1)}, u32[]{:S(2)}, u32[]{:S(2)}) collective-permute-start(bf16[2,128,128]{2,1,0:T(8,128)(2,1)S(1)} %collective-permute-done.8.refs_9_), channel_id=1, source_target_pairs={{0,3},{1,2},{2,1},{3,0},{4,7},{5,6},{6,5},{7,4},{8,11},{9,10},{10,... | collective-permute-start | bytes 196616 | tf_op jit(solution)/shard_map/ppermute | solution.py:21
  26.2 4.3 %collective-permute-start.13 = (bf16[2,128,128]{2,1,0:T(8,128)(2,1)S(1)}, bf16[2,128,128]{2,1,0:T(8,128)(2,1)S(1)}, u32[]{:S(2)}, u32[]{:S(2)}) collective-permute-start(bf16[2,128,128]{2,1,0:T(8,128)(2,1)S(1)} %collective-permute-done.8.refs_9_), channel_id=1, source_target_pairs={{0,2},{1,3},{2,0},{3,1},{4,6},{5,7},{6,4},{7,5},{8,10},{9,11},{10,... | collective-permute-start | bytes 196616 | tf_op jit(solution)/shard_map/ppermute | solution.py:21
  26.2 4.3 %collective-permute-start.12 = (bf16[2,128,128]{2,1,0:T(8,128)(2,1)S(1)}, bf16[2,128,128]{2,1,0:T(8,128)(2,1)S(1)}, u32[]{:S(2)}, u32[]{:S(2)}) collective-permute-start(bf16[2,128,128]{2,1,0:T(8,128)(2,1)S(1)} %collective-permute-done.8.refs_9_), channel_id=1, source_target_pairs={{0,1},{1,0},{2,3},{3,2},{4,5},{5,4},{6,7},{7,6},{8,9},{9,8},{10,11... | collective-permute-start | bytes 196616 | tf_op jit(solution)/shard_map/ppermute | solution.py:21
  32.8 5.7 %collective-permute-start.15 = (bf16[2,128,128]{2,1,0:T(8,128)(2,1)S(1)}, bf16[2,128,128]{2,1,0:T(8,128)(2,1)S(1)}, u32[]{:S(2)}, u32[]{:S(2)}) collective-permute-start(bf16[2,128,128]{2,1,0:T(8,128)(2,1)S(1)} %get-tuple-element.18.refs_1_), channel_id=1, source_target_pairs={{0,4},{1,5},{2,6},{3,7},{4,0},{5,1},{6,2},{7,3},{8,12},{9,13},{10,... | collective-permute-start | bytes 196616 | tf_op jit(solution)/shard_map/ppermute | solution.py:21
  35.0 6.6 %collective-permute-start.18 = (bf16[2,128,128]{2,1,0:T(8,128)(2,1)S(1)}, bf16[2,128,128]{2,1,0:T(8,128)(2,1)S(1)}, u32[]{:S(2)}, u32[]{:S(2)}) collective-permute-start(bf16[2,128,128]{2,1,0:T(8,128)(2,1)S(1)} %get-tuple-element.18.refs_1_), channel_id=1, source_target_pairs={{0,1},{1,0},{2,3},{3,2},{4,5},{5,4},{6,7},{7,6},{8,9},{9,8},{10,11... | collective-permute-start | bytes 196616 | tf_op jit(solution)/shard_map/ppermute | solution.py:21
  36.6 5.6 %collective-permute-start.17 = (bf16[2,128,128]{2,1,0:T(8,128)(2,1)S(1)}, bf16[2,128,128]{2,1,0:T(8,128)(2,1)S(1)}, u32[]{:S(2)}, u32[]{:S(2)}) collective-permute-start(bf16[2,128,128]{2,1,0:T(8,128)(2,1)S(1)} %get-tuple-element.18.refs_1_), channel_id=1, source_target_pairs={{0,2},{1,3},{2,0},{3,1},{4,6},{5,7},{6,4},{7,5},{8,10},{9,11},{10,... | collective-permute-start | bytes 196616 | tf_op jit(solution)/shard_map/ppermute | solution.py:21
  38.5 5.2 %collective-permute-start.16 = (bf16[2,128,128]{2,1,0:T(8,128)(2,1)S(1)}, bf16[2,128,128]{2,1,0:T(8,128)(2,1)S(1)}, u32[]{:S(2)}, u32[]{:S(2)}) collective-permute-start(bf16[2,128,128]{2,1,0:T(8,128)(2,1)S(1)} %get-tuple-element.18.refs_1_), channel_id=1, source_target_pairs={{0,3},{1,2},{2,1},{3,0},{4,7},{5,6},{6,5},{7,4},{8,11},{9,10},{10,... | collective-permute-start | bytes 196616 | tf_op jit(solution)/shard_map/ppermute | solution.py:21
  38.5 5.9 %collective-permute-start.21 = (bf16[2,128,128]{2,1,0:T(8,128)(2,1)S(1)}, bf16[2,128,128]{2,1,0:T(8,128)(2,1)S(1)}, u32[]{:S(2)}, u32[]{:S(2)}) collective-permute-start(bf16[2,128,128]{2,1,0:T(8,128)(2,1)S(1)} %collective-permute-done.15.refs_2_), channel_id=1, source_target_pairs={{0,3},{1,2},{2,1},{3,0},{4,7},{5,6},{6,5},{7,4},{8,11},{9,10},{10,... | collective-permute-start | bytes 196616 | tf_op jit(solution)/shard_map/ppermute | solution.py:21
  41.6 4.3 %collective-permute-start.20 = (bf16[2,128,128]{2,1,0:T(8,128)(2,1)S(1)}, bf16[2,128,128]{2,1,0:T(8,128)(2,1)S(1)}, u32[]{:S(2)}, u32[]{:S(2)}) collective-permute-start(bf16[2,128,128]{2,1,0:T(8,128)(2,1)S(1)} %collective-permute-done.15.refs_2_), channel_id=1, source_target_pairs={{0,2},{1,3},{2,0},{3,1},{4,6},{5,7},{6,4},{7,5},{8,10},{9,11},{10,... | collective-permute-start | bytes 196616 | tf_op jit(solution)/shard_map/ppermute | solution.py:21
  41.6 4.3 %collective-permute-start.19 = (bf16[2,128,128]{2,1,0:T(8,128)(2,1)S(1)}, bf16[2,128,128]{2,1,0:T(8,128)(2,1)S(1)}, u32[]{:S(2)}, u32[]{:S(2)}) collective-permute-start(bf16[2,128,128]{2,1,0:T(8,128)(2,1)S(1)} %collective-permute-done.15.refs_2_), channel_id=1, source_target_pairs={{0,1},{1,0},{2,3},{3,2},{4,5},{5,4},{6,7},{7,6},{8,9},{9,8},{10,11... | collective-permute-start | bytes 196616 | tf_op jit(solution)/shard_map/ppermute | solution.py:21
  48.5 3.4 %collective-permute-start.22 = (f32[1,8,128]{2,1,0:T(8,128)S(1)}, f32[1,8,128]{2,1,0:T(8,128)S(1)}, u32[]{:S(2)}, u32[]{:S(2)}) collective-permute-start(f32[1,8,128]{2,1,0:T(8,128)S(1)} %get-tuple-element.23), channel_id=1, source_target_pairs={{0,8},{1,9},{2,10},{3,11},{4,12},{5,13},{6,14},{7,15},{8,0},{9,1},... | collective-permute-start | bytes 12296 | tf_op jit(solution)/shard_map/ppermute | solution.py:35
  48.6 5.2 %collective-permute-start.25 = (f32[1,8,128]{2,1,0:T(8,128)S(1)}, f32[1,8,128]{2,1,0:T(8,128)S(1)}, u32[]{:S(2)}, u32[]{:S(2)}) collective-permute-start(f32[1,8,128]{2,1,0:T(8,128)S(1)} %get-tuple-element.23), channel_id=1, source_target_pairs={{0,11},{1,10},{2,9},{3,8},{4,15},{5,14},{6,13},{7,12},{8,3},{9,2},... | collective-permute-start | bytes 12296 | tf_op jit(solution)/shard_map/ppermute | solution.py:35
  50.6 3.2 %collective-permute-start.24 = (f32[1,8,128]{2,1,0:T(8,128)S(1)}, f32[1,8,128]{2,1,0:T(8,128)S(1)}, u32[]{:S(2)}, u32[]{:S(2)}) collective-permute-start(f32[1,8,128]{2,1,0:T(8,128)S(1)} %get-tuple-element.23), channel_id=1, source_target_pairs={{0,10},{1,11},{2,8},{3,9},{4,14},{5,15},{6,12},{7,13},{8,2},{9,3},... | collective-permute-start | bytes 12296 | tf_op jit(solution)/shard_map/ppermute | solution.py:35
  50.7 3.0 %collective-permute-start.23 = (f32[1,8,128]{2,1,0:T(8,128)S(1)}, f32[1,8,128]{2,1,0:T(8,128)S(1)}, u32[]{:S(2)}, u32[]{:S(2)}) collective-permute-start(f32[1,8,128]{2,1,0:T(8,128)S(1)} %get-tuple-element.23), channel_id=1, source_target_pairs={{0,9},{1,8},{2,11},{3,10},{4,13},{5,12},{6,15},{7,14},{8,1},{9,0},... | collective-permute-start | bytes 12296 | tf_op jit(solution)/shard_map/ppermute | solution.py:35
  53.8 4.1 %collective-permute-start.27 = (f32[4,8,128]{2,1,0:T(8,128)S(1)}, f32[4,8,128]{2,1,0:T(8,128)S(1)}, u32[]{:S(2)}, u32[]{:S(2)}) collective-permute-start(f32[4,8,128]{2,1,0:T(8,128)S(1)} %constant_dynamic-update-slice_fusion), channel_id=1, source_target_pairs={{0,12},{1,13},{2,14},{3,15},{4,8},{5,9},{6,10},{7,11},{8,4},{9,5},... | collective-permute-start | bytes 49160 | tf_op jit(solution)/shard_map/ppermute | solution.py:35
  55.7 2.2 %collective-permute-start.26 = (f32[4,8,128]{2,1,0:T(8,128)S(1)}, f32[4,8,128]{2,1,0:T(8,128)S(1)}, u32[]{:S(2)}, u32[]{:S(2)}) collective-permute-start(f32[4,8,128]{2,1,0:T(8,128)S(1)} %constant_dynamic-update-slice_fusion), channel_id=1, source_target_pairs={{0,8},{1,9},{2,10},{3,11},{4,12},{5,13},{6,14},{7,15},{8,0},{9,1},... | collective-permute-start | bytes 49160 | tf_op jit(solution)/shard_map/ppermute | solution.py:35

commit v9 on v8

--- a/solution.py
+++ b/solution.py
@@ -14,6 +14,7 @@
 VMEM = pl.BlockSpec(memory_space=pltpu.VMEM)
 HBM = pl.BlockSpec(memory_space=pltpu.HBM)
 APART = (0, 4, 3, 2, 1, 5, 6, 7)
+EARLY = 5
 
 
 def hop(block, distance):
@@ -147,40 +148,60 @@
     apply_operator(codes[...], factors[...], state, left, right, mixed, image)
 
 
-def rayleigh_update(before, images, after):
+def sector_refs(pieces):
+    return [(piece, s) for piece in pieces for s in range(piece.shape[0])]
+
+
+def early_kernel(states, *refs):
+    before, images, sums = refs[:states], refs[states:-1], refs[-1]
+    intersection = jnp.zeros(before[0].shape[1:], jnp.float32)
+    squares = jnp.zeros(before[0].shape[1:], jnp.float32)
+    pictures = sector_refs(images)
+    for at, (piece, s) in enumerate(sector_refs(before)):
+        value = piece[s].astype(jnp.float32)
+        squares += value * value
+        if at < len(pictures):
+            picture, p = pictures[at]
+            intersection += value * picture[p].astype(jnp.float32)
+    for at, total in enumerate((intersection, squares)):
+        sums[at] = jnp.sum(total.reshape(-1, 8, total.shape[1]), axis=0)
+
+
+def rayleigh_update(before, images, early, after):
     shape = before[0].shape[1:]
+    flat, pictures = sector_refs(before), sector_refs(images)
+    done = len(sector_refs(images[:EARLY])) if len(images) > EARLY else 0
     intersection = jnp.zeros(shape, jnp.float32)
     squares = jnp.zeros(shape, jnp.float32)
-    at = 0
-    flat = []
-    for piece in before:
-        flat += [(piece, s) for s in range(piece.shape[0])]
-    pictures = []
-    for piece in images:
-        pictures += [(piece, s) for s in range(piece.shape[0])]
-    for (piece, s), (picture, p) in zip(flat, pictures):
+    for at, ((piece, s), (picture, p)) in enumerate(zip(flat, pictures)):
+        if at < done:
+            continue
         value = piece[s].astype(jnp.float32)
         intersection += value * picture[p].astype(jnp.float32)
-        squares += value * value
-    energy = jnp.sum(intersection, keepdims=True) / jnp.sum(squares, keepdims=True)
+        if done == 0:
+            squares += value * value
+    if done == 0:
+        energy = jnp.sum(intersection, keepdims=True) / jnp.sum(squares, keepdims=True)
+    else:
+        late = jnp.sum(intersection.reshape(-1, 8, shape[1]), axis=0)
+        energy = jnp.sum(early[0] + late, keepdims=True) / jnp.sum(early[1], keepdims=True)
     growth = 1.0 + STEP * energy
-    for (piece, s), (picture, p) in zip(flat, pictures):
+    for at, ((piece, s), (picture, p)) in enumerate(zip(flat, pictures)):
         after[at] = growth * piece[s].astype(jnp.float32) - STEP * picture[p].astype(jnp.float32)
-        at += 1
     return energy
 
 
-def middle_kernel(states, count, codes, factors, left, right, *refs):
+def middle_kernel(states, count, early, codes, factors, left, right, *refs):
     before, images = refs[:states], refs[states : states + count]
     energy, state, image, *mixed = refs[states + count :]
-    energy[...] = jnp.broadcast_to(rayleigh_update(before, images, state), energy.shape)
+    energy[...] = jnp.broadcast_to(rayleigh_update(before, images, early, state), energy.shape)
     apply_operator(codes[...], factors[...], state, left, right, mixed, image)
 
 
-def last_kernel(states, count, codes, factors, ranks, left, right, *refs):
+def last_kernel(states, count, early, codes, factors, ranks, left, right, *refs):
     before, images = refs[:states], refs[states : states + count]
     energy, own, image, sums, state, *mixed = refs[states + count :]
-    energy[...] = jnp.broadcast_to(rayleigh_update(before, images, state), energy.shape)
+    energy[...] = jnp.broadcast_to(rayleigh_update(before, images, early, state), energy.shape)
     apply_operator(codes[...], factors[...], state, left, right, mixed, image)
     blocks, size = image.shape[0], image.shape[1]
     first = first_slot(blocks)
@@ -280,17 +301,29 @@
         name="first_image",
     )(codes, factors, left, right, *states)
     energies = []
+
+    def early_sums(states, images):
+        images = images[:EARLY] if len(images) > EARLY else images
+        return pl.pallas_call(
+            functools.partial(early_kernel, len(states)),
+            out_shape=jax.ShapeDtypeStruct((2, 8, size), jnp.float32),
+            in_specs=[VMEM] * (len(states) + len(images)),
+            out_specs=VMEM,
+            compiler_params=params,
+            name="early_sums",
+        )(*states, *images)
+
     for _ in range(1, ITERS - 1):
         images = gather(image)
         energy, state, image = pl.pallas_call(
             functools.partial(middle_kernel, len(states), len(images)),
             out_shape=(number, jax.ShapeDtypeStruct(whole, jnp.float32), own_type),
-            in_specs=[VMEM] * (4 + len(states) + len(images)),
+            in_specs=[VMEM] * (5 + len(states) + len(images)),
             out_specs=(VMEM, VMEM, VMEM),
             scratch_shapes=mixed,
             compiler_params=params,
             name="middle_image",
-        )(codes, factors, left, right, *states, *images)
+        )(early_sums(states, images), codes, factors, left, right, *states, *images)
         states = [state]
         energies.append(energy)
     images = gather(image)
@@ -302,7 +335,7 @@
             own_type,
             jax.ShapeDtypeStruct((1, 8, 128), jnp.float32),
         ),
-        in_specs=[VMEM] * (5 + len(states) + len(images)),
+        in_specs=[VMEM] * (6 + len(states) + len(images)),
         out_specs=(VMEM, VMEM, VMEM, VMEM),
         scratch_shapes=[
             pltpu.VMEM(whole, jnp.float32),
@@ -310,7 +343,7 @@
         ],
         compiler_params=params,
         name="last_image",
-    )(codes, factors, kept_rank, left, right, *states, *images)
+    )(early_sums(states, images), codes, factors, kept_rank, left, right, *states, *images)
     energies.append(energy)
     gathered = gather_small(sums)
     energies, kept = pl.pallas_call(

time: 58.7 us -> 58.5 us (level)
  no operation moved by 1% of the time
where the time goes in v9:
time: 58.5 us; the launch traced here: 58.3 us
  starting transfers between devices  35.5 us (61%)
  waiting for transfers between devices  12.9 us (22%)
  Pallas kernels  9.17 us (16%)
  between operations  0.74 us (1%)
    ppermute x21, starting transfers between devices, hop(): return lax.ppermute(block, 'sec', [(a, a ^ distance) for a in range(count)])  29.3 us
    ppermute x21, waiting for transfers between devices, hop(): return lax.ppermute(block, 'sec', [(a, a ^ distance) for a in range(count)])  9.2 us
    ppermute x6, starting transfers between devices, cross(): return lax.ppermute(block, ('seg', 'sec'), route)  5.64 us
    ppermute x6, waiting for transfers between devices, cross(): return lax.ppermute(block, ('seg', 'sec'), route)  3.73 us
    pallas_call x1, Pallas kernels, local(): pl.pallas_call(functools.partial(last_kernel, len(states), len(images)),...  2.49 us
    pallas_call x1, Pallas kernels, local(): pl.pallas_call(functools.partial(middle_kernel, len(states), len(images))...  2.21 us
    pallas_call x1, Pallas kernels, local(): pl.pallas_call(functools.partial(first_kernel, len(states)), out_shape=ow...  1.99 us
    pallas_call x1, Pallas kernels, local(): pl.pallas_call(functools.partial(prepare_kernel, devices), out_shape=(int...  1.49 us
  transfers between devices with their start and end apart: 28, of which 12 were waited for; matrix products, arithmetic and copies ran while one was open for 0% of the time, Pallas kernels for 3%

profile of v9, /device:TPU:0, one launch (start us, length us, event | category | flops | bytes accessed | tf_op | source)
XLA Modules:
  0.0 58.3 jit_solution(1229868280389032293)
XLA Ops:
  0.6 0.5 collective-permute-start.7
  1.2 3.7 %collective-permute-start = (bf16[2,128,128]{2,1,0:T(8,128)(2,1)}, bf16[2,128,128]{2,1,0:T(8,128)(2,1)S(1)}, u32[]{:S(2)}, u32[]{:S(2)}) collective-permute-start(bf16[2,128,128]{2,1,0:T(8,128)(2,1)} %bitcast.7), channel_id=1, source_target_pairs={{0,4},{1,5},{2,6},{3,7},{4,0},{5,1},{6,2},{7,3},{8,12},{9,13},{10,... | collective-permute-start | bytes 196616 | tf_op jit(solution)/shard_map/ppermute | solution.py:22
  4.8 1.5 %collective-permute-start.3 = (bf16[2,128,128]{2,1,0:T(8,128)(2,1)}, bf16[2,128,128]{2,1,0:T(8,128)(2,1)S(1)}, u32[]{:S(2)}, u32[]{:S(2)}) collective-permute-start(bf16[2,128,128]{2,1,0:T(8,128)(2,1)} %bitcast.8), channel_id=1, source_target_pairs={{0,1},{1,0},{2,3},{3,2},{4,5},{5,4},{6,7},{7,6},{8,9},{9,8},{10,11... | collective-permute-start | bytes 196616 | tf_op jit(solution)/shard_map/ppermute | solution.py:22
  6.3 1.6 %collective-permute-start.2 = (bf16[2,128,128]{2,1,0:T(8,128)(2,1)}, bf16[2,128,128]{2,1,0:T(8,128)(2,1)S(1)}, u32[]{:S(2)}, u32[]{:S(2)}) collective-permute-start(bf16[2,128,128]{2,1,0:T(8,128)(2,1)} %bitcast.9), channel_id=1, source_target_pairs={{0,2},{1,3},{2,0},{3,1},{4,6},{5,7},{6,4},{7,5},{8,10},{9,11},{10,... | collective-permute-start | bytes 196616 | tf_op jit(solution)/shard_map/ppermute | solution.py:22
  7.9 0.4 collective-permute-start.1
  8.3 0.8 %collective-permute-done.refs_1_ = bf16[2,128,128]{2,1,0:T(8,128)(2,1)S(1)} collective-permute-done((bf16[2,128,128]{2,1,0:T(8,128)(2,1)}, bf16[2,128,128]{2,1,0:T(8,128)(2,1)S(1)}, u32[]{:S(2)}, u32[]{:S(2)}) %collective-permute-start) | collective-permute-done | bytes 65568 | tf_op jit(solution)/shard_map/ppermute | solution.py:22
  9.1 1.8 %collective-permute-start.6 = (bf16[2,128,128]{2,1,0:T(8,128)(2,1)S(1)}, bf16[2,128,128]{2,1,0:T(8,128)(2,1)S(1)}, u32[]{:S(2)}, u32[]{:S(2)}) collective-permute-start(bf16[2,128,128]{2,1,0:T(8,128)(2,1)S(1)} %collective-permute-done.refs_1_), channel_id=1, source_target_pairs={{0,3},{1,2},{2,1},{3,0},{4,7},{5,6},{6,5},{7,4},{8,11},{9,10},{10,... | collective-permute-start | bytes 196616 | tf_op jit(solution)/shard_map/ppermute | solution.py:22
  11.0 1.1 %collective-permute-start.5 = (bf16[2,128,128]{2,1,0:T(8,128)(2,1)S(1)}, bf16[2,128,128]{2,1,0:T(8,128)(2,1)S(1)}, u32[]{:S(2)}, u32[]{:S(2)}) collective-permute-start(bf16[2,128,128]{2,1,0:T(8,128)(2,1)S(1)} %collective-permute-done.refs_1_), channel_id=1, source_target_pairs={{0,2},{1,3},{2,0},{3,1},{4,6},{5,7},{6,4},{7,5},{8,10},{9,11},{10,... | collective-permute-start | bytes 196616 | tf_op jit(solution)/shard_map/ppermute | solution.py:22
  12.1 0.5 collective-permute-start.4
  12.6 1.5 %prepare.1 = (s32[2,32]{1,0:T(2,128)S(1)}, f32[2,32]{1,0:T(2,128)S(1)}, bf16[2,24,128,128]{3,2,1,0:T(8,128)(2,1)S(1)}) custom-call(s32[2,32]{1,0:T(2,128)} %bitcast.15, s32[2,32]{1,0:T(2,128)} %bitcast.16, f32[2,32]{1,0:T(2,128)} %bitcast.17, bf16[2,24,128,128]{3,2,1,0:T(8,128)(2,1)} %bitcast.14), custom_call_target="tpu_custom_call" | custom-call | tf_op jit(solution)/shard_map/prepare/pallas_call | solution.py:273
  14.1 0.7 %collective-permute-done.6.refs_7_ = bf16[2,128,128]{2,1,0:T(8,128)(2,1)S(1)} collective-permute-done((bf16[2,128,128]{2,1,0:T(8,128)(2,1)S(1)}, bf16[2,128,128]{2,1,0:T(8,128)(2,1)S(1)}, u32[]{:S(2)}, u32[]{:S(2)}) %collective-permute-start.6) | collective-permute-done | bytes 65568 | tf_op jit(solution)/shard_map/ppermute | solution.py:22
  14.8 0.6 %collective-permute-done.5.refs_6_ = bf16[2,128,128]{2,1,0:T(8,128)(2,1)S(1)} collective-permute-done((bf16[2,128,128]{2,1,0:T(8,128)(2,1)S(1)}, bf16[2,128,128]{2,1,0:T(8,128)(2,1)S(1)}, u32[]{:S(2)}, u32[]{:S(2)}) %collective-permute-start.5) | collective-permute-done | bytes 65568 | tf_op jit(solution)/shard_map/ppermute | solution.py:22
  15.5 0.9 %collective-permute-done.4.refs_5_ = bf16[2,128,128]{2,1,0:T(8,128)(2,1)S(1)} collective-permute-done((bf16[2,128,128]{2,1,0:T(8,128)(2,1)S(1)}, bf16[2,128,128]{2,1,0:T(8,128)(2,1)S(1)}, u32[]{:S(2)}, u32[]{:S(2)}) %collective-permute-start.4) | collective-permute-done | bytes 65568 | tf_op jit(solution)/shard_map/ppermute | solution.py:22
  16.4 2.0 %first_image.1.refs_8_ = bf16[2,128,128]{2,1,0:T(8,128)(2,1)S(1)} custom-call(s32[2,32]{1,0:T(2,128)S(1)} %get-tuple-element.14.codes, f32[2,32]{1,0:T(2,128)S(1)} %get-tuple-element.15.factors, bf16[2,24,128,128]{3,2,1,0:T(8,128)(2,1)S(1)} %get-tuple-element.16.left, bf16[2,24,128,128]{3,2,1,0:T(8,128)(2,1)S(1)} %collective-permute-done.7.right, ...), custom_call_target="tpu_custom_call" | custom-call | tf_op jit(solution)/shard_map/first_image/pallas_call | solution.py:294
  18.4 2.4 %collective-permute-start.8 = (bf16[2,128,128]{2,1,0:T(8,128)(2,1)S(1)}, bf16[2,128,128]{2,1,0:T(8,128)(2,1)S(1)}, u32[]{:S(2)}, u32[]{:S(2)}) collective-permute-start(bf16[2,128,128]{2,1,0:T(8,128)(2,1)S(1)} %first_image.1.refs_8_), channel_id=1, source_target_pairs={{0,4},{1,5},{2,6},{3,7},{4,0},{5,1},{6,2},{7,3},{8,12},{9,13},{10,... | collective-permute-start | bytes 196616 | tf_op jit(solution)/shard_map/ppermute | solution.py:22
  20.7 0.5 collective-permute-start.11
  21.2 2.0 %collective-permute-start.10 = (bf16[2,128,128]{2,1,0:T(8,128)(2,1)S(1)}, bf16[2,128,128]{2,1,0:T(8,128)(2,1)S(1)}, u32[]{:S(2)}, u32[]{:S(2)}) collective-permute-start(bf16[2,128,128]{2,1,0:T(8,128)(2,1)S(1)} %first_image.1.refs_8_), channel_id=1, source_target_pairs={{0,2},{1,3},{2,0},{3,1},{4,6},{5,7},{6,4},{7,5},{8,10},{9,11},{10,... | collective-permute-start | bytes 196616 | tf_op jit(solution)/shard_map/ppermute | solution.py:22
  23.2 1.0 %collective-permute-start.9 = (bf16[2,128,128]{2,1,0:T(8,128)(2,1)S(1)}, bf16[2,128,128]{2,1,0:T(8,128)(2,1)S(1)}, u32[]{:S(2)}, u32[]{:S(2)}) collective-permute-start(bf16[2,128,128]{2,1,0:T(8,128)(2,1)S(1)} %first_image.1.refs_8_), channel_id=1, source_target_pairs={{0,3},{1,2},{2,1},{3,0},{4,7},{5,6},{6,5},{7,4},{8,11},{9,10},{10,... | collective-permute-start | bytes 196616 | tf_op jit(solution)/shard_map/ppermute | solution.py:22
  24.2 2.0 %collective-permute-start.14 = (bf16[2,128,128]{2,1,0:T(8,128)(2,1)S(1)}, bf16[2,128,128]{2,1,0:T(8,128)(2,1)S(1)}, u32[]{:S(2)}, u32[]{:S(2)}) collective-permute-start(bf16[2,128,128]{2,1,0:T(8,128)(2,1)S(1)} %collective-permute-done.8.refs_9_), channel_id=1, source_target_pairs={{0,3},{1,2},{2,1},{3,0},{4,7},{5,6},{6,5},{7,4},{8,11},{9,10},{10,... | collective-permute-start | bytes 196616 | tf_op jit(solution)/shard_map/ppermute | solution.py:22
  26.2 0.0 collective-permute-start.13
  26.2 1.5 %collective-permute-start.12 = (bf16[2,128,128]{2,1,0:T(8,128)(2,1)S(1)}, bf16[2,128,128]{2,1,0:T(8,128)(2,1)S(1)}, u32[]{:S(2)}, u32[]{:S(2)}) collective-permute-start(bf16[2,128,128]{2,1,0:T(8,128)(2,1)S(1)} %collective-permute-done.8.refs_9_), channel_id=1, source_target_pairs={{0,1},{1,0},{2,3},{3,2},{4,5},{5,4},{6,7},{7,6},{8,9},{9,8},{10,11... | collective-permute-start | bytes 196616 | tf_op jit(solution)/shard_map/ppermute | solution.py:22
  27.7 1.0 %collective-permute-done.9.refs_10_ = bf16[2,128,128]{2,1,0:T(8,128)(2,1)S(1)} collective-permute-done((bf16[2,128,128]{2,1,0:T(8,128)(2,1)S(1)}, bf16[2,128,128]{2,1,0:T(8,128)(2,1)S(1)}, u32[]{:S(2)}, u32[]{:S(2)}) %collective-permute-start.9) | collective-permute-done | bytes 65568 | tf_op jit(solution)/shard_map/ppermute | solution.py:22
  28.7 0.1 early_sums.2.early
  28.8 0.0 copy-start.1
  28.8 0.5 collective-permute-done.14.refs_15_
  29.4 1.1 %collective-permute-done.13.refs_14_ = bf16[2,128,128]{2,1,0:T(8,128)(2,1)S(1)} collective-permute-done((bf16[2,128,128]{2,1,0:T(8,128)(2,1)S(1)}, bf16[2,128,128]{2,1,0:T(8,128)(2,1)S(1)}, u32[]{:S(2)}, u32[]{:S(2)}) %collective-permute-start.13) | collective-permute-done | bytes 65568 | tf_op jit(solution)/shard_map/ppermute | solution.py:22
  30.4 0.0 collective-permute-done.12.refs_13_
  30.5 2.2 %middle_image.1 = (f32[1,128]{1,0:T(1,128)S(1)}, f32[16,128,128]{2,1,0:T(8,128)S(1)}, bf16[2,128,128]{2,1,0:T(8,128)(2,1)S(1)}) custom-call(f32[2,8,128]{2,1,0:T(8,128)S(1)} %early_sums.2.early, s32[2,32]{1,0:T(2,128)S(1)} %get-tuple-element.14.codes, f32[2,32]{1,0:T(2,128)S(1)} %get-tuple-element.15.factors, ...), custom_call_target="tpu_custom_call" | custom-call | tf_op jit(solution)/shard_map/middle_image/pallas_call | solution.py:318
  32.7 2.2 %collective-permute-start.15 = (bf16[2,128,128]{2,1,0:T(8,128)(2,1)S(1)}, bf16[2,128,128]{2,1,0:T(8,128)(2,1)S(1)}, u32[]{:S(2)}, u32[]{:S(2)}) collective-permute-start(bf16[2,128,128]{2,1,0:T(8,128)(2,1)S(1)} %get-tuple-element.18.refs_1_), channel_id=1, source_target_pairs={{0,4},{1,5},{2,6},{3,7},{4,0},{5,1},{6,2},{7,3},{8,12},{9,13},{10,... | collective-permute-start | bytes 196616 | tf_op jit(solution)/shard_map/ppermute | solution.py:22
  34.9 1.6 %collective-permute-start.18 = (bf16[2,128,128]{2,1,0:T(8,128)(2,1)S(1)}, bf16[2,128,128]{2,1,0:T(8,128)(2,1)S(1)}, u32[]{:S(2)}, u32[]{:S(2)}) collective-permute-start(bf16[2,128,128]{2,1,0:T(8,128)(2,1)S(1)} %get-tuple-element.18.refs_1_), channel_id=1, source_target_pairs={{0,1},{1,0},{2,3},{3,2},{4,5},{5,4},{6,7},{7,6},{8,9},{9,8},{10,11... | collective-permute-start | bytes 196616 | tf_op jit(solution)/shard_map/ppermute | solution.py:22
  36.5 1.9 %collective-permute-start.17 = (bf16[2,128,128]{2,1,0:T(8,128)(2,1)S(1)}, bf16[2,128,128]{2,1,0:T(8,128)(2,1)S(1)}, u32[]{:S(2)}, u32[]{:S(2)}) collective-permute-start(bf16[2,128,128]{2,1,0:T(8,128)(2,1)S(1)} %get-tuple-element.18.refs_1_), channel_id=1, source_target_pairs={{0,2},{1,3},{2,0},{3,1},{4,6},{5,7},{6,4},{7,5},{8,10},{9,11},{10,... | collective-permute-start | bytes 196616 | tf_op jit(solution)/shard_map/ppermute | solution.py:22
  38.4 3.1 %collective-permute-start.21 = (bf16[2,128,128]{2,1,0:T(8,128)(2,1)S(1)}, bf16[2,128,128]{2,1,0:T(8,128)(2,1)S(1)}, u32[]{:S(2)}, u32[]{:S(2)}) collective-permute-start(bf16[2,128,128]{2,1,0:T(8,128)(2,1)S(1)} %collective-permute-done.15.refs_2_), channel_id=1, source_target_pairs={{0,3},{1,2},{2,1},{3,0},{4,7},{5,6},{6,5},{7,4},{8,11},{9,10},{10,... | collective-permute-start | bytes 196616 | tf_op jit(solution)/shard_map/ppermute | solution.py:22
  41.5 0.6 collective-permute-start.19
  42.0 1.5 %collective-permute-done.16.refs_3_ = bf16[2,128,128]{2,1,0:T(8,128)(2,1)S(1)} collective-permute-done((bf16[2,128,128]{2,1,0:T(8,128)(2,1)S(1)}, bf16[2,128,128]{2,1,0:T(8,128)(2,1)S(1)}, u32[]{:S(2)}, u32[]{:S(2)}) %collective-permute-start.16) | collective-permute-done | bytes 65568 | tf_op jit(solution)/shard_map/ppermute | solution.py:22
  43.5 0.1 early_sums.3.early
  43.7 0.6 collective-permute-done.21.refs_8_
  44.2 1.5 %collective-permute-done.20.refs_7_ = bf16[2,128,128]{2,1,0:T(8,128)(2,1)S(1)} collective-permute-done((bf16[2,128,128]{2,1,0:T(8,128)(2,1)S(1)}, bf16[2,128,128]{2,1,0:T(8,128)(2,1)S(1)}, u32[]{:S(2)}, u32[]{:S(2)}) %collective-permute-start.20) | collective-permute-done | bytes 65568 | tf_op jit(solution)/shard_map/ppermute | solution.py:22
  45.7 0.0 collective-permute-done.19.refs_6_
  45.7 2.5 %last_image.1 = (f32[1,128]{1,0:T(1,128)S(1)}, f32[2,128,128]{2,1,0:T(8,128)S(1)}, bf16[2,128,128]{2,1,0:T(8,128)(2,1)S(1)}, f32[1,8,128]{2,1,0:T(8,128)S(1)}) custom-call(f32[2,8,128]{2,1,0:T(8,128)S(1)} %early_sums.3.early, s32[2,32]{1,0:T(2,128)S(1)} %get-tuple-element.14.codes, f32[2,32]{1,0:T(2,128)S(1)} %get-tuple-element.15.factors, ...), custom_call_target="tpu_custom_call" | custom-call | tf_op jit(solution)/shard_map/last_image/pallas_call | solution.py:330
  48.2 0.1 collective-permute-start.22
  48.3 2.0 %collective-permute-start.25 = (f32[1,8,128]{2,1,0:T(8,128)S(1)}, f32[1,8,128]{2,1,0:T(8,128)S(1)}, u32[]{:S(2)}, u32[]{:S(2)}) collective-permute-start(f32[1,8,128]{2,1,0:T(8,128)S(1)} %get-tuple-element.23), channel_id=1, source_target_pairs={{0,11},{1,10},{2,9},{3,8},{4,15},{5,14},{6,13},{7,12},{8,3},{9,2},... | collective-permute-start | bytes 12296 | tf_op jit(solution)/shard_map/ppermute | solution.py:36
  50.3 0.2 collective-permute-start.24
  50.4 1.2 %collective-permute-start.23 = (f32[1,8,128]{2,1,0:T(8,128)S(1)}, f32[1,8,128]{2,1,0:T(8,128)S(1)}, u32[]{:S(2)}, u32[]{:S(2)}) collective-permute-start(f32[1,8,128]{2,1,0:T(8,128)S(1)} %get-tuple-element.23), channel_id=1, source_target_pairs={{0,9},{1,8},{2,11},{3,10},{4,13},{5,12},{6,15},{7,14},{8,1},{9,0},... | collective-permute-start | bytes 12296 | tf_op jit(solution)/shard_map/ppermute | solution.py:36
  51.6 1.8 %collective-permute-done.23 = f32[1,8,128]{2,1,0:T(8,128)S(1)} collective-permute-done((f32[1,8,128]{2,1,0:T(8,128)S(1)}, f32[1,8,128]{2,1,0:T(8,128)S(1)}, u32[]{:S(2)}, u32[]{:S(2)}) %collective-permute-start.23) | collective-permute-done | bytes 4128 | tf_op jit(solution)/shard_map/ppermute | solution.py:36
  53.5 1.9 %collective-permute-start.27 = (f32[4,8,128]{2,1,0:T(8,128)S(1)}, f32[4,8,128]{2,1,0:T(8,128)S(1)}, u32[]{:S(2)}, u32[]{:S(2)}) collective-permute-start(f32[4,8,128]{2,1,0:T(8,128)S(1)} %constant_dynamic-update-slice_fusion), channel_id=1, source_target_pairs={{0,12},{1,13},{2,14},{3,15},{4,8},{5,9},{6,10},{7,11},{8,4},{9,5},... | collective-permute-start | bytes 49160 | tf_op jit(solution)/shard_map/ppermute | solution.py:36
  55.4 0.4 collective-permute-start.26
  55.7 1.9 %collective-permute-done.27.refs_3_ = f32[4,8,128]{2,1,0:T(8,128)S(1)} collective-permute-done((f32[4,8,128]{2,1,0:T(8,128)S(1)}, f32[4,8,128]{2,1,0:T(8,128)S(1)}, u32[]{:S(2)}, u32[]{:S(2)}) %collective-permute-start.27) | collective-permute-done | bytes 16416 | tf_op jit(solution)/shard_map/ppermute | solution.py:36
  57.6 0.7 %finish.1 = (f32[1,3]{1,0:T(1,128)}, bf16[2,128,128]{2,1,0:T(8,128)(2,1)}) custom-call(f32[2,128,128]{2,1,0:T(8,128)S(1)} %get-tuple-element.19.own, bf16[2,128,128]{2,1,0:T(8,128)(2,1)S(1)} %get-tuple-element.20.image, f32[1,128]{1,0:T(1,128)S(1)} %get-tuple-element.21.refs_0_, f32[1,128]{1,0:T(1,128)S(1)} %get-tuple-element.22.refs_1_, ...), custom_call_target="tpu_custom_call" | custom-call | tf_op jit(solution)/shard_map/finish/pallas_call | solution.py:349
  (23 shorter events, 0.1 us)
Async XLA Ops:
  0.6 15.7 %copy-start = (bf16[1,2,128,128]{3,2,1,0:T(8,128)(2,1)S(1)}, bf16[1,2,128,128]{3,2,1,0:T(8,128)(2,1)}, u32[]{:S(2)}) copy-start(bf16[1,2,128,128]{3,2,1,0:T(8,128)(2,1)} %param.7) | copy-start | bytes 196612
  0.6 15.7 %collective-permute-start.7 = (bf16[2,24,128,128]{3,2,1,0:T(8,128)(2,1)}, bf16[2,24,128,128]{3,2,1,0:T(8,128)(2,1)S(1)}, u32[]{:S(2)}, u32[]{:S(2)}) collective-permute-start(bf16[2,24,128,128]{3,2,1,0:T(8,128)(2,1)} %bitcast.18), channel_id=1, source_target_pairs={{0,8},{8,0},{1,9},{9,1},{2,10},{10,2},{3,11},{11,3},{4,12},{12,4},... | collective-permute-start | bytes 4718600 | tf_op jit(solution)/shard_map/ppermute | solution.py:263
  1.2 8.0 %collective-permute-start = (bf16[2,128,128]{2,1,0:T(8,128)(2,1)}, bf16[2,128,128]{2,1,0:T(8,128)(2,1)S(1)}, u32[]{:S(2)}, u32[]{:S(2)}) collective-permute-start(bf16[2,128,128]{2,1,0:T(8,128)(2,1)} %bitcast.7), channel_id=1, source_target_pairs={{0,4},{1,5},{2,6},{3,7},{4,0},{5,1},{6,2},{7,3},{8,12},{9,13},{10,... | collective-permute-start | bytes 196616 | tf_op jit(solution)/shard_map/ppermute | solution.py:22
  4.8 6.1 %collective-permute-start.3 = (bf16[2,128,128]{2,1,0:T(8,128)(2,1)}, bf16[2,128,128]{2,1,0:T(8,128)(2,1)S(1)}, u32[]{:S(2)}, u32[]{:S(2)}) collective-permute-start(bf16[2,128,128]{2,1,0:T(8,128)(2,1)} %bitcast.8), channel_id=1, source_target_pairs={{0,1},{1,0},{2,3},{3,2},{4,5},{5,4},{6,7},{7,6},{8,9},{9,8},{10,11... | collective-permute-start | bytes 196616 | tf_op jit(solution)/shard_map/ppermute | solution.py:22
  6.3 5.7 %collective-permute-start.2 = (bf16[2,128,128]{2,1,0:T(8,128)(2,1)}, bf16[2,128,128]{2,1,0:T(8,128)(2,1)S(1)}, u32[]{:S(2)}, u32[]{:S(2)}) collective-permute-start(bf16[2,128,128]{2,1,0:T(8,128)(2,1)} %bitcast.9), channel_id=1, source_target_pairs={{0,2},{1,3},{2,0},{3,1},{4,6},{5,7},{6,4},{7,5},{8,10},{9,11},{10,... | collective-permute-start | bytes 196616 | tf_op jit(solution)/shard_map/ppermute | solution.py:22
  7.9 6.2 %collective-permute-start.1 = (bf16[2,128,128]{2,1,0:T(8,128)(2,1)}, bf16[2,128,128]{2,1,0:T(8,128)(2,1)S(1)}, u32[]{:S(2)}, u32[]{:S(2)}) collective-permute-start(bf16[2,128,128]{2,1,0:T(8,128)(2,1)} %bitcast.10), channel_id=1, source_target_pairs={{0,3},{1,2},{2,1},{3,0},{4,7},{5,6},{6,5},{7,4},{8,11},{9,10},{10,... | collective-permute-start | bytes 196616 | tf_op jit(solution)/shard_map/ppermute | solution.py:22
  9.1 5.7 %collective-permute-start.6 = (bf16[2,128,128]{2,1,0:T(8,128)(2,1)S(1)}, bf16[2,128,128]{2,1,0:T(8,128)(2,1)S(1)}, u32[]{:S(2)}, u32[]{:S(2)}) collective-permute-start(bf16[2,128,128]{2,1,0:T(8,128)(2,1)S(1)} %collective-permute-done.refs_1_), channel_id=1, source_target_pairs={{0,3},{1,2},{2,1},{3,0},{4,7},{5,6},{6,5},{7,4},{8,11},{9,10},{10,... | collective-permute-start | bytes 196616 | tf_op jit(solution)/shard_map/ppermute | solution.py:22
  11.0 4.5 %collective-permute-start.5 = (bf16[2,128,128]{2,1,0:T(8,128)(2,1)S(1)}, bf16[2,128,128]{2,1,0:T(8,128)(2,1)S(1)}, u32[]{:S(2)}, u32[]{:S(2)}) collective-permute-start(bf16[2,128,128]{2,1,0:T(8,128)(2,1)S(1)} %collective-permute-done.refs_1_), channel_id=1, source_target_pairs={{0,2},{1,3},{2,0},{3,1},{4,6},{5,7},{6,4},{7,5},{8,10},{9,11},{10,... | collective-permute-start | bytes 196616 | tf_op jit(solution)/shard_map/ppermute | solution.py:22
  12.1 4.3 %collective-permute-start.4 = (bf16[2,128,128]{2,1,0:T(8,128)(2,1)S(1)}, bf16[2,128,128]{2,1,0:T(8,128)(2,1)S(1)}, u32[]{:S(2)}, u32[]{:S(2)}) collective-permute-start(bf16[2,128,128]{2,1,0:T(8,128)(2,1)S(1)} %collective-permute-done.refs_1_), channel_id=1, source_target_pairs={{0,1},{1,0},{2,3},{3,2},{4,5},{5,4},{6,7},{7,6},{8,9},{9,8},{10,11... | collective-permute-start | bytes 196616 | tf_op jit(solution)/shard_map/ppermute | solution.py:22
  18.4 5.8 %collective-permute-start.8 = (bf16[2,128,128]{2,1,0:T(8,128)(2,1)S(1)}, bf16[2,128,128]{2,1,0:T(8,128)(2,1)S(1)}, u32[]{:S(2)}, u32[]{:S(2)}) collective-permute-start(bf16[2,128,128]{2,1,0:T(8,128)(2,1)S(1)} %first_image.1.refs_8_), channel_id=1, source_target_pairs={{0,4},{1,5},{2,6},{3,7},{4,0},{5,1},{6,2},{7,3},{8,12},{9,13},{10,... | collective-permute-start | bytes 196616 | tf_op jit(solution)/shard_map/ppermute | solution.py:22
  20.7 5.5 %collective-permute-start.11 = (bf16[2,128,128]{2,1,0:T(8,128)(2,1)S(1)}, bf16[2,128,128]{2,1,0:T(8,128)(2,1)S(1)}, u32[]{:S(2)}, u32[]{:S(2)}) collective-permute-start(bf16[2,128,128]{2,1,0:T(8,128)(2,1)S(1)} %first_image.1.refs_8_), channel_id=1, source_target_pairs={{0,1},{1,0},{2,3},{3,2},{4,5},{5,4},{6,7},{7,6},{8,9},{9,8},{10,11... | collective-permute-start | bytes 196616 | tf_op jit(solution)/shard_map/ppermute | solution.py:22
  21.2 6.5 %collective-permute-start.10 = (bf16[2,128,128]{2,1,0:T(8,128)(2,1)S(1)}, bf16[2,128,128]{2,1,0:T(8,128)(2,1)S(1)}, u32[]{:S(2)}, u32[]{:S(2)}) collective-permute-start(bf16[2,128,128]{2,1,0:T(8,128)(2,1)S(1)} %first_image.1.refs_8_), channel_id=1, source_target_pairs={{0,2},{1,3},{2,0},{3,1},{4,6},{5,7},{6,4},{7,5},{8,10},{9,11},{10,... | collective-permute-start | bytes 196616 | tf_op jit(solution)/shard_map/ppermute | solution.py:22
  23.2 5.4 %collective-permute-start.9 = (bf16[2,128,128]{2,1,0:T(8,128)(2,1)S(1)}, bf16[2,128,128]{2,1,0:T(8,128)(2,1)S(1)}, u32[]{:S(2)}, u32[]{:S(2)}) collective-permute-start(bf16[2,128,128]{2,1,0:T(8,128)(2,1)S(1)} %first_image.1.refs_8_), channel_id=1, source_target_pairs={{0,3},{1,2},{2,1},{3,0},{4,7},{5,6},{6,5},{7,4},{8,11},{9,10},{10,... | collective-permute-start | bytes 196616 | tf_op jit(solution)/shard_map/ppermute | solution.py:22
  24.2 5.2 %collective-permute-start.14 = (bf16[2,128,128]{2,1,0:T(8,128)(2,1)S(1)}, bf16[2,128,128]{2,1,0:T(8,128)(2,1)S(1)}, u32[]{:S(2)}, u32[]{:S(2)}) collective-permute-start(bf16[2,128,128]{2,1,0:T(8,128)(2,1)S(1)} %collective-permute-done.8.refs_9_), channel_id=1, source_target_pairs={{0,3},{1,2},{2,1},{3,0},{4,7},{5,6},{6,5},{7,4},{8,11},{9,10},{10,... | collective-permute-start | bytes 196616 | tf_op jit(solution)/shard_map/ppermute | solution.py:22
  26.2 4.3 %collective-permute-start.13 = (bf16[2,128,128]{2,1,0:T(8,128)(2,1)S(1)}, bf16[2,128,128]{2,1,0:T(8,128)(2,1)S(1)}, u32[]{:S(2)}, u32[]{:S(2)}) collective-permute-start(bf16[2,128,128]{2,1,0:T(8,128)(2,1)S(1)} %collective-permute-done.8.refs_9_), channel_id=1, source_target_pairs={{0,2},{1,3},{2,0},{3,1},{4,6},{5,7},{6,4},{7,5},{8,10},{9,11},{10,... | collective-permute-start | bytes 196616 | tf_op jit(solution)/shard_map/ppermute | solution.py:22
  26.2 4.3 %collective-permute-start.12 = (bf16[2,128,128]{2,1,0:T(8,128)(2,1)S(1)}, bf16[2,128,128]{2,1,0:T(8,128)(2,1)S(1)}, u32[]{:S(2)}, u32[]{:S(2)}) collective-permute-start(bf16[2,128,128]{2,1,0:T(8,128)(2,1)S(1)} %collective-permute-done.8.refs_9_), channel_id=1, source_target_pairs={{0,1},{1,0},{2,3},{3,2},{4,5},{5,4},{6,7},{7,6},{8,9},{9,8},{10,11... | collective-permute-start | bytes 196616 | tf_op jit(solution)/shard_map/ppermute | solution.py:22
  28.8 16.9 %copy-start.1 = (s32[1,2]{1,0:T(1,128)S(1)}, s32[1,2]{1,0:T(1,128)}, u32[]{:S(2)}) copy-start(s32[1,2]{1,0:T(1,128)} %ranks.1) | copy-start | bytes 28
  32.7 5.7 %collective-permute-start.15 = (bf16[2,128,128]{2,1,0:T(8,128)(2,1)S(1)}, bf16[2,128,128]{2,1,0:T(8,128)(2,1)S(1)}, u32[]{:S(2)}, u32[]{:S(2)}) collective-permute-start(bf16[2,128,128]{2,1,0:T(8,128)(2,1)S(1)} %get-tuple-element.18.refs_1_), channel_id=1, source_target_pairs={{0,4},{1,5},{2,6},{3,7},{4,0},{5,1},{6,2},{7,3},{8,12},{9,13},{10,... | collective-permute-start | bytes 196616 | tf_op jit(solution)/shard_map/ppermute | solution.py:22
  34.9 6.6 %collective-permute-start.18 = (bf16[2,128,128]{2,1,0:T(8,128)(2,1)S(1)}, bf16[2,128,128]{2,1,0:T(8,128)(2,1)S(1)}, u32[]{:S(2)}, u32[]{:S(2)}) collective-permute-start(bf16[2,128,128]{2,1,0:T(8,128)(2,1)S(1)} %get-tuple-element.18.refs_1_), channel_id=1, source_target_pairs={{0,1},{1,0},{2,3},{3,2},{4,5},{5,4},{6,7},{7,6},{8,9},{9,8},{10,11... | collective-permute-start | bytes 196616 | tf_op jit(solution)/shard_map/ppermute | solution.py:22
  36.5 5.6 %collective-permute-start.17 = (bf16[2,128,128]{2,1,0:T(8,128)(2,1)S(1)}, bf16[2,128,128]{2,1,0:T(8,128)(2,1)S(1)}, u32[]{:S(2)}, u32[]{:S(2)}) collective-permute-start(bf16[2,128,128]{2,1,0:T(8,128)(2,1)S(1)} %get-tuple-element.18.refs_1_), channel_id=1, source_target_pairs={{0,2},{1,3},{2,0},{3,1},{4,6},{5,7},{6,4},{7,5},{8,10},{9,11},{10,... | collective-permute-start | bytes 196616 | tf_op jit(solution)/shard_map/ppermute | solution.py:22
  38.4 5.2 %collective-permute-start.16 = (bf16[2,128,128]{2,1,0:T(8,128)(2,1)S(1)}, bf16[2,128,128]{2,1,0:T(8,128)(2,1)S(1)}, u32[]{:S(2)}, u32[]{:S(2)}) collective-permute-start(bf16[2,128,128]{2,1,0:T(8,128)(2,1)S(1)} %get-tuple-element.18.refs_1_), channel_id=1, source_target_pairs={{0,3},{1,2},{2,1},{3,0},{4,7},{5,6},{6,5},{7,4},{8,11},{9,10},{10,... | collective-permute-start | bytes 196616 | tf_op jit(solution)/shard_map/ppermute | solution.py:22
  38.4 5.9 %collective-permute-start.21 = (bf16[2,128,128]{2,1,0:T(8,128)(2,1)S(1)}, bf16[2,128,128]{2,1,0:T(8,128)(2,1)S(1)}, u32[]{:S(2)}, u32[]{:S(2)}) collective-permute-start(bf16[2,128,128]{2,1,0:T(8,128)(2,1)S(1)} %collective-permute-done.15.refs_2_), channel_id=1, source_target_pairs={{0,3},{1,2},{2,1},{3,0},{4,7},{5,6},{6,5},{7,4},{8,11},{9,10},{10,... | collective-permute-start | bytes 196616 | tf_op jit(solution)/shard_map/ppermute | solution.py:22
  41.4 4.3 %collective-permute-start.20 = (bf16[2,128,128]{2,1,0:T(8,128)(2,1)S(1)}, bf16[2,128,128]{2,1,0:T(8,128)(2,1)S(1)}, u32[]{:S(2)}, u32[]{:S(2)}) collective-permute-start(bf16[2,128,128]{2,1,0:T(8,128)(2,1)S(1)} %collective-permute-done.15.refs_2_), channel_id=1, source_target_pairs={{0,2},{1,3},{2,0},{3,1},{4,6},{5,7},{6,4},{7,5},{8,10},{9,11},{10,... | collective-permute-start | bytes 196616 | tf_op jit(solution)/shard_map/ppermute | solution.py:22
  41.5 4.3 %collective-permute-start.19 = (bf16[2,128,128]{2,1,0:T(8,128)(2,1)S(1)}, bf16[2,128,128]{2,1,0:T(8,128)(2,1)S(1)}, u32[]{:S(2)}, u32[]{:S(2)}) collective-permute-start(bf16[2,128,128]{2,1,0:T(8,128)(2,1)S(1)} %collective-permute-done.15.refs_2_), channel_id=1, source_target_pairs={{0,1},{1,0},{2,3},{3,2},{4,5},{5,4},{6,7},{7,6},{8,9},{9,8},{10,11... | collective-permute-start | bytes 196616 | tf_op jit(solution)/shard_map/ppermute | solution.py:22
  48.2 3.4 %collective-permute-start.22 = (f32[1,8,128]{2,1,0:T(8,128)S(1)}, f32[1,8,128]{2,1,0:T(8,128)S(1)}, u32[]{:S(2)}, u32[]{:S(2)}) collective-permute-start(f32[1,8,128]{2,1,0:T(8,128)S(1)} %get-tuple-element.23), channel_id=1, source_target_pairs={{0,8},{1,9},{2,10},{3,11},{4,12},{5,13},{6,14},{7,15},{8,0},{9,1},... | collective-permute-start | bytes 12296 | tf_op jit(solution)/shard_map/ppermute | solution.py:36
  48.3 5.2 %collective-permute-start.25 = (f32[1,8,128]{2,1,0:T(8,128)S(1)}, f32[1,8,128]{2,1,0:T(8,128)S(1)}, u32[]{:S(2)}, u32[]{:S(2)}) collective-permute-start(f32[1,8,128]{2,1,0:T(8,128)S(1)} %get-tuple-element.23), channel_id=1, source_target_pairs={{0,11},{1,10},{2,9},{3,8},{4,15},{5,14},{6,13},{7,12},{8,3},{9,2},... | collective-permute-start | bytes 12296 | tf_op jit(solution)/shard_map/ppermute | solution.py:36
  50.3 3.2 %collective-permute-start.24 = (f32[1,8,128]{2,1,0:T(8,128)S(1)}, f32[1,8,128]{2,1,0:T(8,128)S(1)}, u32[]{:S(2)}, u32[]{:S(2)}) collective-permute-start(f32[1,8,128]{2,1,0:T(8,128)S(1)} %get-tuple-element.23), channel_id=1, source_target_pairs={{0,10},{1,11},{2,8},{3,9},{4,14},{5,15},{6,12},{7,13},{8,2},{9,3},... | collective-permute-start | bytes 12296 | tf_op jit(solution)/shard_map/ppermute | solution.py:36
  50.4 3.0 %collective-permute-start.23 = (f32[1,8,128]{2,1,0:T(8,128)S(1)}, f32[1,8,128]{2,1,0:T(8,128)S(1)}, u32[]{:S(2)}, u32[]{:S(2)}) collective-permute-start(f32[1,8,128]{2,1,0:T(8,128)S(1)} %get-tuple-element.23), channel_id=1, source_target_pairs={{0,9},{1,8},{2,11},{3,10},{4,13},{5,12},{6,15},{7,14},{8,1},{9,0},... | collective-permute-start | bytes 12296 | tf_op jit(solution)/shard_map/ppermute | solution.py:36
  53.5 4.1 %collective-permute-start.27 = (f32[4,8,128]{2,1,0:T(8,128)S(1)}, f32[4,8,128]{2,1,0:T(8,128)S(1)}, u32[]{:S(2)}, u32[]{:S(2)}) collective-permute-start(f32[4,8,128]{2,1,0:T(8,128)S(1)} %constant_dynamic-update-slice_fusion), channel_id=1, source_target_pairs={{0,12},{1,13},{2,14},{3,15},{4,8},{5,9},{6,10},{7,11},{8,4},{9,5},... | collective-permute-start | bytes 49160 | tf_op jit(solution)/shard_map/ppermute | solution.py:36
  55.4 2.2 %collective-permute-start.26 = (f32[4,8,128]{2,1,0:T(8,128)S(1)}, f32[4,8,128]{2,1,0:T(8,128)S(1)}, u32[]{:S(2)}, u32[]{:S(2)}) collective-permute-start(f32[4,8,128]{2,1,0:T(8,128)S(1)} %constant_dynamic-update-slice_fusion), channel_id=1, source_target_pairs={{0,8},{1,9},{2,10},{3,11},{4,12},{5,13},{6,14},{7,15},{8,0},{9,1},... | collective-permute-start | bytes 49160 | tf_op jit(solution)/shard_map/ppermute | solution.py:36

commit v10 on v9

--- a/solution.py
+++ b/solution.py
@@ -114,6 +114,7 @@
 
 def apply_operator(codes, factors, state, left, right, mixed, image):
     blocks, width = left.shape[0], left.shape[1]
+    nothing = jnp.zeros(image.shape[1:], jnp.bfloat16)
     for t in range(blocks):
         mixed[t][...] = jnp.zeros_like(mixed[t])
     for t in range(blocks):
@@ -121,12 +122,16 @@
     for t in range(blocks):
         result = jnp.zeros(image.shape[1:], jnp.float32)
         for w in range(0, width, 2):
-            halves = [
-                jnp.dot(left[t, v], mixed[t][v], preferred_element_type=jnp.float32).astype(jnp.bfloat16)
-                for v in (w, w + 1)
-            ]
+            pair = jnp.concatenate([left[t, w], left[t, w + 1]], axis=1)
+            apart = jnp.concatenate(
+                [
+                    jnp.concatenate([mixed[t][w], nothing], axis=1),
+                    jnp.concatenate([nothing, mixed[t][w + 1]], axis=1),
+                ],
+                axis=0,
+            )
             result += lax.dot_general(
-                jnp.concatenate(halves, axis=1),
+                jnp.dot(pair, apart, preferred_element_type=jnp.float32).astype(jnp.bfloat16),
                 jnp.concatenate([right[t, w], right[t, w + 1]], axis=1),
                 (((1,), (1,)), ((), ())),
                 preferred_element_type=jnp.float32,

time: 58.5 us -> 58.2 us (level)
  no operation moved by 1% of the time
where the time goes in v10:
time: 58.2 us; the launch traced here: 58 us
  starting transfers between devices  35.5 us (61%)
  waiting for transfers between devices  12.9 us (22%)
  Pallas kernels  8.88 us (15%)
  between operations  0.74 us (1%)
    ppermute x21, starting transfers between devices, hop(): return lax.ppermute(block, 'sec', [(a, a ^ distance) for a in range(count)])  29.3 us
    ppermute x21, waiting for transfers between devices, hop(): return lax.ppermute(block, 'sec', [(a, a ^ distance) for a in range(count)])  9.2 us
    ppermute x6, starting transfers between devices, cross(): return lax.ppermute(block, ('seg', 'sec'), route)  5.66 us
    ppermute x6, waiting for transfers between devices, cross(): return lax.ppermute(block, ('seg', 'sec'), route)  3.7 us
    pallas_call x1, Pallas kernels, local(): pl.pallas_call(functools.partial(last_kernel, len(states), len(images)),...  2.39 us
    pallas_call x1, Pallas kernels, local(): pl.pallas_call(functools.partial(middle_kernel, len(states), len(images))...  2.1 us
    pallas_call x1, Pallas kernels, local(): pl.pallas_call(functools.partial(first_kernel, len(states)), out_shape=ow...  1.92 us
    pallas_call x1, Pallas kernels, local(): pl.pallas_call(functools.partial(prepare_kernel, devices), out_shape=(int...  1.49 us
  transfers between devices with their start and end apart: 28, of which 12 were waited for; matrix products, arithmetic and copies ran while one was open for 0% of the time, Pallas kernels for 3%

profile of v10, /device:TPU:0, one launch (start us, length us, event | category | flops | bytes accessed | tf_op | source)
XLA Modules:
  0.0 58.0 jit_solution(3323456666945235389)
XLA Ops:
  0.6 0.5 collective-permute-start.7
  1.2 3.7 %collective-permute-start = (bf16[2,128,128]{2,1,0:T(8,128)(2,1)}, bf16[2,128,128]{2,1,0:T(8,128)(2,1)S(1)}, u32[]{:S(2)}, u32[]{:S(2)}) collective-permute-start(bf16[2,128,128]{2,1,0:T(8,128)(2,1)} %bitcast.7), channel_id=1, source_target_pairs={{0,4},{1,5},{2,6},{3,7},{4,0},{5,1},{6,2},{7,3},{8,12},{9,13},{10,... | collective-permute-start | bytes 196616 | tf_op jit(solution)/shard_map/ppermute | solution.py:22
  4.8 1.5 %collective-permute-start.3 = (bf16[2,128,128]{2,1,0:T(8,128)(2,1)}, bf16[2,128,128]{2,1,0:T(8,128)(2,1)S(1)}, u32[]{:S(2)}, u32[]{:S(2)}) collective-permute-start(bf16[2,128,128]{2,1,0:T(8,128)(2,1)} %bitcast.8), channel_id=1, source_target_pairs={{0,1},{1,0},{2,3},{3,2},{4,5},{5,4},{6,7},{7,6},{8,9},{9,8},{10,11... | collective-permute-start | bytes 196616 | tf_op jit(solution)/shard_map/ppermute | solution.py:22
  6.3 1.6 %collective-permute-start.2 = (bf16[2,128,128]{2,1,0:T(8,128)(2,1)}, bf16[2,128,128]{2,1,0:T(8,128)(2,1)S(1)}, u32[]{:S(2)}, u32[]{:S(2)}) collective-permute-start(bf16[2,128,128]{2,1,0:T(8,128)(2,1)} %bitcast.9), channel_id=1, source_target_pairs={{0,2},{1,3},{2,0},{3,1},{4,6},{5,7},{6,4},{7,5},{8,10},{9,11},{10,... | collective-permute-start | bytes 196616 | tf_op jit(solution)/shard_map/ppermute | solution.py:22
  7.9 0.4 collective-permute-start.1
  8.3 0.8 %collective-permute-done.refs_1_ = bf16[2,128,128]{2,1,0:T(8,128)(2,1)S(1)} collective-permute-done((bf16[2,128,128]{2,1,0:T(8,128)(2,1)}, bf16[2,128,128]{2,1,0:T(8,128)(2,1)S(1)}, u32[]{:S(2)}, u32[]{:S(2)}) %collective-permute-start) | collective-permute-done | bytes 65568 | tf_op jit(solution)/shard_map/ppermute | solution.py:22
  9.1 1.8 %collective-permute-start.6 = (bf16[2,128,128]{2,1,0:T(8,128)(2,1)S(1)}, bf16[2,128,128]{2,1,0:T(8,128)(2,1)S(1)}, u32[]{:S(2)}, u32[]{:S(2)}) collective-permute-start(bf16[2,128,128]{2,1,0:T(8,128)(2,1)S(1)} %collective-permute-done.refs_1_), channel_id=1, source_target_pairs={{0,3},{1,2},{2,1},{3,0},{4,7},{5,6},{6,5},{7,4},{8,11},{9,10},{10,... | collective-permute-start | bytes 196616 | tf_op jit(solution)/shard_map/ppermute | solution.py:22
  11.0 1.1 %collective-permute-start.5 = (bf16[2,128,128]{2,1,0:T(8,128)(2,1)S(1)}, bf16[2,128,128]{2,1,0:T(8,128)(2,1)S(1)}, u32[]{:S(2)}, u32[]{:S(2)}) collective-permute-start(bf16[2,128,128]{2,1,0:T(8,128)(2,1)S(1)} %collective-permute-done.refs_1_), channel_id=1, source_target_pairs={{0,2},{1,3},{2,0},{3,1},{4,6},{5,7},{6,4},{7,5},{8,10},{9,11},{10,... | collective-permute-start | bytes 196616 | tf_op jit(solution)/shard_map/ppermute | solution.py:22
  12.1 0.5 collective-permute-start.4
  12.6 1.5 %prepare.1 = (s32[2,32]{1,0:T(2,128)S(1)}, f32[2,32]{1,0:T(2,128)S(1)}, bf16[2,24,128,128]{3,2,1,0:T(8,128)(2,1)S(1)}) custom-call(s32[2,32]{1,0:T(2,128)} %bitcast.15, s32[2,32]{1,0:T(2,128)} %bitcast.16, f32[2,32]{1,0:T(2,128)} %bitcast.17, bf16[2,24,128,128]{3,2,1,0:T(8,128)(2,1)} %bitcast.14), custom_call_target="tpu_custom_call" | custom-call | tf_op jit(solution)/shard_map/prepare/pallas_call | solution.py:278
  14.1 0.7 %collective-permute-done.6.refs_7_ = bf16[2,128,128]{2,1,0:T(8,128)(2,1)S(1)} collective-permute-done((bf16[2,128,128]{2,1,0:T(8,128)(2,1)S(1)}, bf16[2,128,128]{2,1,0:T(8,128)(2,1)S(1)}, u32[]{:S(2)}, u32[]{:S(2)}) %collective-permute-start.6) | collective-permute-done | bytes 65568 | tf_op jit(solution)/shard_map/ppermute | solution.py:22
  14.8 0.6 %collective-permute-done.5.refs_6_ = bf16[2,128,128]{2,1,0:T(8,128)(2,1)S(1)} collective-permute-done((bf16[2,128,128]{2,1,0:T(8,128)(2,1)S(1)}, bf16[2,128,128]{2,1,0:T(8,128)(2,1)S(1)}, u32[]{:S(2)}, u32[]{:S(2)}) %collective-permute-start.5) | collective-permute-done | bytes 65568 | tf_op jit(solution)/shard_map/ppermute | solution.py:22
  15.5 0.9 %collective-permute-done.4.refs_5_ = bf16[2,128,128]{2,1,0:T(8,128)(2,1)S(1)} collective-permute-done((bf16[2,128,128]{2,1,0:T(8,128)(2,1)S(1)}, bf16[2,128,128]{2,1,0:T(8,128)(2,1)S(1)}, u32[]{:S(2)}, u32[]{:S(2)}) %collective-permute-start.4) | collective-permute-done | bytes 65568 | tf_op jit(solution)/shard_map/ppermute | solution.py:22
  16.4 1.9 %first_image.1.refs_8_ = bf16[2,128,128]{2,1,0:T(8,128)(2,1)S(1)} custom-call(s32[2,32]{1,0:T(2,128)S(1)} %get-tuple-element.14.codes, f32[2,32]{1,0:T(2,128)S(1)} %get-tuple-element.15.factors, bf16[2,24,128,128]{3,2,1,0:T(8,128)(2,1)S(1)} %get-tuple-element.16.left, bf16[2,24,128,128]{3,2,1,0:T(8,128)(2,1)S(1)} %collective-permute-done.7.right, ...), custom_call_target="tpu_custom_call" | custom-call | tf_op jit(solution)/shard_map/first_image/pallas_call | solution.py:299
  18.3 2.4 %collective-permute-start.8 = (bf16[2,128,128]{2,1,0:T(8,128)(2,1)S(1)}, bf16[2,128,128]{2,1,0:T(8,128)(2,1)S(1)}, u32[]{:S(2)}, u32[]{:S(2)}) collective-permute-start(bf16[2,128,128]{2,1,0:T(8,128)(2,1)S(1)} %first_image.1.refs_8_), channel_id=1, source_target_pairs={{0,4},{1,5},{2,6},{3,7},{4,0},{5,1},{6,2},{7,3},{8,12},{9,13},{10,... | collective-permute-start | bytes 196616 | tf_op jit(solution)/shard_map/ppermute | solution.py:22
  20.6 0.5 collective-permute-start.11
  21.1 2.0 %collective-permute-start.10 = (bf16[2,128,128]{2,1,0:T(8,128)(2,1)S(1)}, bf16[2,128,128]{2,1,0:T(8,128)(2,1)S(1)}, u32[]{:S(2)}, u32[]{:S(2)}) collective-permute-start(bf16[2,128,128]{2,1,0:T(8,128)(2,1)S(1)} %first_image.1.refs_8_), channel_id=1, source_target_pairs={{0,2},{1,3},{2,0},{3,1},{4,6},{5,7},{6,4},{7,5},{8,10},{9,11},{10,... | collective-permute-start | bytes 196616 | tf_op jit(solution)/shard_map/ppermute | solution.py:22
  23.2 1.0 %collective-permute-start.9 = (bf16[2,128,128]{2,1,0:T(8,128)(2,1)S(1)}, bf16[2,128,128]{2,1,0:T(8,128)(2,1)S(1)}, u32[]{:S(2)}, u32[]{:S(2)}) collective-permute-start(bf16[2,128,128]{2,1,0:T(8,128)(2,1)S(1)} %first_image.1.refs_8_), channel_id=1, source_target_pairs={{0,3},{1,2},{2,1},{3,0},{4,7},{5,6},{6,5},{7,4},{8,11},{9,10},{10,... | collective-permute-start | bytes 196616 | tf_op jit(solution)/shard_map/ppermute | solution.py:22
  24.1 2.0 %collective-permute-start.14 = (bf16[2,128,128]{2,1,0:T(8,128)(2,1)S(1)}, bf16[2,128,128]{2,1,0:T(8,128)(2,1)S(1)}, u32[]{:S(2)}, u32[]{:S(2)}) collective-permute-start(bf16[2,128,128]{2,1,0:T(8,128)(2,1)S(1)} %collective-permute-done.8.refs_9_), channel_id=1, source_target_pairs={{0,3},{1,2},{2,1},{3,0},{4,7},{5,6},{6,5},{7,4},{8,11},{9,10},{10,... | collective-permute-start | bytes 196616 | tf_op jit(solution)/shard_map/ppermute | solution.py:22
  26.1 0.0 collective-permute-start.13
  26.1 1.5 %collective-permute-start.12 = (bf16[2,128,128]{2,1,0:T(8,128)(2,1)S(1)}, bf16[2,128,128]{2,1,0:T(8,128)(2,1)S(1)}, u32[]{:S(2)}, u32[]{:S(2)}) collective-permute-start(bf16[2,128,128]{2,1,0:T(8,128)(2,1)S(1)} %collective-permute-done.8.refs_9_), channel_id=1, source_target_pairs={{0,1},{1,0},{2,3},{3,2},{4,5},{5,4},{6,7},{7,6},{8,9},{9,8},{10,11... | collective-permute-start | bytes 196616 | tf_op jit(solution)/shard_map/ppermute | solution.py:22
  27.6 1.0 %collective-permute-done.9.refs_10_ = bf16[2,128,128]{2,1,0:T(8,128)(2,1)S(1)} collective-permute-done((bf16[2,128,128]{2,1,0:T(8,128)(2,1)S(1)}, bf16[2,128,128]{2,1,0:T(8,128)(2,1)S(1)}, u32[]{:S(2)}, u32[]{:S(2)}) %collective-permute-start.9) | collective-permute-done | bytes 65568 | tf_op jit(solution)/shard_map/ppermute | solution.py:22
  28.6 0.1 early_sums.2.early
  28.7 0.0 copy-start.1
  28.8 0.5 collective-permute-done.14.refs_15_
  29.3 1.1 %collective-permute-done.13.refs_14_ = bf16[2,128,128]{2,1,0:T(8,128)(2,1)S(1)} collective-permute-done((bf16[2,128,128]{2,1,0:T(8,128)(2,1)S(1)}, bf16[2,128,128]{2,1,0:T(8,128)(2,1)S(1)}, u32[]{:S(2)}, u32[]{:S(2)}) %collective-permute-start.13) | collective-permute-done | bytes 65568 | tf_op jit(solution)/shard_map/ppermute | solution.py:22
  30.4 0.0 collective-permute-done.12.refs_13_
  30.4 2.1 %middle_image.1 = (f32[1,128]{1,0:T(1,128)S(1)}, f32[16,128,128]{2,1,0:T(8,128)S(1)}, bf16[2,128,128]{2,1,0:T(8,128)(2,1)S(1)}) custom-call(f32[2,8,128]{2,1,0:T(8,128)S(1)} %early_sums.2.early, s32[2,32]{1,0:T(2,128)S(1)} %get-tuple-element.14.codes, f32[2,32]{1,0:T(2,128)S(1)} %get-tuple-element.15.factors, ...), custom_call_target="tpu_custom_call" | custom-call | tf_op jit(solution)/shard_map/middle_image/pallas_call | solution.py:323
  32.5 2.2 %collective-permute-start.15 = (bf16[2,128,128]{2,1,0:T(8,128)(2,1)S(1)}, bf16[2,128,128]{2,1,0:T(8,128)(2,1)S(1)}, u32[]{:S(2)}, u32[]{:S(2)}) collective-permute-start(bf16[2,128,128]{2,1,0:T(8,128)(2,1)S(1)} %get-tuple-element.18.refs_1_), channel_id=1, source_target_pairs={{0,4},{1,5},{2,6},{3,7},{4,0},{5,1},{6,2},{7,3},{8,12},{9,13},{10,... | collective-permute-start | bytes 196616 | tf_op jit(solution)/shard_map/ppermute | solution.py:22
  34.7 1.6 %collective-permute-start.18 = (bf16[2,128,128]{2,1,0:T(8,128)(2,1)S(1)}, bf16[2,128,128]{2,1,0:T(8,128)(2,1)S(1)}, u32[]{:S(2)}, u32[]{:S(2)}) collective-permute-start(bf16[2,128,128]{2,1,0:T(8,128)(2,1)S(1)} %get-tuple-element.18.refs_1_), channel_id=1, source_target_pairs={{0,1},{1,0},{2,3},{3,2},{4,5},{5,4},{6,7},{7,6},{8,9},{9,8},{10,11... | collective-permute-start | bytes 196616 | tf_op jit(solution)/shard_map/ppermute | solution.py:22
  36.3 1.9 %collective-permute-start.17 = (bf16[2,128,128]{2,1,0:T(8,128)(2,1)S(1)}, bf16[2,128,128]{2,1,0:T(8,128)(2,1)S(1)}, u32[]{:S(2)}, u32[]{:S(2)}) collective-permute-start(bf16[2,128,128]{2,1,0:T(8,128)(2,1)S(1)} %get-tuple-element.18.refs_1_), channel_id=1, source_target_pairs={{0,2},{1,3},{2,0},{3,1},{4,6},{5,7},{6,4},{7,5},{8,10},{9,11},{10,... | collective-permute-start | bytes 196616 | tf_op jit(solution)/shard_map/ppermute | solution.py:22
  38.2 3.1 %collective-permute-start.21 = (bf16[2,128,128]{2,1,0:T(8,128)(2,1)S(1)}, bf16[2,128,128]{2,1,0:T(8,128)(2,1)S(1)}, u32[]{:S(2)}, u32[]{:S(2)}) collective-permute-start(bf16[2,128,128]{2,1,0:T(8,128)(2,1)S(1)} %collective-permute-done.15.refs_2_), channel_id=1, source_target_pairs={{0,3},{1,2},{2,1},{3,0},{4,7},{5,6},{6,5},{7,4},{8,11},{9,10},{10,... | collective-permute-start | bytes 196616 | tf_op jit(solution)/shard_map/ppermute | solution.py:22
  41.2 0.6 collective-permute-start.19
  41.8 1.5 %collective-permute-done.16.refs_3_ = bf16[2,128,128]{2,1,0:T(8,128)(2,1)S(1)} collective-permute-done((bf16[2,128,128]{2,1,0:T(8,128)(2,1)S(1)}, bf16[2,128,128]{2,1,0:T(8,128)(2,1)S(1)}, u32[]{:S(2)}, u32[]{:S(2)}) %collective-permute-start.16) | collective-permute-done | bytes 65568 | tf_op jit(solution)/shard_map/ppermute | solution.py:22
  43.3 0.1 early_sums.3.early
  43.5 0.6 collective-permute-done.21.refs_8_
  44.0 1.5 %collective-permute-done.20.refs_7_ = bf16[2,128,128]{2,1,0:T(8,128)(2,1)S(1)} collective-permute-done((bf16[2,128,128]{2,1,0:T(8,128)(2,1)S(1)}, bf16[2,128,128]{2,1,0:T(8,128)(2,1)S(1)}, u32[]{:S(2)}, u32[]{:S(2)}) %collective-permute-start.20) | collective-permute-done | bytes 65568 | tf_op jit(solution)/shard_map/ppermute | solution.py:22
  45.5 0.0 collective-permute-done.19.refs_6_
  45.5 2.4 %last_image.1 = (f32[1,128]{1,0:T(1,128)S(1)}, f32[2,128,128]{2,1,0:T(8,128)S(1)}, bf16[2,128,128]{2,1,0:T(8,128)(2,1)S(1)}, f32[1,8,128]{2,1,0:T(8,128)S(1)}) custom-call(f32[2,8,128]{2,1,0:T(8,128)S(1)} %early_sums.3.early, s32[2,32]{1,0:T(2,128)S(1)} %get-tuple-element.14.codes, f32[2,32]{1,0:T(2,128)S(1)} %get-tuple-element.15.factors, ...), custom_call_target="tpu_custom_call" | custom-call | tf_op jit(solution)/shard_map/last_image/pallas_call | solution.py:335
  47.9 0.1 collective-permute-start.22
  48.0 2.0 %collective-permute-start.25 = (f32[1,8,128]{2,1,0:T(8,128)S(1)}, f32[1,8,128]{2,1,0:T(8,128)S(1)}, u32[]{:S(2)}, u32[]{:S(2)}) collective-permute-start(f32[1,8,128]{2,1,0:T(8,128)S(1)} %get-tuple-element.23), channel_id=1, source_target_pairs={{0,11},{1,10},{2,9},{3,8},{4,15},{5,14},{6,13},{7,12},{8,3},{9,2},... | collective-permute-start | bytes 12296 | tf_op jit(solution)/shard_map/ppermute | solution.py:36
  50.0 0.2 collective-permute-start.24
  50.1 1.2 %collective-permute-start.23 = (f32[1,8,128]{2,1,0:T(8,128)S(1)}, f32[1,8,128]{2,1,0:T(8,128)S(1)}, u32[]{:S(2)}, u32[]{:S(2)}) collective-permute-start(f32[1,8,128]{2,1,0:T(8,128)S(1)} %get-tuple-element.23), channel_id=1, source_target_pairs={{0,9},{1,8},{2,11},{3,10},{4,13},{5,12},{6,15},{7,14},{8,1},{9,0},... | collective-permute-start | bytes 12296 | tf_op jit(solution)/shard_map/ppermute | solution.py:36
  51.3 1.8 %collective-permute-done.23 = f32[1,8,128]{2,1,0:T(8,128)S(1)} collective-permute-done((f32[1,8,128]{2,1,0:T(8,128)S(1)}, f32[1,8,128]{2,1,0:T(8,128)S(1)}, u32[]{:S(2)}, u32[]{:S(2)}) %collective-permute-start.23) | collective-permute-done | bytes 4128 | tf_op jit(solution)/shard_map/ppermute | solution.py:36
  53.2 1.9 %collective-permute-start.27 = (f32[4,8,128]{2,1,0:T(8,128)S(1)}, f32[4,8,128]{2,1,0:T(8,128)S(1)}, u32[]{:S(2)}, u32[]{:S(2)}) collective-permute-start(f32[4,8,128]{2,1,0:T(8,128)S(1)} %constant_dynamic-update-slice_fusion), channel_id=1, source_target_pairs={{0,12},{1,13},{2,14},{3,15},{4,8},{5,9},{6,10},{7,11},{8,4},{9,5},... | collective-permute-start | bytes 49160 | tf_op jit(solution)/shard_map/ppermute | solution.py:36
  55.1 0.4 collective-permute-start.26
  55.4 1.9 %collective-permute-done.27.refs_3_ = f32[4,8,128]{2,1,0:T(8,128)S(1)} collective-permute-done((f32[4,8,128]{2,1,0:T(8,128)S(1)}, f32[4,8,128]{2,1,0:T(8,128)S(1)}, u32[]{:S(2)}, u32[]{:S(2)}) %collective-permute-start.27) | collective-permute-done | bytes 16416 | tf_op jit(solution)/shard_map/ppermute | solution.py:36
  57.3 0.7 %finish.1 = (f32[1,3]{1,0:T(1,128)}, bf16[2,128,128]{2,1,0:T(8,128)(2,1)}) custom-call(f32[2,128,128]{2,1,0:T(8,128)S(1)} %get-tuple-element.19.own, bf16[2,128,128]{2,1,0:T(8,128)(2,1)S(1)} %get-tuple-element.20.image, f32[1,128]{1,0:T(1,128)S(1)} %get-tuple-element.21.refs_0_, f32[1,128]{1,0:T(1,128)S(1)} %get-tuple-element.22.refs_1_, ...), custom_call_target="tpu_custom_call" | custom-call | tf_op jit(solution)/shard_map/finish/pallas_call | solution.py:354
  (23 shorter events, 0.1 us)
Async XLA Ops:
  0.6 15.7 %copy-start = (bf16[1,2,128,128]{3,2,1,0:T(8,128)(2,1)S(1)}, bf16[1,2,128,128]{3,2,1,0:T(8,128)(2,1)}, u32[]{:S(2)}) copy-start(bf16[1,2,128,128]{3,2,1,0:T(8,128)(2,1)} %param.7) | copy-start | bytes 196612
  0.6 15.7 %collective-permute-start.7 = (bf16[2,24,128,128]{3,2,1,0:T(8,128)(2,1)}, bf16[2,24,128,128]{3,2,1,0:T(8,128)(2,1)S(1)}, u32[]{:S(2)}, u32[]{:S(2)}) collective-permute-start(bf16[2,24,128,128]{3,2,1,0:T(8,128)(2,1)} %bitcast.18), channel_id=1, source_target_pairs={{0,8},{8,0},{1,9},{9,1},{2,10},{10,2},{3,11},{11,3},{4,12},{12,4},... | collective-permute-start | bytes 4718600 | tf_op jit(solution)/shard_map/ppermute | solution.py:268
  1.2 8.0 %collective-permute-start = (bf16[2,128,128]{2,1,0:T(8,128)(2,1)}, bf16[2,128,128]{2,1,0:T(8,128)(2,1)S(1)}, u32[]{:S(2)}, u32[]{:S(2)}) collective-permute-start(bf16[2,128,128]{2,1,0:T(8,128)(2,1)} %bitcast.7), channel_id=1, source_target_pairs={{0,4},{1,5},{2,6},{3,7},{4,0},{5,1},{6,2},{7,3},{8,12},{9,13},{10,... | collective-permute-start | bytes 196616 | tf_op jit(solution)/shard_map/ppermute | solution.py:22
  4.8 6.1 %collective-permute-start.3 = (bf16[2,128,128]{2,1,0:T(8,128)(2,1)}, bf16[2,128,128]{2,1,0:T(8,128)(2,1)S(1)}, u32[]{:S(2)}, u32[]{:S(2)}) collective-permute-start(bf16[2,128,128]{2,1,0:T(8,128)(2,1)} %bitcast.8), channel_id=1, source_target_pairs={{0,1},{1,0},{2,3},{3,2},{4,5},{5,4},{6,7},{7,6},{8,9},{9,8},{10,11... | collective-permute-start | bytes 196616 | tf_op jit(solution)/shard_map/ppermute | solution.py:22
  6.3 5.7 %collective-permute-start.2 = (bf16[2,128,128]{2,1,0:T(8,128)(2,1)}, bf16[2,128,128]{2,1,0:T(8,128)(2,1)S(1)}, u32[]{:S(2)}, u32[]{:S(2)}) collective-permute-start(bf16[2,128,128]{2,1,0:T(8,128)(2,1)} %bitcast.9), channel_id=1, source_target_pairs={{0,2},{1,3},{2,0},{3,1},{4,6},{5,7},{6,4},{7,5},{8,10},{9,11},{10,... | collective-permute-start | bytes 196616 | tf_op jit(solution)/shard_map/ppermute | solution.py:22
  7.9 6.2 %collective-permute-start.1 = (bf16[2,128,128]{2,1,0:T(8,128)(2,1)}, bf16[2,128,128]{2,1,0:T(8,128)(2,1)S(1)}, u32[]{:S(2)}, u32[]{:S(2)}) collective-permute-start(bf16[2,128,128]{2,1,0:T(8,128)(2,1)} %bitcast.10), channel_id=1, source_target_pairs={{0,3},{1,2},{2,1},{3,0},{4,7},{5,6},{6,5},{7,4},{8,11},{9,10},{10,... | collective-permute-start | bytes 196616 | tf_op jit(solution)/shard_map/ppermute | solution.py:22
  9.1 5.7 %collective-permute-start.6 = (bf16[2,128,128]{2,1,0:T(8,128)(2,1)S(1)}, bf16[2,128,128]{2,1,0:T(8,128)(2,1)S(1)}, u32[]{:S(2)}, u32[]{:S(2)}) collective-permute-start(bf16[2,128,128]{2,1,0:T(8,128)(2,1)S(1)} %collective-permute-done.refs_1_), channel_id=1, source_target_pairs={{0,3},{1,2},{2,1},{3,0},{4,7},{5,6},{6,5},{7,4},{8,11},{9,10},{10,... | collective-permute-start | bytes 196616 | tf_op jit(solution)/shard_map/ppermute | solution.py:22
  11.0 4.5 %collective-permute-start.5 = (bf16[2,128,128]{2,1,0:T(8,128)(2,1)S(1)}, bf16[2,128,128]{2,1,0:T(8,128)(2,1)S(1)}, u32[]{:S(2)}, u32[]{:S(2)}) collective-permute-start(bf16[2,128,128]{2,1,0:T(8,128)(2,1)S(1)} %collective-permute-done.refs_1_), channel_id=1, source_target_pairs={{0,2},{1,3},{2,0},{3,1},{4,6},{5,7},{6,4},{7,5},{8,10},{9,11},{10,... | collective-permute-start | bytes 196616 | tf_op jit(solution)/shard_map/ppermute | solution.py:22
  12.1 4.3 %collective-permute-start.4 = (bf16[2,128,128]{2,1,0:T(8,128)(2,1)S(1)}, bf16[2,128,128]{2,1,0:T(8,128)(2,1)S(1)}, u32[]{:S(2)}, u32[]{:S(2)}) collective-permute-start(bf16[2,128,128]{2,1,0:T(8,128)(2,1)S(1)} %collective-permute-done.refs_1_), channel_id=1, source_target_pairs={{0,1},{1,0},{2,3},{3,2},{4,5},{5,4},{6,7},{7,6},{8,9},{9,8},{10,11... | collective-permute-start | bytes 196616 | tf_op jit(solution)/shard_map/ppermute | solution.py:22
  18.3 5.8 %collective-permute-start.8 = (bf16[2,128,128]{2,1,0:T(8,128)(2,1)S(1)}, bf16[2,128,128]{2,1,0:T(8,128)(2,1)S(1)}, u32[]{:S(2)}, u32[]{:S(2)}) collective-permute-start(bf16[2,128,128]{2,1,0:T(8,128)(2,1)S(1)} %first_image.1.refs_8_), channel_id=1, source_target_pairs={{0,4},{1,5},{2,6},{3,7},{4,0},{5,1},{6,2},{7,3},{8,12},{9,13},{10,... | collective-permute-start | bytes 196616 | tf_op jit(solution)/shard_map/ppermute | solution.py:22
  20.6 5.5 %collective-permute-start.11 = (bf16[2,128,128]{2,1,0:T(8,128)(2,1)S(1)}, bf16[2,128,128]{2,1,0:T(8,128)(2,1)S(1)}, u32[]{:S(2)}, u32[]{:S(2)}) collective-permute-start(bf16[2,128,128]{2,1,0:T(8,128)(2,1)S(1)} %first_image.1.refs_8_), channel_id=1, source_target_pairs={{0,1},{1,0},{2,3},{3,2},{4,5},{5,4},{6,7},{7,6},{8,9},{9,8},{10,11... | collective-permute-start | bytes 196616 | tf_op jit(solution)/shard_map/ppermute | solution.py:22
  21.1 6.5 %collective-permute-start.10 = (bf16[2,128,128]{2,1,0:T(8,128)(2,1)S(1)}, bf16[2,128,128]{2,1,0:T(8,128)(2,1)S(1)}, u32[]{:S(2)}, u32[]{:S(2)}) collective-permute-start(bf16[2,128,128]{2,1,0:T(8,128)(2,1)S(1)} %first_image.1.refs_8_), channel_id=1, source_target_pairs={{0,2},{1,3},{2,0},{3,1},{4,6},{5,7},{6,4},{7,5},{8,10},{9,11},{10,... | collective-permute-start | bytes 196616 | tf_op jit(solution)/shard_map/ppermute | solution.py:22
  23.2 5.4 %collective-permute-start.9 = (bf16[2,128,128]{2,1,0:T(8,128)(2,1)S(1)}, bf16[2,128,128]{2,1,0:T(8,128)(2,1)S(1)}, u32[]{:S(2)}, u32[]{:S(2)}) collective-permute-start(bf16[2,128,128]{2,1,0:T(8,128)(2,1)S(1)} %first_image.1.refs_8_), channel_id=1, source_target_pairs={{0,3},{1,2},{2,1},{3,0},{4,7},{5,6},{6,5},{7,4},{8,11},{9,10},{10,... | collective-permute-start | bytes 196616 | tf_op jit(solution)/shard_map/ppermute | solution.py:22
  24.1 5.2 %collective-permute-start.14 = (bf16[2,128,128]{2,1,0:T(8,128)(2,1)S(1)}, bf16[2,128,128]{2,1,0:T(8,128)(2,1)S(1)}, u32[]{:S(2)}, u32[]{:S(2)}) collective-permute-start(bf16[2,128,128]{2,1,0:T(8,128)(2,1)S(1)} %collective-permute-done.8.refs_9_), channel_id=1, source_target_pairs={{0,3},{1,2},{2,1},{3,0},{4,7},{5,6},{6,5},{7,4},{8,11},{9,10},{10,... | collective-permute-start | bytes 196616 | tf_op jit(solution)/shard_map/ppermute | solution.py:22
  26.1 4.3 %collective-permute-start.13 = (bf16[2,128,128]{2,1,0:T(8,128)(2,1)S(1)}, bf16[2,128,128]{2,1,0:T(8,128)(2,1)S(1)}, u32[]{:S(2)}, u32[]{:S(2)}) collective-permute-start(bf16[2,128,128]{2,1,0:T(8,128)(2,1)S(1)} %collective-permute-done.8.refs_9_), channel_id=1, source_target_pairs={{0,2},{1,3},{2,0},{3,1},{4,6},{5,7},{6,4},{7,5},{8,10},{9,11},{10,... | collective-permute-start | bytes 196616 | tf_op jit(solution)/shard_map/ppermute | solution.py:22
  26.1 4.3 %collective-permute-start.12 = (bf16[2,128,128]{2,1,0:T(8,128)(2,1)S(1)}, bf16[2,128,128]{2,1,0:T(8,128)(2,1)S(1)}, u32[]{:S(2)}, u32[]{:S(2)}) collective-permute-start(bf16[2,128,128]{2,1,0:T(8,128)(2,1)S(1)} %collective-permute-done.8.refs_9_), channel_id=1, source_target_pairs={{0,1},{1,0},{2,3},{3,2},{4,5},{5,4},{6,7},{7,6},{8,9},{9,8},{10,11... | collective-permute-start | bytes 196616 | tf_op jit(solution)/shard_map/ppermute | solution.py:22
  28.7 16.8 %copy-start.1 = (s32[1,2]{1,0:T(1,128)S(1)}, s32[1,2]{1,0:T(1,128)}, u32[]{:S(2)}) copy-start(s32[1,2]{1,0:T(1,128)} %ranks.1) | copy-start | bytes 28
  32.5 5.7 %collective-permute-start.15 = (bf16[2,128,128]{2,1,0:T(8,128)(2,1)S(1)}, bf16[2,128,128]{2,1,0:T(8,128)(2,1)S(1)}, u32[]{:S(2)}, u32[]{:S(2)}) collective-permute-start(bf16[2,128,128]{2,1,0:T(8,128)(2,1)S(1)} %get-tuple-element.18.refs_1_), channel_id=1, source_target_pairs={{0,4},{1,5},{2,6},{3,7},{4,0},{5,1},{6,2},{7,3},{8,12},{9,13},{10,... | collective-permute-start | bytes 196616 | tf_op jit(solution)/shard_map/ppermute | solution.py:22
  34.7 6.6 %collective-permute-start.18 = (bf16[2,128,128]{2,1,0:T(8,128)(2,1)S(1)}, bf16[2,128,128]{2,1,0:T(8,128)(2,1)S(1)}, u32[]{:S(2)}, u32[]{:S(2)}) collective-permute-start(bf16[2,128,128]{2,1,0:T(8,128)(2,1)S(1)} %get-tuple-element.18.refs_1_), channel_id=1, source_target_pairs={{0,1},{1,0},{2,3},{3,2},{4,5},{5,4},{6,7},{7,6},{8,9},{9,8},{10,11... | collective-permute-start | bytes 196616 | tf_op jit(solution)/shard_map/ppermute | solution.py:22
  36.3 5.5 %collective-permute-start.17 = (bf16[2,128,128]{2,1,0:T(8,128)(2,1)S(1)}, bf16[2,128,128]{2,1,0:T(8,128)(2,1)S(1)}, u32[]{:S(2)}, u32[]{:S(2)}) collective-permute-start(bf16[2,128,128]{2,1,0:T(8,128)(2,1)S(1)} %get-tuple-element.18.refs_1_), channel_id=1, source_target_pairs={{0,2},{1,3},{2,0},{3,1},{4,6},{5,7},{6,4},{7,5},{8,10},{9,11},{10,... | collective-permute-start | bytes 196616 | tf_op jit(solution)/shard_map/ppermute | solution.py:22
  38.2 5.2 %collective-permute-start.16 = (bf16[2,128,128]{2,1,0:T(8,128)(2,1)S(1)}, bf16[2,128,128]{2,1,0:T(8,128)(2,1)S(1)}, u32[]{:S(2)}, u32[]{:S(2)}) collective-permute-start(bf16[2,128,128]{2,1,0:T(8,128)(2,1)S(1)} %get-tuple-element.18.refs_1_), channel_id=1, source_target_pairs={{0,3},{1,2},{2,1},{3,0},{4,7},{5,6},{6,5},{7,4},{8,11},{9,10},{10,... | collective-permute-start | bytes 196616 | tf_op jit(solution)/shard_map/ppermute | solution.py:22
  38.2 5.9 %collective-permute-start.21 = (bf16[2,128,128]{2,1,0:T(8,128)(2,1)S(1)}, bf16[2,128,128]{2,1,0:T(8,128)(2,1)S(1)}, u32[]{:S(2)}, u32[]{:S(2)}) collective-permute-start(bf16[2,128,128]{2,1,0:T(8,128)(2,1)S(1)} %collective-permute-done.15.refs_2_), channel_id=1, source_target_pairs={{0,3},{1,2},{2,1},{3,0},{4,7},{5,6},{6,5},{7,4},{8,11},{9,10},{10,... | collective-permute-start | bytes 196616 | tf_op jit(solution)/shard_map/ppermute | solution.py:22
  41.2 4.3 %collective-permute-start.20 = (bf16[2,128,128]{2,1,0:T(8,128)(2,1)S(1)}, bf16[2,128,128]{2,1,0:T(8,128)(2,1)S(1)}, u32[]{:S(2)}, u32[]{:S(2)}) collective-permute-start(bf16[2,128,128]{2,1,0:T(8,128)(2,1)S(1)} %collective-permute-done.15.refs_2_), channel_id=1, source_target_pairs={{0,2},{1,3},{2,0},{3,1},{4,6},{5,7},{6,4},{7,5},{8,10},{9,11},{10,... | collective-permute-start | bytes 196616 | tf_op jit(solution)/shard_map/ppermute | solution.py:22
  41.2 4.3 %collective-permute-start.19 = (bf16[2,128,128]{2,1,0:T(8,128)(2,1)S(1)}, bf16[2,128,128]{2,1,0:T(8,128)(2,1)S(1)}, u32[]{:S(2)}, u32[]{:S(2)}) collective-permute-start(bf16[2,128,128]{2,1,0:T(8,128)(2,1)S(1)} %collective-permute-done.15.refs_2_), channel_id=1, source_target_pairs={{0,1},{1,0},{2,3},{3,2},{4,5},{5,4},{6,7},{7,6},{8,9},{9,8},{10,11... | collective-permute-start | bytes 196616 | tf_op jit(solution)/shard_map/ppermute | solution.py:22
  47.9 3.4 %collective-permute-start.22 = (f32[1,8,128]{2,1,0:T(8,128)S(1)}, f32[1,8,128]{2,1,0:T(8,128)S(1)}, u32[]{:S(2)}, u32[]{:S(2)}) collective-permute-start(f32[1,8,128]{2,1,0:T(8,128)S(1)} %get-tuple-element.23), channel_id=1, source_target_pairs={{0,8},{1,9},{2,10},{3,11},{4,12},{5,13},{6,14},{7,15},{8,0},{9,1},... | collective-permute-start | bytes 12296 | tf_op jit(solution)/shard_map/ppermute | solution.py:36
  48.0 5.2 %collective-permute-start.25 = (f32[1,8,128]{2,1,0:T(8,128)S(1)}, f32[1,8,128]{2,1,0:T(8,128)S(1)}, u32[]{:S(2)}, u32[]{:S(2)}) collective-permute-start(f32[1,8,128]{2,1,0:T(8,128)S(1)} %get-tuple-element.23), channel_id=1, source_target_pairs={{0,11},{1,10},{2,9},{3,8},{4,15},{5,14},{6,13},{7,12},{8,3},{9,2},... | collective-permute-start | bytes 12296 | tf_op jit(solution)/shard_map/ppermute | solution.py:36
  50.0 3.2 %collective-permute-start.24 = (f32[1,8,128]{2,1,0:T(8,128)S(1)}, f32[1,8,128]{2,1,0:T(8,128)S(1)}, u32[]{:S(2)}, u32[]{:S(2)}) collective-permute-start(f32[1,8,128]{2,1,0:T(8,128)S(1)} %get-tuple-element.23), channel_id=1, source_target_pairs={{0,10},{1,11},{2,8},{3,9},{4,14},{5,15},{6,12},{7,13},{8,2},{9,3},... | collective-permute-start | bytes 12296 | tf_op jit(solution)/shard_map/ppermute | solution.py:36
  50.1 3.0 %collective-permute-start.23 = (f32[1,8,128]{2,1,0:T(8,128)S(1)}, f32[1,8,128]{2,1,0:T(8,128)S(1)}, u32[]{:S(2)}, u32[]{:S(2)}) collective-permute-start(f32[1,8,128]{2,1,0:T(8,128)S(1)} %get-tuple-element.23), channel_id=1, source_target_pairs={{0,9},{1,8},{2,11},{3,10},{4,13},{5,12},{6,15},{7,14},{8,1},{9,0},... | collective-permute-start | bytes 12296 | tf_op jit(solution)/shard_map/ppermute | solution.py:36
  53.2 4.1 %collective-permute-start.27 = (f32[4,8,128]{2,1,0:T(8,128)S(1)}, f32[4,8,128]{2,1,0:T(8,128)S(1)}, u32[]{:S(2)}, u32[]{:S(2)}) collective-permute-start(f32[4,8,128]{2,1,0:T(8,128)S(1)} %constant_dynamic-update-slice_fusion), channel_id=1, source_target_pairs={{0,12},{1,13},{2,14},{3,15},{4,8},{5,9},{6,10},{7,11},{8,4},{9,5},... | collective-permute-start | bytes 49160 | tf_op jit(solution)/shard_map/ppermute | solution.py:36
  55.1 2.2 %collective-permute-start.26 = (f32[4,8,128]{2,1,0:T(8,128)S(1)}, f32[4,8,128]{2,1,0:T(8,128)S(1)}, u32[]{:S(2)}, u32[]{:S(2)}) collective-permute-start(f32[4,8,128]{2,1,0:T(8,128)S(1)} %constant_dynamic-update-slice_fusion), channel_id=1, source_target_pairs={{0,8},{1,9},{2,10},{3,11},{4,12},{5,13},{6,14},{7,15},{8,0},{9,1},... | collective-permute-start | bytes 49160 | tf_op jit(solution)/shard_map/ppermute | solution.py:36
